TPU v7x, 256 devices: a whole 4x4x8 slice. The times are simulated.
256 devices in a mesh: dom: 64 (over z, x, core), feat: 4 (over y).
Axes of the slice: x: 4, y: 4, z: 8, core: 2. Of those that a mesh axis runs over, the one named last changes fastest.
Arguments:
- feats: bfloat16 [16384, 1024], P('dom', 'feat'), may hold values from -16 to 16
- weight: bfloat16 [1024, 1024], P('feat', 'dom'), may hold values from -0.1875 to 0.1875
- bias: float32 [1024], P('feat'), may hold values from -3 to 3
- tile_values: bfloat16 [8192, 128, 128], P('dom'), may hold values from 0 to 10, as said below
- tile_rows: int32 [8192], P('dom'), may hold values from 0 to 1
- tile_cols: int32 [8192], P('dom'), may hold values from 0 to 127
- tile_live: int32 [64], P('dom'), may hold values from 0 to 128, as said below
- cotangent: bfloat16 [16384, 1024], P('dom', 'feat'), may hold values from -6 to 6
Outputs:
- output: bfloat16 [16384, 1024], P('dom', 'feat')
- feats_grad: bfloat16 [16384, 1024], P('dom', 'feat')
- weight_grad: float32 [1024, 1024], P('feat', 'dom')
- bias_grad: float32 [1024], P('feat')
Inputs may be any that keep to these rules, and one draw needn't show every extreme that they name: `tile_live`: device d and device d + 32 have at most 128 live slots together. Live slots are a device's first ones. `tile_values`: nonnegative edge weights.
All inputs are finite; a program needn't handle non-finite values.
Results may differ from a plain program's by a relative error of at most 0.0061.
Values may be sent and summed in bfloat16 or wider, within the bound.
No kernel may reach another device: no remote copies, remote signals or barrier semaphores. Data moves between devices by JAX's collectives and lax.ppermute only.
A program may use at most 128 MiB of HBM per device.

v0:
```python
import jax
import jax.numpy as jnp
from jax import lax
from jax.sharding import PartitionSpec as P


def silu_parts(hidden):
    gate_value = jax.nn.sigmoid(hidden)
    return (hidden * gate_value, gate_value * (1.0 + hidden * (1.0 - gate_value)))


def on_device(feats, weight, bias, tile_values, tile_rows, tile_cols, tile_live, cotangent):
    tile_size = tile_values.shape[1]
    slot_count = tile_values.shape[0]
    row_count = feats.shape[0]
    row_blocks = row_count // tile_size
    width_dev = feats.shape[1]
    live_count = tile_live[0]
    own_live = jnp.arange(slot_count, dtype=jnp.int32) < live_count
    row_sums = jnp.sum(tile_values, axis=2, dtype=jnp.float32)
    degree_ids = jnp.where(own_live, tile_rows, row_blocks)
    degree = 1.0 + jax.ops.segment_sum(row_sums, degree_ids, num_segments=row_blocks).reshape(
        row_count, 1
    )
    gathered = lax.all_gather(feats, "dom", axis=0, tiled=True)
    feat_blocks = gathered.reshape(-1, tile_size, width_dev)
    picked = jnp.take(feat_blocks, tile_cols, axis=0)
    terms = jnp.einsum("sij,sjf->sif", tile_values, picked, preferred_element_type=jnp.float32)
    neighbour_sum = jax.ops.segment_sum(terms, degree_ids, num_segments=row_blocks)
    mixed = (
        (feats.astype(jnp.float32) + neighbour_sum.reshape(row_count, width_dev)) / degree
    ).astype(jnp.bfloat16)
    weight_full = lax.all_gather(weight, "dom", axis=1, tiled=True)
    partial_hidden = jnp.dot(mixed, weight_full, preferred_element_type=jnp.float32)
    hidden = lax.psum_scatter(partial_hidden, "feat", scatter_dimension=1, tiled=True) + bias
    activated, slope = silu_parts(hidden)
    output = activated.astype(jnp.bfloat16)
    dz_full = cotangent.astype(jnp.float32) * slope
    bias_grad = lax.psum(jnp.sum(dz_full, axis=0), "dom")
    dz_local = dz_full.astype(jnp.bfloat16)
    dz_all = lax.all_gather(dz_local, "feat", axis=1, tiled=True)
    weight_part = lax.dot_general(
        mixed, dz_all, (((0,), (0,)), ((), ())), preferred_element_type=jnp.float32
    )
    weight_grad = lax.psum_scatter(weight_part, "dom", scatter_dimension=1, tiled=True)
    dmixed = lax.dot_general(
        dz_all, weight_full, (((1,), (1,)), ((), ())), preferred_element_type=jnp.float32
    )
    scaled = (dmixed / degree).astype(jnp.bfloat16)
    grad_blocks = scaled.reshape(row_blocks, tile_size, width_dev)
    back_terms = jnp.einsum(
        "sji,sjf->sif",
        tile_values,
        jnp.take(grad_blocks, tile_rows, axis=0),
        preferred_element_type=jnp.float32,
    )
    live_cols = jnp.where(own_live, tile_cols, -1)
    segment_count = row_count * lax.axis_size("dom") // tile_size
    local_ids = live_cols
    inside = (local_ids >= 0) & (local_ids < segment_count)
    local_ids = jnp.where(inside, local_ids, segment_count)
    column_sum = lax.psum_scatter(
        jax.ops.segment_sum(back_terms, local_ids, num_segments=segment_count).reshape(
            row_count * lax.axis_size("dom"), width_dev
        ),
        "dom",
        scatter_dimension=0,
        tiled=True,
    )
    steady = lax.optimization_barrier(scaled)
    feats_grad = (steady.astype(jnp.float32) + column_sum).astype(jnp.bfloat16)
    return (output, feats_grad, weight_grad, bias_grad)


def solution(mesh):
    return jax.shard_map(
        on_device,
        mesh=mesh,
        in_specs=(
            P("dom", "feat"),
            P("feat", "dom"),
            P("feat"),
            P("dom", None, None),
            P("dom"),
            P("dom"),
            P("dom"),
            P("dom", "feat"),
        ),
        out_specs=(P("dom", "feat"), P("dom", "feat"), P("feat", "dom"), P("feat")),
        check_vma=False,
    )
```

profile of v0, /device:TPU:1, one launch (start us, length us, event | category | flops | bytes accessed | tf_op | source)
XLA Modules:
  0.0 617.2 jit_solution(16154213924465013523)
XLA Ops:
  7.2 0.0 all-gather.2.cloned.1.call-start
  7.2 0.7 all-gather.2.cloned.1.call-update
  7.9 0.0 reduce-scatter.4.cloned.1.call-start
  8.6 0.7 compare_select_fusion
  9.3 3.4 convert_reduce_fusion
  12.6 1.3 scatter_custom_fusion.1
  14.0 54.6 %all_gather.10 = bf16[256,1024]{0,1:T(8,128)(2,1)S(1)} all-gather(bf16[256,16]{0,1:T(8,128)(2,1)} %param.9), channel_id=1, replica_groups=mesh['dom'=64,'feat'=4] {'dom'}, dimensions={1}, use_global_device_ids=true | all-gather | bytes 532480 | tf_op jit(solution)/shard_map/all_gather | solution.py:33
  68.6 0.7 compare_and_fusion.1
  69.3 28.8 %all-gather.2.cloned.1.call-done = bf16[16384,256]{1,0:T(8,128)(2,1)} async-done(((bf16[256,256]{1,0:T(8,128)(2,1)}), bf16[16384,256]{1,0:T(8,128)(2,1)}) %all-gather.2.cloned.1.call-update) | async-done | bytes 8388624 | tf_op jit(solution)/shard_map/all_gather | solution.py:25
  98.0 10.0 %gather_fusion = bf16[128,128,256]{2,1,0:T(8,128)(2,1)} fusion(bf16[128,128,256]{2,1,0:T(8,128)(2,1)} %bitcast.26, s32[1024]{0:T(1024)S(1)} %pad_clamp_fusion.1), kind=kCustom, calls=%fused_computation | custom fusion | bytes 16777728 | tf_op jit(solution)/shard_map/jit(_take)/gather | solution.py:27
  108.0 13.1 %convolution_bitcast_fusion.1 = f32[128,128,256]{1,2,0:T(8,128)} fusion(bf16[128,128,128]{2,1,0:T(8,128)(2,1)} %param.11, bf16[128,128,256]{2,1,0:T(8,128)(2,1)} %gather_fusion, pred[128]{0:T(512)(128)(4,1)S(1)} %compare_and_fusion.1), kind=kOutput, calls=%fused_computation.6 | convolution fusion | flops 1077936128 | bytes 29360256 | tf_op jit(solution)/shard_map/sij,sjf->sif/dot_general | solution.py:28
  121.1 17.5 %copy.15 = f32[128,128,256]{2,1,0:T(8,128)} copy(f32[128,128,256]{1,2,0:T(8,128)} %convolution_bitcast_fusion.1) | data formatting | bytes 33554432 | tf_op jit(solution)/shard_map/sij,sjf->sif/dot_general | solution.py:28
  138.6 0.0 copy-start
  138.6 0.0 copy-start.3
  138.6 0.0 copy-start.1
  138.6 0.0 copy-start.2
  138.7 23.9 %scatter_fusion = f32[2,128,256]{2,1,0:T(8,128)S(1)} fusion(f32[2,128,256]{2,1,0:T(8,128)S(1)} %broadcast_in_dim.47, s32[128]{0:T(128)S(1)} %get-tuple-element.8, f32[128,128,256]{2,1,0:T(8,128)} %copy.15), kind=kCustom, calls=%fused_computation.2 | custom fusion | flops 4194304 | bytes 50332160 | tf_op jit(solution)/shard_map/scatter-add | solution.py:29
  162.6 0.0 copy-done
  162.6 0.1 fusion.8
  162.7 1.3 fusion.14
  164.1 0.0 reduce-scatter.4.cloned.1.call-update
  164.1 0.0 reduce-scatter.6.cloned.1.call-start
  164.1 0.0 copy-done.3
  164.2 20.9 %reduce-scatter.4.cloned.1.call-done = f32[256,256]{1,0:T(8,128)} async-done(((f32[256,1024]{1,0:T(8,128)}), f32[256,256]{1,0:T(8,128)}) %reduce-scatter.4.cloned.1.call-update) | async-done | bytes 262160 | tf_op jit(solution)/shard_map/reduce_scatter | solution.py:35
  185.1 0.0 copy-done.1
  185.1 0.0 copy-done.2
  185.1 1.7 fusion.13
  186.9 11.5 %all_gather.11 = bf16[256,1024]{1,0:T(8,128)(2,1)S(1)} all-gather(bf16[256,256]{1,0:T(8,128)(2,1)S(1)} %get-tuple-element.5), channel_id=1, replica_groups=mesh['dom'=64,'feat'=4] {'feat'}, dimensions={1}, use_global_device_ids=true | all-gather | bytes 655360 | tf_op jit(solution)/shard_map/all_gather | solution.py:41
  198.3 0.3 fusion.6
  198.6 6.4 %gather_fusion.1 = bf16[128,128,256]{2,1,0:T(8,128)(2,1)} fusion(bf16[2,128,256]{2,1,0:T(8,128)(2,1)S(1)} %bitcast.24, s32[1024]{0:T(1024)S(1)} %pad_clamp_fusion), kind=kCustom, calls=%fused_computation.1 | custom fusion | bytes 16777728 | tf_op jit(solution)/shard_map/jit(_take)/gather | solution.py:54
  205.0 12.8 %convolution_bitcast_fusion = f32[128,128,256]{1,2,0:T(8,128)} fusion(bf16[128,128,128]{2,1,0:T(8,128)(2,1)} %param.11, bf16[128,128,256]{2,1,0:T(8,128)(2,1)} %gather_fusion.1, pred[128]{0:T(512)(128)(4,1)S(1)} %compare_and_fusion), kind=kOutput, calls=%fused_computation.5 | convolution fusion | flops 1077936128 | bytes 29360256 | tf_op jit(solution)/shard_map/sji,sjf->sif/dot_general | solution.py:51
  217.8 17.5 %copy.17 = f32[128,128,256]{2,1,0:T(8,128)} copy(f32[128,128,256]{1,2,0:T(8,128)} %convolution_bitcast_fusion) | data formatting | bytes 33554432 | tf_op jit(solution)/shard_map/sji,sjf->sif/dot_general | solution.py:51
  235.3 7.8 %broadcast_in_dim.54 = f32[128,128,256]{2,1,0:T(8,128)} broadcast(f32[]{:T(128)} %constant.12.clone.1), dimensions={} | broadcast | bytes 16777220 | tf_op jit(solution)/shard_map/broadcast_in_dim | solution.py:63
  243.1 36.0 %scatter_fusion.1 = f32[128,128,256]{2,1,0:T(8,128)} fusion(f32[128,128,256]{2,1,0:T(8,128)} %broadcast_in_dim.54, s32[128]{0:T(128)S(1)} %get-tuple-element.12, f32[128,128,256]{2,1,0:T(8,128)} %copy.17), kind=kCustom, calls=%fused_computation.4 | custom fusion | flops 4194304 | bytes 50332160 | tf_op jit(solution)/shard_map/scatter-add | solution.py:63
  279.1 0.0 reduce-scatter.6.cloned.1.call-update
  279.1 0.0 reduce-scatter.8.cloned.1.call-start
  279.2 1.3 fusion.15
  280.5 0.0 reduce-scatter.8.cloned.1.call-update
  280.6 132.8 %psum.7 = f32[256]{0:T(256)} all-reduce(f32[256]{0:T(256)S(1)} %get-tuple-element.4), channel_id=1, replica_groups=mesh['dom'=64,'feat'=4] {'dom'}, use_global_device_ids=true, to_apply=%region_8.9 | all-reduce | flops 256 | bytes 2048 | tf_op jit(solution)/shard_map/psum | solution.py:39
  413.3 55.7 %reduce-scatter.6.cloned.1.call-done = f32[256,256]{1,0:T(8,128)} async-done(((f32[16384,256]{1,0:T(8,128)}), f32[256,256]{1,0:T(8,128)}) %reduce-scatter.6.cloned.1.call-update) | async-done | bytes 262160 | tf_op jit(solution)/shard_map/reduce_scatter | solution.py:62
  469.1 1.6 add_convert_fusion
  470.7 140.0 %reduce-scatter.8.cloned.1.call-done = f32[256,16]{0,1:T(8,128)} async-done(((f32[256,1024]{0,1:T(8,128)}), f32[256,16]{0,1:T(8,128)}) %reduce-scatter.8.cloned.1.call-update) | async-done | bytes 16400 | tf_op jit(solution)/shard_map/reduce_scatter | solution.py:45
  (4 shorter events, 0.0 us)
Async XLA Ops:
  7.2 90.9 %all-gather.2.cloned.1.call-start = ((), (), s32[]{:S(2)}) async-start(), calls=%async_computation.3 | async-start | bytes 8519680 | tf_op jit(solution)/shard_map/all_gather | solution.py:25
  7.9 177.2 %reduce-scatter.4.cloned.1.call-start = ((), (), s32[]{:S(2)}) async-start(), calls=%async_computation.4 | async-start | bytes 1310720 | tf_op jit(solution)/shard_map/reduce_scatter | solution.py:35
  138.6 24.0 %copy-start = (bf16[256,256]{1,0:T(8,128)(2,1)S(1)}, bf16[256,256]{1,0:T(8,128)(2,1)}, u32[]{:S(2)}) copy-start(bf16[256,256]{1,0:T(8,128)(2,1)} %param.8) | copy-start | bytes 393220
  138.6 25.5 %copy-start.3 = (s32[128]{0:T(128)S(1)}, s32[128]{0:T(128)}, u32[]{:S(2)}) copy-start(s32[128]{0:T(128)} %param.12) | copy-start | bytes 1540
  138.6 46.5 %copy-start.1 = (bf16[256,256]{1,0:T(8,128)(2,1)S(1)}, bf16[256,256]{1,0:T(8,128)(2,1)}, u32[]{:S(2)}) copy-start(bf16[256,256]{1,0:T(8,128)(2,1)} %param.15) | copy-start | bytes 393220
  138.6 46.5 %copy-start.2 = (f32[256]{0:T(256)S(1)}, f32[256]{0:T(256)}, u32[]{:S(2)}) copy-start(f32[256]{0:T(256)} %param.10) | copy-start | bytes 3076
  164.1 305.0 %reduce-scatter.6.cloned.1.call-start = ((), (), s32[]{:S(2)}) async-start(), calls=%async_computation.5 | async-start | bytes 17039360 | tf_op jit(solution)/shard_map/reduce_scatter | solution.py:62
  279.1 331.5 %reduce-scatter.8.cloned.1.call-start = ((), (), s32[]{:S(2)}) async-start(), calls=%async_computation.6 | async-start | bytes 1064960 | tf_op jit(solution)/shard_map/reduce_scatter | solution.py:45
Sparse Core Ops, SparseCore 0:
  10.8 87.2 all-gather.1
  164.2 20.8 reduce-scatter.3
  279.3 189.7 reduce-scatter.5
  474.0 136.6 reduce-scatter.7
where the time goes:
time: 623 us; the launch traced here: 617 us
  waiting for transfers between devices  246 us (39%)
  blocking collectives  199 us (32%)
  other arithmetic  69.5 us (11%)
  local copies, waits for them, and re-layouts  59.2 us (10%)
  matrix products  28.9 us (5%)
  between operations  14.5 us (2%)
    reduce_scatter x1, waiting for transfers between devices, on_device(): lax.psum_scatter(weight_part, 'dom', scatter_dimension=1, tiled=True)  140 us
    psum x1, blocking collectives, on_device(): bias_grad = lax.psum(jnp.sum(dz_full, axis=0), 'dom')  133 us
    reduce_scatter x1, waiting for transfers between devices, on_device(): lax.psum_scatter(jax.ops.segment_sum(back_terms, local_ids, num_segments=...  55.7 us
    all_gather x1, blocking collectives, on_device(): weight_full = lax.all_gather(weight, 'dom', axis=1, tiled=True)  54.6 us
    scatter-add x1, other arithmetic, on_device(): jax.ops.segment_sum(back_terms, local_ids, num_segments=segment_count)  36 us
    all_gather x1, waiting for transfers between devices, on_device(): gathered = lax.all_gather(feats, 'dom', axis=0, tiled=True)  28.8 us
    scatter-add x1, other arithmetic, on_device(): jax.ops.segment_sum(terms, degree_ids, num_segments=row_blocks)  23.9 us
    reduce_scatter x1, waiting for transfers between devices, on_device(): lax.psum_scatter(partial_hidden, 'feat', scatter_dimension=1, tiled=True)  20.9 us
  transfers between devices with their start and end apart: 4, of which 4 were waited for; matrix products, arithmetic and copies ran while one was open for 1% of the time, Pallas kernels for 0%

commit v1 on v0

v1 whole, which is shorter than its diff:
```python
import functools

import jax
import jax.numpy as jnp
from jax import lax
from jax.experimental import pallas as pl
from jax.experimental.pallas import tpu as pltpu
from jax.sharding import PartitionSpec as P

F32 = jnp.float32
BF16 = jnp.bfloat16
NZ, NX, NY = 8, 4, 4
BLK = 128
SLOTS = 128
WIDTH = 256
NODES = 2 * BLK
W_ROWS = 16
ROWS = NODES + W_ROWS
UNROLL = 4
FETCH = 16
MIB = 1 << 20

LOW, HIGH, ACROSS = (0, 1, 7, 2), (6, 3, 5, 4), (0, 1, 3, 2)
GATHER_0 = tuple(
    tuple(k * NZ + j for j in group)
    for k, group in ((0, LOW), (1, LOW), (3, LOW), (2, LOW), (1, HIGH), (3, HIGH), (2, HIGH), (0, HIGH))
)
GATHER_1 = tuple(tuple(k * NZ + j for k in ACROSS) for j in (0, 1, 7, 2, 6, 3, 5, 4))
FAR, NEAR = (4, 5, 3, 6), (2, 7, 1, 0)
SCATTER_0 = tuple(
    tuple((dx, dz) for dz in group)
    for dx, group in ((2, FAR), (2, NEAR), (1, FAR), (3, NEAR), (1, NEAR), (3, FAR), (0, NEAR), (0, FAR))
)
SCATTER_1 = tuple(tuple((dx, dz) for dx in ACROSS) for dz in (4, 5, 3, 6, 2, 7, 1, 0))


def shift(value, core_0=None, core_1=None):
    pairs = []
    for z in range(NZ):
        for x in range(NX):
            for core, step in enumerate((core_0, core_1)):
                if step is not None:
                    target = ((z + step[0]) % NZ * NX + (x + step[1]) % NX) * 2 + core
                    pairs.append(((z * NX + x) * 2 + core, target))
    return lax.ppermute(value, "dom", pairs)


Z_UP, Z_DOWN, X_UP, X_DOWN, X_TWO = (1, 0), (-1, 0), (0, 1), (0, -1), (0, 2)


def swap(value, bit):
    return lax.ppermute(value, "dom", [(i, i ^ bit) for i in range(NZ * NX * 2)])


def y_shift(value, dy):
    return lax.ppermute(value, "feat", [(y, (y + dy) % NY) for y in range(NY)])


def smem():
    return pl.BlockSpec(memory_space=pltpu.SMEM)


def vmem():
    return pl.BlockSpec(memory_space=pltpu.VMEM)


def anywhere():
    return pl.BlockSpec(memory_space=pl.ANY)


def list_kernel(own, sib, place, count, slots, spots):
    core, x, z = place[0], place[1], place[2]
    for row in range(4):
        count[row] = 0

    def scan(meta, first_row, first_slot):
        def step(s, carry):
            column = meta[1, s]
            owner = column // 2
            row = first_row + meta[0, s]

            @pl.when(owner % 2 == core)
            def _():
                chip = owner // 2
                at = count[row]
                slots[row, at] = first_slot + s
                spot = ((x - chip % NX) & (NX - 1)) * NZ + ((z - chip // NX) & (NZ - 1))
                spots[row, at] = spot * 2 + column % 2
                count[row] = at + 1

            return carry

        lax.fori_loop(0, meta[2, 0], step, 0)

    scan(own, 0, 0)
    scan(sib, 2, SLOTS)


def make_lists(own, sib, place):
    return pl.pallas_call(
        list_kernel,
        out_shape=(
            jax.ShapeDtypeStruct((4,), jnp.int32),
            jax.ShapeDtypeStruct((4, 2 * SLOTS), jnp.int32),
            jax.ShapeDtypeStruct((4, 2 * SLOTS), jnp.int32),
        ),
        in_specs=[smem()] * 3,
        out_specs=(smem(),) * 3,
    )(own, sib, place)


def live_tiles(place, own, sib, tiles, sem):
    copies = []
    for which, source in enumerate((own, sib)):
        for step in range(SLOTS // FETCH):
            first = step * FETCH
            copy = pltpu.make_async_copy(
                source.at[pl.ds(first, FETCH)],
                tiles.at[pl.ds(which * SLOTS + first, FETCH)],
                sem.at[which * (SLOTS // FETCH) + step],
            )
            copies.append((first < place[4 + which], copy))
    return copies


def run_if(conditions_and_calls):
    for condition, call in conditions_and_calls:
        if condition is None:
            call()
        else:
            pl.when(condition)(call)


def picked_tiles(it, row, number, slots, spots, tiles):
    lefts, at_spots = [], []
    for u in range(UNROLL):
        at = it * UNROLL + u
        held = jnp.minimum(at, number - 1)
        slot = jnp.where(at < number, slots[row, held], 2 * SLOTS)
        lefts.append(tiles[slot])
        at_spots.append(spots[row, held])
    return jnp.concatenate(lefts, axis=1), at_spots


def forward_kernel(count, slots, spots, place, own, sib, *rest):
    chunks, rest = rest[:9], rest[9:]
    sums, weight_out, blocks, tiles, sem, tile_sem = rest
    core, x, z, y = place[0], place[1], place[2], place[3]
    copies = live_tiles(place, own, sib, tiles, tile_sem)
    for n, chunk in enumerate(chunks):
        row = min(n, 7)
        condition = None if n < 7 else core == n - 7
        for i in range(4):
            spot = jnp.where(core == 0, GATHER_0[row][i], GATHER_1[row][i])
            copies.append((condition, pltpu.make_async_copy(chunk.at[i], blocks.at[spot], sem.at[n * 4 + i])))
    run_if((condition, copy.start) for condition, copy in copies)
    tiles[2 * SLOTS] = jnp.zeros((BLK, BLK), BF16)
    run_if((condition, copy.wait) for condition, copy in copies)
    for row in range(4):
        number = count[row]

        def step(it, total):
            left, at_spots = picked_tiles(it, row, number, slots, spots, tiles)
            rights = []
            for at in at_spots:
                first = pl.multiple_of((at & 1) * BLK, BLK)
                rights.append(blocks[at >> 1, pl.ds(first, BLK), :])
            return total + jnp.dot(left, jnp.concatenate(rights, axis=0), preferred_element_type=F32)

        steps = lax.div(number + (UNROLL - 1), UNROLL)
        sums[row] = lax.fori_loop(0, steps, step, jnp.zeros((BLK, WIDTH), F32))
    for k in range(NX):
        for j in range(NZ):
            column = (x - k) & (NX - 1)
            level = (z - j) & (NZ - 1)
            part = (level // 2 - y) & (NY - 1)
            weight_out[part, (level & 1) * NX + column] = blocks[k * NZ + j, NODES:ROWS, :]


def forward(lists, place, own, sib, chunks):
    return pl.pallas_call(
        forward_kernel,
        out_shape=(
            jax.ShapeDtypeStruct((4, BLK, WIDTH), F32),
            jax.ShapeDtypeStruct((NY, 2 * NX, W_ROWS, WIDTH), BF16),
        ),
        in_specs=[smem()] * 4 + [anywhere()] * (2 + len(chunks)),
        out_specs=(vmem(),) * 2,
        scratch_shapes=[
            pltpu.VMEM((NX * NZ, ROWS, WIDTH), BF16),
            pltpu.VMEM((2 * SLOTS + 1, BLK, BLK), BF16),
            pltpu.SemaphoreType.DMA((36,)),
            pltpu.SemaphoreType.DMA((2 * SLOTS // FETCH,)),
        ],
        compiler_params=pltpu.CompilerParams(vmem_limit_bytes=20 * MIB),
        cost_estimate=pl.CostEstimate(flops=128 * 2 * BLK * BLK * WIDTH, bytes_accessed=9 * MIB, transcendentals=0),
    )(*lists, place, own, sib, *chunks)


def backward_kernel(count, slots, spots, place, own, sib, scaled, weight_sums, *rest):
    outs, rest = rest[:8], rest[8:]
    total, tiles, tile_sem = rest
    core, x, z, y = place[0], place[1], place[2], place[3]
    copies = live_tiles(place, own, sib, tiles, tile_sem)
    run_if((condition, copy.start) for condition, copy in copies)
    total[...] = jnp.zeros_like(total)
    tiles[2 * SLOTS] = jnp.zeros((BLK, BLK), BF16)
    run_if((condition, copy.wait) for condition, copy in copies)
    for row in range(4):
        number = count[row]
        right = scaled[row]

        def step(it, carry):
            left, at_spots = picked_tiles(it, row, number, slots, spots, tiles)
            terms = lax.dot_general(left, right, (((0,), (0,)), ((), ())), preferred_element_type=F32)
            for u in range(UNROLL):
                total[at_spots[u]] += terms[u * BLK : (u + 1) * BLK]
            return carry

        lax.fori_loop(0, lax.div(number + (UNROLL - 1), UNROLL), step, 0)
    for n, out in enumerate(outs):
        for i in range(4):
            dx = jnp.where(core == 0, SCATTER_0[n][i][0], SCATTER_1[n][i][0])
            dz = jnp.where(core == 0, SCATTER_0[n][i][1], SCATTER_1[n][i][1])
            spot = (-dx & (NX - 1)) * NZ + (-dz & (NZ - 1))
            out[i, 0:BLK, :] = total[spot * 2].astype(BF16)
            out[i, BLK:NODES, :] = total[spot * 2 + 1].astype(BF16)
            column = (x + dx) & (NX - 1)
            level = (z + dz) & (NZ - 1)
            part = (level // 2 - y) & (NY - 1)
            out[i, NODES:ROWS, :] = weight_sums[part, (level & 1) * NX + column]


def backward(lists, place, own, sib, scaled, weight_sums):
    return pl.pallas_call(
        backward_kernel,
        out_shape=(jax.ShapeDtypeStruct((4, ROWS, WIDTH), BF16),) * 8,
        in_specs=[smem()] * 4 + [anywhere()] * 2 + [vmem()] * 2,
        out_specs=(vmem(),) * 8,
        scratch_shapes=[
            pltpu.VMEM((2 * NX * NZ, BLK, WIDTH), F32),
            pltpu.VMEM((2 * SLOTS + 1, BLK, BLK), BF16),
            pltpu.SemaphoreType.DMA((2 * SLOTS // FETCH,)),
        ],
        compiler_params=pltpu.CompilerParams(vmem_limit_bytes=28 * MIB),
        cost_estimate=pl.CostEstimate(flops=128 * 2 * BLK * BLK * WIDTH, bytes_accessed=9 * MIB, transcendentals=0),
    )(*lists, place, own, sib, scaled, weight_sums)


def gather(block, core):
    p1 = shift(block, Z_UP, X_UP)
    p2 = shift(block, Z_DOWN, X_DOWN)
    p3 = shift(jnp.where(core == 0, p1, block), Z_UP, X_TWO)
    low = jnp.stack([block, p1, p2, p3])
    c1 = shift(low, X_UP, Z_UP)
    c2 = shift(low, X_DOWN, Z_DOWN)
    p4 = shift(p2, Z_DOWN)
    p5 = shift(p3, Z_UP)
    p6 = shift(p4, Z_DOWN)
    p7 = shift(p6, Z_DOWN)
    high = jnp.stack([p4, p5, p6, p7])
    c3 = shift(c1, X_UP, Z_UP)
    c4 = shift(jnp.where(core == 0, high, c2), X_UP, Z_DOWN)
    c5 = shift(jnp.where(core == 0, high, c3), X_DOWN, Z_UP)
    c6 = shift(jnp.where(core == 0, c5, c4), X_DOWN, Z_DOWN)
    c7 = shift(c5, None, Z_UP)
    return [low, c1, c2, c3, c4, c5, c6, high, c7]


def add(*values):
    total = values[0].astype(F32)
    for value in values[1:]:
        total = total + value.astype(F32)
    return total


def scatter(parts, core, watch):
    a, b, c, d, e, f, g, h = parts
    zero = jnp.zeros((), BF16)
    j1 = shift(a, X_UP, Z_UP)
    j2 = shift(b, X_DOWN, Z_DOWN)
    j3 = shift(add(c, j1).astype(BF16), X_UP, Z_UP)
    j4 = shift(add(d, j2).astype(BF16), X_DOWN, Z_DOWN)
    j5 = shift(add(e, jnp.where(core == 0, zero, j3)).astype(BF16), X_UP, Z_UP)
    j6 = shift(add(f, jnp.where(core == 0, zero, j4)).astype(BF16), X_DOWN, Z_DOWN)
    j7 = shift(add(g, j5).astype(BF16), None, Z_UP)
    watch.extend([j1, j2, j3, j4, j5])

    def far(i):
        return add(h[i], j3[i], j6[i])

    def near(i):
        return add(g[i], j4[i], j5[i])

    def across(i):
        return add(h[i], j6[i], j7[i])

    r1 = shift(jnp.where(core == 0, far(0), across(1)).astype(BF16), Z_UP, X_UP)
    r2 = shift(jnp.where(core == 0, far(1), across(2)).astype(BF16), Z_DOWN, X_DOWN)
    r3 = shift(jnp.where(core == 0, add(far(2), r1), across(3)).astype(BF16), Z_UP, X_TWO)
    r4 = shift(add(far(3), r2).astype(BF16), Z_DOWN)
    r5 = shift(add(near(0), r3).astype(BF16), Z_UP)
    r6 = shift(add(near(1), r4).astype(BF16), Z_DOWN)
    r7 = shift(add(near(2), r5).astype(BF16), Z_UP)
    return jnp.where(core == 0, add(near(3), r6, r7), add(across(0), r1, r2, r3))


def after(value, other):
    return value + jnp.minimum(jnp.abs(other[0, 0, :1].astype(F32)), 0.0)


def silu_parts(hidden):
    gate_value = jax.nn.sigmoid(hidden)
    return (hidden * gate_value, gate_value * (1.0 + hidden * (1.0 - gate_value)))


def on_device(feats, weight, bias, tile_values, tile_rows, tile_cols, tile_live, cotangent):
    dom = lax.axis_index("dom")
    y = lax.axis_index("feat")
    core = dom % 2
    x = (dom // 2) % NX
    z = dom // (2 * NX)

    chunks = gather(jnp.concatenate([feats, weight.T], axis=0), core)

    meta = jnp.stack([tile_rows, tile_cols, jnp.broadcast_to(tile_live, (SLOTS,))])
    other_meta = swap(meta, 1)
    other_tiles = swap(tile_values, 1)
    place = jnp.stack([core, x, z, y, tile_live[0], other_meta[2, 0]]).astype(jnp.int32)
    lists = make_lists(meta, other_meta, place)

    own_live = jnp.arange(SLOTS, dtype=jnp.int32) < tile_live[0]
    row_sums = jnp.sum(tile_values, axis=2, dtype=F32)
    degree = 1.0 + jnp.concatenate(
        [
            jnp.sum(jnp.where((own_live & (tile_rows == row))[:, None], row_sums, 0.0), axis=0)
            for row in range(2)
        ]
    ).reshape(NODES, 1)

    sums, weight_lane = forward(lists, place, tile_values, other_tiles, chunks)
    neighbour_sum = (sums[:2] + swap(sums[2:], 1)).reshape(NODES, WIDTH)
    weight_other = swap(weight_lane, 1)
    mixed = ((feats.astype(F32) + neighbour_sum) / degree).astype(BF16)

    first = jnp.where(core == 0, weight_lane, weight_other)
    second = jnp.where(core == 0, weight_other, weight_lane)
    weight_t = jnp.stack([first, second], axis=2).reshape(NY, WIDTH, WIDTH)

    def hidden_part(dy):
        return lax.dot_general(mixed, weight_t[dy], (((1,), (1,)), ((), ())), preferred_element_type=F32)

    hidden = add(
        hidden_part(0),
        y_shift(hidden_part(1).astype(BF16), 1),
        y_shift(hidden_part(2).astype(BF16), 2),
        y_shift(hidden_part(3).astype(BF16), 3),
    ) + bias
    activated, slope = silu_parts(hidden)
    output = activated.astype(BF16)
    dz_full = cotangent.astype(F32) * slope
    dz_own = dz_full.astype(BF16)
    dz_parts = [dz_own] + [y_shift(dz_own, NY - dy) for dy in range(1, NY)]

    dmixed = sum(jnp.dot(dz_parts[dy], weight_t[dy], preferred_element_type=F32) for dy in range(NY))
    scaled = (dmixed / degree).astype(BF16)
    scaled_blocks = jnp.concatenate([scaled, swap(scaled, 1)], axis=0).reshape(4, BLK, WIDTH)

    weight_part = jnp.stack(
        [
            lax.dot_general(dz_parts[dy], mixed, (((0,), (0,)), ((), ())), preferred_element_type=F32)
            for dy in range(NY)
        ]
    ).reshape(NY, 2 * NX, 2, W_ROWS, WIDTH)
    mine = jnp.where(core == 0, weight_part[:, :, 0], weight_part[:, :, 1])
    others = jnp.where(core == 0, weight_part[:, :, 1], weight_part[:, :, 0])
    bias_part = jnp.sum(dz_full, axis=0, keepdims=True)
    bias_rows = jnp.pad(bias_part, ((0, 7), (0, 0)))
    sent = jnp.concatenate([others.reshape(-1, WIDTH), bias_rows], axis=0)
    got = swap(sent, 1)
    weight_sums = (mine + got[:-8].reshape(mine.shape)).astype(BF16)
    bias_grad = bias_part + got[-8:-7]

    parts = backward(lists, place, tile_values, other_tiles, scaled_blocks, weight_sums)
    watch = []
    column_sum = scatter(parts, core, watch)
    for bit, seen in zip((2, 4, 8, 16, 32), watch):
        bias_grad = bias_grad + swap(after(bias_grad, seen), bit)

    feats_grad = (scaled.astype(F32) + column_sum[:NODES]).astype(BF16)
    weight_grad = column_sum[NODES:].T
    return (output, feats_grad, weight_grad, bias_grad.reshape(WIDTH))


def solution(mesh):
    return jax.shard_map(
        on_device,
        mesh=mesh,
        in_specs=(
            P("dom", "feat"),
            P("feat", "dom"),
            P("feat"),
            P("dom", None, None),
            P("dom"),
            P("dom"),
            P("dom"),
            P("dom", "feat"),
        ),
        out_specs=(P("dom", "feat"), P("dom", "feat"), P("feat", "dom"), P("feat")),
        check_vma=False,
    )
```

time: 623 us -> 223 us (0.36)
  the two profiles are of different devices: /device:TPU:1 before, /device:TPU:2 now
where the time goes in v1:
time: 223 us; the launch traced here: 222 us
  waiting for transfers between devices  85.1 us (38%)
  starting transfers between devices  76.6 us (34%)
  Pallas kernels  28.8 us (13%)
  local copies, waits for them, and re-layouts  12.9 us (6%)
  other arithmetic  10.9 us (5%)
  between operations  5.34 us (2%)
  matrix products  2.48 us (1%)
    ppermute x28, waiting for transfers between devices, shift(): return lax.ppermute(value, 'dom', pairs)  69.2 us
    ppermute x28, starting transfers between devices, shift(): return lax.ppermute(value, 'dom', pairs)  49.7 us
    ppermute x11, starting transfers between devices, swap(): lax.ppermute(value, 'dom', [(i, i ^ bit) for i in range(NZ * NX * 2)])  16.4 us
    pallas_call x1, Pallas kernels, forward(): pl.pallas_call(forward_kernel, out_shape=(jax.ShapeDtypeStruct((4, BLK, W...  11.7 us
    ppermute x6, waiting for transfers between devices, y_shift(): return lax.ppermute(value, 'feat', [(y, (y + dy) % NY) for y in range(NY)])  10.7 us
    ppermute x6, starting transfers between devices, y_shift(): return lax.ppermute(value, 'feat', [(y, (y + dy) % NY) for y in range(NY)])  10.5 us
    pallas_call x1, Pallas kernels, backward(): pl.pallas_call(backward_kernel, out_shape=(jax.ShapeDtypeStruct((4, ROWS,...  9.91 us
    unnamed x38, local copies, waits for them, and re-layouts  7.68 us
  transfers between devices with their start and end apart: 45, of which 22 were waited for; matrix products, arithmetic and copies ran while one was open for 7% of the time, Pallas kernels for 3%

profile of v1, /device:TPU:2, one launch (start us, length us, event | category | flops | bytes accessed | tf_op | source)
XLA Modules:
  0.0 222.3 jit_solution(17669378491815787435)
XLA Ops:
  0.7 0.9 pad_maximum_fusion.4
  1.7 2.0 collective-permute-start.2
  3.7 4.0 %collective-permute-start.3 = (bf16[272,256]{1,0:T(8,128)(2,1)S(1)}, bf16[272,256]{1,0:T(8,128)(2,1)S(1)}, u32[]{:S(2)}, u32[]{:S(2)}) collective-permute-start(bf16[272,256]{1,0:T(8,128)(2,1)S(1)} %pad_maximum_fusion.4), channel_id=1, source_target_pairs={{0,224},{4,28},{8,232},{12,4},{16,240},{20,12},{24,248},{28,20},{3... | collective-permute-start | bytes 417800 | tf_op jit(solution)/shard_map/ppermute | solution.py:45
  7.7 2.9 %collective-permute-done.2 = bf16[272,256]{1,0:T(8,128)(2,1)S(1)} collective-permute-done((bf16[272,256]{1,0:T(8,128)(2,1)S(1)}, bf16[272,256]{1,0:T(8,128)(2,1)S(1)}, u32[]{:S(2)}, u32[]{:S(2)}) %collective-permute-start.2) | collective-permute-done | bytes 139296 | tf_op jit(solution)/shard_map/ppermute | solution.py:45
  10.6 1.0 fusion.29
  11.7 6.2 %collective-permute-done.4 = bf16[272,256]{1,0:T(8,128)(2,1)S(1)} collective-permute-done((bf16[272,256]{1,0:T(8,128)(2,1)S(1)}, bf16[272,256]{1,0:T(8,128)(2,1)S(1)}, u32[]{:S(2)}, u32[]{:S(2)}) %collective-permute-start.4) | collective-permute-done | bytes 139296 | tf_op jit(solution)/shard_map/ppermute | solution.py:45
  18.0 1.6 collective-permute-start.5
  20.1 7.5 %collective-permute-done.5.rest_1_ = bf16[4,272,256]{2,1,0:T(8,128)(2,1)S(1)} collective-permute-done((bf16[4,272,256]{2,1,0:T(8,128)(2,1)S(1)}, bf16[4,272,256]{2,1,0:T(8,128)(2,1)S(1)}, u32[]{:S(2)}, u32[]{:S(2)}) %collective-permute-start.5) | collective-permute-done | bytes 557088 | tf_op jit(solution)/shard_map/ppermute | solution.py:45
  27.6 1.5 collective-permute-start.7
  29.1 0.8 copy-done.2
  29.9 2.7 %collective-permute-start.8 = (bf16[272,256]{1,0:T(8,128)(2,1)S(1)}, bf16[272,256]{1,0:T(8,128)(2,1)S(1)}, u32[]{:S(2)}, u32[]{:S(2)}) collective-permute-start(bf16[272,256]{1,0:T(8,128)(2,1)S(1)} %collective-permute-done.3), channel_id=1, source_target_pairs={{0,224},{8,232},{16,240},{24,248},{32,0},{40,8},{48,16},{56,24},{6... | collective-permute-start | bytes 417800 | tf_op jit(solution)/shard_map/ppermute | solution.py:45
  32.7 4.2 %collective-permute-done.8 = bf16[272,256]{1,0:T(8,128)(2,1)S(1)} collective-permute-done((bf16[272,256]{1,0:T(8,128)(2,1)S(1)}, bf16[272,256]{1,0:T(8,128)(2,1)S(1)}, u32[]{:S(2)}, u32[]{:S(2)}) %collective-permute-start.8) | collective-permute-done | bytes 139296 | tf_op jit(solution)/shard_map/ppermute | solution.py:45
  36.9 3.9 %collective-permute-start.10 = (bf16[272,256]{1,0:T(8,128)(2,1)S(1)}, bf16[272,256]{1,0:T(8,128)(2,1)S(1)}, u32[]{:S(2)}, u32[]{:S(2)}) collective-permute-start(bf16[272,256]{1,0:T(8,128)(2,1)S(1)} %collective-permute-done.8), channel_id=1, source_target_pairs={{0,224},{8,232},{16,240},{24,248},{32,0},{40,8},{48,16},{56,24},{6... | collective-permute-start | bytes 417800 | tf_op jit(solution)/shard_map/ppermute | solution.py:45
  40.8 1.9 collective-permute-start.9
  42.7 2.6 %collective-permute-done.10 = bf16[272,256]{1,0:T(8,128)(2,1)S(1)} collective-permute-done((bf16[272,256]{1,0:T(8,128)(2,1)S(1)}, bf16[272,256]{1,0:T(8,128)(2,1)S(1)}, u32[]{:S(2)}, u32[]{:S(2)}) %collective-permute-start.10) | collective-permute-done | bytes 139296 | tf_op jit(solution)/shard_map/ppermute | solution.py:45
  45.4 4.3 %collective-permute-start.11 = (bf16[272,256]{1,0:T(8,128)(2,1)S(1)}, bf16[272,256]{1,0:T(8,128)(2,1)S(1)}, u32[]{:S(2)}, u32[]{:S(2)}) collective-permute-start(bf16[272,256]{1,0:T(8,128)(2,1)S(1)} %collective-permute-done.10), channel_id=1, source_target_pairs={{0,224},{8,232},{16,240},{24,248},{32,0},{40,8},{48,16},{56,24},{6... | collective-permute-start | bytes 417800 | tf_op jit(solution)/shard_map/ppermute | solution.py:45
  49.7 4.2 %collective-permute-done.11 = bf16[272,256]{1,0:T(8,128)(2,1)S(1)} collective-permute-done((bf16[272,256]{1,0:T(8,128)(2,1)S(1)}, bf16[272,256]{1,0:T(8,128)(2,1)S(1)}, u32[]{:S(2)}, u32[]{:S(2)}) %collective-permute-start.11) | collective-permute-done | bytes 139296 | tf_op jit(solution)/shard_map/ppermute | solution.py:45
  54.0 1.5 collective-permute-start.12
  56.1 7.5 %collective-permute-done.12.rest_4_ = bf16[4,272,256]{2,1,0:T(8,128)(2,1)S(1)} collective-permute-done((bf16[4,272,256]{2,1,0:T(8,128)(2,1)S(1)}, bf16[4,272,256]{2,1,0:T(8,128)(2,1)S(1)}, u32[]{:S(2)}, u32[]{:S(2)}) %collective-permute-start.12) | collective-permute-done | bytes 557088 | tf_op jit(solution)/shard_map/ppermute | solution.py:45
  63.6 1.4 collective-permute-done.13.rest_5_
  65.0 0.9 broadcast_select_fusion
  65.9 1.1 collective-permute-start.14
  67.0 1.5 collective-permute-start.15
  69.4 3.4 %convert_reduce_fusion = f32[128,128]{1,0:T(8,128)S(1)} fusion(bf16[128,128,128]{2,1,0:T(8,128)(2,1)} %own.3), kind=kLoop, calls=%fused_computation | loop fusion | flops 4177920 | bytes 4259840 | tf_op jit(solution)/shard_map/reduce_sum | solution.py:333
  73.4 1.3 stack.85.place
  74.7 7.2 %shard_map.114 = (s32[4]{0:T(128)}, s32[4,256]{1,0:T(4,128)}, s32[4,256]{1,0:T(4,128)}) custom-call(s32[3,128]{1,0:T(4,128)} %copy-done.14, s32[3,128]{1,0:T(4,128)} %copy-done.15, s32[6]{0:T(128)} %stack.85.place), custom_call_target="tpu_custom_call" | custom-call | tf_op jit(solution)/shard_map/pallas_call | solution.py:100
  81.9 2.2 copy-done
  84.1 1.1 copy-done.3
  85.2 0.7 copy-done.4
  85.9 0.7 copy-done.6
  87.9 11.7 %shard_map.115 = (f32[4,128,256]{2,1,0:T(8,128)S(1)}, bf16[4,8,16,256]{3,2,1,0:T(8,128)(2,1)S(1)}) custom-call(s32[4]{0:T(128)S(1)} %copy-done.10, s32[4,256]{1,0:T(4,128)S(1)} %copy-done.4, s32[4,256]{1,0:T(4,128)S(1)} %copy-done.6, s32[6]{0:T(128)S(1)} %copy-done.8, bf16[128,128,128]{2,1,0:T(8,128)(2,1)S(1)} %copy-done, ...), custom_call_target="tpu_custom_call" | custom-call | flops 1073741824 | bytes 9437184 | tf_op jit(solution)/shard_map/pallas_call | solution.py:181
  99.6 1.9 collective-permute-start.17
  101.9 0.9 collective-permute-done.17
  104.1 1.7 collective-permute-start.18
  106.0 3.0 %collective-permute-start.19 = (bf16[256,256]{1,0:T(8,128)(2,1)S(1)}, bf16[256,256]{1,0:T(8,128)(2,1)S(1)}, u32[]{:S(2)}, u32[]{:S(2)}) collective-permute-start(bf16[256,256]{1,0:T(8,128)(2,1)S(1)} %convolution_convert_fusion.1), channel_id=1, source_target_pairs={{0,2},{1,3},{2,0},{3,1},{4,6},{5,7},{6,4},{7,5},{8,10},{9,11},{10,... | collective-permute-start | bytes 393224 | tf_op jit(solution)/shard_map/ppermute | solution.py:56
  109.3 1.4 collective-permute-start.20
  111.2 4.0 %collective-permute-done.19 = bf16[256,256]{1,0:T(8,128)(2,1)S(1)} collective-permute-done((bf16[256,256]{1,0:T(8,128)(2,1)S(1)}, bf16[256,256]{1,0:T(8,128)(2,1)S(1)}, u32[]{:S(2)}, u32[]{:S(2)}) %collective-permute-start.19) | collective-permute-done | bytes 131104 | tf_op jit(solution)/shard_map/ppermute | solution.py:56
  115.2 0.8 fusion.31
  116.3 2.5 %collective-permute-start.21 = (bf16[256,256]{1,0:T(8,128)(2,1)S(1)}, bf16[256,256]{1,0:T(8,128)(2,1)S(1)}, u32[]{:S(2)}, u32[]{:S(2)}) collective-permute-start(bf16[256,256]{1,0:T(8,128)(2,1)S(1)} %get-tuple-element.39), channel_id=1, source_target_pairs={{0,3},{1,0},{2,1},{3,2},{4,7},{5,4},{6,5},{7,6},{8,11},{9,8},{10,9... | collective-permute-start | bytes 393224 | tf_op jit(solution)/shard_map/ppermute | solution.py:56
  118.8 1.5 collective-permute-start.22
  120.9 3.1 %collective-permute-done.21 = bf16[256,256]{1,0:T(8,128)(2,1)S(1)} collective-permute-done((bf16[256,256]{1,0:T(8,128)(2,1)S(1)}, bf16[256,256]{1,0:T(8,128)(2,1)S(1)}, u32[]{:S(2)}, u32[]{:S(2)}) %collective-permute-start.21) | collective-permute-done | bytes 131104 | tf_op jit(solution)/shard_map/ppermute | solution.py:56
  124.2 2.1 collective-permute-done.22
  126.6 1.1 collective-permute-done.23
  129.4 1.0 collective-permute-done.24
  131.3 9.9 %shard_map.116 = (bf16[4,272,256]{2,1,0:T(8,128)(2,1)S(1)}, bf16[4,272,256]{2,1,0:T(8,128)(2,1)S(1)}, bf16[4,272,256]{2,1,0:T(8,128)(2,1)S(1)}, bf16[4,272,256]{...) custom-call(s32[4]{0:T(128)S(1)} %copy-done.11, ...), custom_call_target="tpu_custom_call" | custom-call | flops 1073741824 | bytes 9437184 | tf_op jit(solution)/shard_map/pallas_call | solution.py:235
  141.3 2.0 collective-permute-start.26
  143.3 7.5 %collective-permute-done.28 = bf16[4,272,256]{2,1,0:T(8,128)(2,1)S(1)} collective-permute-done((bf16[4,272,256]{2,1,0:T(8,128)(2,1)S(1)}, bf16[4,272,256]{2,1,0:T(8,128)(2,1)S(1)}, u32[]{:S(2)}, u32[]{:S(2)}) %collective-permute-start.28) | collective-permute-done | bytes 557088 | tf_op jit(solution)/shard_map/ppermute | solution.py:45
  151.4 2.1 collective-permute-start.27
  153.5 7.3 %collective-permute-done.29 = bf16[4,272,256]{2,1,0:T(8,128)(2,1)S(1)} collective-permute-done((bf16[4,272,256]{2,1,0:T(8,128)(2,1)S(1)}, bf16[4,272,256]{2,1,0:T(8,128)(2,1)S(1)}, u32[]{:S(2)}, u32[]{:S(2)}) %collective-permute-start.29) | collective-permute-done | bytes 557088 | tf_op jit(solution)/shard_map/ppermute | solution.py:45
  161.2 2.1 collective-permute-start.31
  163.3 7.3 %collective-permute-done.30 = bf16[4,272,256]{2,1,0:T(8,128)(2,1)S(1)} collective-permute-done((bf16[4,272,256]{2,1,0:T(8,128)(2,1)S(1)}, bf16[4,272,256]{2,1,0:T(8,128)(2,1)S(1)}, u32[]{:S(2)}, u32[]{:S(2)}) %collective-permute-start.30) | collective-permute-done | bytes 557088 | tf_op jit(solution)/shard_map/ppermute | solution.py:45
  170.7 0.7 collective-permute-start.32
  172.8 2.1 collective-permute-start.40
  176.0 9.2 %collective-permute-done.36 = bf16[272,256]{1,0:T(8,128)(2,1)S(1)} collective-permute-done((bf16[272,256]{1,0:T(8,128)(2,1)S(1)}, bf16[272,256]{1,0:T(8,128)(2,1)S(1)}, u32[]{:S(2)}, u32[]{:S(2)}) %collective-permute-start.36) | collective-permute-done | bytes 139296 | tf_op jit(solution)/shard_map/ppermute | solution.py:45
  185.5 1.2 collective-permute-start.33
  186.7 4.7 %collective-permute-start.41 = (f32[1,256]{1,0:T(1,128)S(1)}, f32[1,256]{1,0:T(1,128)S(1)}, u32[]{:S(2)}, u32[]{:S(2)}) collective-permute-start(f32[1,256]{1,0:T(1,128)S(1)} %broadcast_add_fusion.3), channel_id=1, source_target_pairs={{0,16},{4,20},{8,24},{12,28},{16,0},{20,4},{24,8},{28,12},{32,48},... | collective-permute-start | bytes 3080 | tf_op jit(solution)/shard_map/ppermute | solution.py:52
  193.0 4.8 %collective-permute-start.34 = (bf16[272,256]{1,0:T(8,128)(2,1)S(1)}, bf16[272,256]{1,0:T(8,128)(2,1)S(1)}, u32[]{:S(2)}, u32[]{:S(2)}) collective-permute-start(bf16[272,256]{1,0:T(8,128)(2,1)S(1)} %fusion.5), channel_id=1, source_target_pairs={{0,224},{8,232},{16,240},{24,248},{32,0},{40,8},{48,16},{56,24},{6... | collective-permute-start | bytes 417800 | tf_op jit(solution)/shard_map/ppermute | solution.py:45
  199.1 1.3 collective-permute-done.34
  200.5 2.7 %collective-permute-start.38 = (bf16[272,256]{1,0:T(8,128)(2,1)S(1)}, bf16[272,256]{1,0:T(8,128)(2,1)S(1)}, u32[]{:S(2)}, u32[]{:S(2)}) collective-permute-start(bf16[272,256]{1,0:T(8,128)(2,1)S(1)} %get-tuple-element.43), channel_id=1, source_target_pairs={{0,32},{8,40},{16,48},{24,56},{32,64},{40,72},{48,80},{56,88},{64,... | collective-permute-start | bytes 417800 | tf_op jit(solution)/shard_map/ppermute | solution.py:45
  203.2 1.0 collective-permute-start.43
  205.5 4.1 %collective-permute-start.35 = (bf16[272,256]{1,0:T(8,128)(2,1)S(1)}, bf16[272,256]{1,0:T(8,128)(2,1)S(1)}, u32[]{:S(2)}, u32[]{:S(2)}) collective-permute-start(bf16[272,256]{1,0:T(8,128)(2,1)S(1)} %get-tuple-element.42), channel_id=1, source_target_pairs={{0,224},{8,232},{16,240},{24,248},{32,0},{40,8},{48,16},{56,24},{6... | collective-permute-start | bytes 417800 | tf_op jit(solution)/shard_map/ppermute | solution.py:45
  209.7 1.9 collective-permute-start.39
  211.6 5.7 %collective-permute-start.44 = (f32[1,256]{1,0:T(1,128)S(1)}, f32[1,256]{1,0:T(1,128)S(1)}, u32[]{:S(2)}, u32[]{:S(2)}) collective-permute-start(f32[1,256]{1,0:T(1,128)S(1)} %get-tuple-element.32), channel_id=1, source_target_pairs={{0,128},{4,132},{8,136},{12,140},{16,144},{20,148},{24,152},{28,15... | collective-permute-start | bytes 3080 | tf_op jit(solution)/shard_map/ppermute | solution.py:52
  217.3 2.9 %collective-permute-done.44 = f32[1,256]{1,0:T(1,128)S(1)} collective-permute-done((f32[1,256]{1,0:T(1,128)S(1)}, f32[1,256]{1,0:T(1,128)S(1)}, u32[]{:S(2)}, u32[]{:S(2)}) %collective-permute-start.44) | collective-permute-done | bytes 1056 | tf_op jit(solution)/shard_map/ppermute | solution.py:52
  (132 shorter events, 17.2 us)
Async XLA Ops:
  0.6 81.3 %collective-permute-start.1 = (bf16[128,128,128]{2,1,0:T(8,128)(2,1)}, bf16[128,128,128]{2,1,0:T(8,128)(2,1)}, u32[]{:S(2)}, u32[]{:S(2)}) collective-permute-start(bf16[128,128,128]{2,1,0:T(8,128)(2,1)} %own.3), channel_id=1, source_target_pairs={{0,4},{4,0},{8,12},{12,8},{16,20},{20,16},{24,28},{28,24},{32,36},... | collective-permute-start | bytes 12582920 | tf_op jit(solution)/shard_map/ppermute | solution.py:52
  1.7 9.0 %collective-permute-start.2 = (bf16[272,256]{1,0:T(8,128)(2,1)S(1)}, bf16[272,256]{1,0:T(8,128)(2,1)S(1)}, u32[]{:S(2)}, u32[]{:S(2)}) collective-permute-start(bf16[272,256]{1,0:T(8,128)(2,1)S(1)} %pad_maximum_fusion.4), channel_id=1, source_target_pairs={{0,32},{4,12},{8,40},{12,20},{16,48},{20,28},{24,56},{28,4},{32,64... | collective-permute-start | bytes 417800 | tf_op jit(solution)/shard_map/ppermute | solution.py:45
  3.7 8.0 %collective-permute-start.3 = (bf16[272,256]{1,0:T(8,128)(2,1)S(1)}, bf16[272,256]{1,0:T(8,128)(2,1)S(1)}, u32[]{:S(2)}, u32[]{:S(2)}) collective-permute-start(bf16[272,256]{1,0:T(8,128)(2,1)S(1)} %pad_maximum_fusion.4), channel_id=1, source_target_pairs={{0,224},{4,28},{8,232},{12,4},{16,240},{20,12},{24,248},{28,20},{3... | collective-permute-start | bytes 417800 | tf_op jit(solution)/shard_map/ppermute | solution.py:45
  11.6 6.3 %collective-permute-start.4 = (bf16[272,256]{1,0:T(8,128)(2,1)S(1)}, bf16[272,256]{1,0:T(8,128)(2,1)S(1)}, u32[]{:S(2)}, u32[]{:S(2)}) collective-permute-start(bf16[272,256]{1,0:T(8,128)(2,1)S(1)} %get-tuple-element.55), channel_id=1, source_target_pairs={{0,32},{4,20},{8,40},{12,28},{16,48},{20,4},{24,56},{28,12},{32,64... | collective-permute-start | bytes 417800 | tf_op jit(solution)/shard_map/ppermute | solution.py:45
  18.0 9.6 %collective-permute-start.5 = (bf16[4,272,256]{2,1,0:T(8,128)(2,1)S(1)}, bf16[4,272,256]{2,1,0:T(8,128)(2,1)S(1)}, u32[]{:S(2)}, u32[]{:S(2)}) collective-permute-start(bf16[4,272,256]{2,1,0:T(8,128)(2,1)S(1)} %pad_maximum_fusion.1.rest_0_), channel_id=1, source_target_pairs={{0,8},{4,36},{8,16},{12,44},{16,24},{20,52},{24,0},{28,60},{32,40}... | collective-permute-start | bytes 1671176 | tf_op jit(solution)/shard_map/ppermute | solution.py:45
  19.6 34.3 %collective-permute-start.6 = (bf16[4,272,256]{2,1,0:T(8,128)(2,1)S(1)}, bf16[4,272,256]{2,1,0:T(8,128)(2,1)S(1)}, u32[]{:S(2)}, u32[]{:S(2)}) collective-permute-start(bf16[4,272,256]{2,1,0:T(8,128)(2,1)S(1)} %pad_maximum_fusion.1.rest_0_), channel_id=1, source_target_pairs={{0,24},{4,228},{8,0},{12,236},{16,8},{20,244},{24,16},{28,252},{32... | collective-permute-start | bytes 1671176 | tf_op jit(solution)/shard_map/ppermute | solution.py:45
  27.6 26.2 %collective-permute-start.7 = (bf16[4,272,256]{2,1,0:T(8,128)(2,1)S(1)}, bf16[4,272,256]{2,1,0:T(8,128)(2,1)S(1)}, u32[]{:S(2)}, u32[]{:S(2)}) collective-permute-start(bf16[4,272,256]{2,1,0:T(8,128)(2,1)S(1)} %collective-permute-done.5.rest_1_), channel_id=1, source_target_pairs={{0,8},{4,36},{8,16},{12,44},{16,24},{20,52},{24,0},{28,60},{32,40}... | collective-permute-start | bytes 1671176 | tf_op jit(solution)/shard_map/ppermute | solution.py:45
  29.1 0.8 copy-start.2
  29.9 6.9 %collective-permute-start.8 = (bf16[272,256]{1,0:T(8,128)(2,1)S(1)}, bf16[272,256]{1,0:T(8,128)(2,1)S(1)}, u32[]{:S(2)}, u32[]{:S(2)}) collective-permute-start(bf16[272,256]{1,0:T(8,128)(2,1)S(1)} %collective-permute-done.3), channel_id=1, source_target_pairs={{0,224},{8,232},{16,240},{24,248},{32,0},{40,8},{48,16},{56,24},{6... | collective-permute-start | bytes 417800 | tf_op jit(solution)/shard_map/ppermute | solution.py:45
  36.9 8.5 %collective-permute-start.10 = (bf16[272,256]{1,0:T(8,128)(2,1)S(1)}, bf16[272,256]{1,0:T(8,128)(2,1)S(1)}, u32[]{:S(2)}, u32[]{:S(2)}) collective-permute-start(bf16[272,256]{1,0:T(8,128)(2,1)S(1)} %collective-permute-done.8), channel_id=1, source_target_pairs={{0,224},{8,232},{16,240},{24,248},{32,0},{40,8},{48,16},{56,24},{6... | collective-permute-start | bytes 417800 | tf_op jit(solution)/shard_map/ppermute | solution.py:45
  40.8 8.9 %collective-permute-start.9 = (bf16[272,256]{1,0:T(8,128)(2,1)S(1)}, bf16[272,256]{1,0:T(8,128)(2,1)S(1)}, u32[]{:S(2)}, u32[]{:S(2)}) collective-permute-start(bf16[272,256]{1,0:T(8,128)(2,1)S(1)} %collective-permute-done.4), channel_id=1, source_target_pairs={{0,32},{8,40},{16,48},{24,56},{32,64},{40,72},{48,80},{56,88},{64,... | collective-permute-start | bytes 417800 | tf_op jit(solution)/shard_map/ppermute | solution.py:45
  45.4 8.5 %collective-permute-start.11 = (bf16[272,256]{1,0:T(8,128)(2,1)S(1)}, bf16[272,256]{1,0:T(8,128)(2,1)S(1)}, u32[]{:S(2)}, u32[]{:S(2)}) collective-permute-start(bf16[272,256]{1,0:T(8,128)(2,1)S(1)} %collective-permute-done.10), channel_id=1, source_target_pairs={{0,224},{8,232},{16,240},{24,248},{32,0},{40,8},{48,16},{56,24},{6... | collective-permute-start | bytes 417800 | tf_op jit(solution)/shard_map/ppermute | solution.py:45
  54.0 15.2 %copy-start.16 = (s32[128]{0:T(128)S(1)}, s32[128]{0:T(128)}, u32[]{:S(2)}) copy-start(s32[128]{0:T(128)} %param.12) | copy-start | bytes 1540
  54.0 15.2 %copy-start.18 = (s32[128]{0:T(128)S(1)}, s32[128]{0:T(128)}, u32[]{:S(2)}) copy-start(s32[128]{0:T(128)} %param.13) | copy-start | bytes 1540
  54.0 9.6 %collective-permute-start.12 = (bf16[4,272,256]{2,1,0:T(8,128)(2,1)S(1)}, bf16[4,272,256]{2,1,0:T(8,128)(2,1)S(1)}, u32[]{:S(2)}, u32[]{:S(2)}) collective-permute-start(bf16[4,272,256]{2,1,0:T(8,128)(2,1)S(1)} %get-tuple-element.46), channel_id=1, source_target_pairs={{0,8},{4,228},{8,16},{12,236},{16,24},{20,244},{24,0},{28,252},{32... | collective-permute-start | bytes 1671176 | tf_op jit(solution)/shard_map/ppermute | solution.py:45
  55.5 9.5 %collective-permute-start.13 = (bf16[4,272,256]{2,1,0:T(8,128)(2,1)S(1)}, bf16[4,272,256]{2,1,0:T(8,128)(2,1)S(1)}, u32[]{:S(2)}, u32[]{:S(2)}) collective-permute-start(bf16[4,272,256]{2,1,0:T(8,128)(2,1)S(1)} %get-tuple-element.47), channel_id=1, source_target_pairs={{0,24},{4,36},{8,0},{12,44},{16,8},{20,52},{24,16},{28,60},{32,56}... | collective-permute-start | bytes 1671176 | tf_op jit(solution)/shard_map/ppermute | solution.py:45
  65.9 16.0 %collective-permute-start.14 = (bf16[4,272,256]{2,1,0:T(8,128)(2,1)}, bf16[4,272,256]{2,1,0:T(8,128)(2,1)}, u32[]{:S(2)}, u32[]{:S(2)}) collective-permute-start(bf16[4,272,256]{2,1,0:T(8,128)(2,1)} %broadcast_select_fusion), channel_id=1, source_target_pairs={{0,24},{4,228},{8,0},{12,236},{16,8},{20,244},{24,16},{28,252},{32... | collective-permute-start | bytes 1671176 | tf_op jit(solution)/shard_map/ppermute | solution.py:45
  67.0 14.9 %collective-permute-start.15 = (bf16[4,272,256]{2,1,0:T(8,128)(2,1)S(1)}, bf16[4,272,256]{2,1,0:T(8,128)(2,1)}, u32[]{:S(2)}, u32[]{:S(2)}) collective-permute-start(bf16[4,272,256]{2,1,0:T(8,128)(2,1)S(1)} %collective-permute-done.13.rest_5_), channel_id=1, source_target_pairs={{4,36},{12,44},{20,52},{28,60},{36,68},{44,76},{52,84},{60,92},{68... | collective-permute-start | bytes 1671176 | tf_op jit(solution)/shard_map/ppermute | solution.py:45
  69.3 3.4 %copy-start.14 = (s32[3,128]{1,0:T(4,128)}, s32[3,128]{1,0:T(4,128)S(1)}, u32[]{:S(2)}) copy-start(s32[3,128]{1,0:T(4,128)S(1)} %add_add_fusion.1.own) | copy-start | bytes 4612
  69.3 3.5 %collective-permute-start = (s32[3,128]{1,0:T(4,128)S(1)}, s32[3,128]{1,0:T(4,128)S(1)}, u32[]{:S(2)}, u32[]{:S(2)}) collective-permute-start(s32[3,128]{1,0:T(4,128)S(1)} %add_add_fusion.1.own), channel_id=1, source_target_pairs={{0,4},{4,0},{8,12},{12,8},{16,20},{20,16},{24,28},{28,24},{32,36},... | collective-permute-start | bytes 4616 | tf_op jit(solution)/shard_map/ppermute | solution.py:52
  72.8 1.9 copy-start.15
  81.9 2.2 copy-start
  84.1 1.1 copy-start.3
  85.2 0.7 copy-start.4
  85.9 0.7 copy-start.6
  86.6 0.7 copy-start.8
  87.2 0.7 copy-start.10
  99.6 3.1 %collective-permute-start.17 = (bf16[4,8,16,256]{3,2,1,0:T(8,128)(2,1)S(1)}, bf16[4,8,16,256]{3,2,1,0:T(8,128)(2,1)S(1)}, u32[]{:S(2)}, u32[]{:S(2)}) collective-permute-start(bf16[4,8,16,256]{3,2,1,0:T(8,128)(2,1)S(1)} %get-tuple-element.21), channel_id=1, source_target_pairs={{0,4},{4,0},{8,12},{12,8},{16,20},{20,16},{24,28},{28,24},{32,36},... | collective-permute-start | bytes 786440 | tf_op jit(solution)/shard_map/ppermute | solution.py:52
  101.8 1.6 collective-permute-start.16
  102.8 0.9 copy-start.12
  104.1 11.1 %copy-start.13 = (bf16[256,256]{1,0:T(8,128)(2,1)S(1)}, bf16[256,256]{1,0:T(8,128)(2,1)}, u32[]{:S(2)}) copy-start(bf16[256,256]{1,0:T(8,128)(2,1)} %param.15) | copy-start | bytes 393220
  104.1 11.1 %copy-start.17 = (f32[256]{0:T(256)S(1)}, f32[256]{0:T(256)}, u32[]{:S(2)}) copy-start(f32[256]{0:T(256)} %param.10) | copy-start | bytes 3076
  104.1 7.1 %collective-permute-start.18 = (bf16[256,256]{1,0:T(8,128)(2,1)S(1)}, bf16[256,256]{1,0:T(8,128)(2,1)S(1)}, u32[]{:S(2)}, u32[]{:S(2)}) collective-permute-start(bf16[256,256]{1,0:T(8,128)(2,1)S(1)} %convolution_convert_fusion.2), channel_id=1, source_target_pairs={{0,1},{1,2},{2,3},{3,0},{4,5},{5,6},{6,7},{7,4},{8,9},{9,10},{10,1... | collective-permute-start | bytes 393224 | tf_op jit(solution)/shard_map/ppermute | solution.py:56
  106.0 9.2 %collective-permute-start.19 = (bf16[256,256]{1,0:T(8,128)(2,1)S(1)}, bf16[256,256]{1,0:T(8,128)(2,1)S(1)}, u32[]{:S(2)}, u32[]{:S(2)}) collective-permute-start(bf16[256,256]{1,0:T(8,128)(2,1)S(1)} %convolution_convert_fusion.1), channel_id=1, source_target_pairs={{0,2},{1,3},{2,0},{3,1},{4,6},{5,7},{6,4},{7,5},{8,10},{9,11},{10,... | collective-permute-start | bytes 393224 | tf_op jit(solution)/shard_map/ppermute | solution.py:56
  109.3 6.0 %collective-permute-start.20 = (bf16[256,256]{1,0:T(8,128)(2,1)S(1)}, bf16[256,256]{1,0:T(8,128)(2,1)S(1)}, u32[]{:S(2)}, u32[]{:S(2)}) collective-permute-start(bf16[256,256]{1,0:T(8,128)(2,1)S(1)} %convolution_convert_fusion), channel_id=1, source_target_pairs={{0,3},{1,0},{2,1},{3,2},{4,7},{5,4},{6,5},{7,6},{8,11},{9,8},{10,9... | collective-permute-start | bytes 393224 | tf_op jit(solution)/shard_map/ppermute | solution.py:56
  116.3 7.7 %collective-permute-start.21 = (bf16[256,256]{1,0:T(8,128)(2,1)S(1)}, bf16[256,256]{1,0:T(8,128)(2,1)S(1)}, u32[]{:S(2)}, u32[]{:S(2)}) collective-permute-start(bf16[256,256]{1,0:T(8,128)(2,1)S(1)} %get-tuple-element.39), channel_id=1, source_target_pairs={{0,3},{1,0},{2,1},{3,2},{4,7},{5,4},{6,5},{7,6},{8,11},{9,8},{10,9... | collective-permute-start | bytes 393224 | tf_op jit(solution)/shard_map/ppermute | solution.py:56
  118.8 7.5 %collective-permute-start.22 = (bf16[256,256]{1,0:T(8,128)(2,1)S(1)}, bf16[256,256]{1,0:T(8,128)(2,1)S(1)}, u32[]{:S(2)}, u32[]{:S(2)}) collective-permute-start(bf16[256,256]{1,0:T(8,128)(2,1)S(1)} %get-tuple-element.39), channel_id=1, source_target_pairs={{0,2},{1,3},{2,0},{3,1},{4,6},{5,7},{6,4},{7,5},{8,10},{9,11},{10,... | collective-permute-start | bytes 393224 | tf_op jit(solution)/shard_map/ppermute | solution.py:56
  120.2 7.4 %collective-permute-start.23 = (bf16[256,256]{1,0:T(8,128)(2,1)S(1)}, bf16[256,256]{1,0:T(8,128)(2,1)S(1)}, u32[]{:S(2)}, u32[]{:S(2)}) collective-permute-start(bf16[256,256]{1,0:T(8,128)(2,1)S(1)} %get-tuple-element.39), channel_id=1, source_target_pairs={{0,1},{1,2},{2,3},{3,0},{4,5},{5,6},{6,7},{7,4},{8,9},{9,10},{10,1... | collective-permute-start | bytes 393224 | tf_op jit(solution)/shard_map/ppermute | solution.py:56
  128.2 2.3 %collective-permute-start.25 = (f32[520,256]{1,0:T(8,128)S(1)}, f32[520,256]{1,0:T(8,128)S(1)}, u32[]{:S(2)}, u32[]{:S(2)}) collective-permute-start(f32[520,256]{1,0:T(8,128)S(1)} %select_maximum_fusion), channel_id=1, source_target_pairs={{0,4},{4,0},{8,12},{12,8},{16,20},{20,16},{24,28},{28,24},{32,36},... | collective-permute-start | bytes 1597448 | tf_op jit(solution)/shard_map/ppermute | solution.py:52
  128.6 2.2 copy-start.1
  128.8 1.6 collective-permute-start.24
  130.5 0.8 copy-start.5
  130.5 0.8 copy-start.7
  130.5 0.8 copy-start.9
  130.5 0.8 copy-start.11
  141.2 9.6 %collective-permute-start.28 = (bf16[4,272,256]{2,1,0:T(8,128)(2,1)S(1)}, bf16[4,272,256]{2,1,0:T(8,128)(2,1)S(1)}, u32[]{:S(2)}, u32[]{:S(2)}) collective-permute-start(bf16[4,272,256]{2,1,0:T(8,128)(2,1)S(1)} %get-tuple-element.27), channel_id=1, source_target_pairs={{0,8},{4,36},{8,16},{12,44},{16,24},{20,52},{24,0},{28,60},{32,40}... | collective-permute-start | bytes 1671176 | tf_op jit(solution)/shard_map/ppermute | solution.py:45
  141.3 10.0 %collective-permute-start.26 = (bf16[4,272,256]{2,1,0:T(8,128)(2,1)S(1)}, bf16[4,272,256]{2,1,0:T(8,128)(2,1)S(1)}, u32[]{:S(2)}, u32[]{:S(2)}) collective-permute-start(bf16[4,272,256]{2,1,0:T(8,128)(2,1)S(1)} %get-tuple-element.24), channel_id=1, source_target_pairs={{0,24},{4,228},{8,0},{12,236},{16,8},{20,244},{24,16},{28,252},{32... | collective-permute-start | bytes 1671176 | tf_op jit(solution)/shard_map/ppermute | solution.py:45
  150.9 9.8 %collective-permute-start.29 = (bf16[4,272,256]{2,1,0:T(8,128)(2,1)S(1)}, bf16[4,272,256]{2,1,0:T(8,128)(2,1)S(1)}, u32[]{:S(2)}, u32[]{:S(2)}) collective-permute-start(bf16[4,272,256]{2,1,0:T(8,128)(2,1)S(1)} %add_convert_fusion.3), channel_id=1, source_target_pairs={{0,8},{4,36},{8,16},{12,44},{16,24},{20,52},{24,0},{28,60},{32,40}... | collective-permute-start | bytes 1671176 | tf_op jit(solution)/shard_map/ppermute | solution.py:45
  151.4 9.6 %collective-permute-start.27 = (bf16[4,272,256]{2,1,0:T(8,128)(2,1)S(1)}, bf16[4,272,256]{2,1,0:T(8,128)(2,1)S(1)}, u32[]{:S(2)}, u32[]{:S(2)}) collective-permute-start(bf16[4,272,256]{2,1,0:T(8,128)(2,1)S(1)} %add_convert_fusion.4), channel_id=1, source_target_pairs={{0,24},{4,228},{8,0},{12,236},{16,8},{20,244},{24,16},{28,252},{32... | collective-permute-start | bytes 1671176 | tf_op jit(solution)/shard_map/ppermute | solution.py:45
  161.0 9.6 %collective-permute-start.30 = (bf16[4,272,256]{2,1,0:T(8,128)(2,1)S(1)}, bf16[4,272,256]{2,1,0:T(8,128)(2,1)S(1)}, u32[]{:S(2)}, u32[]{:S(2)}) collective-permute-start(bf16[4,272,256]{2,1,0:T(8,128)(2,1)S(1)} %add_convert_fusion.2), channel_id=1, source_target_pairs={{0,8},{4,36},{8,16},{12,44},{16,24},{20,52},{24,0},{28,60},{32,40}... | collective-permute-start | bytes 1671176 | tf_op jit(solution)/shard_map/ppermute | solution.py:45
  161.2 11.3 %collective-permute-start.31 = (bf16[4,272,256]{2,1,0:T(8,128)(2,1)S(1)}, bf16[4,272,256]{2,1,0:T(8,128)(2,1)S(1)}, u32[]{:S(2)}, u32[]{:S(2)}) collective-permute-start(bf16[4,272,256]{2,1,0:T(8,128)(2,1)S(1)} %add_convert_fusion.1), channel_id=1, source_target_pairs={{0,24},{4,228},{8,0},{12,236},{16,8},{20,244},{24,16},{28,252},{32... | collective-permute-start | bytes 1671176 | tf_op jit(solution)/shard_map/ppermute | solution.py:45
  170.7 1.9 collective-permute-start.32
  172.7 12.5 %collective-permute-start.36 = (bf16[272,256]{1,0:T(8,128)(2,1)S(1)}, bf16[272,256]{1,0:T(8,128)(2,1)S(1)}, u32[]{:S(2)}, u32[]{:S(2)}) collective-permute-start(bf16[272,256]{1,0:T(8,128)(2,1)S(1)} %fusion.15), channel_id=1, source_target_pairs={{0,32},{4,12},{8,40},{12,20},{16,48},{20,28},{24,56},{28,4},{32,64... | collective-permute-start | bytes 417800 | tf_op jit(solution)/shard_map/ppermute | solution.py:45
  172.8 13.8 %collective-permute-start.40 = (f32[1,256]{1,0:T(1,128)S(1)}, f32[1,256]{1,0:T(1,128)S(1)}, u32[]{:S(2)}, u32[]{:S(2)}) collective-permute-start(f32[1,256]{1,0:T(1,128)S(1)} %broadcast_add_fusion.4), channel_id=1, source_target_pairs={{0,8},{4,12},{8,0},{12,4},{16,24},{20,28},{24,16},{28,20},{32,40},... | collective-permute-start | bytes 3080 | tf_op jit(solution)/shard_map/ppermute | solution.py:52
  185.5 7.5 %collective-permute-start.33 = (bf16[272,256]{1,0:T(8,128)(2,1)S(1)}, bf16[272,256]{1,0:T(8,128)(2,1)S(1)}, u32[]{:S(2)}, u32[]{:S(2)}) collective-permute-start(bf16[272,256]{1,0:T(8,128)(2,1)S(1)} %get-tuple-element.40), channel_id=1, source_target_pairs={{0,224},{4,28},{8,232},{12,4},{16,240},{20,12},{24,248},{28,20},{3... | collective-permute-start | bytes 417800 | tf_op jit(solution)/shard_map/ppermute | solution.py:45
  186.7 11.2 %collective-permute-start.41 = (f32[1,256]{1,0:T(1,128)S(1)}, f32[1,256]{1,0:T(1,128)S(1)}, u32[]{:S(2)}, u32[]{:S(2)}) collective-permute-start(f32[1,256]{1,0:T(1,128)S(1)} %broadcast_add_fusion.3), channel_id=1, source_target_pairs={{0,16},{4,20},{8,24},{12,28},{16,0},{20,4},{24,8},{28,12},{32,48},... | collective-permute-start | bytes 3080 | tf_op jit(solution)/shard_map/ppermute | solution.py:52
  192.5 6.6 %collective-permute-start.37 = (bf16[272,256]{1,0:T(8,128)(2,1)S(1)}, bf16[272,256]{1,0:T(8,128)(2,1)S(1)}, u32[]{:S(2)}, u32[]{:S(2)}) collective-permute-start(bf16[272,256]{1,0:T(8,128)(2,1)S(1)} %get-tuple-element.41), channel_id=1, source_target_pairs={{0,32},{4,20},{8,40},{12,28},{16,48},{20,4},{24,56},{28,12},{32,64... | collective-permute-start | bytes 417800 | tf_op jit(solution)/shard_map/ppermute | solution.py:45
  193.0 7.3 %collective-permute-start.34 = (bf16[272,256]{1,0:T(8,128)(2,1)S(1)}, bf16[272,256]{1,0:T(8,128)(2,1)S(1)}, u32[]{:S(2)}, u32[]{:S(2)}) collective-permute-start(bf16[272,256]{1,0:T(8,128)(2,1)S(1)} %fusion.5), channel_id=1, source_target_pairs={{0,224},{8,232},{16,240},{24,248},{32,0},{40,8},{48,16},{56,24},{6... | collective-permute-start | bytes 417800 | tf_op jit(solution)/shard_map/ppermute | solution.py:45
  197.9 5.4 %collective-permute-start.42 = (f32[1,256]{1,0:T(1,128)S(1)}, f32[1,256]{1,0:T(1,128)S(1)}, u32[]{:S(2)}, u32[]{:S(2)}) collective-permute-start(f32[1,256]{1,0:T(1,128)S(1)} %get-tuple-element.36), channel_id=1, source_target_pairs={{0,32},{4,36},{8,40},{12,44},{16,48},{20,52},{24,56},{28,60},{32,0... | collective-permute-start | bytes 3080 | tf_op jit(solution)/shard_map/ppermute | solution.py:52
  200.5 9.0 %collective-permute-start.38 = (bf16[272,256]{1,0:T(8,128)(2,1)S(1)}, bf16[272,256]{1,0:T(8,128)(2,1)S(1)}, u32[]{:S(2)}, u32[]{:S(2)}) collective-permute-start(bf16[272,256]{1,0:T(8,128)(2,1)S(1)} %get-tuple-element.43), channel_id=1, source_target_pairs={{0,32},{8,40},{16,48},{24,56},{32,64},{40,72},{48,80},{56,88},{64,... | collective-permute-start | bytes 417800 | tf_op jit(solution)/shard_map/ppermute | solution.py:45
  203.2 8.4 %collective-permute-start.43 = (f32[1,256]{1,0:T(1,128)S(1)}, f32[1,256]{1,0:T(1,128)S(1)}, u32[]{:S(2)}, u32[]{:S(2)}) collective-permute-start(f32[1,256]{1,0:T(1,128)S(1)} %get-tuple-element.34), channel_id=1, source_target_pairs={{0,64},{4,68},{8,72},{12,76},{16,80},{20,84},{24,88},{28,92},{32,9... | collective-permute-start | bytes 3080 | tf_op jit(solution)/shard_map/ppermute | solution.py:52
  205.5 15.3 %collective-permute-start.35 = (bf16[272,256]{1,0:T(8,128)(2,1)S(1)}, bf16[272,256]{1,0:T(8,128)(2,1)S(1)}, u32[]{:S(2)}, u32[]{:S(2)}) collective-permute-start(bf16[272,256]{1,0:T(8,128)(2,1)S(1)} %get-tuple-element.42), channel_id=1, source_target_pairs={{0,224},{8,232},{16,240},{24,248},{32,0},{40,8},{48,16},{56,24},{6... | collective-permute-start | bytes 417800 | tf_op jit(solution)/shard_map/ppermute | solution.py:45
  209.7 11.1 %collective-permute-start.39 = (bf16[272,256]{1,0:T(8,128)(2,1)S(1)}, bf16[272,256]{1,0:T(8,128)(2,1)S(1)}, u32[]{:S(2)}, u32[]{:S(2)}) collective-permute-start(bf16[272,256]{1,0:T(8,128)(2,1)S(1)} %fusion.18), channel_id=1, source_target_pairs={{0,32},{8,40},{16,48},{24,56},{32,64},{40,72},{48,80},{56,88},{64,... | collective-permute-start | bytes 417800 | tf_op jit(solution)/shard_map/ppermute | solution.py:45
  211.6 8.6 %collective-permute-start.44 = (f32[1,256]{1,0:T(1,128)S(1)}, f32[1,256]{1,0:T(1,128)S(1)}, u32[]{:S(2)}, u32[]{:S(2)}) collective-permute-start(f32[1,256]{1,0:T(1,128)S(1)} %get-tuple-element.32), channel_id=1, source_target_pairs={{0,128},{4,132},{8,136},{12,140},{16,144},{20,148},{24,152},{28,15... | collective-permute-start | bytes 3080 | tf_op jit(solution)/shard_map/ppermute | solution.py:52

commit v2 on v1

v2 whole, which is shorter than its diff:
```python
import functools

import jax
import jax.numpy as jnp
from jax import lax
from jax.experimental import pallas as pl
from jax.experimental.pallas import tpu as pltpu
from jax.sharding import PartitionSpec as P

F32 = jnp.float32
BF16 = jnp.bfloat16
NZ, NX, NY = 8, 4, 4
BLK = 128
SLOTS = 128
WIDTH = 256
NODES = 2 * BLK
W_ROWS = 16
ROWS = NODES + W_ROWS
UNROLL = 8
FETCH = 16
BIAS_ROWS = 16
SUM_ROWS = 4 * ROWS + BIAS_ROWS
MIB = 1 << 20
VMEM = 54 * MIB

LOW, HIGH, ACROSS = (0, 1, 7, 2), (6, 3, 5, 4), (0, 1, 3, 2)
GATHER_0 = tuple(
    tuple(k * NZ + j for j in group)
    for k, group in ((0, LOW), (1, LOW), (3, LOW), (2, LOW), (3, HIGH), (1, HIGH), (2, HIGH), (0, HIGH))
)
GATHER_1 = tuple(tuple(k * NZ + j for k in ACROSS) for j in (0, 1, 7, 2, 6, 3, 5, 4))
FORWARD_CHUNKS = ((0, 1, 2, 3, 4, 7), (5, 6), (8,))
BACKWARD_CHUNKS = ((0, 1), (2, 3, 4, 5, 6, 7))
FAR, NEAR = (4, 5, 3, 6), (2, 7, 1, 0)
SCATTER_0 = tuple(
    tuple((dx, dz) for dz in group)
    for dx, group in ((2, FAR), (2, NEAR), (1, FAR), (3, NEAR), (1, NEAR), (3, FAR), (0, NEAR), (0, FAR))
)
SCATTER_1 = tuple(tuple((dx, dz) for dx in ACROSS) for dz in (4, 5, 3, 6, 2, 7, 1, 0))


def shift(value, core_0=None, core_1=None):
    pairs = []
    for z in range(NZ):
        for x in range(NX):
            for core, step in enumerate((core_0, core_1)):
                if step is not None:
                    target = ((z + step[0]) % NZ * NX + (x + step[1]) % NX) * 2 + core
                    pairs.append(((z * NX + x) * 2 + core, target))
    return lax.ppermute(value, "dom", pairs)


Z_UP, Z_DOWN, Z_UP_2, Z_DOWN_2 = (1, 0), (-1, 0), (2, 0), (-2, 0)
X_UP, X_DOWN, X_TWO = (0, 1), (0, -1), (0, 2)


def swap(value, bit):
    return lax.ppermute(value, "dom", [(i, i ^ bit) for i in range(NZ * NX * 2)])


def y_shift(value, dy):
    return lax.ppermute(value, "feat", [(y, (y + dy) % NY) for y in range(NY)])


def smem():
    return pl.BlockSpec(memory_space=pltpu.SMEM)


def vmem():
    return pl.BlockSpec(memory_space=pltpu.VMEM)


def anywhere():
    return pl.BlockSpec(memory_space=pl.ANY)


def list_kernel(place, own, sib, lists):
    core, x, z = place[0], place[1], place[2]
    wide = (1, 2 * SLOTS)
    column = jnp.concatenate([own[1:2], sib[1:2]], axis=1)
    row = jnp.concatenate([own[0:1], sib[0:1] + 2], axis=1)
    slot = lax.broadcasted_iota(jnp.int32, wide, 1)
    live = slot < jnp.where(slot < SLOTS, place[4], SLOTS + place[5])
    owner = column >> 1
    chip = owner >> 1
    k = (x - (chip & (NX - 1))) & (NX - 1)
    j = (z - (chip >> 2)) & (NZ - 1)
    spot = (k * NZ + j) * 2 + (column & 1)
    mine = live & ((owner & 1) == core)
    on_0 = jnp.where(((k == 1) | (k == 2)) & (j >= 3) & (j <= 6), 1, 0)
    on_1 = jnp.where(j == 4, 2, jnp.where((j == 3) | (j == 5), 1, 0))
    forward_call = jnp.where(core == 0, on_0, on_1)
    backward_call = jnp.where(core == 0, jnp.where(k == 2, 0, 1), jnp.where((j == 3) | (j == 4), 0, 1))
    square = (2 * SLOTS, 2 * SLOTS)
    first = lax.broadcasted_iota(jnp.int32, square, 0)
    second = lax.broadcasted_iota(jnp.int32, square, 1)
    up_to = jnp.where(first <= second, 1.0, 0.0).astype(BF16)
    group_of = lax.broadcasted_iota(jnp.int32, (16, 2 * SLOTS), 0)
    lane = lax.broadcasted_iota(jnp.int32, (16, 2 * SLOTS), 1)
    before = jnp.where(
        lax.broadcasted_iota(jnp.int32, (16, 16), 1) < lax.broadcasted_iota(jnp.int32, (16, 16), 0), 1.0, 0.0
    ).astype(BF16)
    values = jnp.concatenate([slot, spot], axis=0).astype(F32)
    values = jnp.concatenate([values, jnp.zeros((14, 2 * SLOTS), F32)], axis=0).astype(BF16)
    lists[...] = jnp.zeros_like(lists)
    for at, call in ((0, forward_call), (3, backward_call)):
        group = jnp.where(mine, call * 4 + row, -1)
        member = jnp.where(group_of == group, 1.0, 0.0)
        rank = jnp.dot(member.astype(BF16), up_to, preferred_element_type=F32)
        counts = jnp.sum(member, axis=1, keepdims=True)
        earlier = jnp.dot(before, member.astype(BF16), preferred_element_type=F32)
        starts = jnp.sum(earlier, axis=1, keepdims=True)
        goal = jnp.sum(member * (starts + rank), axis=0, keepdims=True).astype(jnp.int32) - 1
        moved = jnp.where(first == goal, 1.0, 0.0).astype(BF16)
        ordered = lax.dot_general(values, moved, (((1,), (1,)), ((), ())), preferred_element_type=F32)
        lists[at : at + 1, :] = jnp.sum(jnp.where(group_of == lane, counts, 0.0), axis=0, keepdims=True).astype(jnp.int32)
        lists[at + 1 : at + 2, :] = jnp.sum(jnp.where(group_of == lane, starts, 0.0), axis=0, keepdims=True).astype(jnp.int32)
        lists[at + 2 : at + 3, :] = (ordered[0:1] * 64.0 + ordered[1:2]).astype(jnp.int32)
    told = jnp.zeros(wide, jnp.int32)
    for i in range(6):
        told = jnp.where(slot == i, place[i], told)
    lists[6:7, :] = told


def make_lists(place, own, sib):
    return pl.pallas_call(
        list_kernel,
        out_shape=jax.ShapeDtypeStruct((8, 2 * SLOTS), jnp.int32),
        in_specs=[smem(), vmem(), vmem()],
        out_specs=vmem(),
    )(place, own, sib)


def place_of(lists):
    return [lists[6, i] for i in range(4)]


def copy_each(copies, action):
    for condition, copy in copies:
        call = getattr(copy, action)
        if condition is None:
            call()
        else:
            pl.when(condition)(call)


class Tiles:
    def __init__(self, lists, at, call, every, own, sib, held, sem):
        self.lists, self.at, self.call, self.every = lists, at, call, every
        self.own, self.sib, self.held, self.sem = own, sib, held, sem
        self.begin = lists[at + 1, call * 4]
        self.end = lists[at + 1, call * 4 + 3] + lists[at, call * 4 + 3]

    def bulk(self):
        copies = []
        for which, source in enumerate((self.own, self.sib)):
            for step in range(SLOTS // FETCH):
                first = step * FETCH
                copy = pltpu.make_async_copy(
                    source.at[pl.ds(first, FETCH)],
                    self.held.at[pl.ds(which * SLOTS + first, FETCH)],
                    self.sem.at[which * (SLOTS // FETCH) + step],
                )
                copies.append((first < self.lists[6, 4 + which], copy))
        return copies

    def each(self, action):
        def step(p, carry):
            slot = self.lists[self.at + 2, p] >> 6
            goal = self.held.at[p]

            @pl.when(slot < SLOTS)
            def _():
                getattr(pltpu.make_async_copy(self.own.at[jnp.minimum(slot, SLOTS - 1)], goal, self.sem.at[0]), action)()

            @pl.when(slot >= SLOTS)
            def _():
                getattr(pltpu.make_async_copy(self.sib.at[jnp.maximum(slot - SLOTS, 0)], goal, self.sem.at[0]), action)()

            return carry

        lax.fori_loop(self.begin, self.end, step, 0)

    def start(self):
        if self.every:
            copy_each(self.bulk(), "start")
        else:
            self.each("start")
        self.held[2 * SLOTS] = jnp.zeros((BLK, BLK), BF16)

    def wait(self):
        if self.every:
            copy_each(self.bulk(), "wait")
        else:
            self.each("wait")

    def rows(self):
        for row in range(4):
            group = self.call * 4 + row
            number, first = self.lists[self.at, group], self.lists[self.at + 1, group]

            def pick(it, number=number, first=first):
                lefts, spots = [], []
                for u in range(UNROLL):
                    p = it * UNROLL + u
                    entry = self.lists[self.at + 2, first + jnp.minimum(p, number - 1)]
                    place = entry >> 6 if self.every else first + p
                    lefts.append(self.held[jnp.where(p < number, place, 2 * SLOTS)])
                    spots.append(entry & 63)
                return jnp.concatenate(lefts, axis=1), spots

            yield row, lax.div(number + (UNROLL - 1), UNROLL), pick


def forward_kernel(call, lists, own, sib, *rest):
    chosen = FORWARD_CHUNKS[call]
    chunks, rest = rest[: len(chosen)], rest[len(chosen) :]
    if call:
        sums_before, weight_before, *rest = rest
    sums, weight_out, blocks, held, sem, tile_sem = rest
    core, x, z, y = place_of(lists)
    tiles = Tiles(lists, 0, call, call == 0, own, sib, held, tile_sem)
    tiles.start()
    copies, arrived = [], []
    for n, chunk in zip(chosen, chunks):
        table = min(n, 7)
        condition = None if n < 7 else core == n - 7
        for i in range(4):
            spot = jnp.where(core == 0, GATHER_0[table][i], GATHER_1[table][i])
            copies.append((condition, pltpu.make_async_copy(chunk.at[i], blocks.at[spot], sem.at[len(copies)])))
            arrived.append((condition, spot))
    copy_each(copies, "start")
    copy_each(copies, "wait")
    tiles.wait()
    for row, steps, pick in tiles.rows():

        def step(it, total):
            left, spots = pick(it)
            rights = []
            for spot in spots:
                first = pl.multiple_of((spot & 1) * BLK, BLK)
                rights.append(blocks[spot >> 1, pl.ds(first, BLK), :])
            return total + jnp.dot(left, jnp.concatenate(rights, axis=0), preferred_element_type=F32)

        sums[row] = lax.fori_loop(0, steps, step, sums_before[row] if call else jnp.zeros((BLK, WIDTH), F32))
    if call:
        weight_out[...] = weight_before[...]
    for condition, spot in arrived:

        def keep(spot=spot):
            column = (x - (spot >> 3)) & (NX - 1)
            level = (z - spot) & (NZ - 1)
            part = ((level >> 1) - y) & (NY - 1)
            weight_out[part, (level & 1) * NX + column] = blocks[spot, NODES:ROWS, :]

        if condition is None:
            keep()
        else:
            pl.when(condition)(keep)


def forward(call, lists, own, sib, chunks, before):
    chosen = [chunks[n] for n in FORWARD_CHUNKS[call]]
    return pl.pallas_call(
        functools.partial(forward_kernel, call),
        out_shape=(
            jax.ShapeDtypeStruct((4, BLK, WIDTH), F32),
            jax.ShapeDtypeStruct((NY, 2 * NX, W_ROWS, WIDTH), BF16),
        ),
        in_specs=[smem()] + [anywhere()] * (2 + len(chosen)) + [vmem()] * len(before),
        out_specs=(vmem(),) * 2,
        scratch_shapes=[
            pltpu.VMEM((NX * NZ, ROWS, WIDTH), BF16),
            pltpu.VMEM((2 * SLOTS + 1, BLK, BLK), BF16),
            pltpu.SemaphoreType.DMA((24,)),
            pltpu.SemaphoreType.DMA((2 * SLOTS // FETCH,)),
        ],
        compiler_params=pltpu.CompilerParams(vmem_limit_bytes=VMEM),
        cost_estimate=pl.CostEstimate(
            flops=2 * BLK * BLK * WIDTH * len(chosen) * 16, bytes_accessed=len(chosen) * MIB, transcendentals=0
        ),
    )(lists, own, sib, *chosen, *before)


def backward_kernel(call, lists, own, sib, scaled, weight_sums, bias_rows, *rest):
    chosen = BACKWARD_CHUNKS[call]
    outs, rest = rest[: len(chosen)], rest[len(chosen) :]
    total, held, tile_sem = rest
    core, x, z, y = place_of(lists)
    tiles = Tiles(lists, 3, call, call == 1, own, sib, held, tile_sem)
    tiles.start()
    targets = {}
    for n in chosen:
        for i in range(4):
            dx = jnp.where(core == 0, SCATTER_0[n][i][0], SCATTER_1[n][i][0])
            dz = jnp.where(core == 0, SCATTER_0[n][i][1], SCATTER_1[n][i][1])
            spot = ((0 - dx) & (NX - 1)) * NZ + ((0 - dz) & (NZ - 1))
            targets[n, i] = dx, dz, spot
            total[spot * 2] = jnp.zeros((BLK, WIDTH), F32)
            total[spot * 2 + 1] = jnp.zeros((BLK, WIDTH), F32)
    tiles.wait()
    for row, steps, pick in tiles.rows():
        right = scaled[row]

        def step(it, carry):
            left, spots = pick(it)
            terms = lax.dot_general(left, right, (((0,), (0,)), ((), ())), preferred_element_type=F32)
            for u, spot in enumerate(spots):
                total[spot] += terms[u * BLK : (u + 1) * BLK]
            return carry

        lax.fori_loop(0, steps, step, 0)
    for n, out in zip(chosen, outs):
        for i in range(4):
            dx, dz, spot = targets[n, i]
            first = i * ROWS
            out[first : first + BLK, :] = total[spot * 2].astype(BF16)
            out[first + BLK : first + NODES, :] = total[spot * 2 + 1].astype(BF16)
            column = (x + dx) & (NX - 1)
            level = (z + dz) & (NZ - 1)
            part = ((level >> 1) - y) & (NY - 1)
            out[first + NODES : first + ROWS, :] = weight_sums[part, (level & 1) * NX + column]
        out[4 * ROWS : SUM_ROWS, :] = bias_rows[...] if call == 0 else jnp.zeros((BIAS_ROWS, WIDTH), BF16)


def backward(call, lists, own, sib, scaled, weight_sums, bias_rows):
    number = len(BACKWARD_CHUNKS[call])
    return pl.pallas_call(
        functools.partial(backward_kernel, call),
        out_shape=(jax.ShapeDtypeStruct((SUM_ROWS, WIDTH), BF16),) * number,
        in_specs=[smem()] + [anywhere()] * 2 + [vmem()] * 3,
        out_specs=(vmem(),) * number,
        scratch_shapes=[
            pltpu.VMEM((2 * NX * NZ, BLK, WIDTH), F32),
            pltpu.VMEM((2 * SLOTS + 1, BLK, BLK), BF16),
            pltpu.SemaphoreType.DMA((2 * SLOTS // FETCH,)),
        ],
        compiler_params=pltpu.CompilerParams(vmem_limit_bytes=VMEM),
        cost_estimate=pl.CostEstimate(
            flops=2 * BLK * BLK * WIDTH * number * 16, bytes_accessed=number * MIB, transcendentals=0
        ),
    )(lists, own, sib, scaled, weight_sums, bias_rows)


def gather(block, core, ready, sorted_lists, call):
    p1 = shift(block, Z_UP, X_UP)
    p2 = shift(block, Z_DOWN, X_DOWN)
    p3 = shift(block, Z_UP_2, X_TWO)
    p4 = shift(block, Z_DOWN_2)
    low = jnp.stack([block, p1, p2, p3]) + (ready + nothing(p4[0, 0]))
    c1 = shift(low, X_UP, Z_UP)
    c2 = shift(low, X_DOWN, Z_DOWN)
    p5 = shift(p3, Z_UP)
    p6 = shift(p4, Z_DOWN)
    p7 = shift(p3, Z_UP_2)
    high = jnp.stack([p4, p5, p6, p7])
    c3 = shift(c1 + nothing(high[1:, 0, 0].sum()), X_UP, Z_UP)
    c4 = shift(jnp.where(core == 0, high, c2) + sorted_lists, X_DOWN, Z_DOWN)
    c5 = shift(jnp.where(core == 0, high, c3), X_UP, Z_UP)
    c6 = shift(c4, X_DOWN, Z_DOWN)
    chunks = [low, c1, c2, c3, c4, c5, c6, high]
    sums = call(0, chunks, ())
    c7 = shift(c5 + nothing(sums[0][0, 0, 0]), None, Z_UP)
    chunks.append(c7)
    sums = call(1, chunks, sums)
    return call(2, chunks, sums)


def add(*values):
    total = values[0].astype(F32)
    for value in values[1:]:
        total = total + value.astype(F32)
    return total


def split(value):
    high = lax.reduce_precision(value, 8, 7)
    middle = lax.reduce_precision(value - high, 8, 7)
    rows = jnp.concatenate([high, middle, value - high - middle], axis=0)
    return jnp.pad(rows, ((0, BIAS_ROWS - 3), (0, 0))).astype(BF16)


def joined(block, first=0):
    rows = block[first : first + 3].astype(F32)
    return rows[0:1] + rows[1:2] + rows[2:3]


def in_order(values, place):
    count = len(values)
    rows = jnp.concatenate([values[k] for k in range(count - 1, -1, -1)] * 2, axis=0)
    rows = lax.dynamic_slice_in_dim(rows, count - 1 - place, count, 0)
    total = rows[0:1]
    for i in range(1, count):
        total = total + rows[i : i + 1]
    return total


def scatter(parts, core, x, z, chip_bias):
    a, b, c, d, e, f, g, h = parts
    zero = jnp.zeros((), BF16)
    j1 = shift(a, X_UP, Z_UP)
    j2 = shift(b, X_DOWN, Z_DOWN)
    j3 = shift(add(c, j1).astype(BF16), X_UP, Z_UP)
    j4 = shift(add(d, j2).astype(BF16), X_DOWN, Z_DOWN)
    j5 = shift(add(e, jnp.where(core == 0, zero, j3)).astype(BF16), X_UP, Z_UP)
    j6 = shift(add(f, jnp.where(core == 0, zero, j4)).astype(BF16), X_DOWN, Z_DOWN)
    j7 = shift(add(g, j5).astype(BF16), None, Z_UP)

    def tail(value):
        return value[4 * ROWS :]

    line_bias = in_order([chip_bias, joined(tail(j1)), joined(tail(j3)), joined(tail(j2))], x)
    own_rows = split(line_bias)

    def block(value, i):
        return value[i * ROWS : (i + 1) * ROWS]

    def far(i):
        return add(block(h, i), block(j3, i), block(j6, i))

    def near(i):
        return add(block(g, i), block(j4, i), block(j5, i))

    def across(i):
        return add(block(h, i), block(j6, i), block(j7, i))

    def message(value, rows=own_rows):
        return jnp.concatenate([value.astype(BF16), rows], axis=0)

    r4 = shift(message(far(0)), Z_UP_2)
    r31 = shift(jnp.concatenate([message(far(2)), message(near(2))], axis=0), Z_UP)
    r57 = shift(jnp.concatenate([message(far(1)), message(near(1))], axis=0), Z_DOWN)
    size = ROWS + BIAS_ROWS
    r3, r1, r5, r7 = r31[:size], r31[size:], r57[:size], r57[size:]
    rows = jnp.concatenate([own_rows[:3], r4[ROWS : ROWS + 3], r3[ROWS : ROWS + 3], own_rows[9:]], axis=0)
    on_0 = message(add(near(0), r4[:ROWS], r3[:ROWS], nothing(r57[0, 0])), rows)
    r2 = shift(jnp.where(core == 0, on_0, message(across(1))), Z_UP_2, X_UP)
    rows = jnp.concatenate([own_rows[:3], r5[ROWS : ROWS + 3], own_rows[6:]], axis=0)
    on_0 = message(add(far(3), r5[:ROWS]), rows)
    r6 = shift(jnp.where(core == 0, on_0, message(across(2))), Z_DOWN_2, X_DOWN)
    r0 = shift(across(3).astype(BF16), None, X_TWO)
    total = jnp.where(
        core == 0,
        add(near(3), r1[:ROWS], r2[:ROWS], r6[:ROWS], r7[:ROWS]),
        add(across(0), r2[:ROWS], r6[:ROWS], r0),
    )
    bias = in_order(
        [
            line_bias,
            joined(r1, ROWS),
            joined(r2, ROWS),
            joined(r2, ROWS + 6),
            joined(r2, ROWS + 3),
            joined(r6, ROWS + 3),
            joined(r6, ROWS),
            joined(r7, ROWS),
        ],
        z,
    )
    return total, bias


def nothing(value):
    return jnp.minimum(jnp.abs(value.astype(F32)), 0.0).astype(BF16)


def silu_parts(hidden):
    gate_value = jax.nn.sigmoid(hidden)
    return (hidden * gate_value, gate_value * (1.0 + hidden * (1.0 - gate_value)))


def on_device(feats, weight, bias, tile_values, tile_rows, tile_cols, tile_live, cotangent):
    dom = lax.axis_index("dom")
    y = lax.axis_index("feat")
    core = dom % 2
    x = (dom // 2) % NX
    z = dom // (2 * NX)

    meta = jnp.stack([tile_rows, tile_cols, jnp.broadcast_to(tile_live, (SLOTS,))])
    other_meta = swap(meta, 1)
    other_tiles = swap(tile_values, 1)
    place = jnp.stack([core, x, z, y, tile_live[0], other_meta[2, 0]]).astype(jnp.int32)
    lists = make_lists(place, meta, other_meta)

    own_live = jnp.arange(SLOTS, dtype=jnp.int32) < tile_live[0]
    row_sums = jnp.sum(tile_values, axis=2, dtype=F32)
    degree = 1.0 + jnp.concatenate(
        [
            jnp.sum(jnp.where((own_live & (tile_rows == row))[:, None], row_sums, 0.0), axis=0)
            for row in range(2)
        ]
    ).reshape(NODES, 1)

    sums, weight_lane = gather(
        jnp.concatenate([feats, weight.T], axis=0),
        core,
        nothing(other_tiles[0, 0, 0]) + nothing(other_meta[0, 0]),
        nothing(lists[0, 0]),
        lambda call, chunks, before: forward(call, lists, tile_values, other_tiles, chunks, before),
    )
    neighbour_sum = (sums[:2] + swap(sums[2:], 1)).reshape(NODES, WIDTH)
    weight_other = swap(weight_lane, 1)
    mixed = ((feats.astype(F32) + neighbour_sum) / degree).astype(BF16)

    first = jnp.where(core == 0, weight_lane, weight_other)
    second = jnp.where(core == 0, weight_other, weight_lane)
    weight_t = jnp.stack([first, second], axis=2).reshape(NY, WIDTH, WIDTH)

    def hidden_part(dy):
        return lax.dot_general(mixed, weight_t[dy], (((1,), (1,)), ((), ())), preferred_element_type=F32)

    hidden = add(
        hidden_part(0),
        y_shift(hidden_part(1).astype(BF16), 1),
        y_shift(hidden_part(2).astype(BF16), 2),
        y_shift(hidden_part(3).astype(BF16), 3),
    ) + bias
    activated, slope = silu_parts(hidden)
    output = activated.astype(BF16)
    dz_full = cotangent.astype(F32) * slope
    dz_own = dz_full.astype(BF16)
    dz_parts = [dz_own] + [y_shift(dz_own, NY - dy) for dy in range(1, NY)]

    dmixed = sum(jnp.dot(dz_parts[dy], weight_t[dy], preferred_element_type=F32) for dy in range(NY))
    scaled = (dmixed / degree).astype(BF16)
    scaled_blocks = jnp.concatenate([scaled, swap(scaled, 1)], axis=0).reshape(4, BLK, WIDTH)

    weight_part = jnp.stack(
        [
            lax.dot_general(dz_parts[dy], mixed, (((0,), (0,)), ((), ())), preferred_element_type=F32)
            for dy in range(NY)
        ]
    ).reshape(NY, 2 * NX, 2, W_ROWS, WIDTH)
    mine = jnp.where(core == 0, weight_part[:, :, 0], weight_part[:, :, 1])
    others = jnp.where(core == 0, weight_part[:, :, 1], weight_part[:, :, 0])
    bias_part = jnp.sum(dz_full, axis=0, keepdims=True)
    bias_rows = jnp.pad(bias_part, ((0, 7), (0, 0)))
    sent = jnp.concatenate([others.reshape(-1, WIDTH), bias_rows], axis=0)
    got = swap(sent, 1)
    weight_sums = (mine + got[:-8].reshape(mine.shape)).astype(BF16)

    chip_bias = bias_part + got[-8:-7]
    parts = []
    for call in range(len(BACKWARD_CHUNKS)):
        parts += backward(call, lists, tile_values, other_tiles, scaled_blocks, weight_sums, split(chip_bias))
    column_sum, bias_sum = scatter(parts, core, x, z, chip_bias)
    from_core_0 = lax.ppermute(bias_sum, "dom", [(i, i + 1) for i in range(0, NZ * NX * 2, 2)])
    bias_grad = jnp.where(core == 0, bias_sum, from_core_0)

    feats_grad = (scaled.astype(F32) + column_sum[:NODES]).astype(BF16)
    weight_grad = column_sum[NODES:].T
    return (output, feats_grad, weight_grad, bias_grad.reshape(WIDTH))


def solution(mesh):
    return jax.shard_map(
        on_device,
        mesh=mesh,
        in_specs=(
            P("dom", "feat"),
            P("feat", "dom"),
            P("feat"),
            P("dom", None, None),
            P("dom"),
            P("dom"),
            P("dom"),
            P("dom", "feat"),
        ),
        out_specs=(P("dom", "feat"), P("dom", "feat"), P("feat", "dom"), P("feat")),
        check_vma=False,
    )
```

time: 223 us -> 224 us (level)
  the two profiles are of different devices: /device:TPU:2 before, /device:TPU:1 now
where the time goes in v2:
time: 224 us
  waiting for transfers between devices  74.8 us (33%)
  starting transfers between devices  60.9 us (27%)
  Pallas kernels  34.7 us (15%)
  other arithmetic  23.6 us (11%)
  local copies, waits for them, and re-layouts  20.4 us (9%)
  between operations  6.93 us (3%)
  matrix products  2.49 us (1%)
    ppermute x27, waiting for transfers between devices, shift(): return lax.ppermute(value, 'dom', pairs)  48.1 us
    ppermute x27, starting transfers between devices, shift(): return lax.ppermute(value, 'dom', pairs)  34.2 us
    ppermute x6, starting transfers between devices, swap(): lax.ppermute(value, 'dom', [(i, i ^ bit) for i in range(NZ * NX * 2)])  18.7 us
    pallas_call x3, Pallas kernels, forward(): pl.pallas_call(functools.partial(forward_kernel, call), out_shape=(jax.Sh...  18.2 us
    pallas_call x2, Pallas kernels, backward(): pl.pallas_call(functools.partial(backward_kernel, call), out_shape=(jax.S...  14.6 us
    ppermute x6, waiting for transfers between devices, y_shift(): return lax.ppermute(value, 'feat', [(y, (y + dy) % NY) for y in range(NY)])  13 us
    ppermute x1, waiting for transfers between devices, on_device(): lax.ppermute(bias_sum, 'dom', [(i, i + 1) for i in range(0, NZ * NX * 2,...  10.2 us
    ppermute x6, starting transfers between devices, y_shift(): return lax.ppermute(value, 'feat', [(y, (y + dy) % NY) for y in range(NY)])  6.79 us
  transfers between devices with their start and end apart: 40, of which 19 were waited for; matrix products, arithmetic and copies ran while one was open for 14% of the time, Pallas kernels for 11%

profile of v2, /device:TPU:1, one launch (start us, length us, event | category | flops | bytes accessed | tf_op | source)
XLA Modules:
  0.0 223.9 jit_solution(17218813485588513447)
XLA Ops:
  0.6 3.3 %collective-permute-start.1 = (bf16[128,128,128]{2,1,0:T(8,128)(2,1)}, bf16[128,128,128]{2,1,0:T(8,128)(2,1)S(1)}, u32[]{:S(2)}, u32[]{:S(2)}) collective-permute-start(bf16[128,128,128]{2,1,0:T(8,128)(2,1)} %own.9), channel_id=1, source_target_pairs={{0,4},{4,0},{8,12},{12,8},{16,20},{20,16},{24,28},{28,24},{32,36},... | collective-permute-start | bytes 12582920 | tf_op jit(solution)/shard_map/ppermute | solution.py:58
  5.5 0.9 fusion.53
  7.1 1.1 collective-permute-start.3
  8.2 0.9 collective-permute-start.8
  9.0 1.7 collective-permute-done.sib
  13.2 2.0 copy-done.1
  16.5 1.2 collective-permute-start.9
  21.0 4.0 %collective-permute-start.12 = (bf16[4,272,256]{2,1,0:T(8,128)(2,1)S(1)}, bf16[4,272,256]{2,1,0:T(8,128)(2,1)S(1)}, u32[]{:S(2)}, u32[]{:S(2)}) collective-permute-start(bf16[4,272,256]{2,1,0:T(8,128)(2,1)S(1)} %maximum_add_fusion.rest_0_), channel_id=1, source_target_pairs={{0,24},{4,228},{8,0},{12,236},{16,8},{20,244},{24,16},{28,252},{32... | collective-permute-start | bytes 1671176 | tf_op jit(solution)/shard_map/ppermute | solution.py:50
  25.1 3.9 %collective-permute-done.9.rest_1_ = bf16[4,272,256]{2,1,0:T(8,128)(2,1)S(1)} collective-permute-done((bf16[4,272,256]{2,1,0:T(8,128)(2,1)S(1)}, bf16[4,272,256]{2,1,0:T(8,128)(2,1)S(1)}, u32[]{:S(2)}, u32[]{:S(2)}) %collective-permute-start.9) | collective-permute-done | bytes 557088 | tf_op jit(solution)/shard_map/ppermute | solution.py:50
  29.2 1.2 stack.87.place
  30.4 1.8 shard_map.114.lists
  32.2 1.2 slice.491
  34.1 7.8 %collective-permute-done.10.rest_3_ = bf16[4,272,256]{2,1,0:T(8,128)(2,1)S(1)} collective-permute-done((bf16[4,272,256]{2,1,0:T(8,128)(2,1)S(1)}, bf16[4,272,256]{2,1,0:T(8,128)(2,1)S(1)}, u32[]{:S(2)}, u32[]{:S(2)}) %collective-permute-start.10) | collective-permute-done | bytes 557088 | tf_op jit(solution)/shard_map/ppermute | solution.py:50
  41.9 1.0 pad_maximum_fusion.1
  42.9 1.0 collective-permute-start.13
  44.5 7.2 %collective-permute-done.13.rest_4_ = bf16[4,272,256]{2,1,0:T(8,128)(2,1)S(1)} collective-permute-done((bf16[4,272,256]{2,1,0:T(8,128)(2,1)S(1)}, bf16[4,272,256]{2,1,0:T(8,128)(2,1)S(1)}, u32[]{:S(2)}, u32[]{:S(2)}) %collective-permute-start.13) | collective-permute-done | bytes 557088 | tf_op jit(solution)/shard_map/ppermute | solution.py:50
  52.5 8.0 %shard_map.115 = (f32[4,128,256]{2,1,0:T(8,128)}, bf16[4,8,16,256]{3,2,1,0:T(8,128)(2,1)}) custom-call(s32[8,256]{1,0:T(8,128)} %shard_map.114.lists, bf16[128,128,128]{2,1,0:T(8,128)(2,1)} %own.9, bf16[128,128,128]{2,1,0:T(8,128)(2,1)} %copy-done.1, bf16[4,272,256]{2,1,0:T(8,128)(2,1)} %copy-done.5, bf16[4,272,256]{2,1,0:T(8,128)(2,1)} %copy-done.6, ...), custom_call_target="tpu_custom_call" | custom-call | flops 805306368 | bytes 6291456 | tf_op jit(solution)/shard_map/pallas_call | solution.py:264
  60.6 1.2 slice.383
  62.4 3.7 %collective-permute-start.15 = (bf16[4,272,256]{2,1,0:T(8,128)(2,1)}, bf16[4,272,256]{2,1,0:T(8,128)(2,1)S(1)}, u32[]{:S(2)}, u32[]{:S(2)}) collective-permute-start(bf16[4,272,256]{2,1,0:T(8,128)(2,1)} %copy-done.12), channel_id=1, source_target_pairs={{0,24},{4,228},{8,0},{12,236},{16,8},{20,244},{24,16},{28,252},{32... | collective-permute-start | bytes 1671176 | tf_op jit(solution)/shard_map/ppermute | solution.py:50
  66.1 1.9 collective-permute-start.14
  68.1 1.2 convert_reduce_fusion
  69.2 3.6 %collective-permute-done.15.rest_1_ = bf16[4,272,256]{2,1,0:T(8,128)(2,1)S(1)} collective-permute-done((bf16[4,272,256]{2,1,0:T(8,128)(2,1)}, bf16[4,272,256]{2,1,0:T(8,128)(2,1)S(1)}, u32[]{:S(2)}, u32[]{:S(2)}) %collective-permute-start.15) | collective-permute-done | bytes 557088 | tf_op jit(solution)/shard_map/ppermute | solution.py:50
  73.7 5.8 %shard_map.116 = (f32[4,128,256]{2,1,0:T(8,128)}, bf16[4,8,16,256]{3,2,1,0:T(8,128)(2,1)}) custom-call(s32[8,256]{1,0:T(8,128)} %shard_map.114.lists, bf16[128,128,128]{2,1,0:T(8,128)(2,1)} %own.9, bf16[128,128,128]{2,1,0:T(8,128)(2,1)} %copy-done.1, bf16[4,272,256]{2,1,0:T(8,128)(2,1)} %copy-done.7, bf16[4,272,256]{2,1,0:T(8,128)(2,1)} %copy-done.13, ...), custom_call_target="tpu_custom_call" | custom-call | flops 268435456 | bytes 2097152 | tf_op jit(solution)/shard_map/pallas_call | solution.py:264
  80.3 4.4 %shard_map.117 = (f32[4,128,256]{2,1,0:T(8,128)}, bf16[4,8,16,256]{3,2,1,0:T(8,128)(2,1)}) custom-call(s32[8,256]{1,0:T(8,128)} %shard_map.114.lists, bf16[128,128,128]{2,1,0:T(8,128)(2,1)} %own.9, bf16[128,128,128]{2,1,0:T(8,128)(2,1)} %copy-done.1, bf16[4,272,256]{2,1,0:T(8,128)(2,1)} %copy-done.14, f32[4,128,256]{2,1,0:T(8,128)} %get-tuple-element.20.rest_1_, ...), custom_call_target="tpu_custom_call" | custom-call | flops 134217728 | bytes 1048576 | tf_op jit(solution)/shard_map/pallas_call | solution.py:264
  84.7 12.8 %collective-permute-start.17 = (bf16[4,8,16,256]{3,2,1,0:T(8,128)(2,1)}, bf16[4,8,16,256]{3,2,1,0:T(8,128)(2,1)S(1)}, u32[]{:S(2)}, u32[]{:S(2)}) collective-permute-start(bf16[4,8,16,256]{3,2,1,0:T(8,128)(2,1)} %get-tuple-element.23), channel_id=1, source_target_pairs={{0,4},{4,0},{8,12},{12,8},{16,20},{20,16},{24,28},{28,24},{32,36},... | collective-permute-start | bytes 786440 | tf_op jit(solution)/shard_map/ppermute | solution.py:58
  97.6 1.0 slice.385
  98.9 1.0 select_bitcast_fusion.1
  101.2 2.8 %collective-permute-start.20 = (bf16[256,256]{1,0:T(8,128)(2,1)S(1)}, bf16[256,256]{1,0:T(8,128)(2,1)S(1)}, u32[]{:S(2)}, u32[]{:S(2)}) collective-permute-start(bf16[256,256]{1,0:T(8,128)(2,1)S(1)} %convolution_convert_fusion), channel_id=1, source_target_pairs={{0,3},{1,0},{2,1},{3,2},{4,7},{5,4},{6,5},{7,6},{8,11},{9,8},{10,9... | collective-permute-start | bytes 393224 | tf_op jit(solution)/shard_map/ppermute | solution.py:62
  105.9 3.3 %collective-permute-done.20 = bf16[256,256]{1,0:T(8,128)(2,1)S(1)} collective-permute-done((bf16[256,256]{1,0:T(8,128)(2,1)S(1)}, bf16[256,256]{1,0:T(8,128)(2,1)S(1)}, u32[]{:S(2)}, u32[]{:S(2)}) %collective-permute-start.20) | collective-permute-done | bytes 131104 | tf_op jit(solution)/shard_map/ppermute | solution.py:62
  109.2 1.0 collective-permute-done.19
  110.2 3.8 %collective-permute-done.18 = bf16[256,256]{1,0:T(8,128)(2,1)S(1)} collective-permute-done((bf16[256,256]{1,0:T(8,128)(2,1)S(1)}, bf16[256,256]{1,0:T(8,128)(2,1)S(1)}, u32[]{:S(2)}, u32[]{:S(2)}) %collective-permute-start.18) | collective-permute-done | bytes 131104 | tf_op jit(solution)/shard_map/ppermute | solution.py:62
  115.1 2.8 %collective-permute-start.21 = (bf16[256,256]{1,0:T(8,128)(2,1)S(1)}, bf16[256,256]{1,0:T(8,128)(2,1)S(1)}, u32[]{:S(2)}, u32[]{:S(2)}) collective-permute-start(bf16[256,256]{1,0:T(8,128)(2,1)S(1)} %get-tuple-element.39), channel_id=1, source_target_pairs={{0,3},{1,0},{2,1},{3,2},{4,7},{5,4},{6,5},{7,6},{8,11},{9,8},{10,9... | collective-permute-start | bytes 393224 | tf_op jit(solution)/shard_map/ppermute | solution.py:62
  118.0 2.6 %collective-permute-done.23 = bf16[256,256]{1,0:T(8,128)(2,1)S(1)} collective-permute-done((bf16[256,256]{1,0:T(8,128)(2,1)S(1)}, bf16[256,256]{1,0:T(8,128)(2,1)S(1)}, u32[]{:S(2)}, u32[]{:S(2)}) %collective-permute-start.23) | collective-permute-done | bytes 131104 | tf_op jit(solution)/shard_map/ppermute | solution.py:62
  120.9 2.3 %collective-permute-done.22 = bf16[256,256]{1,0:T(8,128)(2,1)S(1)} collective-permute-done((bf16[256,256]{1,0:T(8,128)(2,1)S(1)}, bf16[256,256]{1,0:T(8,128)(2,1)S(1)}, u32[]{:S(2)}, u32[]{:S(2)}) %collective-permute-start.22) | collective-permute-done | bytes 131104 | tf_op jit(solution)/shard_map/ppermute | solution.py:62
  123.9 2.3 %collective-permute-start.25 = (f32[520,256]{1,0:T(8,128)S(1)}, f32[520,256]{1,0:T(8,128)S(1)}, u32[]{:S(2)}, u32[]{:S(2)}) collective-permute-start(f32[520,256]{1,0:T(8,128)S(1)} %select_maximum_fusion), channel_id=1, source_target_pairs={{0,4},{4,0},{8,12},{12,8},{16,20},{20,16},{24,28},{28,24},{32,36},... | collective-permute-start | bytes 1597448 | tf_op jit(solution)/shard_map/ppermute | solution.py:58
  126.8 1.3 collective-permute-done.24
  130.4 4.9 %shard_map.119 = (bf16[1104,256]{1,0:T(8,128)(2,1)}, bf16[1104,256]{1,0:T(8,128)(2,1)}) custom-call(s32[8,256]{1,0:T(8,128)} %shard_map.114.lists, bf16[128,128,128]{2,1,0:T(8,128)(2,1)} %own.9, bf16[128,128,128]{2,1,0:T(8,128)(2,1)} %copy-done.1, bf16[4,128,256]{2,1,0:T(8,128)(2,1)} %bitcast.91, bf16[4,8,16,256]{3,2,1,0:T(8,128)(2,1)} %fusion.3.weight_sums, ...), custom_call_target="tpu_custom_call" | custom-call | flops 268435456 | bytes 2097152 | tf_op jit(solution)/shard_map/pallas_call | solution.py:328
  135.5 2.7 %collective-permute-start.26 = (bf16[1104,256]{1,0:T(8,128)(2,1)}, bf16[1104,256]{1,0:T(8,128)(2,1)S(1)}, u32[]{:S(2)}, u32[]{:S(2)}) collective-permute-start(bf16[1104,256]{1,0:T(8,128)(2,1)} %get-tuple-element.26), channel_id=1, source_target_pairs={{0,24},{4,228},{8,0},{12,236},{16,8},{20,244},{24,16},{28,252},{32... | collective-permute-start | bytes 1695752 | tf_op jit(solution)/shard_map/ppermute | solution.py:50
  138.1 9.7 %shard_map.118 = (bf16[1104,256]{1,0:T(8,128)(2,1)}, bf16[1104,256]{1,0:T(8,128)(2,1)}, bf16[1104,256]{1,0:T(8,128)(2,1)}, bf16[1104,256]{1,0:T(8,128)(2,1)}, bf...) custom-call(s32[8,256]{1,0:T(8,128)} %shard_map.114.lists, bf16[128,128,128]{2,1,0:T(8,128)(2,1)} %own.9, ...), custom_call_target="tpu_custom_call" | custom-call | flops 805306368 | bytes 6291456 | tf_op jit(solution)/shard_map/pallas_call | solution.py:328
  147.9 1.3 add_convert_fusion.3
  149.4 2.7 %collective-permute-start.27 = (bf16[1104,256]{1,0:T(8,128)(2,1)S(1)}, bf16[1104,256]{1,0:T(8,128)(2,1)S(1)}, u32[]{:S(2)}, u32[]{:S(2)}) collective-permute-start(bf16[1104,256]{1,0:T(8,128)(2,1)S(1)} %add_convert_fusion.4), channel_id=1, source_target_pairs={{0,24},{4,228},{8,0},{12,236},{16,8},{20,244},{24,16},{28,252},{32... | collective-permute-start | bytes 1695752 | tf_op jit(solution)/shard_map/ppermute | solution.py:50
  152.2 7.0 %collective-permute-done.29 = bf16[1104,256]{1,0:T(8,128)(2,1)S(1)} collective-permute-done((bf16[1104,256]{1,0:T(8,128)(2,1)S(1)}, bf16[1104,256]{1,0:T(8,128)(2,1)S(1)}, u32[]{:S(2)}, u32[]{:S(2)}) %collective-permute-start.29) | collective-permute-done | bytes 565280 | tf_op jit(solution)/shard_map/ppermute | solution.py:50
  159.5 1.0 add_convert_fusion.1
  160.5 2.6 %collective-permute-start.31 = (bf16[1104,256]{1,0:T(8,128)(2,1)}, bf16[1104,256]{1,0:T(8,128)(2,1)S(1)}, u32[]{:S(2)}, u32[]{:S(2)}) collective-permute-start(bf16[1104,256]{1,0:T(8,128)(2,1)} %add_convert_fusion.1), channel_id=1, source_target_pairs={{0,24},{4,228},{8,0},{12,236},{16,8},{20,244},{24,16},{28,252},{32... | collective-permute-start | bytes 1695752 | tf_op jit(solution)/shard_map/ppermute | solution.py:50
  163.3 6.2 %collective-permute-done.30 = bf16[1104,256]{1,0:T(8,128)(2,1)S(1)} collective-permute-done((bf16[1104,256]{1,0:T(8,128)(2,1)S(1)}, bf16[1104,256]{1,0:T(8,128)(2,1)S(1)}, u32[]{:S(2)}, u32[]{:S(2)}) %collective-permute-start.30) | collective-permute-done | bytes 565280 | tf_op jit(solution)/shard_map/ppermute | solution.py:50
  169.6 1.9 collective-permute-start.35
  172.3 8.9 %collective-permute-done.35 = bf16[1104,256]{1,0:T(8,128)(2,1)S(1)} collective-permute-done((bf16[1104,256]{1,0:T(8,128)(2,1)S(1)}, bf16[1104,256]{1,0:T(8,128)(2,1)S(1)}, u32[]{:S(2)}, u32[]{:S(2)}) %collective-permute-start.35) | collective-permute-done | bytes 565280 | tf_op jit(solution)/shard_map/ppermute | solution.py:50
  181.2 1.0 fusion.14
  182.9 1.4 collective-permute-start.34
  184.3 1.9 collective-permute-start.38
  186.3 1.7 fusion.10
  190.2 1.3 collective-permute-start.33
  191.5 1.2 slice.531
  193.4 1.3 slice_convert_fusion.6
  195.3 2.4 %concatenate.68 = bf16[288,256]{1,0:T(8,128)(2,1)S(1)} concatenate(bf16[272,256]{1,0:T(8,128)(2,1)} %get-tuple-element.44, bf16[1,256]{1,0:T(2,128)(2,1)} %copy-done.26, bf16[1,256]{1,0:T(2,128)(2,1)} %copy-done.24, bf16[1,256]{1,0:T(2,128)(2,1)} %copy-done.25, bf16[3,256]{1,0:T(4,128)(2,1)} %get-tuple-element.62, bf16[10,256]{1,0:T(8,128)(2,1)} %slice.445), dimensions={0} | concatenate | bytes 294912 | tf_op jit(solution)/shard_map/concatenate | solution.py:428
  197.7 1.3 slice.532
  200.3 1.1 add_convert_fusion.5
  201.4 1.6 concatenate.66
  203.2 1.4 collective-permute-start.36
  205.4 1.7 collective-permute-done.37
  207.1 1.8 collective-permute-done.36
  208.9 1.3 fusion.20
  211.1 1.3 collective-permute-start.39
  213.0 10.2 %collective-permute-done.39 = f32[1,256]{1,0:T(1,128)S(1)} collective-permute-done((f32[1,256]{1,0:T(1,128)S(1)}, f32[1,256]{1,0:T(1,128)S(1)}, u32[]{:S(2)}, u32[]{:S(2)}) %collective-permute-start.39) | collective-permute-done | bytes 1056 | tf_op jit(solution)/shard_map/ppermute | solution.py:547
  (182 shorter events, 27.1 us)
Async XLA Ops:
  0.6 12.5 %collective-permute-start.1 = (bf16[128,128,128]{2,1,0:T(8,128)(2,1)}, bf16[128,128,128]{2,1,0:T(8,128)(2,1)S(1)}, u32[]{:S(2)}, u32[]{:S(2)}) collective-permute-start(bf16[128,128,128]{2,1,0:T(8,128)(2,1)} %own.9), channel_id=1, source_target_pairs={{0,4},{4,0},{8,12},{12,8},{16,20},{20,16},{24,28},{28,24},{32,36},... | collective-permute-start | bytes 12582920 | tf_op jit(solution)/shard_map/ppermute | solution.py:58
  5.4 23.6 %copy-start.30 = (s32[3,128]{1,0:T(4,128)}, s32[3,128]{1,0:T(4,128)S(1)}, u32[]{:S(2)}) copy-start(s32[3,128]{1,0:T(4,128)S(1)} %add_add_fusion.1.own) | copy-start | bytes 4612
  5.4 5.3 %collective-permute-start = (s32[3,128]{1,0:T(4,128)S(1)}, s32[3,128]{1,0:T(4,128)S(1)}, u32[]{:S(2)}, u32[]{:S(2)}) collective-permute-start(s32[3,128]{1,0:T(4,128)S(1)} %add_add_fusion.1.own), channel_id=1, source_target_pairs={{0,4},{4,0},{8,12},{12,8},{16,20},{20,16},{24,28},{28,24},{32,36},... | collective-permute-start | bytes 4616 | tf_op jit(solution)/shard_map/ppermute | solution.py:58
  6.4 5.6 %collective-permute-start.2 = (bf16[272,256]{1,0:T(8,128)(2,1)S(1)}, bf16[272,256]{1,0:T(8,128)(2,1)S(1)}, u32[]{:S(2)}, u32[]{:S(2)}) collective-permute-start(bf16[272,256]{1,0:T(8,128)(2,1)S(1)} %get-tuple-element.69), channel_id=1, source_target_pairs={{0,192},{8,200},{16,208},{24,216},{32,224},{40,232},{48,240},{56,2... | collective-permute-start | bytes 417800 | tf_op jit(solution)/shard_map/ppermute | solution.py:50
  7.1 9.3 %collective-permute-start.3 = (bf16[272,256]{1,0:T(8,128)(2,1)S(1)}, bf16[272,256]{1,0:T(8,128)(2,1)S(1)}, u32[]{:S(2)}, u32[]{:S(2)}) collective-permute-start(bf16[272,256]{1,0:T(8,128)(2,1)S(1)} %get-tuple-element.69), channel_id=1, source_target_pairs={{0,64},{4,20},{8,72},{12,28},{16,80},{20,4},{24,88},{28,12},{32,96... | collective-permute-start | bytes 417800 | tf_op jit(solution)/shard_map/ppermute | solution.py:50
  8.2 8.2 %collective-permute-start.8 = (bf16[272,256]{1,0:T(8,128)(2,1)S(1)}, bf16[272,256]{1,0:T(8,128)(2,1)S(1)}, u32[]{:S(2)}, u32[]{:S(2)}) collective-permute-start(bf16[272,256]{1,0:T(8,128)(2,1)S(1)} %get-tuple-element.69), channel_id=1, source_target_pairs={{0,224},{4,28},{8,232},{12,4},{16,240},{20,12},{24,248},{28,20},{3... | collective-permute-start | bytes 417800 | tf_op jit(solution)/shard_map/ppermute | solution.py:50
  10.7 18.3 %copy-start.31 = (s32[3,128]{1,0:T(4,128)}, s32[3,128]{1,0:T(4,128)S(1)}, u32[]{:S(2)}) copy-start(s32[3,128]{1,0:T(4,128)S(1)} %collective-permute-done.sib) | copy-start | bytes 4612
  10.7 5.7 %collective-permute-start.7 = (bf16[272,256]{1,0:T(8,128)(2,1)S(1)}, bf16[272,256]{1,0:T(8,128)(2,1)S(1)}, u32[]{:S(2)}, u32[]{:S(2)}) collective-permute-start(bf16[272,256]{1,0:T(8,128)(2,1)S(1)} %get-tuple-element.69), channel_id=1, source_target_pairs={{0,32},{4,12},{8,40},{12,20},{16,48},{20,28},{24,56},{28,4},{32,64... | collective-permute-start | bytes 417800 | tf_op jit(solution)/shard_map/ppermute | solution.py:50
  13.2 2.0 copy-start.1
  16.5 26.4 %copy-start.5 = (bf16[4,272,256]{2,1,0:T(8,128)(2,1)}, bf16[4,272,256]{2,1,0:T(8,128)(2,1)S(1)}, u32[]{:S(2)}) copy-start(bf16[4,272,256]{2,1,0:T(8,128)(2,1)S(1)} %maximum_add_fusion.rest_0_) | copy-start | bytes 1671172
  16.5 12.5 %collective-permute-start.9 = (bf16[4,272,256]{2,1,0:T(8,128)(2,1)S(1)}, bf16[4,272,256]{2,1,0:T(8,128)(2,1)S(1)}, u32[]{:S(2)}, u32[]{:S(2)}) collective-permute-start(bf16[4,272,256]{2,1,0:T(8,128)(2,1)S(1)} %maximum_add_fusion.rest_0_), channel_id=1, source_target_pairs={{0,8},{4,36},{8,16},{12,44},{16,24},{20,52},{24,0},{28,60},{32,40}... | collective-permute-start | bytes 1671176 | tf_op jit(solution)/shard_map/ppermute | solution.py:50
  17.7 2.0 collective-permute-start.6
  18.4 1.4 collective-permute-start.5
  19.1 0.7 collective-permute-start.4
  21.0 13.1 %collective-permute-start.12 = (bf16[4,272,256]{2,1,0:T(8,128)(2,1)S(1)}, bf16[4,272,256]{2,1,0:T(8,128)(2,1)S(1)}, u32[]{:S(2)}, u32[]{:S(2)}) collective-permute-start(bf16[4,272,256]{2,1,0:T(8,128)(2,1)S(1)} %maximum_add_fusion.rest_0_), channel_id=1, source_target_pairs={{0,24},{4,228},{8,0},{12,236},{16,8},{20,244},{24,16},{28,252},{32... | collective-permute-start | bytes 1671176 | tf_op jit(solution)/shard_map/ppermute | solution.py:50
  29.0 13.9 %copy-start.6 = (bf16[4,272,256]{2,1,0:T(8,128)(2,1)}, bf16[4,272,256]{2,1,0:T(8,128)(2,1)S(1)}, u32[]{:S(2)}) copy-start(bf16[4,272,256]{2,1,0:T(8,128)(2,1)S(1)} %collective-permute-done.9.rest_1_) | copy-start | bytes 1671172
  29.1 12.8 %collective-permute-start.10 = (bf16[4,272,256]{2,1,0:T(8,128)(2,1)S(1)}, bf16[4,272,256]{2,1,0:T(8,128)(2,1)S(1)}, u32[]{:S(2)}, u32[]{:S(2)}) collective-permute-start(bf16[4,272,256]{2,1,0:T(8,128)(2,1)S(1)} %broadcast_add_fusion.1), channel_id=1, source_target_pairs={{0,8},{4,36},{8,16},{12,44},{16,24},{20,52},{24,0},{28,60},{32,40}... | collective-permute-start | bytes 1671176 | tf_op jit(solution)/shard_map/ppermute | solution.py:50
  34.1 8.8 %copy-start.3 = (bf16[4,272,256]{2,1,0:T(8,128)(2,1)}, bf16[4,272,256]{2,1,0:T(8,128)(2,1)S(1)}, u32[]{:S(2)}) copy-start(bf16[4,272,256]{2,1,0:T(8,128)(2,1)S(1)} %collective-permute-done.12.rest_2_) | copy-start | bytes 1671172
  42.9 8.8 %collective-permute-start.13 = (bf16[4,272,256]{2,1,0:T(8,128)(2,1)S(1)}, bf16[4,272,256]{2,1,0:T(8,128)(2,1)S(1)}, u32[]{:S(2)}, u32[]{:S(2)}) collective-permute-start(bf16[4,272,256]{2,1,0:T(8,128)(2,1)S(1)} %get-tuple-element.52), channel_id=1, source_target_pairs={{0,24},{4,228},{8,0},{12,236},{16,8},{20,244},{24,16},{28,252},{32... | collective-permute-start | bytes 1671176 | tf_op jit(solution)/shard_map/ppermute | solution.py:50
  43.9 22.2 %collective-permute-start.11 = (bf16[4,272,256]{2,1,0:T(8,128)(2,1)S(1)}, bf16[4,272,256]{2,1,0:T(8,128)(2,1)S(1)}, u32[]{:S(2)}, u32[]{:S(2)}) collective-permute-start(bf16[4,272,256]{2,1,0:T(8,128)(2,1)S(1)} %get-tuple-element.51), channel_id=1, source_target_pairs={{0,8},{4,36},{8,16},{12,44},{16,24},{20,52},{24,0},{28,60},{32,40}... | collective-permute-start | bytes 1671176 | tf_op jit(solution)/shard_map/ppermute | solution.py:50
  52.5 15.5 %copy-start = (bf16[128,128,128]{2,1,0:T(8,128)(2,1)S(1)}, bf16[128,128,128]{2,1,0:T(8,128)(2,1)}, u32[]{:S(2)}) copy-start(bf16[128,128,128]{2,1,0:T(8,128)(2,1)} %own.9) | copy-start | bytes 12582916
  62.4 10.5 %collective-permute-start.15 = (bf16[4,272,256]{2,1,0:T(8,128)(2,1)}, bf16[4,272,256]{2,1,0:T(8,128)(2,1)S(1)}, u32[]{:S(2)}, u32[]{:S(2)}) collective-permute-start(bf16[4,272,256]{2,1,0:T(8,128)(2,1)} %copy-done.12), channel_id=1, source_target_pairs={{0,24},{4,228},{8,0},{12,236},{16,8},{20,244},{24,16},{28,252},{32... | collective-permute-start | bytes 1671176 | tf_op jit(solution)/shard_map/ppermute | solution.py:50
  66.1 3.2 %copy-start.7 = (bf16[4,272,256]{2,1,0:T(8,128)(2,1)}, bf16[4,272,256]{2,1,0:T(8,128)(2,1)S(1)}, u32[]{:S(2)}) copy-start(bf16[4,272,256]{2,1,0:T(8,128)(2,1)S(1)} %collective-permute-done.11.rest_0_) | copy-start | bytes 1671172
  66.1 13.3 %collective-permute-start.14 = (bf16[4,272,256]{2,1,0:T(8,128)(2,1)S(1)}, bf16[4,272,256]{2,1,0:T(8,128)(2,1)S(1)}, u32[]{:S(2)}, u32[]{:S(2)}) collective-permute-start(bf16[4,272,256]{2,1,0:T(8,128)(2,1)S(1)} %broadcast_add_fusion), channel_id=1, source_target_pairs={{4,36},{12,44},{20,52},{28,60},{36,68},{44,76},{52,84},{60,92},{68... | collective-permute-start | bytes 1671176 | tf_op jit(solution)/shard_map/ppermute | solution.py:50
  80.3 17.2 %copy-start.32 = (s32[128]{0:T(128)S(1)}, s32[128]{0:T(128)}, u32[]{:S(2)}) copy-start(s32[128]{0:T(128)} %param.12) | copy-start | bytes 1540
  84.7 14.2 %collective-permute-start.17 = (bf16[4,8,16,256]{3,2,1,0:T(8,128)(2,1)}, bf16[4,8,16,256]{3,2,1,0:T(8,128)(2,1)S(1)}, u32[]{:S(2)}, u32[]{:S(2)}) collective-permute-start(bf16[4,8,16,256]{3,2,1,0:T(8,128)(2,1)} %get-tuple-element.23), channel_id=1, source_target_pairs={{0,4},{4,0},{8,12},{12,8},{16,20},{20,16},{24,28},{28,24},{32,36},... | collective-permute-start | bytes 786440 | tf_op jit(solution)/shard_map/ppermute | solution.py:58
  98.6 1.6 collective-permute-start.16
  101.1 12.9 %copy-start.23 = (bf16[256,256]{1,0:T(8,128)(2,1)S(1)}, bf16[256,256]{1,0:T(8,128)(2,1)}, u32[]{:S(2)}) copy-start(bf16[256,256]{1,0:T(8,128)(2,1)} %param.15) | copy-start | bytes 393220
  101.1 12.9 %copy-start.33 = (f32[256]{0:T(256)S(1)}, f32[256]{0:T(256)}, u32[]{:S(2)}) copy-start(f32[256]{0:T(256)} %param.10) | copy-start | bytes 3076
  101.2 8.0 %collective-permute-start.20 = (bf16[256,256]{1,0:T(8,128)(2,1)S(1)}, bf16[256,256]{1,0:T(8,128)(2,1)S(1)}, u32[]{:S(2)}, u32[]{:S(2)}) collective-permute-start(bf16[256,256]{1,0:T(8,128)(2,1)S(1)} %convolution_convert_fusion), channel_id=1, source_target_pairs={{0,3},{1,0},{2,1},{3,2},{4,7},{5,4},{6,5},{7,6},{8,11},{9,8},{10,9... | collective-permute-start | bytes 393224 | tf_op jit(solution)/shard_map/ppermute | solution.py:62
  104.2 6.0 %collective-permute-start.19 = (bf16[256,256]{1,0:T(8,128)(2,1)S(1)}, bf16[256,256]{1,0:T(8,128)(2,1)S(1)}, u32[]{:S(2)}, u32[]{:S(2)}) collective-permute-start(bf16[256,256]{1,0:T(8,128)(2,1)S(1)} %convolution_convert_fusion.1), channel_id=1, source_target_pairs={{0,2},{1,3},{2,0},{3,1},{4,6},{5,7},{6,4},{7,5},{8,10},{9,11},{10,... | collective-permute-start | bytes 393224 | tf_op jit(solution)/shard_map/ppermute | solution.py:62
  104.9 9.1 %collective-permute-start.18 = (bf16[256,256]{1,0:T(8,128)(2,1)S(1)}, bf16[256,256]{1,0:T(8,128)(2,1)S(1)}, u32[]{:S(2)}, u32[]{:S(2)}) collective-permute-start(bf16[256,256]{1,0:T(8,128)(2,1)S(1)} %convolution_convert_fusion.2), channel_id=1, source_target_pairs={{0,1},{1,2},{2,3},{3,0},{4,5},{5,6},{6,7},{7,4},{8,9},{9,10},{10,1... | collective-permute-start | bytes 393224 | tf_op jit(solution)/shard_map/ppermute | solution.py:62
  114.9 5.8 %collective-permute-start.23 = (bf16[256,256]{1,0:T(8,128)(2,1)S(1)}, bf16[256,256]{1,0:T(8,128)(2,1)S(1)}, u32[]{:S(2)}, u32[]{:S(2)}) collective-permute-start(bf16[256,256]{1,0:T(8,128)(2,1)S(1)} %get-tuple-element.39), channel_id=1, source_target_pairs={{0,1},{1,2},{2,3},{3,0},{4,5},{5,6},{6,7},{7,4},{8,9},{9,10},{10,1... | collective-permute-start | bytes 393224 | tf_op jit(solution)/shard_map/ppermute | solution.py:62
  115.1 8.3 %collective-permute-start.21 = (bf16[256,256]{1,0:T(8,128)(2,1)S(1)}, bf16[256,256]{1,0:T(8,128)(2,1)S(1)}, u32[]{:S(2)}, u32[]{:S(2)}) collective-permute-start(bf16[256,256]{1,0:T(8,128)(2,1)S(1)} %get-tuple-element.39), channel_id=1, source_target_pairs={{0,3},{1,0},{2,1},{3,2},{4,7},{5,4},{6,5},{7,6},{8,11},{9,8},{10,9... | collective-permute-start | bytes 393224 | tf_op jit(solution)/shard_map/ppermute | solution.py:62
  117.8 5.3 %collective-permute-start.22 = (bf16[256,256]{1,0:T(8,128)(2,1)S(1)}, bf16[256,256]{1,0:T(8,128)(2,1)S(1)}, u32[]{:S(2)}, u32[]{:S(2)}) collective-permute-start(bf16[256,256]{1,0:T(8,128)(2,1)S(1)} %get-tuple-element.39), channel_id=1, source_target_pairs={{0,2},{1,3},{2,0},{3,1},{4,6},{5,7},{6,4},{7,5},{8,10},{9,11},{10,... | collective-permute-start | bytes 393224 | tf_op jit(solution)/shard_map/ppermute | solution.py:62
  123.9 5.1 %collective-permute-start.25 = (f32[520,256]{1,0:T(8,128)S(1)}, f32[520,256]{1,0:T(8,128)S(1)}, u32[]{:S(2)}, u32[]{:S(2)}) collective-permute-start(f32[520,256]{1,0:T(8,128)S(1)} %select_maximum_fusion), channel_id=1, source_target_pairs={{0,4},{4,0},{8,12},{12,8},{16,20},{20,16},{24,28},{28,24},{32,36},... | collective-permute-start | bytes 1597448 | tf_op jit(solution)/shard_map/ppermute | solution.py:58
  126.7 2.2 copy-start.20
  126.7 1.4 collective-permute-start.24
  135.4 12.5 %collective-permute-start.28 = (bf16[1104,256]{1,0:T(8,128)(2,1)}, bf16[1104,256]{1,0:T(8,128)(2,1)S(1)}, u32[]{:S(2)}, u32[]{:S(2)}) collective-permute-start(bf16[1104,256]{1,0:T(8,128)(2,1)} %get-tuple-element.29), channel_id=1, source_target_pairs={{0,8},{4,36},{8,16},{12,44},{16,24},{20,52},{24,0},{28,60},{32,40}... | collective-permute-start | bytes 1695752 | tf_op jit(solution)/shard_map/ppermute | solution.py:50
  135.5 13.8 %collective-permute-start.26 = (bf16[1104,256]{1,0:T(8,128)(2,1)}, bf16[1104,256]{1,0:T(8,128)(2,1)S(1)}, u32[]{:S(2)}, u32[]{:S(2)}) collective-permute-start(bf16[1104,256]{1,0:T(8,128)(2,1)} %get-tuple-element.26), channel_id=1, source_target_pairs={{0,24},{4,228},{8,0},{12,236},{16,8},{20,244},{24,16},{28,252},{32... | collective-permute-start | bytes 1695752 | tf_op jit(solution)/shard_map/ppermute | solution.py:50
  149.1 10.1 %copy-start.10 = (bf16[1104,256]{1,0:T(8,128)(2,1)S(1)}, bf16[1104,256]{1,0:T(8,128)(2,1)}, u32[]{:S(2)}) copy-start(bf16[1104,256]{1,0:T(8,128)(2,1)} %get-tuple-element.27) | copy-start | bytes 1695748
  149.1 10.1 %collective-permute-start.29 = (bf16[1104,256]{1,0:T(8,128)(2,1)S(1)}, bf16[1104,256]{1,0:T(8,128)(2,1)S(1)}, u32[]{:S(2)}, u32[]{:S(2)}) collective-permute-start(bf16[1104,256]{1,0:T(8,128)(2,1)S(1)} %add_convert_fusion.3), channel_id=1, source_target_pairs={{0,8},{4,36},{8,16},{12,44},{16,24},{20,52},{24,0},{28,60},{32,40}... | collective-permute-start | bytes 1695752 | tf_op jit(solution)/shard_map/ppermute | solution.py:50
  149.4 10.1 %copy-start.9 = (bf16[1104,256]{1,0:T(8,128)(2,1)S(1)}, bf16[1104,256]{1,0:T(8,128)(2,1)}, u32[]{:S(2)}) copy-start(bf16[1104,256]{1,0:T(8,128)(2,1)} %get-tuple-element.31) | copy-start | bytes 1695748
  149.4 10.0 %collective-permute-start.27 = (bf16[1104,256]{1,0:T(8,128)(2,1)S(1)}, bf16[1104,256]{1,0:T(8,128)(2,1)S(1)}, u32[]{:S(2)}, u32[]{:S(2)}) collective-permute-start(bf16[1104,256]{1,0:T(8,128)(2,1)S(1)} %add_convert_fusion.4), channel_id=1, source_target_pairs={{0,24},{4,228},{8,0},{12,236},{16,8},{20,244},{24,16},{28,252},{32... | collective-permute-start | bytes 1695752 | tf_op jit(solution)/shard_map/ppermute | solution.py:50
  159.4 10.1 %copy-start.2 = (bf16[1104,256]{1,0:T(8,128)(2,1)S(1)}, bf16[1104,256]{1,0:T(8,128)(2,1)}, u32[]{:S(2)}) copy-start(bf16[1104,256]{1,0:T(8,128)(2,1)} %get-tuple-element.24) | copy-start | bytes 1695748
  159.4 10.1 %collective-permute-start.30 = (bf16[1104,256]{1,0:T(8,128)(2,1)S(1)}, bf16[1104,256]{1,0:T(8,128)(2,1)S(1)}, u32[]{:S(2)}, u32[]{:S(2)}) collective-permute-start(bf16[1104,256]{1,0:T(8,128)(2,1)S(1)} %add_convert_fusion.2), channel_id=1, source_target_pairs={{0,8},{4,36},{8,16},{12,44},{16,24},{20,52},{24,0},{28,60},{32,40}... | collective-permute-start | bytes 1695752 | tf_op jit(solution)/shard_map/ppermute | solution.py:50
  160.5 11.8 %collective-permute-start.31 = (bf16[1104,256]{1,0:T(8,128)(2,1)}, bf16[1104,256]{1,0:T(8,128)(2,1)S(1)}, u32[]{:S(2)}, u32[]{:S(2)}) collective-permute-start(bf16[1104,256]{1,0:T(8,128)(2,1)} %add_convert_fusion.1), channel_id=1, source_target_pairs={{0,24},{4,228},{8,0},{12,236},{16,8},{20,244},{24,16},{28,252},{32... | collective-permute-start | bytes 1695752 | tf_op jit(solution)/shard_map/ppermute | solution.py:50
  163.3 8.4 %copy-start.26 = (bf16[1,256]{1,0:T(2,128)(2,1)}, bf16[1,256]{1,0:T(2,128)(2,1)S(1)}, u32[]{:S(2)}) copy-start(bf16[1,256]{1,0:T(2,128)(2,1)S(1)} %get-tuple-element.34) | copy-start | bytes 1540
  163.3 8.3 %copy-start.27 = (f32[1,256]{1,0:T(1,128)}, f32[1,256]{1,0:T(1,128)S(1)}, u32[]{:S(2)}) copy-start(f32[1,256]{1,0:T(1,128)S(1)} %get-tuple-element.35) | copy-start | bytes 3076
  169.5 11.8 %copy-start.8 = (bf16[1104,256]{1,0:T(8,128)(2,1)S(1)}, bf16[1104,256]{1,0:T(8,128)(2,1)}, u32[]{:S(2)}) copy-start(bf16[1104,256]{1,0:T(8,128)(2,1)} %get-tuple-element.30) | copy-start | bytes 1695748
  169.6 11.6 %collective-permute-start.35 = (bf16[1104,256]{1,0:T(8,128)(2,1)S(1)}, bf16[1104,256]{1,0:T(8,128)(2,1)S(1)}, u32[]{:S(2)}, u32[]{:S(2)}) collective-permute-start(bf16[1104,256]{1,0:T(8,128)(2,1)S(1)} %add_convert_fusion), channel_id=1, source_target_pairs={{4,36},{12,44},{20,52},{28,60},{36,68},{44,76},{52,84},{60,92},{68... | collective-permute-start | bytes 1695752 | tf_op jit(solution)/shard_map/ppermute | solution.py:50
  181.2 1.7 copy-start.17
  182.9 3.3 %collective-permute-start.34 = (bf16[576,256]{1,0:T(8,128)(2,1)}, bf16[576,256]{1,0:T(8,128)(2,1)}, u32[]{:S(2)}, u32[]{:S(2)}) collective-permute-start(bf16[576,256]{1,0:T(8,128)(2,1)} %pad_maximum_fusion.2), channel_id=1, source_target_pairs={{0,224},{8,232},{16,240},{24,248},{32,0},{40,8},{48,16},{56,24},{6... | collective-permute-start | bytes 884744 | tf_op jit(solution)/shard_map/ppermute | solution.py:50
  184.3 21.1 %collective-permute-start.38 = (bf16[272,256]{1,0:T(8,128)(2,1)}, bf16[272,256]{1,0:T(8,128)(2,1)}, u32[]{:S(2)}, u32[]{:S(2)}) collective-permute-start(bf16[272,256]{1,0:T(8,128)(2,1)} %get-tuple-element.41), channel_id=1, source_target_pairs={{4,20},{12,28},{20,4},{28,12},{36,52},{44,60},{52,36},{60,44},{68,... | collective-permute-start | bytes 417800 | tf_op jit(solution)/shard_map/ppermute | solution.py:50
  188.7 14.2 %copy-start.15 = (bf16[272,256]{1,0:T(8,128)(2,1)S(1)}, bf16[272,256]{1,0:T(8,128)(2,1)}, u32[]{:S(2)}) copy-start(bf16[272,256]{1,0:T(8,128)(2,1)} %get-tuple-element.40) | copy-start | bytes 417796
  188.7 14.2 %copy-start.16 = (bf16[272,256]{1,0:T(8,128)(2,1)S(1)}, bf16[272,256]{1,0:T(8,128)(2,1)}, u32[]{:S(2)}) copy-start(bf16[272,256]{1,0:T(8,128)(2,1)} %get-tuple-element.42) | copy-start | bytes 417796
  188.7 10.2 %collective-permute-start.32 = (bf16[576,256]{1,0:T(8,128)(2,1)}, bf16[576,256]{1,0:T(8,128)(2,1)S(1)}, u32[]{:S(2)}, u32[]{:S(2)}) collective-permute-start(bf16[576,256]{1,0:T(8,128)(2,1)} %pad_maximum_fusion.3), channel_id=1, source_target_pairs={{0,32},{8,40},{16,48},{24,56},{32,64},{40,72},{48,80},{56,88},{64,... | collective-permute-start | bytes 884744 | tf_op jit(solution)/shard_map/ppermute | solution.py:50
  190.2 7.5 %collective-permute-start.33 = (bf16[288,256]{1,0:T(8,128)(2,1)}, bf16[288,256]{1,0:T(8,128)(2,1)}, u32[]{:S(2)}, u32[]{:S(2)}) collective-permute-start(bf16[288,256]{1,0:T(8,128)(2,1)} %pad_maximum_fusion.9), channel_id=1, source_target_pairs={{0,64},{8,72},{16,80},{24,88},{32,96},{40,104},{48,112},{56,120},{... | collective-permute-start | bytes 442376 | tf_op jit(solution)/shard_map/ppermute | solution.py:50
  203.0 7.3 %copy-start.21 = (bf16[256,256]{1,0:T(8,128)(2,1)S(1)}, bf16[256,256]{1,0:T(8,128)(2,1)}, u32[]{:S(2)}) copy-start(bf16[256,256]{1,0:T(8,128)(2,1)} %copy-done.20) | copy-start | bytes 393220
  203.1 4.1 %collective-permute-start.37 = (bf16[288,256]{1,0:T(8,128)(2,1)S(1)}, bf16[288,256]{1,0:T(8,128)(2,1)S(1)}, u32[]{:S(2)}, u32[]{:S(2)}) collective-permute-start(bf16[288,256]{1,0:T(8,128)(2,1)S(1)} %get-tuple-element.71), channel_id=1, source_target_pairs={{0,192},{4,28},{8,200},{12,4},{16,208},{20,12},{24,216},{28,20},{3... | collective-permute-start | bytes 442376 | tf_op jit(solution)/shard_map/ppermute | solution.py:50
  203.2 5.7 %collective-permute-start.36 = (bf16[288,256]{1,0:T(8,128)(2,1)S(1)}, bf16[288,256]{1,0:T(8,128)(2,1)S(1)}, u32[]{:S(2)}, u32[]{:S(2)}) collective-permute-start(bf16[288,256]{1,0:T(8,128)(2,1)S(1)} %get-tuple-element.70), channel_id=1, source_target_pairs={{0,64},{4,12},{8,72},{12,20},{16,80},{20,28},{24,88},{28,4},{32,96... | collective-permute-start | bytes 442376 | tf_op jit(solution)/shard_map/ppermute | solution.py:50
  205.4 5.6 %copy-start.29 = (f32[3,256]{1,0:T(4,128)S(1)}, f32[3,256]{1,0:T(4,128)}, u32[]{:S(2)}) copy-start(f32[3,256]{1,0:T(4,128)} %get-tuple-element.59) | copy-start | bytes 9220
  205.4 5.6 %copy-start.28 = (f32[1,256]{1,0:T(1,128)S(1)}, f32[1,256]{1,0:T(1,128)}, u32[]{:S(2)}) copy-start(f32[1,256]{1,0:T(1,128)} %copy-done.27) | copy-start | bytes 3076
  211.1 12.2 %collective-permute-start.39 = (f32[1,256]{1,0:T(1,128)S(1)}, f32[1,256]{1,0:T(1,128)S(1)}, u32[]{:S(2)}, u32[]{:S(2)}) collective-permute-start(f32[1,256]{1,0:T(1,128)S(1)} %fusion.44), channel_id=1, source_target_pairs={{0,4},{8,12},{16,20},{24,28},{32,36},{40,44},{48,52},{56,60},{64,6... | collective-permute-start | bytes 3080 | tf_op jit(solution)/shard_map/ppermute | solution.py:547
  (10 other events, 9.3 us)

commit v3 on v2

--- a/solution.py
+++ b/solution.py
@@ -23,20 +23,34 @@
 MIB = 1 << 20
 VMEM = 54 * MIB
 
-LOW, HIGH, ACROSS = (0, 1, 7, 2), (6, 3, 5, 4), (0, 1, 3, 2)
+LOW, HIGH, ACROSS = (0, 1, 7, 4), (2, 3, 6, 5), (0, 1, 3, 2)
 GATHER_0 = tuple(
     tuple(k * NZ + j for j in group)
     for k, group in ((0, LOW), (1, LOW), (3, LOW), (2, LOW), (3, HIGH), (1, HIGH), (2, HIGH), (0, HIGH))
 )
-GATHER_1 = tuple(tuple(k * NZ + j for k in ACROSS) for j in (0, 1, 7, 2, 6, 3, 5, 4))
-FORWARD_CHUNKS = ((0, 1, 2, 3, 4, 7), (5, 6), (8,))
-BACKWARD_CHUNKS = ((0, 1), (2, 3, 4, 5, 6, 7))
-FAR, NEAR = (4, 5, 3, 6), (2, 7, 1, 0)
-SCATTER_0 = tuple(
-    tuple((dx, dz) for dz in group)
-    for dx, group in ((2, FAR), (2, NEAR), (1, FAR), (3, NEAR), (1, NEAR), (3, FAR), (0, NEAR), (0, FAR))
+GATHER_1 = tuple(tuple(k * NZ + j for k in ACROSS) for j in (0, 1, 7, 2, 6, 3, 5)) + (
+    None,
+    tuple(k * NZ + 4 for k in ACROSS[:2]),
+    tuple(k * NZ + 4 for k in ACROSS[2:]),
 )
-SCATTER_1 = tuple(tuple((dx, dz) for dx in ACROSS) for dz in (4, 5, 3, 6, 2, 7, 1, 0))
+FORWARD_CHUNKS = ((0, 1, 2, 3, 4, 5, 6, 7), (8, 9))
+SCATTER = (
+    (
+        (None, tuple((dx, 4) for dx in ACROSS)),
+        (tuple((2, dz) for dz in HIGH), None),
+        (tuple((3, dz) for dz in HIGH), None),
+    ),
+    (
+        (None, tuple((dx, 3) for dx in ACROSS)),
+        (None, tuple((dx, 5) for dx in ACROSS)),
+        (tuple((1, dz) for dz in HIGH), tuple((dx, 2) for dx in ACROSS)),
+        (tuple((2, dz) for dz in LOW), tuple((dx, 6) for dx in ACROSS)),
+        (tuple((1, dz) for dz in LOW), tuple((dx, 1) for dx in ACROSS)),
+        (tuple((3, dz) for dz in LOW), tuple((dx, 7) for dx in ACROSS)),
+        (tuple((0, dz) for dz in HIGH), None),
+        (tuple((0, dz) for dz in LOW), tuple((dx, 0) for dx in ACROSS)),
+    ),
+)
 
 
 def shift(value, core_0=None, core_1=None):
@@ -50,7 +64,7 @@
     return lax.ppermute(value, "dom", pairs)
 
 
-Z_UP, Z_DOWN, Z_UP_2, Z_DOWN_2 = (1, 0), (-1, 0), (2, 0), (-2, 0)
+Z_UP, Z_DOWN, Z_UP_2, Z_DOWN_2, Z_FOUR = (1, 0), (-1, 0), (2, 0), (-2, 0), (4, 0)
 X_UP, X_DOWN, X_TWO = (0, 1), (0, -1), (0, 2)
 
 
@@ -87,10 +101,9 @@
     j = (z - (chip >> 2)) & (NZ - 1)
     spot = (k * NZ + j) * 2 + (column & 1)
     mine = live & ((owner & 1) == core)
-    on_0 = jnp.where(((k == 1) | (k == 2)) & (j >= 3) & (j <= 6), 1, 0)
-    on_1 = jnp.where(j == 4, 2, jnp.where((j == 3) | (j == 5), 1, 0))
-    forward_call = jnp.where(core == 0, on_0, on_1)
-    backward_call = jnp.where(core == 0, jnp.where(k == 2, 0, 1), jnp.where((j == 3) | (j == 4), 0, 1))
+    high = ((j >= 2) & (j <= 6)) & (j != 4)
+    forward_call = jnp.where((core == 1) & (j == 4), 1, 0)
+    backward_call = jnp.where(core == 0, jnp.where(high & ((k == 1) | (k == 2)), 0, 1), jnp.where(j == 4, 0, 1))
     square = (2 * SLOTS, 2 * SLOTS)
     first = lax.broadcasted_iota(jnp.int32, square, 0)
     second = lax.broadcasted_iota(jnp.int32, square, 1)
@@ -223,10 +236,12 @@
     tiles.start()
     copies, arrived = [], []
     for n, chunk in zip(chosen, chunks):
-        table = min(n, 7)
-        condition = None if n < 7 else core == n - 7
-        for i in range(4):
-            spot = jnp.where(core == 0, GATHER_0[table][i], GATHER_1[table][i])
+        condition = None if n < 7 else core == (0 if n == 7 else 1)
+        for i in range(chunk.shape[0]):
+            if n < 7:
+                spot = jnp.where(core == 0, GATHER_0[n][i], GATHER_1[n][i])
+            else:
+                spot = GATHER_0[n][i] if n == 7 else GATHER_1[n][i]
             copies.append((condition, pltpu.make_async_copy(chunk.at[i], blocks.at[spot], sem.at[len(copies)])))
             arrived.append((condition, spot))
     copy_each(copies, "start")
@@ -272,7 +287,7 @@
         scratch_shapes=[
             pltpu.VMEM((NX * NZ, ROWS, WIDTH), BF16),
             pltpu.VMEM((2 * SLOTS + 1, BLK, BLK), BF16),
-            pltpu.SemaphoreType.DMA((24,)),
+            pltpu.SemaphoreType.DMA((32,)),
             pltpu.SemaphoreType.DMA((2 * SLOTS // FETCH,)),
         ],
         compiler_params=pltpu.CompilerParams(vmem_limit_bytes=VMEM),
@@ -283,36 +298,36 @@
 
 
 def backward_kernel(call, lists, own, sib, scaled, weight_sums, bias_rows, *rest):
-    chosen = BACKWARD_CHUNKS[call]
-    outs, rest = rest[: len(chosen)], rest[len(chosen) :]
+    chunks = SCATTER[call]
+    outs, rest = rest[: len(chunks)], rest[len(chunks) :]
     total, held, tile_sem = rest
     core, x, z, y = place_of(lists)
     tiles = Tiles(lists, 3, call, call == 1, own, sib, held, tile_sem)
     tiles.start()
-    targets = {}
-    for n in chosen:
-        for i in range(4):
-            dx = jnp.where(core == 0, SCATTER_0[n][i][0], SCATTER_1[n][i][0])
-            dz = jnp.where(core == 0, SCATTER_0[n][i][1], SCATTER_1[n][i][1])
-            spot = ((0 - dx) & (NX - 1)) * NZ + ((0 - dz) & (NZ - 1))
-            targets[n, i] = dx, dz, spot
+
+    def each_chunk(action):
+        for out, chunk in zip(outs, chunks):
+            if None in chunk:
+                side = 1 if chunk[0] is None else 0
+
+                @pl.when(core == side)
+                def _(out=out, places=chunk[side]):
+                    action(out, places)
+            else:
+                action(out, [[jnp.where(core == 0, p, q) for p, q in zip(*pair)] for pair in zip(*chunk)])
+
+    def spot_of(dx, dz):
+        return ((0 - dx) & (NX - 1)) * NZ + ((0 - dz) & (NZ - 1))
+
+    def clear(out, places):
+        for dx, dz in places:
+            spot = spot_of(dx, dz)
             total[spot * 2] = jnp.zeros((BLK, WIDTH), F32)
             total[spot * 2 + 1] = jnp.zeros((BLK, WIDTH), F32)
-    tiles.wait()
-    for row, steps, pick in tiles.rows():
-        right = scaled[row]
-
-        def step(it, carry):
-            left, spots = pick(it)
-            terms = lax.dot_general(left, right, (((0,), (0,)), ((), ())), preferred_element_type=F32)
-            for u, spot in enumerate(spots):
-                total[spot] += terms[u * BLK : (u + 1) * BLK]
-            return carry
-
-        lax.fori_loop(0, steps, step, 0)
-    for n, out in zip(chosen, outs):
-        for i in range(4):
-            dx, dz, spot = targets[n, i]
+
+    def emit(out, places):
+        for i, (dx, dz) in enumerate(places):
+            spot = spot_of(dx, dz)
             first = i * ROWS
             out[first : first + BLK, :] = total[spot * 2].astype(BF16)
             out[first + BLK : first + NODES, :] = total[spot * 2 + 1].astype(BF16)
@@ -322,14 +337,31 @@
             out[first + NODES : first + ROWS, :] = weight_sums[part, (level & 1) * NX + column]
         out[4 * ROWS : SUM_ROWS, :] = bias_rows[...] if call == 0 else jnp.zeros((BIAS_ROWS, WIDTH), BF16)
 
+    each_chunk(clear)
+    tiles.wait()
+    for row, steps, pick in tiles.rows():
+        right = scaled[row]
+
+        def step(it, carry):
+            left, spots = pick(it)
+            terms = lax.dot_general(left, right, (((0,), (0,)), ((), ())), preferred_element_type=F32)
+            for u, spot in enumerate(spots):
+                total[spot] += terms[u * BLK : (u + 1) * BLK]
+            return carry
+
+        lax.fori_loop(0, steps, step, 0)
+    each_chunk(emit)
+
 
 def backward(call, lists, own, sib, scaled, weight_sums, bias_rows):
-    number = len(BACKWARD_CHUNKS[call])
+    shapes = []
+    for _ in SCATTER[call]:
+        shapes.append(jax.ShapeDtypeStruct((SUM_ROWS, WIDTH), BF16))
     return pl.pallas_call(
         functools.partial(backward_kernel, call),
-        out_shape=(jax.ShapeDtypeStruct((SUM_ROWS, WIDTH), BF16),) * number,
+        out_shape=tuple(shapes),
         in_specs=[smem()] + [anywhere()] * 2 + [vmem()] * 3,
-        out_specs=(vmem(),) * number,
+        out_specs=(vmem(),) * len(shapes),
         scratch_shapes=[
             pltpu.VMEM((2 * NX * NZ, BLK, WIDTH), F32),
             pltpu.VMEM((2 * SLOTS + 1, BLK, BLK), BF16),
@@ -337,33 +369,30 @@
         ],
         compiler_params=pltpu.CompilerParams(vmem_limit_bytes=VMEM),
         cost_estimate=pl.CostEstimate(
-            flops=2 * BLK * BLK * WIDTH * number * 16, bytes_accessed=number * MIB, transcendentals=0
+            flops=2 * BLK * BLK * WIDTH * len(shapes) * 16, bytes_accessed=len(shapes) * MIB, transcendentals=0
         ),
     )(lists, own, sib, scaled, weight_sums, bias_rows)
 
 
-def gather(block, core, ready, sorted_lists, call):
+def gather(block, core, early, call):
     p1 = shift(block, Z_UP, X_UP)
     p2 = shift(block, Z_DOWN, X_DOWN)
-    p3 = shift(block, Z_UP_2, X_TWO)
-    p4 = shift(block, Z_DOWN_2)
-    low = jnp.stack([block, p1, p2, p3]) + (ready + nothing(p4[0, 0]))
+    p3 = shift(block, Z_FOUR, X_TWO)
+    pa = shift(jnp.stack([block, p1]), Z_UP_2)
+    pb = shift(jnp.stack([block, p2]), Z_DOWN_2)
+    low, *early = lax.optimization_barrier((jnp.stack([block, p1, p2, p3]), *early))
     c1 = shift(low, X_UP, Z_UP)
     c2 = shift(low, X_DOWN, Z_DOWN)
-    p5 = shift(p3, Z_UP)
-    p6 = shift(p4, Z_DOWN)
-    p7 = shift(p3, Z_UP_2)
-    high = jnp.stack([p4, p5, p6, p7])
-    c3 = shift(c1 + nothing(high[1:, 0, 0].sum()), X_UP, Z_UP)
-    c4 = shift(jnp.where(core == 0, high, c2) + sorted_lists, X_DOWN, Z_DOWN)
+    c1, c2, pa, pb = lax.optimization_barrier((c1, c2, pa, pb))
+    high = jnp.concatenate([pa, pb], axis=0)
+    c3 = shift(c1, X_UP, Z_UP)
+    c4 = shift(jnp.where(core == 0, high, c2), X_DOWN, Z_DOWN)
     c5 = shift(jnp.where(core == 0, high, c3), X_UP, Z_UP)
     c6 = shift(c4, X_DOWN, Z_DOWN)
-    chunks = [low, c1, c2, c3, c4, c5, c6, high]
-    sums = call(0, chunks, ())
-    c7 = shift(c5 + nothing(sums[0][0, 0, 0]), None, Z_UP)
-    chunks.append(c7)
-    sums = call(1, chunks, sums)
-    return call(2, chunks, sums)
+    c7 = shift(c5[:2], None, Z_UP)
+    c8 = shift(c6[2:], None, Z_DOWN)
+    chunks = [low, c1, c2, c3, c4, c5, c6, high, c7, c8]
+    return call(1, early, chunks, call(0, early, chunks, ()))
 
 
 def add(*values):
@@ -380,84 +409,124 @@
     return jnp.pad(rows, ((0, BIAS_ROWS - 3), (0, 0))).astype(BF16)
 
 
+def rows_of(value):
+    high = value.astype(BF16)
+    middle = (value - high.astype(F32)).astype(BF16)
+    low = (value - high.astype(F32) - middle.astype(F32)).astype(BF16)
+    return [high.astype(F32), middle.astype(F32), low.astype(F32)]
+
+
+def bias_block(rows):
+    used = sum(row.shape[0] for row in rows)
+    rows = rows + [jnp.zeros((BIAS_ROWS - used, WIDTH), F32)]
+    return jnp.concatenate(rows, axis=0).astype(BF16)
+
+
 def joined(block, first=0):
-    rows = block[first : first + 3].astype(F32)
-    return rows[0:1] + rows[1:2] + rows[2:3]
-
-
-def in_order(values, place):
+    rows = block.astype(F32)
+    return rows[first : first + 1] + rows[first + 1 : first + 2] + rows[first + 2 : first + 3]
+
+
+def in_order(values, place, held):
     count = len(values)
-    rows = jnp.concatenate([values[k] for k in range(count - 1, -1, -1)] * 2, axis=0)
-    rows = lax.dynamic_slice_in_dim(rows, count - 1 - place, count, 0)
-    total = rows[0:1]
+    for k, value in enumerate(values):
+        held[k : k + 1, :] = value
+    total = held[pl.ds(place & (count - 1), 1), :]
     for i in range(1, count):
-        total = total + rows[i : i + 1]
+        total = total + held[pl.ds((place - i) & (count - 1), 1), :]
     return total
 
 
-def scatter(parts, core, x, z, chip_bias):
-    a, b, c, d, e, f, g, h = parts
+def block_sum(i, *chunks):
+    total = chunks[0][i * ROWS : (i + 1) * ROWS, :].astype(F32)
+    for chunk in chunks[1:]:
+        total = total + chunk[i * ROWS : (i + 1) * ROWS, :].astype(F32)
+    return total
+
+
+def tail_of(chunk):
+    return chunk[4 * ROWS : SUM_ROWS, :]
+
+
+def pair_kernel(lists, chip_bias, h0, ja1, ja2, jb1, pair_a, pair_b, line_bias, held):
+    line = in_order([chip_bias[...], joined(tail_of(ja1)), joined(tail_of(jb1)), joined(tail_of(ja2))], lists[6, 1], held)
+    line_bias[...] = line
+    rows = bias_block(rows_of(line))
+    for pair, first in ((pair_a, 0), (pair_b, 2)):
+        for i in range(2):
+            pair[i * ROWS : (i + 1) * ROWS, :] = block_sum(first + i, h0, jb1, ja2).astype(BF16)
+        pair[2 * ROWS : 2 * ROWS + BIAS_ROWS, :] = rows
+
+
+def message_kernel(line_bias, h1, jc1, jc2, ra, rb, m1, m2, m3, rest):
+    own = rows_of(line_bias[...])
+    rest[...] = block_sum(0, h1, jc1, jc2) + block_sum(0, ra, rb)
+    relayed = [chunk[2 * ROWS : 2 * ROWS + BIAS_ROWS, :].astype(F32)[0:3] for chunk in (ra, rb)]
+    m1[0:ROWS, :] = (block_sum(1, h1, jc1, jc2) + block_sum(1, ra)).astype(BF16)
+    m1[ROWS:, :] = bias_block(own + [relayed[0]])
+    m2[0:ROWS, :] = (block_sum(2, h1, jc1, jc2) + block_sum(1, rb)).astype(BF16)
+    m2[ROWS:, :] = bias_block(own + [relayed[1]])
+    m3[0:ROWS, :] = block_sum(3, h1, jc1, jc2).astype(BF16)
+    m3[ROWS:, :] = bias_block(own)
+
+
+def last_kernel(lists, line_bias, rest, r1, r2, r3, ra, rb, scaled, feats_grad, weight_grad, bias, held):
+    total = rest[...] + block_sum(0, r1, r2, r3)
+    feats_grad[...] = (scaled[...].astype(F32) + total[0:NODES]).astype(BF16)
+    weight_grad[...] = total[NODES:ROWS]
+    t1, t2, t3 = (chunk[ROWS:, :] for chunk in (r1, r2, r3))
+    ta, tb = (chunk[2 * ROWS :, :] for chunk in (ra, rb))
+    values = [line_bias[...], joined(t1), joined(ta), joined(t1, 3), joined(t3), joined(t2, 3), joined(tb), joined(t2)]
+    bias[...] = in_order(values, lists[6, 2], held)
+
+
+def small_call(kernel, shapes, lists, operands, scratch):
+    first = [] if lists is None else [lists]
+    return pl.pallas_call(
+        kernel,
+        out_shape=tuple(jax.ShapeDtypeStruct(shape, dtype) for shape, dtype in shapes),
+        in_specs=[smem()] * len(first) + [vmem()] * len(operands),
+        out_specs=(vmem(),) * len(shapes),
+        scratch_shapes=[pltpu.VMEM((8, WIDTH), F32)] * scratch,
+        compiler_params=pltpu.CompilerParams(vmem_limit_bytes=16 * MIB),
+    )(*first, *operands)
+
+
+def scatter(first, second, core, lists, chip_bias, scaled):
+    first_up, x1, x2 = first
+    y1, y2, b1, b2, q1, q2, h0, h1 = second
     zero = jnp.zeros((), BF16)
-    j1 = shift(a, X_UP, Z_UP)
-    j2 = shift(b, X_DOWN, Z_DOWN)
-    j3 = shift(add(c, j1).astype(BF16), X_UP, Z_UP)
-    j4 = shift(add(d, j2).astype(BF16), X_DOWN, Z_DOWN)
-    j5 = shift(add(e, jnp.where(core == 0, zero, j3)).astype(BF16), X_UP, Z_UP)
-    j6 = shift(add(f, jnp.where(core == 0, zero, j4)).astype(BF16), X_DOWN, Z_DOWN)
-    j7 = shift(add(g, j5).astype(BF16), None, Z_UP)
-
-    def tail(value):
-        return value[4 * ROWS :]
-
-    line_bias = in_order([chip_bias, joined(tail(j1)), joined(tail(j3)), joined(tail(j2))], x)
-    own_rows = split(line_bias)
-
-    def block(value, i):
-        return value[i * ROWS : (i + 1) * ROWS]
-
-    def far(i):
-        return add(block(h, i), block(j3, i), block(j6, i))
-
-    def near(i):
-        return add(block(g, i), block(j4, i), block(j5, i))
-
-    def across(i):
-        return add(block(h, i), block(j6, i), block(j7, i))
-
-    def message(value, rows=own_rows):
-        return jnp.concatenate([value.astype(BF16), rows], axis=0)
-
-    r4 = shift(message(far(0)), Z_UP_2)
-    r31 = shift(jnp.concatenate([message(far(2)), message(near(2))], axis=0), Z_UP)
-    r57 = shift(jnp.concatenate([message(far(1)), message(near(1))], axis=0), Z_DOWN)
-    size = ROWS + BIAS_ROWS
-    r3, r1, r5, r7 = r31[:size], r31[size:], r57[:size], r57[size:]
-    rows = jnp.concatenate([own_rows[:3], r4[ROWS : ROWS + 3], r3[ROWS : ROWS + 3], own_rows[9:]], axis=0)
-    on_0 = message(add(near(0), r4[:ROWS], r3[:ROWS], nothing(r57[0, 0])), rows)
-    r2 = shift(jnp.where(core == 0, on_0, message(across(1))), Z_UP_2, X_UP)
-    rows = jnp.concatenate([own_rows[:3], r5[ROWS : ROWS + 3], own_rows[6:]], axis=0)
-    on_0 = message(add(far(3), r5[:ROWS]), rows)
-    r6 = shift(jnp.where(core == 0, on_0, message(across(2))), Z_DOWN_2, X_DOWN)
-    r0 = shift(across(3).astype(BF16), None, X_TWO)
-    total = jnp.where(
-        core == 0,
-        add(near(3), r1[:ROWS], r2[:ROWS], r6[:ROWS], r7[:ROWS]),
-        add(across(0), r2[:ROWS], r6[:ROWS], r0),
+    j0 = shift(first_up, None, Z_UP)
+    ja1 = shift(jnp.where(core == 0, x1, add(y1, j0).astype(BF16)), X_UP, Z_UP)
+    ja2 = shift(jnp.where(core == 0, x2, y2), X_DOWN, Z_DOWN)
+    jb1 = shift(add(b1, ja1).astype(BF16), X_UP, Z_UP)
+    jb2 = shift(add(b2, jnp.where(core == 0, zero, ja2)).astype(BF16), X_DOWN, Z_DOWN)
+    wide = (2 * ROWS + BIAS_ROWS, WIDTH)
+    pair_a, pair_b, line_bias = small_call(
+        pair_kernel, ((wide, BF16), (wide, BF16), ((1, WIDTH), F32)), lists, (chip_bias, h0, ja1, ja2, jb1), 1
     )
-    bias = in_order(
-        [
-            line_bias,
-            joined(r1, ROWS),
-            joined(r2, ROWS),
-            joined(r2, ROWS + 6),
-            joined(r2, ROWS + 3),
-            joined(r6, ROWS + 3),
-            joined(r6, ROWS),
-            joined(r7, ROWS),
-        ],
-        z,
+    ra = shift(pair_a, Z_UP_2)
+    rb = shift(pair_b, Z_DOWN_2)
+    jc1 = shift(add(q1, jnp.where(core == 0, zero, jb1)).astype(BF16), X_UP, Z_UP)
+    jc2 = shift(add(q2, jb2).astype(BF16), X_DOWN, Z_DOWN)
+    size = (ROWS + BIAS_ROWS, WIDTH)
+    m1, m2, m3, rest = small_call(
+        message_kernel,
+        ((size, BF16), (size, BF16), (size, BF16), ((ROWS, WIDTH), F32)),
+        None,
+        (line_bias, h1, jc1, jc2, ra, rb),
+        0,
     )
-    return total, bias
+    r1 = shift(m1, Z_UP, X_UP)
+    r2 = shift(m2, Z_DOWN, X_DOWN)
+    r3 = shift(m3, Z_FOUR, X_TWO)
+    return small_call(
+        last_kernel,
+        (((NODES, WIDTH), BF16), ((W_ROWS, WIDTH), F32), ((1, WIDTH), F32)),
+        lists,
+        (line_bias, rest, r1, r2, r3, ra, rb, scaled),
+        1,
+    )
 
 
 def nothing(value):
@@ -478,7 +547,6 @@
 
     meta = jnp.stack([tile_rows, tile_cols, jnp.broadcast_to(tile_live, (SLOTS,))])
     other_meta = swap(meta, 1)
-    other_tiles = swap(tile_values, 1)
     place = jnp.stack([core, x, z, y, tile_live[0], other_meta[2, 0]]).astype(jnp.int32)
     lists = make_lists(place, meta, other_meta)
 
@@ -491,12 +559,12 @@
         ]
     ).reshape(NODES, 1)
 
+    other_tiles = swap(tile_values, 1)
     sums, weight_lane = gather(
         jnp.concatenate([feats, weight.T], axis=0),
         core,
-        nothing(other_tiles[0, 0, 0]) + nothing(other_meta[0, 0]),
-        nothing(lists[0, 0]),
-        lambda call, chunks, before: forward(call, lists, tile_values, other_tiles, chunks, before),
+        (lists, other_tiles),
+        lambda call, early, chunks, before: forward(call, early[0], tile_values, early[1], chunks, before),
     )
     neighbour_sum = (sums[:2] + swap(sums[2:], 1)).reshape(NODES, WIDTH)
     weight_other = swap(weight_lane, 1)
@@ -534,22 +602,21 @@
     mine = jnp.where(core == 0, weight_part[:, :, 0], weight_part[:, :, 1])
     others = jnp.where(core == 0, weight_part[:, :, 1], weight_part[:, :, 0])
     bias_part = jnp.sum(dz_full, axis=0, keepdims=True)
-    bias_rows = jnp.pad(bias_part, ((0, 7), (0, 0)))
-    sent = jnp.concatenate([others.reshape(-1, WIDTH), bias_rows], axis=0)
+    sent = jnp.concatenate([others.reshape(-1, WIDTH), jnp.pad(bias_part, ((0, 7), (0, 0)))], axis=0)
     got = swap(sent, 1)
     weight_sums = (mine + got[:-8].reshape(mine.shape)).astype(BF16)
 
     chip_bias = bias_part + got[-8:-7]
-    parts = []
-    for call in range(len(BACKWARD_CHUNKS)):
-        parts += backward(call, lists, tile_values, other_tiles, scaled_blocks, weight_sums, split(chip_bias))
-    column_sum, bias_sum = scatter(parts, core, x, z, chip_bias)
+    bias_rows = split(chip_bias)
+    parts = [
+        backward(call, lists, tile_values, other_tiles, scaled_blocks, weight_sums, bias_rows)
+        for call in range(len(SCATTER))
+    ]
+    feats_grad, weight_sum, bias_sum = scatter(*parts, core, lists, chip_bias, scaled)
     from_core_0 = lax.ppermute(bias_sum, "dom", [(i, i + 1) for i in range(0, NZ * NX * 2, 2)])
     bias_grad = jnp.where(core == 0, bias_sum, from_core_0)
 
-    feats_grad = (scaled.astype(F32) + column_sum[:NODES]).astype(BF16)
-    weight_grad = column_sum[NODES:].T
-    return (output, feats_grad, weight_grad, bias_grad.reshape(WIDTH))
+    return (output, feats_grad, weight_sum.T, bias_grad.reshape(WIDTH))
 
 
 def solution(mesh):

time: 224 us -> 200 us (0.89); the launches traced: 224 us -> 197 us
  local copies, waits for them, and re-layouts: 20.4 us -> 5.43 us
  other arithmetic: 23.6 us -> 10.5 us
  waiting for transfers between devices: 74.8 us -> 86.4 us
  starting transfers between devices: 60.9 us -> 53.9 us
  between operations: 6.93 us -> 2.01 us
    ppermute x27 -> x25, waiting for transfers between devices: 48.1 us -> 68.4 us  [shift(): return lax.ppermute(value, 'dom', pairs)]
    convert_element_type x17 -> x5, other arithmetic: 9.33 us -> 1.55 us  [the longest x1 0.84 us: on_device(): dz_own = dz_full.astype(BF16)]
    ppermute x27 -> x25, starting transfers between devices: 34.2 us -> 26.6 us  [shift(): return lax.ppermute(value, 'dom', pairs)]
    slice x9 -> x3, local copies, waits for them, and re-layouts: 7 us -> 0.61 us  [the longest x1 0.58 us: on_device(): other_meta[2, 0]]
    pallas_call x2 -> x5, Pallas kernels: 14.6 us -> 19.9 us  [the longest x2 17.2 us: backward(): pl.pallas_call(functools.partial(backward_kernel, call), out_shape=tuple(...]
    concatenate x4 -> x1, local copies, waits for them, and re-layouts: 4.11 us -> 0.02 us  [gather(): high = jnp.concatenate([pa, pb], axis=0)]
    unnamed x68 -> x57, local copies, waits for them, and re-layouts: 6.33 us -> 2.33 us
    ppermute x1, waiting for transfers between devices: 10.2 us -> 6.34 us  [on_device(): lax.ppermute(bias_sum, 'dom', [(i, i + 1) for i in range(0, NZ * NX * 2,...]
  transfers between devices with their start and end apart: 40 -> 38, of which waited for: 19 -> 22; matrix products, arithmetic and copies ran while one was open for 14% -> 6% of each run, Pallas kernels for 11% -> 13%
where the time goes in v3:
time: 200 us; the launch traced here: 197 us
  waiting for transfers between devices  86.4 us (43%)
  starting transfers between devices  53.9 us (27%)
  Pallas kernels  36.7 us (18%)
  other arithmetic  10.5 us (5%)
  local copies, waits for them, and re-layouts  5.43 us (3%)
  matrix products  2.47 us (1%)
  between operations  2.01 us (1%)
    ppermute x25, waiting for transfers between devices, shift(): return lax.ppermute(value, 'dom', pairs)  68.4 us
    ppermute x25, starting transfers between devices, shift(): return lax.ppermute(value, 'dom', pairs)  26.6 us
    pallas_call x2, Pallas kernels, backward(): pl.pallas_call(functools.partial(backward_kernel, call), out_shape=tuple(...  17.2 us
    ppermute x6, starting transfers between devices, swap(): lax.ppermute(value, 'dom', [(i, i ^ bit) for i in range(NZ * NX * 2)])  16.2 us
    pallas_call x2, Pallas kernels, forward(): pl.pallas_call(functools.partial(forward_kernel, call), out_shape=(jax.Sh...  15 us
    ppermute x6, starting transfers between devices, y_shift(): return lax.ppermute(value, 'feat', [(y, (y + dy) % NY) for y in range(NY)])  9.89 us
    ppermute x6, waiting for transfers between devices, y_shift(): return lax.ppermute(value, 'feat', [(y, (y + dy) % NY) for y in range(NY)])  9.11 us
    ppermute x1, waiting for transfers between devices, on_device(): lax.ppermute(bias_sum, 'dom', [(i, i + 1) for i in range(0, NZ * NX * 2,...  6.34 us
  transfers between devices with their start and end apart: 38, of which 22 were waited for; matrix products, arithmetic and copies ran while one was open for 6% of the time, Pallas kernels for 13%

profile of v3, /device:TPU:1, one launch (start us, length us, event | category | flops | bytes accessed | tf_op | source)
XLA Modules:
  0.0 197.4 jit_solution(18070488470127837840)
XLA Ops:
  0.6 3.3 %collective-permute-start.4 = (bf16[128,128,128]{2,1,0:T(8,128)(2,1)}, bf16[128,128,128]{2,1,0:T(8,128)(2,1)}, u32[]{:S(2)}, u32[]{:S(2)}) collective-permute-start(bf16[128,128,128]{2,1,0:T(8,128)(2,1)} %own.7), channel_id=1, source_target_pairs={{0,4},{4,0},{8,12},{12,8},{16,20},{20,16},{24,28},{28,24},{32,36},... | collective-permute-start | bytes 12582920 | tf_op jit(solution)/shard_map/ppermute | solution.py:72
  4.0 0.9 fusion.17
  4.9 0.8 collective-permute-start.1
  5.7 0.7 collective-permute-start
  6.4 1.0 collective-permute-start.2
  8.2 0.7 add_add_fusion.1.own
  8.9 5.1 %collective-permute-start.3 = (s32[3,128]{1,0:T(4,128)S(1)}, s32[3,128]{1,0:T(4,128)S(1)}, u32[]{:S(2)}, u32[]{:S(2)}) collective-permute-start(s32[3,128]{1,0:T(4,128)S(1)} %add_add_fusion.1.own), channel_id=1, source_target_pairs={{0,4},{4,0},{8,12},{12,8},{16,20},{20,16},{24,28},{28,24},{32,36},... | collective-permute-start | bytes 4616 | tf_op jit(solution)/shard_map/ppermute | solution.py:72
  14.0 0.8 collective-permute-done.3.sib
  15.4 1.3 stack.85.place
  16.7 1.8 shard_map.114.lists
  18.6 1.1 collective-permute-start.6
  20.2 0.7 collective-permute-start.8
  21.6 5.8 %collective-permute-done.6.rest_2_ = bf16[4,272,256]{2,1,0:T(8,128)(2,1)S(1)} collective-permute-done((bf16[4,272,256]{2,1,0:T(8,128)(2,1)S(1)}, bf16[4,272,256]{2,1,0:T(8,128)(2,1)S(1)}, u32[]{:S(2)}, u32[]{:S(2)}) %collective-permute-start.6) | collective-permute-done | bytes 557088 | tf_op jit(solution)/shard_map/ppermute | solution.py:64
  27.4 2.2 %collective-permute-done.5.rest_1_ = bf16[4,272,256]{2,1,0:T(8,128)(2,1)S(1)} collective-permute-done((bf16[4,272,256]{2,1,0:T(8,128)(2,1)S(1)}, bf16[4,272,256]{2,1,0:T(8,128)(2,1)S(1)}, u32[]{:S(2)}, u32[]{:S(2)}) %collective-permute-start.5) | collective-permute-done | bytes 557088 | tf_op jit(solution)/shard_map/ppermute | solution.py:64
  29.7 15.2 %collective-permute-done.9.rest_3_ = bf16[4,272,256]{2,1,0:T(8,128)(2,1)S(1)} collective-permute-done((bf16[4,272,256]{2,1,0:T(8,128)(2,1)S(1)}, bf16[4,272,256]{2,1,0:T(8,128)(2,1)S(1)}, u32[]{:S(2)}, u32[]{:S(2)}) %collective-permute-start.9) | collective-permute-done | bytes 557088 | tf_op jit(solution)/shard_map/ppermute | solution.py:64
  45.0 0.7 copy-done.7
  45.7 1.5 collective-permute-start.10
  47.2 6.9 %collective-permute-done.12.rest_4_ = bf16[4,272,256]{2,1,0:T(8,128)(2,1)S(1)} collective-permute-done((bf16[4,272,256]{2,1,0:T(8,128)(2,1)S(1)}, bf16[4,272,256]{2,1,0:T(8,128)(2,1)S(1)}, u32[]{:S(2)}, u32[]{:S(2)}) %collective-permute-start.12) | collective-permute-done | bytes 557088 | tf_op jit(solution)/shard_map/ppermute | solution.py:64
  54.1 1.2 collective-permute-start.13
  55.3 2.2 %collective-permute-start.11 = (bf16[2,272,256]{2,1,0:T(8,128)(2,1)S(1)}, bf16[2,272,256]{2,1,0:T(8,128)(2,1)S(1)}, u32[]{:S(2)}, u32[]{:S(2)}) collective-permute-start(bf16[2,272,256]{2,1,0:T(8,128)(2,1)S(1)} %slice.62), channel_id=1, source_target_pairs={{4,36},{12,44},{20,52},{28,60},{36,68},{44,76},{52,84},{60,92},{68... | collective-permute-start | bytes 835592 | tf_op jit(solution)/shard_map/ppermute | solution.py:64
  57.5 5.3 %collective-permute-done.13.rest_6_ = bf16[4,272,256]{2,1,0:T(8,128)(2,1)S(1)} collective-permute-done((bf16[4,272,256]{2,1,0:T(8,128)(2,1)S(1)}, bf16[4,272,256]{2,1,0:T(8,128)(2,1)S(1)}, u32[]{:S(2)}, u32[]{:S(2)}) %collective-permute-start.13) | collective-permute-done | bytes 557088 | tf_op jit(solution)/shard_map/ppermute | solution.py:64
  62.8 4.3 %collective-permute-start.14 = (bf16[2,272,256]{2,1,0:T(8,128)(2,1)S(1)}, bf16[2,272,256]{2,1,0:T(8,128)(2,1)S(1)}, u32[]{:S(2)}, u32[]{:S(2)}) collective-permute-start(bf16[2,272,256]{2,1,0:T(8,128)(2,1)S(1)} %slice.63), channel_id=1, source_target_pairs={{4,228},{12,236},{20,244},{28,252},{36,4},{44,12},{52,20},{60,28},... | collective-permute-start | bytes 835592 | tf_op jit(solution)/shard_map/ppermute | solution.py:64
  67.2 1.2 convert_reduce_fusion
  68.4 10.0 %shard_map.115 = (f32[4,128,256]{2,1,0:T(8,128)}, bf16[4,8,16,256]{3,2,1,0:T(8,128)(2,1)}) custom-call(s32[8,256]{1,0:T(8,128)} %shard_map.114.lists, bf16[128,128,128]{2,1,0:T(8,128)(2,1)} %own.7, bf16[128,128,128]{2,1,0:T(8,128)(2,1)} %collective-permute-done.4.sib, bf16[4,272,256]{2,1,0:T(8,128)(2,1)} %copy-done.5, bf16[4,272,256]{2,1,0:T(8,128)(2,1)} %copy-done.17, ...), custom_call_target="tpu_custom_call" | custom-call | flops 1073741824 | bytes 8388608 | tf_op jit(solution)/shard_map/pallas_call | solution.py:279
  79.2 4.9 %shard_map.116 = (f32[4,128,256]{2,1,0:T(8,128)}, bf16[4,8,16,256]{3,2,1,0:T(8,128)(2,1)}) custom-call(s32[8,256]{1,0:T(8,128)} %shard_map.114.lists, bf16[128,128,128]{2,1,0:T(8,128)(2,1)} %own.7, bf16[128,128,128]{2,1,0:T(8,128)(2,1)} %collective-permute-done.4.sib, bf16[2,272,256]{2,1,0:T(8,128)(2,1)} %copy-done.21, bf16[2,272,256]{2,1,0:T(8,128)(2,1)} %copy-done.22, ...), custom_call_target="tpu_custom_call" | custom-call | flops 268435456 | bytes 2097152 | tf_op jit(solution)/shard_map/pallas_call | solution.py:279
  84.2 6.2 %collective-permute-start.16 = (bf16[4,8,16,256]{3,2,1,0:T(8,128)(2,1)}, bf16[4,8,16,256]{3,2,1,0:T(8,128)(2,1)S(1)}, u32[]{:S(2)}, u32[]{:S(2)}) collective-permute-start(bf16[4,8,16,256]{3,2,1,0:T(8,128)(2,1)} %get-tuple-element.46), channel_id=1, source_target_pairs={{0,4},{4,0},{8,12},{12,8},{16,20},{20,16},{24,28},{28,24},{32,36},... | collective-permute-start | bytes 786440 | tf_op jit(solution)/shard_map/ppermute | solution.py:72
  90.5 1.0 slice.53
  91.7 1.0 select_bitcast_fusion.1
  93.1 0.7 copy-done.19
  94.7 3.0 %collective-permute-start.18 = (bf16[256,256]{1,0:T(8,128)(2,1)S(1)}, bf16[256,256]{1,0:T(8,128)(2,1)S(1)}, u32[]{:S(2)}, u32[]{:S(2)}) collective-permute-start(bf16[256,256]{1,0:T(8,128)(2,1)S(1)} %convolution_convert_fusion.1), channel_id=1, source_target_pairs={{0,2},{1,3},{2,0},{3,1},{4,6},{5,7},{6,4},{7,5},{8,10},{9,11},{10,... | collective-permute-start | bytes 393224 | tf_op jit(solution)/shard_map/ppermute | solution.py:76
  97.7 0.8 collective-permute-start.19
  98.5 0.7 collective-permute-start.17
  99.4 1.6 collective-permute-done.18
  101.0 3.2 %collective-permute-done.19 = bf16[256,256]{1,0:T(8,128)(2,1)S(1)} collective-permute-done((bf16[256,256]{1,0:T(8,128)(2,1)S(1)}, bf16[256,256]{1,0:T(8,128)(2,1)S(1)}, u32[]{:S(2)}, u32[]{:S(2)}) %collective-permute-start.19) | collective-permute-done | bytes 131104 | tf_op jit(solution)/shard_map/ppermute | solution.py:76
  104.1 0.8 fusion.18
  105.2 1.7 collective-permute-start.22
  106.9 2.6 %collective-permute-start.21 = (bf16[256,256]{1,0:T(8,128)(2,1)S(1)}, bf16[256,256]{1,0:T(8,128)(2,1)S(1)}, u32[]{:S(2)}, u32[]{:S(2)}) collective-permute-start(bf16[256,256]{1,0:T(8,128)(2,1)S(1)} %get-tuple-element.72), channel_id=1, source_target_pairs={{0,2},{1,3},{2,0},{3,1},{4,6},{5,7},{6,4},{7,5},{8,10},{9,11},{10,... | collective-permute-start | bytes 393224 | tf_op jit(solution)/shard_map/ppermute | solution.py:76
  109.5 1.1 collective-permute-start.20
  111.1 4.3 %collective-permute-done.21 = bf16[256,256]{1,0:T(8,128)(2,1)S(1)} collective-permute-done((bf16[256,256]{1,0:T(8,128)(2,1)S(1)}, bf16[256,256]{1,0:T(8,128)(2,1)S(1)}, u32[]{:S(2)}, u32[]{:S(2)}) %collective-permute-start.21) | collective-permute-done | bytes 131104 | tf_op jit(solution)/shard_map/ppermute | solution.py:76
  116.1 1.4 collective-permute-start.23
  118.3 1.3 collective-permute-done.24
  119.6 0.7 pad_maximum_fusion.4
  120.3 0.8 fusion.4.weight_sums
  121.8 5.1 %shard_map.118 = (bf16[1104,256]{1,0:T(8,128)(2,1)}, bf16[1104,256]{1,0:T(8,128)(2,1)}, bf16[1104,256]{1,0:T(8,128)(2,1)}) custom-call(s32[8,256]{1,0:T(8,128)} %shard_map.114.lists, bf16[128,128,128]{2,1,0:T(8,128)(2,1)} %own.7, bf16[128,128,128]{2,1,0:T(8,128)(2,1)} %collective-permute-done.4.sib, bf16[4,128,256]{2,1,0:T(8,128)(2,1)} %bitcast.79, ...), custom_call_target="tpu_custom_call" | custom-call | flops 402653184 | bytes 3145728 | tf_op jit(solution)/shard_map/pallas_call | solution.py:360
  126.9 2.1 %collective-permute-start.25 = (bf16[1104,256]{1,0:T(8,128)(2,1)}, bf16[1104,256]{1,0:T(8,128)(2,1)S(1)}, u32[]{:S(2)}, u32[]{:S(2)}) collective-permute-start(bf16[1104,256]{1,0:T(8,128)(2,1)} %get-tuple-element.50), channel_id=1, source_target_pairs={{4,36},{12,44},{20,52},{28,60},{36,68},{44,76},{52,84},{60,92},{68... | collective-permute-start | bytes 1695752 | tf_op jit(solution)/shard_map/ppermute | solution.py:64
  129.0 12.1 %shard_map.117 = (bf16[1104,256]{1,0:T(8,128)(2,1)}, bf16[1104,256]{1,0:T(8,128)(2,1)}, bf16[1104,256]{1,0:T(8,128)(2,1)}, bf16[1104,256]{1,0:T(8,128)(2,1)}, bf...) custom-call(s32[8,256]{1,0:T(8,128)} %shard_map.114.lists, ...), custom_call_target="tpu_custom_call" | custom-call | flops 1073741824 | bytes 8388608 | tf_op jit(solution)/shard_map/pallas_call | solution.py:360
  141.2 1.2 broadcast_select_fusion
  142.8 1.5 collective-permute-start.26
  144.3 6.9 %collective-permute-done.27.ja2 = bf16[1104,256]{1,0:T(8,128)(2,1)S(1)} collective-permute-done((bf16[1104,256]{1,0:T(8,128)(2,1)S(1)}, bf16[1104,256]{1,0:T(8,128)(2,1)S(1)}, u32[]{:S(2)}, u32[]{:S(2)}) %collective-permute-start.27) | collective-permute-done | bytes 565280 | tf_op jit(solution)/shard_map/ppermute | solution.py:64
  151.4 1.3 collective-permute-start.30
  153.3 7.0 %collective-permute-done.30 = bf16[1104,256]{1,0:T(8,128)(2,1)S(1)} collective-permute-done((bf16[1104,256]{1,0:T(8,128)(2,1)S(1)}, bf16[1104,256]{1,0:T(8,128)(2,1)S(1)}, u32[]{:S(2)}, u32[]{:S(2)}) %collective-permute-start.30) | collective-permute-done | bytes 565280 | tf_op jit(solution)/shard_map/ppermute | solution.py:64
  160.5 2.5 %collective-permute-start.31 = (bf16[1104,256]{1,0:T(8,128)(2,1)S(1)}, bf16[1104,256]{1,0:T(8,128)(2,1)S(1)}, u32[]{:S(2)}, u32[]{:S(2)}) collective-permute-start(bf16[1104,256]{1,0:T(8,128)(2,1)S(1)} %add_convert_fusion), channel_id=1, source_target_pairs={{0,24},{4,228},{8,0},{12,236},{16,8},{20,244},{24,16},{28,252},{32... | collective-permute-start | bytes 1695752 | tf_op jit(solution)/shard_map/ppermute | solution.py:64
  163.4 1.0 shard_map.119
  164.4 0.7 collective-permute-start.32
  165.0 0.7 collective-permute-start.33
  165.7 3.8 %collective-permute-done.31.jc2 = bf16[1104,256]{1,0:T(8,128)(2,1)S(1)} collective-permute-done((bf16[1104,256]{1,0:T(8,128)(2,1)S(1)}, bf16[1104,256]{1,0:T(8,128)(2,1)S(1)}, u32[]{:S(2)}, u32[]{:S(2)}) %collective-permute-start.31) | collective-permute-done | bytes 565280 | tf_op jit(solution)/shard_map/ppermute | solution.py:64
  169.6 9.6 %collective-permute-done.29.jc1 = bf16[1104,256]{1,0:T(8,128)(2,1)S(1)} collective-permute-done((bf16[1104,256]{1,0:T(8,128)(2,1)S(1)}, bf16[1104,256]{1,0:T(8,128)(2,1)S(1)}, u32[]{:S(2)}, u32[]{:S(2)}) %collective-permute-start.29) | collective-permute-done | bytes 565280 | tf_op jit(solution)/shard_map/ppermute | solution.py:64
  179.6 2.7 %collective-permute-start.35 = (bf16[288,256]{1,0:T(8,128)(2,1)S(1)}, bf16[288,256]{1,0:T(8,128)(2,1)S(1)}, u32[]{:S(2)}, u32[]{:S(2)}) collective-permute-start(bf16[288,256]{1,0:T(8,128)(2,1)S(1)} %get-tuple-element.63), channel_id=1, source_target_pairs={{0,224},{4,28},{8,232},{12,4},{16,240},{20,12},{24,248},{28,20},{3... | collective-permute-start | bytes 442376 | tf_op jit(solution)/shard_map/ppermute | solution.py:64
  182.2 2.5 %collective-permute-done.34.r1 = bf16[288,256]{1,0:T(8,128)(2,1)S(1)} collective-permute-done((bf16[288,256]{1,0:T(8,128)(2,1)S(1)}, bf16[288,256]{1,0:T(8,128)(2,1)S(1)}, u32[]{:S(2)}, u32[]{:S(2)}) %collective-permute-start.34) | collective-permute-done | bytes 147488 | tf_op jit(solution)/shard_map/ppermute | solution.py:64
  184.8 1.1 collective-permute-done.35.r2
  185.9 1.8 collective-permute-done.36.r3
  187.7 1.4 shard_map.121
  189.2 1.3 collective-permute-start.37
  190.5 6.3 %collective-permute-done.37 = f32[1,256]{1,0:T(1,128)S(1)} collective-permute-done((f32[1,256]{1,0:T(1,128)S(1)}, f32[1,256]{1,0:T(1,128)S(1)}, u32[]{:S(2)}, u32[]{:S(2)}) %collective-permute-start.37) | collective-permute-done | bytes 1056 | tf_op jit(solution)/shard_map/ppermute | solution.py:616
  (131 shorter events, 9.9 us)
Async XLA Ops:
  0.6 18.0 %collective-permute-start.4 = (bf16[128,128,128]{2,1,0:T(8,128)(2,1)}, bf16[128,128,128]{2,1,0:T(8,128)(2,1)}, u32[]{:S(2)}, u32[]{:S(2)}) collective-permute-start(bf16[128,128,128]{2,1,0:T(8,128)(2,1)} %own.7), channel_id=1, source_target_pairs={{0,4},{4,0},{8,12},{12,8},{16,20},{20,16},{24,28},{28,24},{32,36},... | collective-permute-start | bytes 12582920 | tf_op jit(solution)/shard_map/ppermute | solution.py:72
  4.9 13.6 %collective-permute-start.1 = (bf16[272,256]{1,0:T(8,128)(2,1)S(1)}, bf16[272,256]{1,0:T(8,128)(2,1)S(1)}, u32[]{:S(2)}, u32[]{:S(2)}) collective-permute-start(bf16[272,256]{1,0:T(8,128)(2,1)S(1)} %get-tuple-element.86), channel_id=1, source_target_pairs={{0,224},{4,28},{8,232},{12,4},{16,240},{20,12},{24,248},{28,20},{3... | collective-permute-start | bytes 417800 | tf_op jit(solution)/shard_map/ppermute | solution.py:64
  5.7 12.8 %collective-permute-start = (bf16[272,256]{1,0:T(8,128)(2,1)S(1)}, bf16[272,256]{1,0:T(8,128)(2,1)S(1)}, u32[]{:S(2)}, u32[]{:S(2)}) collective-permute-start(bf16[272,256]{1,0:T(8,128)(2,1)S(1)} %get-tuple-element.86), channel_id=1, source_target_pairs={{0,32},{4,12},{8,40},{12,20},{16,48},{20,28},{24,56},{28,4},{32,64... | collective-permute-start | bytes 417800 | tf_op jit(solution)/shard_map/ppermute | solution.py:64
  6.4 12.1 %collective-permute-start.2 = (bf16[272,256]{1,0:T(8,128)(2,1)S(1)}, bf16[272,256]{1,0:T(8,128)(2,1)S(1)}, u32[]{:S(2)}, u32[]{:S(2)}) collective-permute-start(bf16[272,256]{1,0:T(8,128)(2,1)S(1)} %get-tuple-element.86), channel_id=1, source_target_pairs={{0,128},{4,20},{8,136},{12,28},{16,144},{20,4},{24,152},{28,12},{3... | collective-permute-start | bytes 417800 | tf_op jit(solution)/shard_map/ppermute | solution.py:64
  8.9 7.8 %copy-start.24 = (s32[3,128]{1,0:T(4,128)}, s32[3,128]{1,0:T(4,128)S(1)}, u32[]{:S(2)}) copy-start(s32[3,128]{1,0:T(4,128)S(1)} %add_add_fusion.1.own) | copy-start | bytes 4612
  8.9 5.9 %collective-permute-start.3 = (s32[3,128]{1,0:T(4,128)S(1)}, s32[3,128]{1,0:T(4,128)S(1)}, u32[]{:S(2)}, u32[]{:S(2)}) collective-permute-start(s32[3,128]{1,0:T(4,128)S(1)} %add_add_fusion.1.own), channel_id=1, source_target_pairs={{0,4},{4,0},{8,12},{12,8},{16,20},{20,16},{24,28},{28,24},{32,36},... | collective-permute-start | bytes 4616 | tf_op jit(solution)/shard_map/ppermute | solution.py:72
  14.8 1.9 copy-start.25
  18.6 26.4 %copy-start.5 = (bf16[4,272,256]{2,1,0:T(8,128)(2,1)}, bf16[4,272,256]{2,1,0:T(8,128)(2,1)S(1)}, u32[]{:S(2)}) copy-start(bf16[4,272,256]{2,1,0:T(8,128)(2,1)S(1)} %pad_maximum_fusion.1.rest_0_) | copy-start | bytes 1671172
  18.6 8.8 %collective-permute-start.6 = (bf16[4,272,256]{2,1,0:T(8,128)(2,1)S(1)}, bf16[4,272,256]{2,1,0:T(8,128)(2,1)S(1)}, u32[]{:S(2)}, u32[]{:S(2)}) collective-permute-start(bf16[4,272,256]{2,1,0:T(8,128)(2,1)S(1)} %pad_maximum_fusion.1.rest_0_), channel_id=1, source_target_pairs={{0,24},{4,228},{8,0},{12,236},{16,8},{20,244},{24,16},{28,252},{32... | collective-permute-start | bytes 1671176 | tf_op jit(solution)/shard_map/ppermute | solution.py:64
  19.8 9.9 %collective-permute-start.5 = (bf16[4,272,256]{2,1,0:T(8,128)(2,1)S(1)}, bf16[4,272,256]{2,1,0:T(8,128)(2,1)S(1)}, u32[]{:S(2)}, u32[]{:S(2)}) collective-permute-start(bf16[4,272,256]{2,1,0:T(8,128)(2,1)S(1)} %pad_maximum_fusion.1.rest_0_), channel_id=1, source_target_pairs={{0,8},{4,36},{8,16},{12,44},{16,24},{20,52},{24,0},{28,60},{32,40}... | collective-permute-start | bytes 1671176 | tf_op jit(solution)/shard_map/ppermute | solution.py:64
  20.2 1.4 collective-permute-start.8
  20.9 0.7 collective-permute-start.7
  27.4 17.6 %copy-start.6 = (bf16[4,272,256]{2,1,0:T(8,128)(2,1)}, bf16[4,272,256]{2,1,0:T(8,128)(2,1)S(1)}, u32[]{:S(2)}) copy-start(bf16[4,272,256]{2,1,0:T(8,128)(2,1)S(1)} %collective-permute-done.6.rest_2_) | copy-start | bytes 1671172
  29.6 15.4 %copy-start.17 = (bf16[4,272,256]{2,1,0:T(8,128)(2,1)}, bf16[4,272,256]{2,1,0:T(8,128)(2,1)S(1)}, u32[]{:S(2)}) copy-start(bf16[4,272,256]{2,1,0:T(8,128)(2,1)S(1)} %collective-permute-done.5.rest_1_) | copy-start | bytes 1671172
  29.6 15.2 %collective-permute-start.9 = (bf16[4,272,256]{2,1,0:T(8,128)(2,1)S(1)}, bf16[4,272,256]{2,1,0:T(8,128)(2,1)S(1)}, u32[]{:S(2)}, u32[]{:S(2)}) collective-permute-start(bf16[4,272,256]{2,1,0:T(8,128)(2,1)S(1)} %collective-permute-done.5.rest_1_), channel_id=1, source_target_pairs={{0,8},{4,36},{8,16},{12,44},{16,24},{20,52},{24,0},{28,60},{32,40}... | collective-permute-start | bytes 1671176 | tf_op jit(solution)/shard_map/ppermute | solution.py:64
  29.7 37.5 %copy-start.3 = (bf16[128,128,128]{2,1,0:T(8,128)(2,1)S(1)}, bf16[128,128,128]{2,1,0:T(8,128)(2,1)}, u32[]{:S(2)}) copy-start(bf16[128,128,128]{2,1,0:T(8,128)(2,1)} %own.7) | copy-start | bytes 12582916
  29.7 15.3 %copy-start.4 = (bf16[4,272,256]{2,1,0:T(8,128)(2,1)}, bf16[4,272,256]{2,1,0:T(8,128)(2,1)S(1)}, u32[]{:S(2)}) copy-start(bf16[4,272,256]{2,1,0:T(8,128)(2,1)S(1)} %constant_dynamic-update-slice_fusion.rest_7_) | copy-start | bytes 1671172
  44.9 0.8 copy-start.7
  45.7 8.4 %collective-permute-start.12 = (bf16[4,272,256]{2,1,0:T(8,128)(2,1)S(1)}, bf16[4,272,256]{2,1,0:T(8,128)(2,1)S(1)}, u32[]{:S(2)}, u32[]{:S(2)}) collective-permute-start(bf16[4,272,256]{2,1,0:T(8,128)(2,1)S(1)} %get-tuple-element.75), channel_id=1, source_target_pairs={{0,24},{4,228},{8,0},{12,236},{16,8},{20,244},{24,16},{28,252},{32... | collective-permute-start | bytes 1671176 | tf_op jit(solution)/shard_map/ppermute | solution.py:64
  45.7 9.6 %collective-permute-start.10 = (bf16[4,272,256]{2,1,0:T(8,128)(2,1)S(1)}, bf16[4,272,256]{2,1,0:T(8,128)(2,1)S(1)}, u32[]{:S(2)}, u32[]{:S(2)}) collective-permute-start(bf16[4,272,256]{2,1,0:T(8,128)(2,1)S(1)} %get-tuple-element.76), channel_id=1, source_target_pairs={{0,8},{4,36},{8,16},{12,44},{16,24},{20,52},{24,0},{28,60},{32,40}... | collective-permute-start | bytes 1671176 | tf_op jit(solution)/shard_map/ppermute | solution.py:64
  54.1 14.2 %copy-start.18 = (bf16[4,272,256]{2,1,0:T(8,128)(2,1)}, bf16[4,272,256]{2,1,0:T(8,128)(2,1)S(1)}, u32[]{:S(2)}) copy-start(bf16[4,272,256]{2,1,0:T(8,128)(2,1)S(1)} %collective-permute-done.12.rest_4_) | copy-start | bytes 1671172
  54.1 8.7 %collective-permute-start.13 = (bf16[4,272,256]{2,1,0:T(8,128)(2,1)S(1)}, bf16[4,272,256]{2,1,0:T(8,128)(2,1)S(1)}, u32[]{:S(2)}, u32[]{:S(2)}) collective-permute-start(bf16[4,272,256]{2,1,0:T(8,128)(2,1)S(1)} %collective-permute-done.12.rest_4_), channel_id=1, source_target_pairs={{0,24},{4,228},{8,0},{12,236},{16,8},{20,244},{24,16},{28,252},{32... | collective-permute-start | bytes 1671176 | tf_op jit(solution)/shard_map/ppermute | solution.py:64
  55.3 13.0 %copy-start.8 = (bf16[4,272,256]{2,1,0:T(8,128)(2,1)}, bf16[4,272,256]{2,1,0:T(8,128)(2,1)S(1)}, u32[]{:S(2)}) copy-start(bf16[4,272,256]{2,1,0:T(8,128)(2,1)S(1)} %collective-permute-done.10.rest_5_) | copy-start | bytes 1671172
  55.3 23.1 %collective-permute-start.11 = (bf16[2,272,256]{2,1,0:T(8,128)(2,1)S(1)}, bf16[2,272,256]{2,1,0:T(8,128)(2,1)S(1)}, u32[]{:S(2)}, u32[]{:S(2)}) collective-permute-start(bf16[2,272,256]{2,1,0:T(8,128)(2,1)S(1)} %slice.62), channel_id=1, source_target_pairs={{4,36},{12,44},{20,52},{28,60},{36,68},{44,76},{52,84},{60,92},{68... | collective-permute-start | bytes 835592 | tf_op jit(solution)/shard_map/ppermute | solution.py:64
  62.8 5.6 %copy-start.9 = (bf16[4,272,256]{2,1,0:T(8,128)(2,1)}, bf16[4,272,256]{2,1,0:T(8,128)(2,1)S(1)}, u32[]{:S(2)}) copy-start(bf16[4,272,256]{2,1,0:T(8,128)(2,1)S(1)} %collective-permute-done.13.rest_6_) | copy-start | bytes 1671172
  62.8 15.6 %collective-permute-start.14 = (bf16[2,272,256]{2,1,0:T(8,128)(2,1)S(1)}, bf16[2,272,256]{2,1,0:T(8,128)(2,1)S(1)}, u32[]{:S(2)}, u32[]{:S(2)}) collective-permute-start(bf16[2,272,256]{2,1,0:T(8,128)(2,1)S(1)} %slice.63), channel_id=1, source_target_pairs={{4,228},{12,236},{20,244},{28,252},{36,4},{44,12},{52,20},{60,28},... | collective-permute-start | bytes 835592 | tf_op jit(solution)/shard_map/ppermute | solution.py:64
  79.2 11.1 %copy-start.26 = (s32[128]{0:T(128)S(1)}, s32[128]{0:T(128)}, u32[]{:S(2)}) copy-start(s32[128]{0:T(128)} %param.12) | copy-start | bytes 1540
  84.2 7.5 %collective-permute-start.16 = (bf16[4,8,16,256]{3,2,1,0:T(8,128)(2,1)}, bf16[4,8,16,256]{3,2,1,0:T(8,128)(2,1)S(1)}, u32[]{:S(2)}, u32[]{:S(2)}) collective-permute-start(bf16[4,8,16,256]{3,2,1,0:T(8,128)(2,1)} %get-tuple-element.46), channel_id=1, source_target_pairs={{0,4},{4,0},{8,12},{12,8},{16,20},{20,16},{24,28},{28,24},{32,36},... | collective-permute-start | bytes 786440 | tf_op jit(solution)/shard_map/ppermute | solution.py:72
  91.5 1.6 collective-permute-start.15
  92.7 1.0 copy-start.19
  92.8 1.1 copy-start.20
  93.8 10.3 %copy-start.23 = (bf16[256,256]{1,0:T(8,128)(2,1)S(1)}, bf16[256,256]{1,0:T(8,128)(2,1)}, u32[]{:S(2)}) copy-start(bf16[256,256]{1,0:T(8,128)(2,1)} %param.15) | copy-start | bytes 393220
  93.8 10.3 %copy-start.27 = (f32[256]{0:T(256)S(1)}, f32[256]{0:T(256)}, u32[]{:S(2)}) copy-start(f32[256]{0:T(256)} %param.10) | copy-start | bytes 3076
  94.7 6.3 %collective-permute-start.18 = (bf16[256,256]{1,0:T(8,128)(2,1)S(1)}, bf16[256,256]{1,0:T(8,128)(2,1)S(1)}, u32[]{:S(2)}, u32[]{:S(2)}) collective-permute-start(bf16[256,256]{1,0:T(8,128)(2,1)S(1)} %convolution_convert_fusion.1), channel_id=1, source_target_pairs={{0,2},{1,3},{2,0},{3,1},{4,6},{5,7},{6,4},{7,5},{8,10},{9,11},{10,... | collective-permute-start | bytes 393224 | tf_op jit(solution)/shard_map/ppermute | solution.py:76
  97.7 6.5 %collective-permute-start.19 = (bf16[256,256]{1,0:T(8,128)(2,1)S(1)}, bf16[256,256]{1,0:T(8,128)(2,1)S(1)}, u32[]{:S(2)}, u32[]{:S(2)}) collective-permute-start(bf16[256,256]{1,0:T(8,128)(2,1)S(1)} %convolution_convert_fusion), channel_id=1, source_target_pairs={{0,3},{1,0},{2,1},{3,2},{4,7},{5,4},{6,5},{7,6},{8,11},{9,8},{10,9... | collective-permute-start | bytes 393224 | tf_op jit(solution)/shard_map/ppermute | solution.py:76
  98.5 5.7 %collective-permute-start.17 = (bf16[256,256]{1,0:T(8,128)(2,1)S(1)}, bf16[256,256]{1,0:T(8,128)(2,1)S(1)}, u32[]{:S(2)}, u32[]{:S(2)}) collective-permute-start(bf16[256,256]{1,0:T(8,128)(2,1)S(1)} %convolution_convert_fusion.2), channel_id=1, source_target_pairs={{0,1},{1,2},{2,3},{3,0},{4,5},{5,6},{6,7},{7,4},{8,9},{9,10},{10,1... | collective-permute-start | bytes 393224 | tf_op jit(solution)/shard_map/ppermute | solution.py:76
  105.2 5.7 %collective-permute-start.22 = (bf16[256,256]{1,0:T(8,128)(2,1)S(1)}, bf16[256,256]{1,0:T(8,128)(2,1)S(1)}, u32[]{:S(2)}, u32[]{:S(2)}) collective-permute-start(bf16[256,256]{1,0:T(8,128)(2,1)S(1)} %get-tuple-element.72), channel_id=1, source_target_pairs={{0,1},{1,2},{2,3},{3,0},{4,5},{5,6},{6,7},{7,4},{8,9},{9,10},{10,1... | collective-permute-start | bytes 393224 | tf_op jit(solution)/shard_map/ppermute | solution.py:76
  106.9 8.5 %collective-permute-start.21 = (bf16[256,256]{1,0:T(8,128)(2,1)S(1)}, bf16[256,256]{1,0:T(8,128)(2,1)S(1)}, u32[]{:S(2)}, u32[]{:S(2)}) collective-permute-start(bf16[256,256]{1,0:T(8,128)(2,1)S(1)} %get-tuple-element.72), channel_id=1, source_target_pairs={{0,2},{1,3},{2,0},{3,1},{4,6},{5,7},{6,4},{7,5},{8,10},{9,11},{10,... | collective-permute-start | bytes 393224 | tf_op jit(solution)/shard_map/ppermute | solution.py:76
  109.5 6.1 %collective-permute-start.20 = (bf16[256,256]{1,0:T(8,128)(2,1)S(1)}, bf16[256,256]{1,0:T(8,128)(2,1)S(1)}, u32[]{:S(2)}, u32[]{:S(2)}) collective-permute-start(bf16[256,256]{1,0:T(8,128)(2,1)S(1)} %get-tuple-element.72), channel_id=1, source_target_pairs={{0,3},{1,0},{2,1},{3,2},{4,7},{5,4},{6,5},{7,6},{8,11},{9,8},{10,9... | collective-permute-start | bytes 393224 | tf_op jit(solution)/shard_map/ppermute | solution.py:76
  116.1 4.2 %collective-permute-start.23 = (f32[520,256]{1,0:T(8,128)S(1)}, f32[520,256]{1,0:T(8,128)S(1)}, u32[]{:S(2)}, u32[]{:S(2)}) collective-permute-start(f32[520,256]{1,0:T(8,128)S(1)} %select_maximum_fusion), channel_id=1, source_target_pairs={{0,4},{4,0},{8,12},{12,8},{16,20},{20,16},{24,28},{28,24},{32,36},... | collective-permute-start | bytes 1597448 | tf_op jit(solution)/shard_map/ppermute | solution.py:72
  118.1 1.4 collective-permute-start.24
  126.9 14.2 %copy-start.16 = (bf16[1104,256]{1,0:T(8,128)(2,1)S(1)}, bf16[1104,256]{1,0:T(8,128)(2,1)}, u32[]{:S(2)}) copy-start(bf16[1104,256]{1,0:T(8,128)(2,1)} %get-tuple-element.51) | copy-start | bytes 1695748
  126.9 15.6 %collective-permute-start.25 = (bf16[1104,256]{1,0:T(8,128)(2,1)}, bf16[1104,256]{1,0:T(8,128)(2,1)S(1)}, u32[]{:S(2)}, u32[]{:S(2)}) collective-permute-start(bf16[1104,256]{1,0:T(8,128)(2,1)} %get-tuple-element.50), channel_id=1, source_target_pairs={{4,36},{12,44},{20,52},{28,60},{36,68},{44,76},{52,84},{60,92},{68... | collective-permute-start | bytes 1695752 | tf_op jit(solution)/shard_map/ppermute | solution.py:64
  141.1 1.4 copy-start.14
  141.1 1.4 copy-start.15
  142.4 8.8 %collective-permute-start.27 = (bf16[1104,256]{1,0:T(8,128)(2,1)S(1)}, bf16[1104,256]{1,0:T(8,128)(2,1)S(1)}, u32[]{:S(2)}, u32[]{:S(2)}) collective-permute-start(bf16[1104,256]{1,0:T(8,128)(2,1)S(1)} %broadcast_select_fusion), channel_id=1, source_target_pairs={{0,24},{4,228},{8,0},{12,236},{16,8},{20,244},{24,16},{28,252},{32... | collective-permute-start | bytes 1695752 | tf_op jit(solution)/shard_map/ppermute | solution.py:64
  142.5 8.7 %copy-start.13 = (bf16[1104,256]{1,0:T(8,128)(2,1)S(1)}, bf16[1104,256]{1,0:T(8,128)(2,1)}, u32[]{:S(2)}) copy-start(bf16[1104,256]{1,0:T(8,128)(2,1)} %get-tuple-element.58) | copy-start | bytes 1695748
  142.8 10.1 %copy-start.12 = (bf16[1104,256]{1,0:T(8,128)(2,1)S(1)}, bf16[1104,256]{1,0:T(8,128)(2,1)}, u32[]{:S(2)}) copy-start(bf16[1104,256]{1,0:T(8,128)(2,1)} %get-tuple-element.53) | copy-start | bytes 1695748
  142.8 10.1 %collective-permute-start.26 = (bf16[1104,256]{1,0:T(8,128)(2,1)S(1)}, bf16[1104,256]{1,0:T(8,128)(2,1)S(1)}, u32[]{:S(2)}, u32[]{:S(2)}) collective-permute-start(bf16[1104,256]{1,0:T(8,128)(2,1)S(1)} %fusion.3), channel_id=1, source_target_pairs={{0,8},{4,36},{8,16},{12,44},{16,24},{20,52},{24,0},{28,60},{32,40}... | collective-permute-start | bytes 1695752 | tf_op jit(solution)/shard_map/ppermute | solution.py:64
  151.4 8.9 %copy-start.11 = (bf16[1104,256]{1,0:T(8,128)(2,1)S(1)}, bf16[1104,256]{1,0:T(8,128)(2,1)}, u32[]{:S(2)}) copy-start(bf16[1104,256]{1,0:T(8,128)(2,1)} %get-tuple-element.57) | copy-start | bytes 1695748
  151.4 8.8 %collective-permute-start.30 = (bf16[1104,256]{1,0:T(8,128)(2,1)S(1)}, bf16[1104,256]{1,0:T(8,128)(2,1)S(1)}, u32[]{:S(2)}, u32[]{:S(2)}) collective-permute-start(bf16[1104,256]{1,0:T(8,128)(2,1)S(1)} %add_convert_fusion.1), channel_id=1, source_target_pairs={{0,24},{4,228},{8,0},{12,236},{16,8},{20,244},{24,16},{28,252},{32... | collective-permute-start | bytes 1695752 | tf_op jit(solution)/shard_map/ppermute | solution.py:64
  153.0 10.1 %copy-start.10 = (bf16[1104,256]{1,0:T(8,128)(2,1)S(1)}, bf16[1104,256]{1,0:T(8,128)(2,1)}, u32[]{:S(2)}) copy-start(bf16[1104,256]{1,0:T(8,128)(2,1)} %get-tuple-element.56) | copy-start | bytes 1695748
  153.0 10.1 %collective-permute-start.28 = (bf16[1104,256]{1,0:T(8,128)(2,1)S(1)}, bf16[1104,256]{1,0:T(8,128)(2,1)S(1)}, u32[]{:S(2)}, u32[]{:S(2)}) collective-permute-start(bf16[1104,256]{1,0:T(8,128)(2,1)S(1)} %add_convert_fusion.3), channel_id=1, source_target_pairs={{0,8},{4,36},{8,16},{12,44},{16,24},{20,52},{24,0},{28,60},{32,40}... | collective-permute-start | bytes 1695752 | tf_op jit(solution)/shard_map/ppermute | solution.py:64
  160.5 2.9 %copy-start.1 = (bf16[1104,256]{1,0:T(8,128)(2,1)S(1)}, bf16[1104,256]{1,0:T(8,128)(2,1)}, u32[]{:S(2)}) copy-start(bf16[1104,256]{1,0:T(8,128)(2,1)} %get-tuple-element.47.h0) | copy-start | bytes 1695748
  160.5 2.9 %copy-start.2 = (s32[8,256]{1,0:T(8,128)S(1)}, s32[8,256]{1,0:T(8,128)}, u32[]{:S(2)}) copy-start(s32[8,256]{1,0:T(8,128)} %shard_map.114.lists) | copy-start | bytes 24580
  160.5 9.1 %collective-permute-start.31 = (bf16[1104,256]{1,0:T(8,128)(2,1)S(1)}, bf16[1104,256]{1,0:T(8,128)(2,1)S(1)}, u32[]{:S(2)}, u32[]{:S(2)}) collective-permute-start(bf16[1104,256]{1,0:T(8,128)(2,1)S(1)} %add_convert_fusion), channel_id=1, source_target_pairs={{0,24},{4,228},{8,0},{12,236},{16,8},{20,244},{24,16},{28,252},{32... | collective-permute-start | bytes 1695752 | tf_op jit(solution)/shard_map/ppermute | solution.py:64
  163.3 15.9 %collective-permute-start.29 = (bf16[1104,256]{1,0:T(8,128)(2,1)S(1)}, bf16[1104,256]{1,0:T(8,128)(2,1)S(1)}, u32[]{:S(2)}, u32[]{:S(2)}) collective-permute-start(bf16[1104,256]{1,0:T(8,128)(2,1)S(1)} %add_convert_fusion.2), channel_id=1, source_target_pairs={{0,8},{4,36},{8,16},{12,44},{16,24},{20,52},{24,0},{28,60},{32,40}... | collective-permute-start | bytes 1695752 | tf_op jit(solution)/shard_map/ppermute | solution.py:64
  163.4 15.8 %copy-start = (bf16[1104,256]{1,0:T(8,128)(2,1)S(1)}, bf16[1104,256]{1,0:T(8,128)(2,1)}, u32[]{:S(2)}) copy-start(bf16[1104,256]{1,0:T(8,128)(2,1)} %get-tuple-element.55.h1) | copy-start | bytes 1695748
  164.4 5.2 %collective-permute-start.32 = (bf16[560,256]{1,0:T(8,128)(2,1)S(1)}, bf16[560,256]{1,0:T(8,128)(2,1)S(1)}, u32[]{:S(2)}, u32[]{:S(2)}) collective-permute-start(bf16[560,256]{1,0:T(8,128)(2,1)S(1)} %get-tuple-element.59), channel_id=1, source_target_pairs={{0,64},{8,72},{16,80},{24,88},{32,96},{40,104},{48,112},{56,120},{... | collective-permute-start | bytes 860168 | tf_op jit(solution)/shard_map/ppermute | solution.py:64
  165.0 4.5 %collective-permute-start.33 = (bf16[560,256]{1,0:T(8,128)(2,1)S(1)}, bf16[560,256]{1,0:T(8,128)(2,1)S(1)}, u32[]{:S(2)}, u32[]{:S(2)}) collective-permute-start(bf16[560,256]{1,0:T(8,128)(2,1)S(1)} %get-tuple-element.60), channel_id=1, source_target_pairs={{0,192},{8,200},{16,208},{24,216},{32,224},{40,232},{48,240},{56,2... | collective-permute-start | bytes 860168 | tf_op jit(solution)/shard_map/ppermute | solution.py:64
  179.5 5.3 %collective-permute-start.34 = (bf16[288,256]{1,0:T(8,128)(2,1)S(1)}, bf16[288,256]{1,0:T(8,128)(2,1)S(1)}, u32[]{:S(2)}, u32[]{:S(2)}) collective-permute-start(bf16[288,256]{1,0:T(8,128)(2,1)S(1)} %get-tuple-element.62), channel_id=1, source_target_pairs={{0,32},{4,12},{8,40},{12,20},{16,48},{20,28},{24,56},{28,4},{32,64... | collective-permute-start | bytes 442376 | tf_op jit(solution)/shard_map/ppermute | solution.py:64
  179.6 6.3 %collective-permute-start.35 = (bf16[288,256]{1,0:T(8,128)(2,1)S(1)}, bf16[288,256]{1,0:T(8,128)(2,1)S(1)}, u32[]{:S(2)}, u32[]{:S(2)}) collective-permute-start(bf16[288,256]{1,0:T(8,128)(2,1)S(1)} %get-tuple-element.63), channel_id=1, source_target_pairs={{0,224},{4,28},{8,232},{12,4},{16,240},{20,12},{24,248},{28,20},{3... | collective-permute-start | bytes 442376 | tf_op jit(solution)/shard_map/ppermute | solution.py:64
  182.2 5.5 %collective-permute-start.36 = (bf16[288,256]{1,0:T(8,128)(2,1)S(1)}, bf16[288,256]{1,0:T(8,128)(2,1)S(1)}, u32[]{:S(2)}, u32[]{:S(2)}) collective-permute-start(bf16[288,256]{1,0:T(8,128)(2,1)S(1)} %get-tuple-element.64), channel_id=1, source_target_pairs={{0,128},{4,20},{8,136},{12,28},{16,144},{20,4},{24,152},{28,12},{3... | collective-permute-start | bytes 442376 | tf_op jit(solution)/shard_map/ppermute | solution.py:64
  189.2 7.6 %collective-permute-start.37 = (f32[1,256]{1,0:T(1,128)S(1)}, f32[1,256]{1,0:T(1,128)S(1)}, u32[]{:S(2)}, u32[]{:S(2)}) collective-permute-start(f32[1,256]{1,0:T(1,128)S(1)} %get-tuple-element.67), channel_id=1, source_target_pairs={{0,4},{8,12},{16,20},{24,28},{32,36},{40,44},{48,52},{56,60},{64,6... | collective-permute-start | bytes 3080 | tf_op jit(solution)/shard_map/ppermute | solution.py:616
  (2 other events, 1.5 us)

commit v4 on v3

--- a/solution.py
+++ b/solution.py
@@ -33,7 +33,7 @@
     tuple(k * NZ + 4 for k in ACROSS[:2]),
     tuple(k * NZ + 4 for k in ACROSS[2:]),
 )
-FORWARD_CHUNKS = ((0, 1, 2, 3, 4, 5, 6, 7), (8, 9))
+FORWARD_CHUNKS = ((0, 1, 2, 3, 4, 7), (5, 6), (8, 9))
 SCATTER = (
     (
         (None, tuple((dx, 4) for dx in ACROSS)),
@@ -102,7 +102,9 @@
     spot = (k * NZ + j) * 2 + (column & 1)
     mine = live & ((owner & 1) == core)
     high = ((j >= 2) & (j <= 6)) & (j != 4)
-    forward_call = jnp.where((core == 1) & (j == 4), 1, 0)
+    on_0 = jnp.where(high & ((k == 1) | (k == 2)), 1, 0)
+    on_1 = jnp.where(j == 4, 2, jnp.where((j == 3) | (j == 5), 1, 0))
+    forward_call = jnp.where(core == 0, on_0, on_1)
     backward_call = jnp.where(core == 0, jnp.where(high & ((k == 1) | (k == 2)), 0, 1), jnp.where(j == 4, 0, 1))
     square = (2 * SLOTS, 2 * SLOTS)
     first = lax.broadcasted_iota(jnp.int32, square, 0)
@@ -380,19 +382,22 @@
     p3 = shift(block, Z_FOUR, X_TWO)
     pa = shift(jnp.stack([block, p1]), Z_UP_2)
     pb = shift(jnp.stack([block, p2]), Z_DOWN_2)
-    low, *early = lax.optimization_barrier((jnp.stack([block, p1, p2, p3]), *early))
+    low, pa, pb, *early = lax.optimization_barrier((jnp.stack([block, p1, p2, p3]), pa, pb, *early))
     c1 = shift(low, X_UP, Z_UP)
     c2 = shift(low, X_DOWN, Z_DOWN)
-    c1, c2, pa, pb = lax.optimization_barrier((c1, c2, pa, pb))
     high = jnp.concatenate([pa, pb], axis=0)
+    c1, c2 = lax.optimization_barrier((c1, c2))
     c3 = shift(c1, X_UP, Z_UP)
     c4 = shift(jnp.where(core == 0, high, c2), X_DOWN, Z_DOWN)
+    c3, c4 = lax.optimization_barrier((c3, c4))
+    chunks = [low, c1, c2, c3, c4, None, None, high]
+    sums = call(0, early, chunks, ())
     c5 = shift(jnp.where(core == 0, high, c3), X_UP, Z_UP)
     c6 = shift(c4, X_DOWN, Z_DOWN)
-    c7 = shift(c5[:2], None, Z_UP)
-    c8 = shift(c6[2:], None, Z_DOWN)
-    chunks = [low, c1, c2, c3, c4, c5, c6, high, c7, c8]
-    return call(1, early, chunks, call(0, early, chunks, ()))
+    c5, c6, sums = lax.optimization_barrier((c5, c6, sums))
+    chunks[5:7] = c5, c6
+    chunks += [shift(c5[:2], None, Z_UP), shift(c6[2:], None, Z_DOWN)]
+    return call(2, early, chunks, call(1, early, chunks, sums))
 
 
 def add(*values):
@@ -499,16 +504,19 @@
     j0 = shift(first_up, None, Z_UP)
     ja1 = shift(jnp.where(core == 0, x1, add(y1, j0).astype(BF16)), X_UP, Z_UP)
     ja2 = shift(jnp.where(core == 0, x2, y2), X_DOWN, Z_DOWN)
+    ja1, ja2 = lax.optimization_barrier((ja1, ja2))
     jb1 = shift(add(b1, ja1).astype(BF16), X_UP, Z_UP)
     jb2 = shift(add(b2, jnp.where(core == 0, zero, ja2)).astype(BF16), X_DOWN, Z_DOWN)
+    jb1, jb2 = lax.optimization_barrier((jb1, jb2))
     wide = (2 * ROWS + BIAS_ROWS, WIDTH)
     pair_a, pair_b, line_bias = small_call(
         pair_kernel, ((wide, BF16), (wide, BF16), ((1, WIDTH), F32)), lists, (chip_bias, h0, ja1, ja2, jb1), 1
     )
+    jc1 = shift(add(q1, jnp.where(core == 0, zero, jb1)).astype(BF16), X_UP, Z_UP)
+    jc2 = shift(add(q2, jb2).astype(BF16), X_DOWN, Z_DOWN)
+    jc1, jc2, pair_a, pair_b = lax.optimization_barrier((jc1, jc2, pair_a, pair_b))
     ra = shift(pair_a, Z_UP_2)
     rb = shift(pair_b, Z_DOWN_2)
-    jc1 = shift(add(q1, jnp.where(core == 0, zero, jb1)).astype(BF16), X_UP, Z_UP)
-    jc2 = shift(add(q2, jb2).astype(BF16), X_DOWN, Z_DOWN)
     size = (ROWS + BIAS_ROWS, WIDTH)
     m1, m2, m3, rest = small_call(
         message_kernel,

time: 200 us -> 200 us (level); the launches traced: 197 us -> 201 us
  Pallas kernels: 36.7 us -> 44.3 us
  waiting for transfers between devices: 86.4 us -> 79.4 us
  starting transfers between devices: 53.9 us -> 57.9 us
    ppermute x25, waiting for transfers between devices: 68.4 us -> 49.8 us  [shift(): return lax.ppermute(value, 'dom', pairs)]
    ppermute x1, waiting for transfers between devices: 6.34 us -> 17.9 us  [on_device(): lax.ppermute(bias_sum, 'dom', [(i, i + 1) for i in range(0, NZ * NX * 2,...]
    pallas_call x2 -> x3, Pallas kernels: 15 us -> 21.2 us  [forward(): pl.pallas_call(functools.partial(forward_kernel, call), out_shape=(jax.Sh...]
    ppermute x6, starting transfers between devices: 16.2 us -> 18.3 us  [swap(): lax.ppermute(value, 'dom', [(i, i ^ bit) for i in range(NZ * NX * 2)])]
  transfers between devices with their start and end apart: 38 -> 38, of which waited for: 22 -> 22; matrix products, arithmetic and copies ran while one was open for 6% -> 5% of each run, Pallas kernels for 13% -> 16%
where the time goes in v4:
time: 200 us; the launch traced here: 201 us
  waiting for transfers between devices  79.4 us (40%)
  starting transfers between devices  57.9 us (29%)
  Pallas kernels  44.3 us (22%)
  other arithmetic  9.8 us (5%)
  local copies, waits for them, and re-layouts  4.67 us (2%)
  matrix products  2.47 us (1%)
  between operations  2.08 us (1%)
    ppermute x25, waiting for transfers between devices, shift(): return lax.ppermute(value, 'dom', pairs)  49.8 us
    ppermute x25, starting transfers between devices, shift(): return lax.ppermute(value, 'dom', pairs)  28.4 us
    pallas_call x3, Pallas kernels, forward(): pl.pallas_call(functools.partial(forward_kernel, call), out_shape=(jax.Sh...  21.2 us
    pallas_call x2, Pallas kernels, backward(): pl.pallas_call(functools.partial(backward_kernel, call), out_shape=tuple(...  18.6 us
    ppermute x6, starting transfers between devices, swap(): lax.ppermute(value, 'dom', [(i, i ^ bit) for i in range(NZ * NX * 2)])  18.3 us
    ppermute x1, waiting for transfers between devices, on_device(): lax.ppermute(bias_sum, 'dom', [(i, i + 1) for i in range(0, NZ * NX * 2,...  17.9 us
    ppermute x6, starting transfers between devices, y_shift(): return lax.ppermute(value, 'feat', [(y, (y + dy) % NY) for y in range(NY)])  9.9 us
    ppermute x6, waiting for transfers between devices, y_shift(): return lax.ppermute(value, 'feat', [(y, (y + dy) % NY) for y in range(NY)])  9.11 us
  transfers between devices with their start and end apart: 38, of which 22 were waited for; matrix products, arithmetic and copies ran while one was open for 5% of the time, Pallas kernels for 16%

profile of v4, /device:TPU:1, one launch (start us, length us, event | category | flops | bytes accessed | tf_op | source)
XLA Modules:
  0.0 200.6 jit_solution(3547970471682655830)
XLA Ops:
  0.7 3.3 %collective-permute-start.6 = (bf16[128,128,128]{2,1,0:T(8,128)(2,1)}, bf16[128,128,128]{2,1,0:T(8,128)(2,1)}, u32[]{:S(2)}, u32[]{:S(2)}) collective-permute-start(bf16[128,128,128]{2,1,0:T(8,128)(2,1)} %own.9), channel_id=1, source_target_pairs={{0,4},{4,0},{8,12},{12,8},{16,20},{20,16},{24,28},{28,24},{32,36},... | collective-permute-start | bytes 12582920 | tf_op jit(solution)/shard_map/ppermute | solution.py:72
  4.0 0.9 fusion.17
  4.9 0.8 collective-permute-start.1
  5.7 0.7 collective-permute-start
  6.5 1.0 collective-permute-start.2
  8.2 1.0 collective-permute-done.1
  9.2 3.2 %collective-permute-done = bf16[272,256]{1,0:T(8,128)(2,1)S(1)} collective-permute-done((bf16[272,256]{1,0:T(8,128)(2,1)S(1)}, bf16[272,256]{1,0:T(8,128)(2,1)S(1)}, u32[]{:S(2)}, u32[]{:S(2)}) %collective-permute-start) | collective-permute-done | bytes 139296 | tf_op jit(solution)/shard_map/ppermute | solution.py:64
  12.4 0.7 collective-permute-start.4
  13.9 11.5 %collective-permute-start.5 = (s32[3,128]{1,0:T(4,128)S(1)}, s32[3,128]{1,0:T(4,128)S(1)}, u32[]{:S(2)}, u32[]{:S(2)}) collective-permute-start(s32[3,128]{1,0:T(4,128)S(1)} %add_add_fusion.1.own), channel_id=1, source_target_pairs={{0,4},{4,0},{8,12},{12,8},{16,20},{20,16},{24,28},{28,24},{32,36},... | collective-permute-start | bytes 4616 | tf_op jit(solution)/shard_map/ppermute | solution.py:72
  25.3 0.8 collective-permute-done.5.sib
  26.7 1.3 stack.87.place
  28.0 1.8 shard_map.114.lists
  30.5 1.0 collective-permute-start.7
  31.5 7.2 %collective-permute-done.8.rest_2_ = bf16[4,272,256]{2,1,0:T(8,128)(2,1)S(1)} collective-permute-done((bf16[4,272,256]{2,1,0:T(8,128)(2,1)S(1)}, bf16[4,272,256]{2,1,0:T(8,128)(2,1)S(1)}, u32[]{:S(2)}, u32[]{:S(2)}) %collective-permute-start.8) | collective-permute-done | bytes 557088 | tf_op jit(solution)/shard_map/ppermute | solution.py:64
  38.7 1.4 collective-permute-done.7.rest_1_
  40.6 1.2 collective-permute-start.9
  41.7 6.9 %collective-permute-done.10.rest_4_ = bf16[4,272,256]{2,1,0:T(8,128)(2,1)S(1)} collective-permute-done((bf16[4,272,256]{2,1,0:T(8,128)(2,1)S(1)}, bf16[4,272,256]{2,1,0:T(8,128)(2,1)S(1)}, u32[]{:S(2)}, u32[]{:S(2)}) %collective-permute-start.10) | collective-permute-done | bytes 557088 | tf_op jit(solution)/shard_map/ppermute | solution.py:64
  48.7 1.5 collective-permute-done.9.rest_3_
  50.6 2.4 %collective-permute-start.12 = (bf16[4,272,256]{2,1,0:T(8,128)(2,1)S(1)}, bf16[4,272,256]{2,1,0:T(8,128)(2,1)S(1)}, u32[]{:S(2)}, u32[]{:S(2)}) collective-permute-start(bf16[4,272,256]{2,1,0:T(8,128)(2,1)S(1)} %collective-permute-done.10.rest_4_), channel_id=1, source_target_pairs={{0,24},{4,228},{8,0},{12,236},{16,8},{20,244},{24,16},{28,252},{32... | collective-permute-start | bytes 1671176 | tf_op jit(solution)/shard_map/ppermute | solution.py:64
  53.0 10.0 %shard_map.115 = (f32[4,128,256]{2,1,0:T(8,128)}, bf16[4,8,16,256]{3,2,1,0:T(8,128)(2,1)}) custom-call(s32[8,256]{1,0:T(8,128)} %shard_map.114.lists, bf16[128,128,128]{2,1,0:T(8,128)(2,1)} %own.9, bf16[128,128,128]{2,1,0:T(8,128)(2,1)} %collective-permute-done.6.sib, bf16[4,272,256]{2,1,0:T(8,128)(2,1)} %copy-done.7, bf16[4,272,256]{2,1,0:T(8,128)(2,1)} %copy-done.17, ...), custom_call_target="tpu_custom_call" | custom-call | flops 805306368 | bytes 6291456 | tf_op jit(solution)/shard_map/pallas_call | solution.py:281
  63.1 1.9 collective-permute-start.13
  65.0 4.6 %collective-permute-start.14 = (bf16[2,272,256]{2,1,0:T(8,128)(2,1)S(1)}, bf16[2,272,256]{2,1,0:T(8,128)(2,1)S(1)}, u32[]{:S(2)}, u32[]{:S(2)}) collective-permute-start(bf16[2,272,256]{2,1,0:T(8,128)(2,1)S(1)} %slice.51), channel_id=1, source_target_pairs={{4,228},{12,236},{20,244},{28,252},{36,4},{44,12},{52,20},{60,28},... | collective-permute-start | bytes 835592 | tf_op jit(solution)/shard_map/ppermute | solution.py:64
  69.6 1.2 convert_reduce_fusion
  70.8 6.1 %shard_map.116 = (f32[4,128,256]{2,1,0:T(8,128)}, bf16[4,8,16,256]{3,2,1,0:T(8,128)(2,1)}) custom-call(s32[8,256]{1,0:T(8,128)} %shard_map.114.lists, bf16[128,128,128]{2,1,0:T(8,128)(2,1)} %own.9, bf16[128,128,128]{2,1,0:T(8,128)(2,1)} %collective-permute-done.6.sib, bf16[4,272,256]{2,1,0:T(8,128)(2,1)} %copy-done.8, bf16[4,272,256]{2,1,0:T(8,128)(2,1)} %copy-done.9, ...), custom_call_target="tpu_custom_call" | custom-call | flops 268435456 | bytes 2097152 | tf_op jit(solution)/shard_map/pallas_call | solution.py:281
  77.7 5.1 %shard_map.117 = (f32[4,128,256]{2,1,0:T(8,128)}, bf16[4,8,16,256]{3,2,1,0:T(8,128)(2,1)}) custom-call(s32[8,256]{1,0:T(8,128)} %shard_map.114.lists, bf16[128,128,128]{2,1,0:T(8,128)(2,1)} %own.9, bf16[128,128,128]{2,1,0:T(8,128)(2,1)} %collective-permute-done.6.sib, bf16[2,272,256]{2,1,0:T(8,128)(2,1)} %copy-done.21, bf16[2,272,256]{2,1,0:T(8,128)(2,1)} %copy-done.22, ...), custom_call_target="tpu_custom_call" | custom-call | flops 268435456 | bytes 2097152 | tf_op jit(solution)/shard_map/pallas_call | solution.py:281
  82.9 1.9 collective-permute-start.16
  84.9 1.0 slice.53
  86.2 1.0 select_bitcast_fusion.1
  87.5 0.7 copy-done.19
  89.1 3.0 %collective-permute-start.18 = (bf16[256,256]{1,0:T(8,128)(2,1)S(1)}, bf16[256,256]{1,0:T(8,128)(2,1)S(1)}, u32[]{:S(2)}, u32[]{:S(2)}) collective-permute-start(bf16[256,256]{1,0:T(8,128)(2,1)S(1)} %convolution_convert_fusion.1), channel_id=1, source_target_pairs={{0,2},{1,3},{2,0},{3,1},{4,6},{5,7},{6,4},{7,5},{8,10},{9,11},{10,... | collective-permute-start | bytes 393224 | tf_op jit(solution)/shard_map/ppermute | solution.py:76
  92.1 0.8 collective-permute-start.19
  92.9 0.7 collective-permute-start.17
  93.8 1.6 collective-permute-done.18
  95.4 3.2 %collective-permute-done.19 = bf16[256,256]{1,0:T(8,128)(2,1)S(1)} collective-permute-done((bf16[256,256]{1,0:T(8,128)(2,1)S(1)}, bf16[256,256]{1,0:T(8,128)(2,1)S(1)}, u32[]{:S(2)}, u32[]{:S(2)}) %collective-permute-start.19) | collective-permute-done | bytes 131104 | tf_op jit(solution)/shard_map/ppermute | solution.py:76
  98.6 0.8 fusion.18
  99.6 1.8 collective-permute-start.22
  101.3 2.6 %collective-permute-start.21 = (bf16[256,256]{1,0:T(8,128)(2,1)S(1)}, bf16[256,256]{1,0:T(8,128)(2,1)S(1)}, u32[]{:S(2)}, u32[]{:S(2)}) collective-permute-start(bf16[256,256]{1,0:T(8,128)(2,1)S(1)} %get-tuple-element.104), channel_id=1, source_target_pairs={{0,2},{1,3},{2,0},{3,1},{4,6},{5,7},{6,4},{7,5},{8,10},{9,11},{10,... | collective-permute-start | bytes 393224 | tf_op jit(solution)/shard_map/ppermute | solution.py:76
  104.0 1.1 collective-permute-start.20
  105.5 4.3 %collective-permute-done.21 = bf16[256,256]{1,0:T(8,128)(2,1)S(1)} collective-permute-done((bf16[256,256]{1,0:T(8,128)(2,1)S(1)}, bf16[256,256]{1,0:T(8,128)(2,1)S(1)}, u32[]{:S(2)}, u32[]{:S(2)}) %collective-permute-start.21) | collective-permute-done | bytes 131104 | tf_op jit(solution)/shard_map/ppermute | solution.py:76
  110.6 1.4 collective-permute-start.23
  112.7 1.3 collective-permute-done.24
  114.0 0.7 pad_maximum_fusion.4
  114.8 0.8 fusion.4.weight_sums
  116.3 5.1 %shard_map.119 = (bf16[1104,256]{1,0:T(8,128)(2,1)}, bf16[1104,256]{1,0:T(8,128)(2,1)}, bf16[1104,256]{1,0:T(8,128)(2,1)}) custom-call(s32[8,256]{1,0:T(8,128)} %shard_map.114.lists, bf16[128,128,128]{2,1,0:T(8,128)(2,1)} %own.9, bf16[128,128,128]{2,1,0:T(8,128)(2,1)} %collective-permute-done.6.sib, bf16[4,128,256]{2,1,0:T(8,128)(2,1)} %bitcast.79, ...), custom_call_target="tpu_custom_call" | custom-call | flops 402653184 | bytes 3145728 | tf_op jit(solution)/shard_map/pallas_call | solution.py:362
  121.4 2.1 %collective-permute-start.25 = (bf16[1104,256]{1,0:T(8,128)(2,1)}, bf16[1104,256]{1,0:T(8,128)(2,1)S(1)}, u32[]{:S(2)}, u32[]{:S(2)}) collective-permute-start(bf16[1104,256]{1,0:T(8,128)(2,1)} %get-tuple-element.74), channel_id=1, source_target_pairs={{4,36},{12,44},{20,52},{28,60},{36,68},{44,76},{52,84},{60,92},{68... | collective-permute-start | bytes 1695752 | tf_op jit(solution)/shard_map/ppermute | solution.py:64
  123.5 13.5 %shard_map.118 = (bf16[1104,256]{1,0:T(8,128)(2,1)}, bf16[1104,256]{1,0:T(8,128)(2,1)}, bf16[1104,256]{1,0:T(8,128)(2,1)}, bf16[1104,256]{1,0:T(8,128)(2,1)}, bf...) custom-call(s32[8,256]{1,0:T(8,128)} %shard_map.114.lists, ...), custom_call_target="tpu_custom_call" | custom-call | flops 1073741824 | bytes 8388608 | tf_op jit(solution)/shard_map/pallas_call | solution.py:362
  137.0 1.2 broadcast_select_fusion
  138.6 1.5 collective-permute-start.26
  140.1 6.9 %collective-permute-done.27.ja2 = bf16[1104,256]{1,0:T(8,128)(2,1)S(1)} collective-permute-done((bf16[1104,256]{1,0:T(8,128)(2,1)S(1)}, bf16[1104,256]{1,0:T(8,128)(2,1)S(1)}, u32[]{:S(2)}, u32[]{:S(2)}) %collective-permute-start.27) | collective-permute-done | bytes 565280 | tf_op jit(solution)/shard_map/ppermute | solution.py:64
  147.0 1.3 collective-permute-done.26.ja1
  148.8 1.5 collective-permute-start.28
  150.4 7.0 %collective-permute-done.29 = bf16[1104,256]{1,0:T(8,128)(2,1)S(1)} collective-permute-done((bf16[1104,256]{1,0:T(8,128)(2,1)S(1)}, bf16[1104,256]{1,0:T(8,128)(2,1)S(1)}, u32[]{:S(2)}, u32[]{:S(2)}) %collective-permute-start.29) | collective-permute-done | bytes 565280 | tf_op jit(solution)/shard_map/ppermute | solution.py:64
  157.4 1.5 collective-permute-done.28.jb1
  159.6 2.5 %collective-permute-start.31 = (bf16[1104,256]{1,0:T(8,128)(2,1)S(1)}, bf16[1104,256]{1,0:T(8,128)(2,1)S(1)}, u32[]{:S(2)}, u32[]{:S(2)}) collective-permute-start(bf16[1104,256]{1,0:T(8,128)(2,1)S(1)} %add_convert_fusion), channel_id=1, source_target_pairs={{0,24},{4,228},{8,0},{12,236},{16,8},{20,244},{24,16},{28,252},{32... | collective-permute-start | bytes 1695752 | tf_op jit(solution)/shard_map/ppermute | solution.py:64
  162.1 1.0 shard_map.120
  163.1 6.1 %collective-permute-done.30.jc1 = bf16[1104,256]{1,0:T(8,128)(2,1)S(1)} collective-permute-done((bf16[1104,256]{1,0:T(8,128)(2,1)S(1)}, bf16[1104,256]{1,0:T(8,128)(2,1)S(1)}, u32[]{:S(2)}, u32[]{:S(2)}) %collective-permute-start.30) | collective-permute-done | bytes 565280 | tf_op jit(solution)/shard_map/ppermute | solution.py:64
  169.8 0.7 collective-permute-start.33
  170.9 2.7 %collective-permute-start.35 = (bf16[288,256]{1,0:T(8,128)(2,1)S(1)}, bf16[288,256]{1,0:T(8,128)(2,1)S(1)}, u32[]{:S(2)}, u32[]{:S(2)}) collective-permute-start(bf16[288,256]{1,0:T(8,128)(2,1)S(1)} %get-tuple-element.95), channel_id=1, source_target_pairs={{0,224},{4,28},{8,232},{12,4},{16,240},{20,12},{24,248},{28,20},{3... | collective-permute-start | bytes 442376 | tf_op jit(solution)/shard_map/ppermute | solution.py:64
  173.6 2.5 %collective-permute-done.34.r1 = bf16[288,256]{1,0:T(8,128)(2,1)S(1)} collective-permute-done((bf16[288,256]{1,0:T(8,128)(2,1)S(1)}, bf16[288,256]{1,0:T(8,128)(2,1)S(1)}, u32[]{:S(2)}, u32[]{:S(2)}) %collective-permute-start.34) | collective-permute-done | bytes 147488 | tf_op jit(solution)/shard_map/ppermute | solution.py:64
  176.1 1.1 collective-permute-done.35.r2
  177.3 2.1 %collective-permute-done.36.r3 = bf16[288,256]{1,0:T(8,128)(2,1)S(1)} collective-permute-done((bf16[288,256]{1,0:T(8,128)(2,1)S(1)}, bf16[288,256]{1,0:T(8,128)(2,1)S(1)}, u32[]{:S(2)}, u32[]{:S(2)}) %collective-permute-start.36) | collective-permute-done | bytes 147488 | tf_op jit(solution)/shard_map/ppermute | solution.py:64
  179.4 1.4 shard_map.122
  180.8 1.3 collective-permute-start.37
  182.1 17.9 %collective-permute-done.37 = f32[1,256]{1,0:T(1,128)S(1)} collective-permute-done((f32[1,256]{1,0:T(1,128)S(1)}, f32[1,256]{1,0:T(1,128)S(1)}, u32[]{:S(2)}, u32[]{:S(2)}) %collective-permute-start.37) | collective-permute-done | bytes 1056 | tf_op jit(solution)/shard_map/ppermute | solution.py:624
  (135 shorter events, 11.4 us)
Async XLA Ops:
  0.6 13.1 %copy-start.26 = (s32[128]{0:T(128)S(1)}, s32[128]{0:T(128)}, u32[]{:S(2)}) copy-start(s32[128]{0:T(128)} %param.12) | copy-start | bytes 1540
  0.6 13.1 %copy-start.28 = (s32[128]{0:T(128)S(1)}, s32[128]{0:T(128)}, u32[]{:S(2)}) copy-start(s32[128]{0:T(128)} %param.13) | copy-start | bytes 1540
  0.7 29.3 %collective-permute-start.6 = (bf16[128,128,128]{2,1,0:T(8,128)(2,1)}, bf16[128,128,128]{2,1,0:T(8,128)(2,1)}, u32[]{:S(2)}, u32[]{:S(2)}) collective-permute-start(bf16[128,128,128]{2,1,0:T(8,128)(2,1)} %own.9), channel_id=1, source_target_pairs={{0,4},{4,0},{8,12},{12,8},{16,20},{20,16},{24,28},{28,24},{32,36},... | collective-permute-start | bytes 12582920 | tf_op jit(solution)/shard_map/ppermute | solution.py:72
  4.9 4.3 %collective-permute-start.1 = (bf16[272,256]{1,0:T(8,128)(2,1)S(1)}, bf16[272,256]{1,0:T(8,128)(2,1)S(1)}, u32[]{:S(2)}, u32[]{:S(2)}) collective-permute-start(bf16[272,256]{1,0:T(8,128)(2,1)S(1)} %get-tuple-element.116), channel_id=1, source_target_pairs={{0,224},{4,28},{8,232},{12,4},{16,240},{20,12},{24,248},{28,20},{3... | collective-permute-start | bytes 417800 | tf_op jit(solution)/shard_map/ppermute | solution.py:64
  5.7 6.6 %collective-permute-start = (bf16[272,256]{1,0:T(8,128)(2,1)S(1)}, bf16[272,256]{1,0:T(8,128)(2,1)S(1)}, u32[]{:S(2)}, u32[]{:S(2)}) collective-permute-start(bf16[272,256]{1,0:T(8,128)(2,1)S(1)} %get-tuple-element.116), channel_id=1, source_target_pairs={{0,32},{4,12},{8,40},{12,20},{16,48},{20,28},{24,56},{28,4},{32,64... | collective-permute-start | bytes 417800 | tf_op jit(solution)/shard_map/ppermute | solution.py:64
  6.5 23.4 %collective-permute-start.2 = (bf16[272,256]{1,0:T(8,128)(2,1)S(1)}, bf16[272,256]{1,0:T(8,128)(2,1)S(1)}, u32[]{:S(2)}, u32[]{:S(2)}) collective-permute-start(bf16[272,256]{1,0:T(8,128)(2,1)S(1)} %get-tuple-element.116), channel_id=1, source_target_pairs={{0,128},{4,20},{8,136},{12,28},{16,144},{20,4},{24,152},{28,12},{3... | collective-permute-start | bytes 417800 | tf_op jit(solution)/shard_map/ppermute | solution.py:64
  12.4 17.5 %collective-permute-start.4 = (bf16[2,272,256]{2,1,0:T(8,128)(2,1)S(1)}, bf16[2,272,256]{2,1,0:T(8,128)(2,1)S(1)}, u32[]{:S(2)}, u32[]{:S(2)}) collective-permute-start(bf16[2,272,256]{2,1,0:T(8,128)(2,1)S(1)} %get-tuple-element.113), channel_id=1, source_target_pairs={{0,192},{8,200},{16,208},{24,216},{32,224},{40,232},{48,240},{56,2... | collective-permute-start | bytes 835592 | tf_op jit(solution)/shard_map/ppermute | solution.py:64
  13.1 16.8 %collective-permute-start.3 = (bf16[2,272,256]{2,1,0:T(8,128)(2,1)S(1)}, bf16[2,272,256]{2,1,0:T(8,128)(2,1)S(1)}, u32[]{:S(2)}, u32[]{:S(2)}) collective-permute-start(bf16[2,272,256]{2,1,0:T(8,128)(2,1)S(1)} %get-tuple-element.114), channel_id=1, source_target_pairs={{0,64},{8,72},{16,80},{24,88},{32,96},{40,104},{48,112},{56,120},{... | collective-permute-start | bytes 835592 | tf_op jit(solution)/shard_map/ppermute | solution.py:64
  13.9 14.1 %copy-start.24 = (s32[3,128]{1,0:T(4,128)}, s32[3,128]{1,0:T(4,128)S(1)}, u32[]{:S(2)}) copy-start(s32[3,128]{1,0:T(4,128)S(1)} %add_add_fusion.1.own) | copy-start | bytes 4612
  13.9 12.3 %collective-permute-start.5 = (s32[3,128]{1,0:T(4,128)S(1)}, s32[3,128]{1,0:T(4,128)S(1)}, u32[]{:S(2)}, u32[]{:S(2)}) collective-permute-start(s32[3,128]{1,0:T(4,128)S(1)} %add_add_fusion.1.own), channel_id=1, source_target_pairs={{0,4},{4,0},{8,12},{12,8},{16,20},{20,16},{24,28},{28,24},{32,36},... | collective-permute-start | bytes 4616 | tf_op jit(solution)/shard_map/ppermute | solution.py:72
  26.1 1.9 copy-start.25
  29.9 10.3 %copy-start.7 = (bf16[4,272,256]{2,1,0:T(8,128)(2,1)}, bf16[4,272,256]{2,1,0:T(8,128)(2,1)S(1)}, u32[]{:S(2)}) copy-start(bf16[4,272,256]{2,1,0:T(8,128)(2,1)S(1)} %pad_maximum_fusion.1.rest_0_) | copy-start | bytes 1671172
  29.9 8.8 %collective-permute-start.8 = (bf16[4,272,256]{2,1,0:T(8,128)(2,1)S(1)}, bf16[4,272,256]{2,1,0:T(8,128)(2,1)S(1)}, u32[]{:S(2)}, u32[]{:S(2)}) collective-permute-start(bf16[4,272,256]{2,1,0:T(8,128)(2,1)S(1)} %pad_maximum_fusion.1.rest_0_), channel_id=1, source_target_pairs={{0,24},{4,228},{8,0},{12,236},{16,8},{20,244},{24,16},{28,252},{32... | collective-permute-start | bytes 1671176 | tf_op jit(solution)/shard_map/ppermute | solution.py:64
  30.5 9.6 %collective-permute-start.7 = (bf16[4,272,256]{2,1,0:T(8,128)(2,1)S(1)}, bf16[4,272,256]{2,1,0:T(8,128)(2,1)S(1)}, u32[]{:S(2)}, u32[]{:S(2)}) collective-permute-start(bf16[4,272,256]{2,1,0:T(8,128)(2,1)S(1)} %pad_maximum_fusion.1.rest_0_), channel_id=1, source_target_pairs={{0,8},{4,36},{8,16},{12,44},{16,24},{20,52},{24,0},{28,60},{32,40}... | collective-permute-start | bytes 1671176 | tf_op jit(solution)/shard_map/ppermute | solution.py:64
  31.5 18.7 %copy-start.4 = (bf16[4,272,256]{2,1,0:T(8,128)(2,1)}, bf16[4,272,256]{2,1,0:T(8,128)(2,1)S(1)}, u32[]{:S(2)}) copy-start(bf16[4,272,256]{2,1,0:T(8,128)(2,1)S(1)} %constant_dynamic-update-slice_fusion.rest_5_) | copy-start | bytes 1671172
  38.7 11.5 %copy-start.5 = (bf16[4,272,256]{2,1,0:T(8,128)(2,1)}, bf16[4,272,256]{2,1,0:T(8,128)(2,1)S(1)}, u32[]{:S(2)}) copy-start(bf16[4,272,256]{2,1,0:T(8,128)(2,1)S(1)} %collective-permute-done.8.rest_2_) | copy-start | bytes 1671172
  40.1 10.1 %copy-start.17 = (bf16[4,272,256]{2,1,0:T(8,128)(2,1)}, bf16[4,272,256]{2,1,0:T(8,128)(2,1)S(1)}, u32[]{:S(2)}) copy-start(bf16[4,272,256]{2,1,0:T(8,128)(2,1)S(1)} %collective-permute-done.7.rest_1_) | copy-start | bytes 1671172
  40.2 8.5 %collective-permute-start.10 = (bf16[4,272,256]{2,1,0:T(8,128)(2,1)S(1)}, bf16[4,272,256]{2,1,0:T(8,128)(2,1)S(1)}, u32[]{:S(2)}, u32[]{:S(2)}) collective-permute-start(bf16[4,272,256]{2,1,0:T(8,128)(2,1)S(1)} %broadcast_select_fusion.2), channel_id=1, source_target_pairs={{0,24},{4,228},{8,0},{12,236},{16,8},{20,244},{24,16},{28,252},{32... | collective-permute-start | bytes 1671176 | tf_op jit(solution)/shard_map/ppermute | solution.py:64
  40.6 9.6 %collective-permute-start.9 = (bf16[4,272,256]{2,1,0:T(8,128)(2,1)S(1)}, bf16[4,272,256]{2,1,0:T(8,128)(2,1)S(1)}, u32[]{:S(2)}, u32[]{:S(2)}) collective-permute-start(bf16[4,272,256]{2,1,0:T(8,128)(2,1)S(1)} %collective-permute-done.7.rest_1_), channel_id=1, source_target_pairs={{0,8},{4,36},{8,16},{12,44},{16,24},{20,52},{24,0},{28,60},{32,40}... | collective-permute-start | bytes 1671176 | tf_op jit(solution)/shard_map/ppermute | solution.py:64
  48.7 4.4 %copy-start.18 = (bf16[4,272,256]{2,1,0:T(8,128)(2,1)}, bf16[4,272,256]{2,1,0:T(8,128)(2,1)S(1)}, u32[]{:S(2)}) copy-start(bf16[4,272,256]{2,1,0:T(8,128)(2,1)S(1)} %collective-permute-done.10.rest_4_) | copy-start | bytes 1671172
  50.2 2.9 %copy-start.6 = (bf16[4,272,256]{2,1,0:T(8,128)(2,1)}, bf16[4,272,256]{2,1,0:T(8,128)(2,1)S(1)}, u32[]{:S(2)}) copy-start(bf16[4,272,256]{2,1,0:T(8,128)(2,1)S(1)} %collective-permute-done.9.rest_3_) | copy-start | bytes 1671172
  50.3 12.8 %collective-permute-start.11 = (bf16[4,272,256]{2,1,0:T(8,128)(2,1)S(1)}, bf16[4,272,256]{2,1,0:T(8,128)(2,1)S(1)}, u32[]{:S(2)}, u32[]{:S(2)}) collective-permute-start(bf16[4,272,256]{2,1,0:T(8,128)(2,1)S(1)} %broadcast_select_fusion.1), channel_id=1, source_target_pairs={{0,8},{4,36},{8,16},{12,44},{16,24},{20,52},{24,0},{28,60},{32,40}... | collective-permute-start | bytes 1671176 | tf_op jit(solution)/shard_map/ppermute | solution.py:64
  50.6 12.5 %collective-permute-start.12 = (bf16[4,272,256]{2,1,0:T(8,128)(2,1)S(1)}, bf16[4,272,256]{2,1,0:T(8,128)(2,1)S(1)}, u32[]{:S(2)}, u32[]{:S(2)}) collective-permute-start(bf16[4,272,256]{2,1,0:T(8,128)(2,1)S(1)} %collective-permute-done.10.rest_4_), channel_id=1, source_target_pairs={{0,24},{4,228},{8,0},{12,236},{16,8},{20,244},{24,16},{28,252},{32... | collective-permute-start | bytes 1671176 | tf_op jit(solution)/shard_map/ppermute | solution.py:64
  53.0 16.6 %copy-start.3 = (bf16[128,128,128]{2,1,0:T(8,128)(2,1)S(1)}, bf16[128,128,128]{2,1,0:T(8,128)(2,1)}, u32[]{:S(2)}) copy-start(bf16[128,128,128]{2,1,0:T(8,128)(2,1)} %own.9) | copy-start | bytes 12582916
  63.0 7.8 %copy-start.8 = (bf16[4,272,256]{2,1,0:T(8,128)(2,1)}, bf16[4,272,256]{2,1,0:T(8,128)(2,1)S(1)}, u32[]{:S(2)}) copy-start(bf16[4,272,256]{2,1,0:T(8,128)(2,1)S(1)} %collective-permute-done.11.rest_0_) | copy-start | bytes 1671172
  63.1 7.8 %copy-start.9 = (bf16[4,272,256]{2,1,0:T(8,128)(2,1)}, bf16[4,272,256]{2,1,0:T(8,128)(2,1)S(1)}, u32[]{:S(2)}) copy-start(bf16[4,272,256]{2,1,0:T(8,128)(2,1)S(1)} %collective-permute-done.12.rest_1_) | copy-start | bytes 1671172
  63.1 13.8 %collective-permute-start.13 = (bf16[2,272,256]{2,1,0:T(8,128)(2,1)S(1)}, bf16[2,272,256]{2,1,0:T(8,128)(2,1)S(1)}, u32[]{:S(2)}, u32[]{:S(2)}) collective-permute-start(bf16[2,272,256]{2,1,0:T(8,128)(2,1)S(1)} %slice.50), channel_id=1, source_target_pairs={{4,36},{12,44},{20,52},{28,60},{36,68},{44,76},{52,84},{60,92},{68... | collective-permute-start | bytes 835592 | tf_op jit(solution)/shard_map/ppermute | solution.py:64
  65.0 11.9 %collective-permute-start.14 = (bf16[2,272,256]{2,1,0:T(8,128)(2,1)S(1)}, bf16[2,272,256]{2,1,0:T(8,128)(2,1)S(1)}, u32[]{:S(2)}, u32[]{:S(2)}) collective-permute-start(bf16[2,272,256]{2,1,0:T(8,128)(2,1)S(1)} %slice.51), channel_id=1, source_target_pairs={{4,228},{12,236},{20,244},{28,252},{36,4},{44,12},{52,20},{60,28},... | collective-permute-start | bytes 835592 | tf_op jit(solution)/shard_map/ppermute | solution.py:64
  82.9 3.3 %collective-permute-start.16 = (bf16[4,8,16,256]{3,2,1,0:T(8,128)(2,1)}, bf16[4,8,16,256]{3,2,1,0:T(8,128)(2,1)S(1)}, u32[]{:S(2)}, u32[]{:S(2)}) collective-permute-start(bf16[4,8,16,256]{3,2,1,0:T(8,128)(2,1)} %get-tuple-element.70), channel_id=1, source_target_pairs={{0,4},{4,0},{8,12},{12,8},{16,20},{20,16},{24,28},{28,24},{32,36},... | collective-permute-start | bytes 786440 | tf_op jit(solution)/shard_map/ppermute | solution.py:72
  85.9 1.6 collective-permute-start.15
  87.2 1.1 copy-start.20
  88.3 10.3 %copy-start.23 = (bf16[256,256]{1,0:T(8,128)(2,1)S(1)}, bf16[256,256]{1,0:T(8,128)(2,1)}, u32[]{:S(2)}) copy-start(bf16[256,256]{1,0:T(8,128)(2,1)} %param.15) | copy-start | bytes 393220
  88.3 10.3 %copy-start.27 = (f32[256]{0:T(256)S(1)}, f32[256]{0:T(256)}, u32[]{:S(2)}) copy-start(f32[256]{0:T(256)} %param.10) | copy-start | bytes 3076
  89.1 6.3 %collective-permute-start.18 = (bf16[256,256]{1,0:T(8,128)(2,1)S(1)}, bf16[256,256]{1,0:T(8,128)(2,1)S(1)}, u32[]{:S(2)}, u32[]{:S(2)}) collective-permute-start(bf16[256,256]{1,0:T(8,128)(2,1)S(1)} %convolution_convert_fusion.1), channel_id=1, source_target_pairs={{0,2},{1,3},{2,0},{3,1},{4,6},{5,7},{6,4},{7,5},{8,10},{9,11},{10,... | collective-permute-start | bytes 393224 | tf_op jit(solution)/shard_map/ppermute | solution.py:76
  92.1 6.5 %collective-permute-start.19 = (bf16[256,256]{1,0:T(8,128)(2,1)S(1)}, bf16[256,256]{1,0:T(8,128)(2,1)S(1)}, u32[]{:S(2)}, u32[]{:S(2)}) collective-permute-start(bf16[256,256]{1,0:T(8,128)(2,1)S(1)} %convolution_convert_fusion), channel_id=1, source_target_pairs={{0,3},{1,0},{2,1},{3,2},{4,7},{5,4},{6,5},{7,6},{8,11},{9,8},{10,9... | collective-permute-start | bytes 393224 | tf_op jit(solution)/shard_map/ppermute | solution.py:76
  92.9 5.7 %collective-permute-start.17 = (bf16[256,256]{1,0:T(8,128)(2,1)S(1)}, bf16[256,256]{1,0:T(8,128)(2,1)S(1)}, u32[]{:S(2)}, u32[]{:S(2)}) collective-permute-start(bf16[256,256]{1,0:T(8,128)(2,1)S(1)} %convolution_convert_fusion.2), channel_id=1, source_target_pairs={{0,1},{1,2},{2,3},{3,0},{4,5},{5,6},{6,7},{7,4},{8,9},{9,10},{10,1... | collective-permute-start | bytes 393224 | tf_op jit(solution)/shard_map/ppermute | solution.py:76
  99.6 5.7 %collective-permute-start.22 = (bf16[256,256]{1,0:T(8,128)(2,1)S(1)}, bf16[256,256]{1,0:T(8,128)(2,1)S(1)}, u32[]{:S(2)}, u32[]{:S(2)}) collective-permute-start(bf16[256,256]{1,0:T(8,128)(2,1)S(1)} %get-tuple-element.104), channel_id=1, source_target_pairs={{0,1},{1,2},{2,3},{3,0},{4,5},{5,6},{6,7},{7,4},{8,9},{9,10},{10,1... | collective-permute-start | bytes 393224 | tf_op jit(solution)/shard_map/ppermute | solution.py:76
  101.3 8.5 %collective-permute-start.21 = (bf16[256,256]{1,0:T(8,128)(2,1)S(1)}, bf16[256,256]{1,0:T(8,128)(2,1)S(1)}, u32[]{:S(2)}, u32[]{:S(2)}) collective-permute-start(bf16[256,256]{1,0:T(8,128)(2,1)S(1)} %get-tuple-element.104), channel_id=1, source_target_pairs={{0,2},{1,3},{2,0},{3,1},{4,6},{5,7},{6,4},{7,5},{8,10},{9,11},{10,... | collective-permute-start | bytes 393224 | tf_op jit(solution)/shard_map/ppermute | solution.py:76
  104.0 6.1 %collective-permute-start.20 = (bf16[256,256]{1,0:T(8,128)(2,1)S(1)}, bf16[256,256]{1,0:T(8,128)(2,1)S(1)}, u32[]{:S(2)}, u32[]{:S(2)}) collective-permute-start(bf16[256,256]{1,0:T(8,128)(2,1)S(1)} %get-tuple-element.104), channel_id=1, source_target_pairs={{0,3},{1,0},{2,1},{3,2},{4,7},{5,4},{6,5},{7,6},{8,11},{9,8},{10,9... | collective-permute-start | bytes 393224 | tf_op jit(solution)/shard_map/ppermute | solution.py:76
  110.6 4.2 %collective-permute-start.23 = (f32[520,256]{1,0:T(8,128)S(1)}, f32[520,256]{1,0:T(8,128)S(1)}, u32[]{:S(2)}, u32[]{:S(2)}) collective-permute-start(f32[520,256]{1,0:T(8,128)S(1)} %select_maximum_fusion), channel_id=1, source_target_pairs={{0,4},{4,0},{8,12},{12,8},{16,20},{20,16},{24,28},{28,24},{32,36},... | collective-permute-start | bytes 1597448 | tf_op jit(solution)/shard_map/ppermute | solution.py:72
  112.6 1.4 collective-permute-start.24
  121.4 15.6 %copy-start.16 = (bf16[1104,256]{1,0:T(8,128)(2,1)S(1)}, bf16[1104,256]{1,0:T(8,128)(2,1)}, u32[]{:S(2)}) copy-start(bf16[1104,256]{1,0:T(8,128)(2,1)} %get-tuple-element.75) | copy-start | bytes 1695748
  121.4 16.9 %collective-permute-start.25 = (bf16[1104,256]{1,0:T(8,128)(2,1)}, bf16[1104,256]{1,0:T(8,128)(2,1)S(1)}, u32[]{:S(2)}, u32[]{:S(2)}) collective-permute-start(bf16[1104,256]{1,0:T(8,128)(2,1)} %get-tuple-element.74), channel_id=1, source_target_pairs={{4,36},{12,44},{20,52},{28,60},{36,68},{44,76},{52,84},{60,92},{68... | collective-permute-start | bytes 1695752 | tf_op jit(solution)/shard_map/ppermute | solution.py:64
  136.9 1.4 copy-start.14
  136.9 1.4 copy-start.15
  138.2 8.8 %collective-permute-start.27 = (bf16[1104,256]{1,0:T(8,128)(2,1)S(1)}, bf16[1104,256]{1,0:T(8,128)(2,1)S(1)}, u32[]{:S(2)}, u32[]{:S(2)}) collective-permute-start(bf16[1104,256]{1,0:T(8,128)(2,1)S(1)} %broadcast_select_fusion), channel_id=1, source_target_pairs={{0,24},{4,228},{8,0},{12,236},{16,8},{20,244},{24,16},{28,252},{32... | collective-permute-start | bytes 1695752 | tf_op jit(solution)/shard_map/ppermute | solution.py:64
  138.3 10.0 %copy-start.13 = (bf16[1104,256]{1,0:T(8,128)(2,1)S(1)}, bf16[1104,256]{1,0:T(8,128)(2,1)}, u32[]{:S(2)}) copy-start(bf16[1104,256]{1,0:T(8,128)(2,1)} %get-tuple-element.80) | copy-start | bytes 1695748
  138.6 10.1 %copy-start.12 = (bf16[1104,256]{1,0:T(8,128)(2,1)S(1)}, bf16[1104,256]{1,0:T(8,128)(2,1)}, u32[]{:S(2)}) copy-start(bf16[1104,256]{1,0:T(8,128)(2,1)} %get-tuple-element.79) | copy-start | bytes 1695748
  138.6 9.8 %collective-permute-start.26 = (bf16[1104,256]{1,0:T(8,128)(2,1)S(1)}, bf16[1104,256]{1,0:T(8,128)(2,1)S(1)}, u32[]{:S(2)}, u32[]{:S(2)}) collective-permute-start(bf16[1104,256]{1,0:T(8,128)(2,1)S(1)} %fusion.3), channel_id=1, source_target_pairs={{0,8},{4,36},{8,16},{12,44},{16,24},{20,52},{24,0},{28,60},{32,40}... | collective-permute-start | bytes 1695752 | tf_op jit(solution)/shard_map/ppermute | solution.py:64
  148.5 10.3 %copy-start.11 = (bf16[1104,256]{1,0:T(8,128)(2,1)S(1)}, bf16[1104,256]{1,0:T(8,128)(2,1)}, u32[]{:S(2)}) copy-start(bf16[1104,256]{1,0:T(8,128)(2,1)} %get-tuple-element.84) | copy-start | bytes 1695748
  148.6 8.8 %collective-permute-start.29 = (bf16[1104,256]{1,0:T(8,128)(2,1)S(1)}, bf16[1104,256]{1,0:T(8,128)(2,1)S(1)}, u32[]{:S(2)}, u32[]{:S(2)}) collective-permute-start(bf16[1104,256]{1,0:T(8,128)(2,1)S(1)} %add_convert_fusion.2), channel_id=1, source_target_pairs={{0,24},{4,228},{8,0},{12,236},{16,8},{20,244},{24,16},{28,252},{32... | collective-permute-start | bytes 1695752 | tf_op jit(solution)/shard_map/ppermute | solution.py:64
  148.8 10.6 %copy-start.10 = (bf16[1104,256]{1,0:T(8,128)(2,1)S(1)}, bf16[1104,256]{1,0:T(8,128)(2,1)}, u32[]{:S(2)}) copy-start(bf16[1104,256]{1,0:T(8,128)(2,1)} %get-tuple-element.85) | copy-start | bytes 1695748
  148.8 10.1 %collective-permute-start.28 = (bf16[1104,256]{1,0:T(8,128)(2,1)S(1)}, bf16[1104,256]{1,0:T(8,128)(2,1)S(1)}, u32[]{:S(2)}, u32[]{:S(2)}) collective-permute-start(bf16[1104,256]{1,0:T(8,128)(2,1)S(1)} %add_convert_fusion.3), channel_id=1, source_target_pairs={{0,8},{4,36},{8,16},{12,44},{16,24},{20,52},{24,0},{28,60},{32,40}... | collective-permute-start | bytes 1695752 | tf_op jit(solution)/shard_map/ppermute | solution.py:64
  159.1 3.0 %copy-start.1 = (bf16[1104,256]{1,0:T(8,128)(2,1)S(1)}, bf16[1104,256]{1,0:T(8,128)(2,1)}, u32[]{:S(2)}) copy-start(bf16[1104,256]{1,0:T(8,128)(2,1)} %get-tuple-element.71.h0) | copy-start | bytes 1695748
  159.1 3.0 %copy-start.2 = (s32[8,256]{1,0:T(8,128)S(1)}, s32[8,256]{1,0:T(8,128)}, u32[]{:S(2)}) copy-start(s32[8,256]{1,0:T(8,128)} %shard_map.114.lists) | copy-start | bytes 24580
  159.1 10.1 %collective-permute-start.30 = (bf16[1104,256]{1,0:T(8,128)(2,1)S(1)}, bf16[1104,256]{1,0:T(8,128)(2,1)S(1)}, u32[]{:S(2)}, u32[]{:S(2)}) collective-permute-start(bf16[1104,256]{1,0:T(8,128)(2,1)S(1)} %add_convert_fusion.1), channel_id=1, source_target_pairs={{0,8},{4,36},{8,16},{12,44},{16,24},{20,52},{24,0},{28,60},{32,40}... | collective-permute-start | bytes 1695752 | tf_op jit(solution)/shard_map/ppermute | solution.py:64
  159.6 9.6 %collective-permute-start.31 = (bf16[1104,256]{1,0:T(8,128)(2,1)S(1)}, bf16[1104,256]{1,0:T(8,128)(2,1)S(1)}, u32[]{:S(2)}, u32[]{:S(2)}) collective-permute-start(bf16[1104,256]{1,0:T(8,128)(2,1)S(1)} %add_convert_fusion), channel_id=1, source_target_pairs={{0,24},{4,228},{8,0},{12,236},{16,8},{20,244},{24,16},{28,252},{32... | collective-permute-start | bytes 1695752 | tf_op jit(solution)/shard_map/ppermute | solution.py:64
  162.1 8.4 %copy-start = (bf16[1104,256]{1,0:T(8,128)(2,1)S(1)}, bf16[1104,256]{1,0:T(8,128)(2,1)}, u32[]{:S(2)}) copy-start(bf16[1104,256]{1,0:T(8,128)(2,1)} %get-tuple-element.83.h1) | copy-start | bytes 1695748
  169.2 1.4 collective-permute-start.32
  169.8 0.7 collective-permute-start.33
  170.8 5.3 %collective-permute-start.34 = (bf16[288,256]{1,0:T(8,128)(2,1)S(1)}, bf16[288,256]{1,0:T(8,128)(2,1)S(1)}, u32[]{:S(2)}, u32[]{:S(2)}) collective-permute-start(bf16[288,256]{1,0:T(8,128)(2,1)S(1)} %get-tuple-element.94), channel_id=1, source_target_pairs={{0,32},{4,12},{8,40},{12,20},{16,48},{20,28},{24,56},{28,4},{32,64... | collective-permute-start | bytes 442376 | tf_op jit(solution)/shard_map/ppermute | solution.py:64
  170.9 6.3 %collective-permute-start.35 = (bf16[288,256]{1,0:T(8,128)(2,1)S(1)}, bf16[288,256]{1,0:T(8,128)(2,1)S(1)}, u32[]{:S(2)}, u32[]{:S(2)}) collective-permute-start(bf16[288,256]{1,0:T(8,128)(2,1)S(1)} %get-tuple-element.95), channel_id=1, source_target_pairs={{0,224},{4,28},{8,232},{12,4},{16,240},{20,12},{24,248},{28,20},{3... | collective-permute-start | bytes 442376 | tf_op jit(solution)/shard_map/ppermute | solution.py:64
  173.6 5.8 %collective-permute-start.36 = (bf16[288,256]{1,0:T(8,128)(2,1)S(1)}, bf16[288,256]{1,0:T(8,128)(2,1)S(1)}, u32[]{:S(2)}, u32[]{:S(2)}) collective-permute-start(bf16[288,256]{1,0:T(8,128)(2,1)S(1)} %get-tuple-element.96), channel_id=1, source_target_pairs={{0,128},{4,20},{8,136},{12,28},{16,144},{20,4},{24,152},{28,12},{3... | collective-permute-start | bytes 442376 | tf_op jit(solution)/shard_map/ppermute | solution.py:64
  180.8 19.2 %collective-permute-start.37 = (f32[1,256]{1,0:T(1,128)S(1)}, f32[1,256]{1,0:T(1,128)S(1)}, u32[]{:S(2)}, u32[]{:S(2)}) collective-permute-start(f32[1,256]{1,0:T(1,128)S(1)} %get-tuple-element.99), channel_id=1, source_target_pairs={{0,4},{8,12},{16,20},{24,28},{32,36},{40,44},{48,52},{56,60},{64,6... | collective-permute-start | bytes 3080 | tf_op jit(solution)/shard_map/ppermute | solution.py:624
  (3 other events, 2.5 us)

commit v5 on v4

--- a/solution.py
+++ b/solution.py
@@ -23,7 +23,8 @@
 MIB = 1 << 20
 VMEM = 54 * MIB
 
-LOW, HIGH, ACROSS = (0, 1, 7, 4), (2, 3, 6, 5), (0, 1, 3, 2)
+LOW, HIGH, ACROSS = (0, 1, 7, 4), (3, 5, 2, 6), (0, 1, 3, 2)
+HIGH_STEPS = (3, -3, 2, -2)
 GATHER_0 = tuple(
     tuple(k * NZ + j for j in group)
     for k, group in ((0, LOW), (1, LOW), (3, LOW), (2, LOW), (3, HIGH), (1, HIGH), (2, HIGH), (0, HIGH))
@@ -64,7 +65,7 @@
     return lax.ppermute(value, "dom", pairs)
 
 
-Z_UP, Z_DOWN, Z_UP_2, Z_DOWN_2, Z_FOUR = (1, 0), (-1, 0), (2, 0), (-2, 0), (4, 0)
+Z_UP, Z_DOWN, Z_FOUR = (1, 0), (-1, 0), (4, 0)
 X_UP, X_DOWN, X_TWO = (0, 1), (0, -1), (0, 2)
 
 
@@ -231,8 +232,8 @@
     chosen = FORWARD_CHUNKS[call]
     chunks, rest = rest[: len(chosen)], rest[len(chosen) :]
     if call:
-        sums_before, weight_before, *rest = rest
-    sums, weight_out, blocks, held, sem, tile_sem = rest
+        own_before, sib_before, weight_before, *rest = rest
+    own_sums, sib_sums, weight_out, blocks, held, sem, tile_sem = rest
     core, x, z, y = place_of(lists)
     tiles = Tiles(lists, 0, call, call == 0, own, sib, held, tile_sem)
     tiles.start()
@@ -259,7 +260,11 @@
                 rights.append(blocks[spot >> 1, pl.ds(first, BLK), :])
             return total + jnp.dot(left, jnp.concatenate(rights, axis=0), preferred_element_type=F32)
 
-        sums[row] = lax.fori_loop(0, steps, step, sums_before[row] if call else jnp.zeros((BLK, WIDTH), F32))
+        sums, at = (own_sums, row) if row < 2 else (sib_sums, row - 2)
+        before = jnp.zeros((BLK, WIDTH), F32)
+        if call:
+            before = own_before[at] if row < 2 else sib_before[at]
+        sums[at] = lax.fori_loop(0, steps, step, before)
     if call:
         weight_out[...] = weight_before[...]
     for condition, spot in arrived:
@@ -281,11 +286,12 @@
     return pl.pallas_call(
         functools.partial(forward_kernel, call),
         out_shape=(
-            jax.ShapeDtypeStruct((4, BLK, WIDTH), F32),
+            jax.ShapeDtypeStruct((2, BLK, WIDTH), F32),
+            jax.ShapeDtypeStruct((2, BLK, WIDTH), F32),
             jax.ShapeDtypeStruct((NY, 2 * NX, W_ROWS, WIDTH), BF16),
         ),
         in_specs=[smem()] + [anywhere()] * (2 + len(chosen)) + [vmem()] * len(before),
-        out_specs=(vmem(),) * 2,
+        out_specs=(vmem(),) * 3,
         scratch_shapes=[
             pltpu.VMEM((NX * NZ, ROWS, WIDTH), BF16),
             pltpu.VMEM((2 * SLOTS + 1, BLK, BLK), BF16),
@@ -376,20 +382,20 @@
     )(lists, own, sib, scaled, weight_sums, bias_rows)
 
 
-def gather(block, core, early, call):
+def gather(block, core, lists, other_tiles, call):
     p1 = shift(block, Z_UP, X_UP)
     p2 = shift(block, Z_DOWN, X_DOWN)
     p3 = shift(block, Z_FOUR, X_TWO)
-    pa = shift(jnp.stack([block, p1]), Z_UP_2)
-    pb = shift(jnp.stack([block, p2]), Z_DOWN_2)
-    low, pa, pb, *early = lax.optimization_barrier((jnp.stack([block, p1, p2, p3]), pa, pb, *early))
+    far = [shift(block, (dz, 0)) for dz in HIGH_STEPS]
+    low, high = jnp.stack([block, p1, p2, p3]), jnp.stack(far)
+    low, high, other_tiles = lax.optimization_barrier((low, high, other_tiles))
     c1 = shift(low, X_UP, Z_UP)
     c2 = shift(low, X_DOWN, Z_DOWN)
-    high = jnp.concatenate([pa, pb], axis=0)
     c1, c2 = lax.optimization_barrier((c1, c2))
     c3 = shift(c1, X_UP, Z_UP)
     c4 = shift(jnp.where(core == 0, high, c2), X_DOWN, Z_DOWN)
-    c3, c4 = lax.optimization_barrier((c3, c4))
+    c3, c4, lists = lax.optimization_barrier((c3, c4, lists))
+    early = lists, other_tiles
     chunks = [low, c1, c2, c3, c4, None, None, high]
     sums = call(0, early, chunks, ())
     c5 = shift(jnp.where(core == 0, high, c3), X_UP, Z_UP)
@@ -453,36 +459,33 @@
     return chunk[4 * ROWS : SUM_ROWS, :]
 
 
-def pair_kernel(lists, chip_bias, h0, ja1, ja2, jb1, pair_a, pair_b, line_bias, held):
+def high_kernel(lists, chip_bias, h0, ja1, ja2, jb1, *rest):
+    messages, (line_bias, held) = rest[:4], rest[4:]
     line = in_order([chip_bias[...], joined(tail_of(ja1)), joined(tail_of(jb1)), joined(tail_of(ja2))], lists[6, 1], held)
     line_bias[...] = line
     rows = bias_block(rows_of(line))
-    for pair, first in ((pair_a, 0), (pair_b, 2)):
-        for i in range(2):
-            pair[i * ROWS : (i + 1) * ROWS, :] = block_sum(first + i, h0, jb1, ja2).astype(BF16)
-        pair[2 * ROWS : 2 * ROWS + BIAS_ROWS, :] = rows
-
-
-def message_kernel(line_bias, h1, jc1, jc2, ra, rb, m1, m2, m3, rest):
-    own = rows_of(line_bias[...])
-    rest[...] = block_sum(0, h1, jc1, jc2) + block_sum(0, ra, rb)
-    relayed = [chunk[2 * ROWS : 2 * ROWS + BIAS_ROWS, :].astype(F32)[0:3] for chunk in (ra, rb)]
-    m1[0:ROWS, :] = (block_sum(1, h1, jc1, jc2) + block_sum(1, ra)).astype(BF16)
-    m1[ROWS:, :] = bias_block(own + [relayed[0]])
-    m2[0:ROWS, :] = (block_sum(2, h1, jc1, jc2) + block_sum(1, rb)).astype(BF16)
-    m2[ROWS:, :] = bias_block(own + [relayed[1]])
-    m3[0:ROWS, :] = block_sum(3, h1, jc1, jc2).astype(BF16)
-    m3[ROWS:, :] = bias_block(own)
-
-
-def last_kernel(lists, line_bias, rest, r1, r2, r3, ra, rb, scaled, feats_grad, weight_grad, bias, held):
-    total = rest[...] + block_sum(0, r1, r2, r3)
+    for i, message in enumerate(messages):
+        message[0:ROWS, :] = block_sum(i, h0, jb1, ja2).astype(BF16)
+        message[ROWS:, :] = rows
+
+
+def low_kernel(line_bias, h1, jc1, jc2, m1, m2, m3, rest):
+    rows = bias_block(rows_of(line_bias[...]))
+    rest[...] = block_sum(0, h1, jc1, jc2)
+    for i, message in enumerate((m1, m2, m3)):
+        message[0:ROWS, :] = block_sum(i + 1, h1, jc1, jc2).astype(BF16)
+        message[ROWS:, :] = rows
+
+
+def last_kernel(lists, line_bias, rest, scaled, *more):
+    arrived, (feats_grad, weight_grad, bias, held) = more[:7], more[7:]
+    total = rest[...] + block_sum(0, *arrived)
     feats_grad[...] = (scaled[...].astype(F32) + total[0:NODES]).astype(BF16)
     weight_grad[...] = total[NODES:ROWS]
-    t1, t2, t3 = (chunk[ROWS:, :] for chunk in (r1, r2, r3))
-    ta, tb = (chunk[2 * ROWS :, :] for chunk in (ra, rb))
-    values = [line_bias[...], joined(t1), joined(ta), joined(t1, 3), joined(t3), joined(t2, 3), joined(tb), joined(t2)]
-    bias[...] = in_order(values, lists[6, 2], held)
+    values = {0: line_bias[...]}
+    for dz, message in zip(LOW[1:] + HIGH, arrived):
+        values[dz] = joined(message[ROWS:, :])
+    bias[...] = in_order([values[dz] for dz in range(NZ)], lists[6, 2], held)
 
 
 def small_call(kernel, shapes, lists, operands, scratch):
@@ -508,31 +511,23 @@
     jb1 = shift(add(b1, ja1).astype(BF16), X_UP, Z_UP)
     jb2 = shift(add(b2, jnp.where(core == 0, zero, ja2)).astype(BF16), X_DOWN, Z_DOWN)
     jb1, jb2 = lax.optimization_barrier((jb1, jb2))
-    wide = (2 * ROWS + BIAS_ROWS, WIDTH)
-    pair_a, pair_b, line_bias = small_call(
-        pair_kernel, ((wide, BF16), (wide, BF16), ((1, WIDTH), F32)), lists, (chip_bias, h0, ja1, ja2, jb1), 1
+    size = (ROWS + BIAS_ROWS, WIDTH)
+    *high, line_bias = small_call(
+        high_kernel, [(size, BF16)] * 4 + [((1, WIDTH), F32)], lists, (chip_bias, h0, ja1, ja2, jb1), 1
     )
     jc1 = shift(add(q1, jnp.where(core == 0, zero, jb1)).astype(BF16), X_UP, Z_UP)
     jc2 = shift(add(q2, jb2).astype(BF16), X_DOWN, Z_DOWN)
-    jc1, jc2, pair_a, pair_b = lax.optimization_barrier((jc1, jc2, pair_a, pair_b))
-    ra = shift(pair_a, Z_UP_2)
-    rb = shift(pair_b, Z_DOWN_2)
-    size = (ROWS + BIAS_ROWS, WIDTH)
-    m1, m2, m3, rest = small_call(
-        message_kernel,
-        ((size, BF16), (size, BF16), (size, BF16), ((ROWS, WIDTH), F32)),
-        None,
-        (line_bias, h1, jc1, jc2, ra, rb),
-        0,
+    jc1, jc2, *high = lax.optimization_barrier((jc1, jc2, *high))
+    *low, rest = small_call(
+        low_kernel, [(size, BF16)] * 3 + [((ROWS, WIDTH), F32)], None, (line_bias, h1, jc1, jc2), 0
     )
-    r1 = shift(m1, Z_UP, X_UP)
-    r2 = shift(m2, Z_DOWN, X_DOWN)
-    r3 = shift(m3, Z_FOUR, X_TWO)
+    arrived = [shift(low[0], Z_UP, X_UP), shift(low[1], Z_DOWN, X_DOWN), shift(low[2], Z_FOUR, X_TWO)]
+    arrived += [shift(message, (dz, 0)) for dz, message in zip(HIGH_STEPS, high)]
     return small_call(
         last_kernel,
         (((NODES, WIDTH), BF16), ((W_ROWS, WIDTH), F32), ((1, WIDTH), F32)),
         lists,
-        (line_bias, rest, r1, r2, r3, ra, rb, scaled),
+        (line_bias, rest, scaled, *arrived),
         1,
     )
 
@@ -568,13 +563,14 @@
     ).reshape(NODES, 1)
 
     other_tiles = swap(tile_values, 1)
-    sums, weight_lane = gather(
+    sums, other_sums, weight_lane = gather(
         jnp.concatenate([feats, weight.T], axis=0),
         core,
-        (lists, other_tiles),
+        lists,
+        other_tiles,
         lambda call, early, chunks, before: forward(call, early[0], tile_values, early[1], chunks, before),
     )
-    neighbour_sum = (sums[:2] + swap(sums[2:], 1)).reshape(NODES, WIDTH)
+    neighbour_sum = (sums + swap(other_sums, 1)).reshape(NODES, WIDTH)
     weight_other = swap(weight_lane, 1)
     mixed = ((feats.astype(F32) + neighbour_sum) / degree).astype(BF16)
 

time: 200 us -> 204 us (1.020); the launches traced: 201 us -> 202 us
  starting transfers between devices: 57.9 us -> 78.8 us
  Pallas kernels: 44.3 us -> 31.3 us
  waiting for transfers between devices: 79.4 us -> 73.1 us
    ppermute x25 -> x29, starting transfers between devices: 28.4 us -> 45.3 us  [shift(): return lax.ppermute(value, 'dom', pairs)]
    ppermute x25 -> x29, waiting for transfers between devices: 49.8 us -> 39 us  [shift(): return lax.ppermute(value, 'dom', pairs)]
    pallas_call x2, Pallas kernels: 18.6 us -> 11.7 us  [backward(): pl.pallas_call(functools.partial(backward_kernel, call), out_shape=tuple(...]
    pallas_call x3, Pallas kernels: 21.2 us -> 15.1 us  [forward(): pl.pallas_call(functools.partial(forward_kernel, call), out_shape=(jax.Sh...]
    ppermute x6, starting transfers between devices: 18.3 us -> 22.5 us  [swap(): lax.ppermute(value, 'dom', [(i, i ^ bit) for i in range(NZ * NX * 2)])]
    ppermute x1, waiting for transfers between devices: 17.9 us -> 21.6 us  [on_device(): lax.ppermute(bias_sum, 'dom', [(i, i + 1) for i in range(0, NZ * NX * 2,...]
  transfers between devices with their start and end apart: 38 -> 42, of which waited for: 22 -> 21; matrix products, arithmetic and copies ran while one was open for 5% -> 5% of each run, Pallas kernels for 16% -> 10%
where the time goes in v5:
time: 204 us; the launch traced here: 202 us
  starting transfers between devices  78.8 us (39%)
  waiting for transfers between devices  73.1 us (36%)
  Pallas kernels  31.3 us (15%)
  other arithmetic  10.7 us (5%)
  local copies, waits for them, and re-layouts  3.83 us (2%)
  matrix products  2.47 us (1%)
  between operations  2.07 us (1%)
    ppermute x29, starting transfers between devices, shift(): return lax.ppermute(value, 'dom', pairs)  45.3 us
    ppermute x29, waiting for transfers between devices, shift(): return lax.ppermute(value, 'dom', pairs)  39 us
    ppermute x6, starting transfers between devices, swap(): lax.ppermute(value, 'dom', [(i, i ^ bit) for i in range(NZ * NX * 2)])  22.5 us
    ppermute x1, waiting for transfers between devices, on_device(): lax.ppermute(bias_sum, 'dom', [(i, i + 1) for i in range(0, NZ * NX * 2,...  21.6 us
    pallas_call x3, Pallas kernels, forward(): pl.pallas_call(functools.partial(forward_kernel, call), out_shape=(jax.Sh...  15.1 us
    pallas_call x2, Pallas kernels, backward(): pl.pallas_call(functools.partial(backward_kernel, call), out_shape=tuple(...  11.7 us
    ppermute x6, starting transfers between devices, y_shift(): return lax.ppermute(value, 'feat', [(y, (y + dy) % NY) for y in range(NY)])  9.63 us
    ppermute x6, waiting for transfers between devices, y_shift(): return lax.ppermute(value, 'feat', [(y, (y + dy) % NY) for y in range(NY)])  9.39 us
  transfers between devices with their start and end apart: 42, of which 21 were waited for; matrix products, arithmetic and copies ran while one was open for 5% of the time, Pallas kernels for 10%

profile of v5, /device:TPU:1, one launch (start us, length us, event | category | flops | bytes accessed | tf_op | source)
XLA Modules:
  0.0 202.4 jit_solution(7128524774557499902)
XLA Ops:
  0.6 3.3 %collective-permute-start.7 = (bf16[128,128,128]{2,1,0:T(8,128)(2,1)}, bf16[128,128,128]{2,1,0:T(8,128)(2,1)}, u32[]{:S(2)}, u32[]{:S(2)}) collective-permute-start(bf16[128,128,128]{2,1,0:T(8,128)(2,1)} %own.9), channel_id=1, source_target_pairs={{0,4},{4,0},{8,12},{12,8},{16,20},{20,16},{24,28},{28,24},{32,36},... | collective-permute-start | bytes 12582920 | tf_op jit(solution)/shard_map/ppermute | solution.py:73
  4.0 0.9 fusion.17
  4.9 1.1 collective-permute-start.2
  6.0 0.9 collective-permute-start.1
  8.1 2.3 %collective-permute-done.2 = bf16[272,256]{1,0:T(8,128)(2,1)S(1)} collective-permute-done((bf16[272,256]{1,0:T(8,128)(2,1)S(1)}, bf16[272,256]{1,0:T(8,128)(2,1)S(1)}, u32[]{:S(2)}, u32[]{:S(2)}) %collective-permute-start.2) | collective-permute-done | bytes 139296 | tf_op jit(solution)/shard_map/ppermute | solution.py:65
  11.1 0.7 collective-permute-start.3
  13.2 5.7 %collective-permute-start.9 = (bf16[4,272,256]{2,1,0:T(8,128)(2,1)S(1)}, bf16[4,272,256]{2,1,0:T(8,128)(2,1)S(1)}, u32[]{:S(2)}, u32[]{:S(2)}) collective-permute-start(bf16[4,272,256]{2,1,0:T(8,128)(2,1)S(1)} %pad_maximum_fusion.1.rest_0_), channel_id=1, source_target_pairs={{0,24},{4,228},{8,0},{12,236},{16,8},{20,244},{24,16},{28,252},{32... | collective-permute-start | bytes 1671176 | tf_op jit(solution)/shard_map/ppermute | solution.py:65
  18.9 11.0 %collective-permute-done.9.rest_2_ = bf16[4,272,256]{2,1,0:T(8,128)(2,1)S(1)} collective-permute-done((bf16[4,272,256]{2,1,0:T(8,128)(2,1)S(1)}, bf16[4,272,256]{2,1,0:T(8,128)(2,1)S(1)}, u32[]{:S(2)}, u32[]{:S(2)}) %collective-permute-start.9) | collective-permute-done | bytes 557088 | tf_op jit(solution)/shard_map/ppermute | solution.py:65
  29.8 1.0 broadcast_select_fusion.2
  30.8 3.4 %collective-permute-start.11 = (bf16[4,272,256]{2,1,0:T(8,128)(2,1)}, bf16[4,272,256]{2,1,0:T(8,128)(2,1)S(1)}, u32[]{:S(2)}, u32[]{:S(2)}) collective-permute-start(bf16[4,272,256]{2,1,0:T(8,128)(2,1)} %broadcast_select_fusion.2), channel_id=1, source_target_pairs={{0,24},{4,228},{8,0},{12,236},{16,8},{20,244},{24,16},{28,252},{32... | collective-permute-start | bytes 1671176 | tf_op jit(solution)/shard_map/ppermute | solution.py:65
  35.0 17.0 %collective-permute-start.12 = (s32[3,128]{1,0:T(4,128)S(1)}, s32[3,128]{1,0:T(4,128)S(1)}, u32[]{:S(2)}, u32[]{:S(2)}) collective-permute-start(s32[3,128]{1,0:T(4,128)S(1)} %add_add_fusion.1.own), channel_id=1, source_target_pairs={{0,4},{4,0},{8,12},{12,8},{16,20},{20,16},{24,28},{28,24},{32,36},... | collective-permute-start | bytes 4616 | tf_op jit(solution)/shard_map/ppermute | solution.py:73
  52.0 0.8 collective-permute-done.12.sib
  53.4 1.3 stack.95.place
  54.8 1.8 shard_map.114.lists
  56.7 3.1 %collective-permute-start.13 = (bf16[4,272,256]{2,1,0:T(8,128)(2,1)S(1)}, bf16[4,272,256]{2,1,0:T(8,128)(2,1)S(1)}, u32[]{:S(2)}, u32[]{:S(2)}) collective-permute-start(bf16[4,272,256]{2,1,0:T(8,128)(2,1)S(1)} %broadcast_select_fusion.1), channel_id=1, source_target_pairs={{0,8},{4,36},{8,16},{12,44},{16,24},{20,52},{24,0},{28,60},{32,40}... | collective-permute-start | bytes 1671176 | tf_op jit(solution)/shard_map/ppermute | solution.py:65
  60.2 6.1 %shard_map.115 = (f32[2,128,256]{2,1,0:T(8,128)}, f32[2,128,256]{2,1,0:T(8,128)}, bf16[4,8,16,256]{3,2,1,0:T(8,128)(2,1)}) custom-call(s32[8,256]{1,0:T(8,128)} %shard_map.114.lists, bf16[128,128,128]{2,1,0:T(8,128)(2,1)} %own.9, bf16[128,128,128]{2,1,0:T(8,128)(2,1)} %collective-permute-done.7.sib, bf16[4,272,256]{2,1,0:T(8,128)(2,1)} %copy-done.7, ...), custom_call_target="tpu_custom_call" | custom-call | flops 805306368 | bytes 6291456 | tf_op jit(solution)/shard_map/pallas_call | solution.py:286
  66.3 1.0 collective-permute-done.13.rest_0_
  67.3 1.2 collective-permute-done.14.rest_1_
  68.6 3.4 %collective-permute-start.15 = (bf16[2,272,256]{2,1,0:T(8,128)(2,1)S(1)}, bf16[2,272,256]{2,1,0:T(8,128)(2,1)S(1)}, u32[]{:S(2)}, u32[]{:S(2)}) collective-permute-start(bf16[2,272,256]{2,1,0:T(8,128)(2,1)S(1)} %slice.44), channel_id=1, source_target_pairs={{4,36},{12,44},{20,52},{28,60},{36,68},{44,76},{52,84},{60,92},{68... | collective-permute-start | bytes 835592 | tf_op jit(solution)/shard_map/ppermute | solution.py:65
  72.0 3.1 %collective-permute-start.16 = (bf16[2,272,256]{2,1,0:T(8,128)(2,1)S(1)}, bf16[2,272,256]{2,1,0:T(8,128)(2,1)S(1)}, u32[]{:S(2)}, u32[]{:S(2)}) collective-permute-start(bf16[2,272,256]{2,1,0:T(8,128)(2,1)S(1)} %slice.45), channel_id=1, source_target_pairs={{4,228},{12,236},{20,244},{28,252},{36,4},{44,12},{52,20},{60,28},... | collective-permute-start | bytes 835592 | tf_op jit(solution)/shard_map/ppermute | solution.py:65
  75.1 1.2 convert_reduce_fusion
  76.3 4.8 %shard_map.116 = (f32[2,128,256]{2,1,0:T(8,128)}, f32[2,128,256]{2,1,0:T(8,128)}, bf16[4,8,16,256]{3,2,1,0:T(8,128)(2,1)}) custom-call(s32[8,256]{1,0:T(8,128)} %shard_map.114.lists, bf16[128,128,128]{2,1,0:T(8,128)(2,1)} %own.9, bf16[128,128,128]{2,1,0:T(8,128)(2,1)} %collective-permute-done.7.sib, bf16[4,272,256]{2,1,0:T(8,128)(2,1)} %copy-done.8, ...), custom_call_target="tpu_custom_call" | custom-call | flops 268435456 | bytes 2097152 | tf_op jit(solution)/shard_map/pallas_call | solution.py:286
  81.1 0.7 copy-done.20
  81.9 4.2 %shard_map.117 = (f32[2,128,256]{2,1,0:T(8,128)}, f32[2,128,256]{2,1,0:T(8,128)}, bf16[4,8,16,256]{3,2,1,0:T(8,128)(2,1)}) custom-call(s32[8,256]{1,0:T(8,128)} %shard_map.114.lists, bf16[128,128,128]{2,1,0:T(8,128)(2,1)} %own.9, bf16[128,128,128]{2,1,0:T(8,128)(2,1)} %collective-permute-done.7.sib, bf16[2,272,256]{2,1,0:T(8,128)(2,1)} %copy-done.20, ...), custom_call_target="tpu_custom_call" | custom-call | flops 268435456 | bytes 2097152 | tf_op jit(solution)/shard_map/pallas_call | solution.py:286
  86.9 1.0 collective-permute-done.18
  88.0 1.0 select_bitcast_fusion.1
  89.1 0.8 copy-done.22
  90.8 3.0 %collective-permute-start.20 = (bf16[256,256]{1,0:T(8,128)(2,1)S(1)}, bf16[256,256]{1,0:T(8,128)(2,1)S(1)}, u32[]{:S(2)}, u32[]{:S(2)}) collective-permute-start(bf16[256,256]{1,0:T(8,128)(2,1)S(1)} %convolution_convert_fusion.1), channel_id=1, source_target_pairs={{0,2},{1,3},{2,0},{3,1},{4,6},{5,7},{6,4},{7,5},{8,10},{9,11},{10,... | collective-permute-start | bytes 393224 | tf_op jit(solution)/shard_map/ppermute | solution.py:77
  93.8 0.8 collective-permute-start.21
  94.6 0.7 collective-permute-start.19
  95.5 1.9 collective-permute-done.20
  97.4 3.2 %collective-permute-done.21 = bf16[256,256]{1,0:T(8,128)(2,1)S(1)} collective-permute-done((bf16[256,256]{1,0:T(8,128)(2,1)S(1)}, bf16[256,256]{1,0:T(8,128)(2,1)S(1)}, u32[]{:S(2)}, u32[]{:S(2)}) %collective-permute-start.21) | collective-permute-done | bytes 131104 | tf_op jit(solution)/shard_map/ppermute | solution.py:77
  100.5 0.8 fusion.18
  101.6 1.5 collective-permute-start.24
  103.1 2.6 %collective-permute-start.23 = (bf16[256,256]{1,0:T(8,128)(2,1)S(1)}, bf16[256,256]{1,0:T(8,128)(2,1)S(1)}, u32[]{:S(2)}, u32[]{:S(2)}) collective-permute-start(bf16[256,256]{1,0:T(8,128)(2,1)S(1)} %get-tuple-element.118), channel_id=1, source_target_pairs={{0,2},{1,3},{2,0},{3,1},{4,6},{5,7},{6,4},{7,5},{8,10},{9,11},{10,... | collective-permute-start | bytes 393224 | tf_op jit(solution)/shard_map/ppermute | solution.py:77
  105.7 1.1 collective-permute-start.22
  107.2 4.4 %collective-permute-done.23 = bf16[256,256]{1,0:T(8,128)(2,1)S(1)} collective-permute-done((bf16[256,256]{1,0:T(8,128)(2,1)S(1)}, bf16[256,256]{1,0:T(8,128)(2,1)S(1)}, u32[]{:S(2)}, u32[]{:S(2)}) %collective-permute-start.23) | collective-permute-done | bytes 131104 | tf_op jit(solution)/shard_map/ppermute | solution.py:77
  112.3 1.4 collective-permute-start.25
  114.4 1.3 collective-permute-done.26
  115.7 0.7 pad_maximum_fusion.3
  116.5 0.8 fusion.4.weight_sums
  118.0 4.2 %shard_map.119 = (bf16[1104,256]{1,0:T(8,128)(2,1)}, bf16[1104,256]{1,0:T(8,128)(2,1)}, bf16[1104,256]{1,0:T(8,128)(2,1)}) custom-call(s32[8,256]{1,0:T(8,128)} %shard_map.114.lists, bf16[128,128,128]{2,1,0:T(8,128)(2,1)} %own.9, bf16[128,128,128]{2,1,0:T(8,128)(2,1)} %collective-permute-done.7.sib, bf16[4,128,256]{2,1,0:T(8,128)(2,1)} %bitcast.83, ...), custom_call_target="tpu_custom_call" | custom-call | flops 402653184 | bytes 3145728 | tf_op jit(solution)/shard_map/pallas_call | solution.py:368
  122.2 4.8 %collective-permute-start.27 = (bf16[1104,256]{1,0:T(8,128)(2,1)}, bf16[1104,256]{1,0:T(8,128)(2,1)S(1)}, u32[]{:S(2)}, u32[]{:S(2)}) collective-permute-start(bf16[1104,256]{1,0:T(8,128)(2,1)} %get-tuple-element.84), channel_id=1, source_target_pairs={{4,36},{12,44},{20,52},{28,60},{36,68},{44,76},{52,84},{60,92},{68... | collective-permute-start | bytes 1695752 | tf_op jit(solution)/shard_map/ppermute | solution.py:65
  126.9 7.5 %shard_map.118 = (bf16[1104,256]{1,0:T(8,128)(2,1)}, bf16[1104,256]{1,0:T(8,128)(2,1)}, bf16[1104,256]{1,0:T(8,128)(2,1)}, bf16[1104,256]{1,0:T(8,128)(2,1)}, bf...) custom-call(s32[8,256]{1,0:T(8,128)} %shard_map.114.lists, ...), custom_call_target="tpu_custom_call" | custom-call | flops 1073741824 | bytes 8388608 | tf_op jit(solution)/shard_map/pallas_call | solution.py:368
  134.5 1.2 broadcast_select_fusion
  135.7 2.6 %collective-permute-start.29 = (bf16[1104,256]{1,0:T(8,128)(2,1)S(1)}, bf16[1104,256]{1,0:T(8,128)(2,1)S(1)}, u32[]{:S(2)}, u32[]{:S(2)}) collective-permute-start(bf16[1104,256]{1,0:T(8,128)(2,1)S(1)} %broadcast_select_fusion), channel_id=1, source_target_pairs={{0,24},{4,228},{8,0},{12,236},{16,8},{20,244},{24,16},{28,252},{32... | collective-permute-start | bytes 1695752 | tf_op jit(solution)/shard_map/ppermute | solution.py:65
  138.6 2.6 %collective-permute-start.28 = (bf16[1104,256]{1,0:T(8,128)(2,1)S(1)}, bf16[1104,256]{1,0:T(8,128)(2,1)S(1)}, u32[]{:S(2)}, u32[]{:S(2)}) collective-permute-start(bf16[1104,256]{1,0:T(8,128)(2,1)S(1)} %fusion.3), channel_id=1, source_target_pairs={{0,8},{4,36},{8,16},{12,44},{16,24},{20,52},{24,0},{28,60},{32,40}... | collective-permute-start | bytes 1695752 | tf_op jit(solution)/shard_map/ppermute | solution.py:65
  141.2 6.6 %collective-permute-done.29.ja2 = bf16[1104,256]{1,0:T(8,128)(2,1)S(1)} collective-permute-done((bf16[1104,256]{1,0:T(8,128)(2,1)S(1)}, bf16[1104,256]{1,0:T(8,128)(2,1)S(1)}, u32[]{:S(2)}, u32[]{:S(2)}) %collective-permute-start.29) | collective-permute-done | bytes 565280 | tf_op jit(solution)/shard_map/ppermute | solution.py:65
  148.8 1.5 collective-permute-start.30
  150.3 7.0 %collective-permute-done.31 = bf16[1104,256]{1,0:T(8,128)(2,1)S(1)} collective-permute-done((bf16[1104,256]{1,0:T(8,128)(2,1)S(1)}, bf16[1104,256]{1,0:T(8,128)(2,1)S(1)}, u32[]{:S(2)}, u32[]{:S(2)}) %collective-permute-start.31) | collective-permute-done | bytes 565280 | tf_op jit(solution)/shard_map/ppermute | solution.py:65
  157.4 1.2 collective-permute-done.30.jb1
  158.8 0.8 collective-permute-start.32
  159.8 2.0 collective-permute-start.33
  161.8 1.0 shard_map.120
  162.8 6.1 %collective-permute-done.32.jc1 = bf16[1104,256]{1,0:T(8,128)(2,1)S(1)} collective-permute-done((bf16[1104,256]{1,0:T(8,128)(2,1)S(1)}, bf16[1104,256]{1,0:T(8,128)(2,1)S(1)}, u32[]{:S(2)}, u32[]{:S(2)}) %collective-permute-start.32) | collective-permute-done | bytes 565280 | tf_op jit(solution)/shard_map/ppermute | solution.py:65
  169.1 2.1 %collective-permute-start.34 = (bf16[288,256]{1,0:T(8,128)(2,1)S(1)}, bf16[288,256]{1,0:T(8,128)(2,1)S(1)}, u32[]{:S(2)}, u32[]{:S(2)}) collective-permute-start(bf16[288,256]{1,0:T(8,128)(2,1)S(1)} %get-tuple-element.104), channel_id=1, source_target_pairs={{0,32},{4,12},{8,40},{12,20},{16,48},{20,28},{24,56},{28,4},{32,64... | collective-permute-start | bytes 442376 | tf_op jit(solution)/shard_map/ppermute | solution.py:65
  171.9 1.3 collective-permute-start.36
  173.8 0.7 collective-permute-start.38
  174.7 0.7 collective-permute-start.39
  175.6 0.7 collective-permute-start.40
  176.2 1.2 collective-permute-done.36.more_2_
  177.4 1.6 shard_map.122
  179.0 1.3 collective-permute-start.41
  180.3 21.6 %collective-permute-done.41 = f32[1,256]{1,0:T(1,128)S(1)} collective-permute-done((f32[1,256]{1,0:T(1,128)S(1)}, f32[1,256]{1,0:T(1,128)S(1)}, u32[]{:S(2)}, u32[]{:S(2)}) %collective-permute-start.41) | collective-permute-done | bytes 1056 | tf_op jit(solution)/shard_map/ppermute | solution.py:620
  (140 shorter events, 13.4 us)
Async XLA Ops:
  0.6 12.6 %collective-permute-start.7 = (bf16[128,128,128]{2,1,0:T(8,128)(2,1)}, bf16[128,128,128]{2,1,0:T(8,128)(2,1)}, u32[]{:S(2)}, u32[]{:S(2)}) collective-permute-start(bf16[128,128,128]{2,1,0:T(8,128)(2,1)} %own.9), channel_id=1, source_target_pairs={{0,4},{4,0},{8,12},{12,8},{16,20},{20,16},{24,28},{28,24},{32,36},... | collective-permute-start | bytes 12582920 | tf_op jit(solution)/shard_map/ppermute | solution.py:73
  4.9 5.5 %collective-permute-start.2 = (bf16[272,256]{1,0:T(8,128)(2,1)S(1)}, bf16[272,256]{1,0:T(8,128)(2,1)S(1)}, u32[]{:S(2)}, u32[]{:S(2)}) collective-permute-start(bf16[272,256]{1,0:T(8,128)(2,1)S(1)} %get-tuple-element.128), channel_id=1, source_target_pairs={{0,128},{4,20},{8,136},{12,28},{16,144},{20,4},{24,152},{28,12},{3... | collective-permute-start | bytes 417800 | tf_op jit(solution)/shard_map/ppermute | solution.py:65
  6.0 5.1 %collective-permute-start.1 = (bf16[272,256]{1,0:T(8,128)(2,1)S(1)}, bf16[272,256]{1,0:T(8,128)(2,1)S(1)}, u32[]{:S(2)}, u32[]{:S(2)}) collective-permute-start(bf16[272,256]{1,0:T(8,128)(2,1)S(1)} %get-tuple-element.128), channel_id=1, source_target_pairs={{0,224},{4,28},{8,232},{12,4},{16,240},{20,12},{24,248},{28,20},{3... | collective-permute-start | bytes 417800 | tf_op jit(solution)/shard_map/ppermute | solution.py:65
  6.9 5.4 %collective-permute-start = (bf16[272,256]{1,0:T(8,128)(2,1)S(1)}, bf16[272,256]{1,0:T(8,128)(2,1)S(1)}, u32[]{:S(2)}, u32[]{:S(2)}) collective-permute-start(bf16[272,256]{1,0:T(8,128)(2,1)S(1)} %get-tuple-element.128), channel_id=1, source_target_pairs={{0,32},{4,12},{8,40},{12,20},{16,48},{20,28},{24,56},{28,4},{32,64... | collective-permute-start | bytes 417800 | tf_op jit(solution)/shard_map/ppermute | solution.py:65
  7.5 5.6 %collective-permute-start.5 = (bf16[272,256]{1,0:T(8,128)(2,1)S(1)}, bf16[272,256]{1,0:T(8,128)(2,1)S(1)}, u32[]{:S(2)}, u32[]{:S(2)}) collective-permute-start(bf16[272,256]{1,0:T(8,128)(2,1)S(1)} %get-tuple-element.128), channel_id=1, source_target_pairs={{0,64},{8,72},{16,80},{24,88},{32,96},{40,104},{48,112},{56,120},{... | collective-permute-start | bytes 417800 | tf_op jit(solution)/shard_map/ppermute | solution.py:65
  10.4 2.6 %collective-permute-start.4 = (bf16[272,256]{1,0:T(8,128)(2,1)S(1)}, bf16[272,256]{1,0:T(8,128)(2,1)S(1)}, u32[]{:S(2)}, u32[]{:S(2)}) collective-permute-start(bf16[272,256]{1,0:T(8,128)(2,1)S(1)} %get-tuple-element.128), channel_id=1, source_target_pairs={{0,160},{8,168},{16,176},{24,184},{32,192},{40,200},{48,208},{56,2... | collective-permute-start | bytes 417800 | tf_op jit(solution)/shard_map/ppermute | solution.py:65
  11.1 2.0 collective-permute-start.3
  12.3 0.8 collective-permute-start.6
  13.0 17.8 %copy-start.7 = (bf16[4,272,256]{2,1,0:T(8,128)(2,1)}, bf16[4,272,256]{2,1,0:T(8,128)(2,1)S(1)}, u32[]{:S(2)}) copy-start(bf16[4,272,256]{2,1,0:T(8,128)(2,1)S(1)} %pad_maximum_fusion.1.rest_0_) | copy-start | bytes 1671172
  13.2 43.5 %copy-start.4 = (bf16[4,272,256]{2,1,0:T(8,128)(2,1)}, bf16[4,272,256]{2,1,0:T(8,128)(2,1)S(1)}, u32[]{:S(2)}) copy-start(bf16[4,272,256]{2,1,0:T(8,128)(2,1)S(1)} %pad_maximum_fusion.2.rest_5_) | copy-start | bytes 1671172
  13.2 21.8 %copy-start.26 = (s32[128]{0:T(128)S(1)}, s32[128]{0:T(128)}, u32[]{:S(2)}) copy-start(s32[128]{0:T(128)} %param.12) | copy-start | bytes 1540
  13.2 21.8 %copy-start.28 = (s32[128]{0:T(128)S(1)}, s32[128]{0:T(128)}, u32[]{:S(2)}) copy-start(s32[128]{0:T(128)} %param.13) | copy-start | bytes 1540
  13.2 16.6 %collective-permute-start.9 = (bf16[4,272,256]{2,1,0:T(8,128)(2,1)S(1)}, bf16[4,272,256]{2,1,0:T(8,128)(2,1)S(1)}, u32[]{:S(2)}, u32[]{:S(2)}) collective-permute-start(bf16[4,272,256]{2,1,0:T(8,128)(2,1)S(1)} %pad_maximum_fusion.1.rest_0_), channel_id=1, source_target_pairs={{0,24},{4,228},{8,0},{12,236},{16,8},{20,244},{24,16},{28,252},{32... | collective-permute-start | bytes 1671176 | tf_op jit(solution)/shard_map/ppermute | solution.py:65
  18.8 11.0 %collective-permute-start.8 = (bf16[4,272,256]{2,1,0:T(8,128)(2,1)S(1)}, bf16[4,272,256]{2,1,0:T(8,128)(2,1)S(1)}, u32[]{:S(2)}, u32[]{:S(2)}) collective-permute-start(bf16[4,272,256]{2,1,0:T(8,128)(2,1)S(1)} %pad_maximum_fusion.1.rest_0_), channel_id=1, source_target_pairs={{0,8},{4,36},{8,16},{12,44},{16,24},{20,52},{24,0},{28,60},{32,40}... | collective-permute-start | bytes 1671176 | tf_op jit(solution)/shard_map/ppermute | solution.py:65
  29.8 26.9 %copy-start.5 = (bf16[4,272,256]{2,1,0:T(8,128)(2,1)}, bf16[4,272,256]{2,1,0:T(8,128)(2,1)S(1)}, u32[]{:S(2)}) copy-start(bf16[4,272,256]{2,1,0:T(8,128)(2,1)S(1)} %collective-permute-done.9.rest_2_) | copy-start | bytes 1671172
  29.8 26.9 %copy-start.17 = (bf16[4,272,256]{2,1,0:T(8,128)(2,1)}, bf16[4,272,256]{2,1,0:T(8,128)(2,1)S(1)}, u32[]{:S(2)}) copy-start(bf16[4,272,256]{2,1,0:T(8,128)(2,1)S(1)} %collective-permute-done.8.rest_1_) | copy-start | bytes 1671172
  30.8 25.8 %collective-permute-start.11 = (bf16[4,272,256]{2,1,0:T(8,128)(2,1)}, bf16[4,272,256]{2,1,0:T(8,128)(2,1)S(1)}, u32[]{:S(2)}, u32[]{:S(2)}) collective-permute-start(bf16[4,272,256]{2,1,0:T(8,128)(2,1)} %broadcast_select_fusion.2), channel_id=1, source_target_pairs={{0,24},{4,228},{8,0},{12,236},{16,8},{20,244},{24,16},{28,252},{32... | collective-permute-start | bytes 1671176 | tf_op jit(solution)/shard_map/ppermute | solution.py:65
  34.2 22.4 %collective-permute-start.10 = (bf16[4,272,256]{2,1,0:T(8,128)(2,1)S(1)}, bf16[4,272,256]{2,1,0:T(8,128)(2,1)S(1)}, u32[]{:S(2)}, u32[]{:S(2)}) collective-permute-start(bf16[4,272,256]{2,1,0:T(8,128)(2,1)S(1)} %collective-permute-done.8.rest_1_), channel_id=1, source_target_pairs={{0,8},{4,36},{8,16},{12,44},{16,24},{20,52},{24,0},{28,60},{32,40}... | collective-permute-start | bytes 1671176 | tf_op jit(solution)/shard_map/ppermute | solution.py:65
  35.0 19.8 %copy-start.24 = (s32[3,128]{1,0:T(4,128)}, s32[3,128]{1,0:T(4,128)S(1)}, u32[]{:S(2)}) copy-start(s32[3,128]{1,0:T(4,128)S(1)} %add_add_fusion.1.own) | copy-start | bytes 4612
  35.0 17.8 %collective-permute-start.12 = (s32[3,128]{1,0:T(4,128)S(1)}, s32[3,128]{1,0:T(4,128)S(1)}, u32[]{:S(2)}, u32[]{:S(2)}) collective-permute-start(s32[3,128]{1,0:T(4,128)S(1)} %add_add_fusion.1.own), channel_id=1, source_target_pairs={{0,4},{4,0},{8,12},{12,8},{16,20},{20,16},{24,28},{28,24},{32,36},... | collective-permute-start | bytes 4616 | tf_op jit(solution)/shard_map/ppermute | solution.py:73
  56.6 3.6 %copy-start.18 = (bf16[4,272,256]{2,1,0:T(8,128)(2,1)}, bf16[4,272,256]{2,1,0:T(8,128)(2,1)S(1)}, u32[]{:S(2)}) copy-start(bf16[4,272,256]{2,1,0:T(8,128)(2,1)S(1)} %collective-permute-done.11.rest_4_) | copy-start | bytes 1671172
  56.6 3.6 %copy-start.6 = (bf16[4,272,256]{2,1,0:T(8,128)(2,1)}, bf16[4,272,256]{2,1,0:T(8,128)(2,1)S(1)}, u32[]{:S(2)}) copy-start(bf16[4,272,256]{2,1,0:T(8,128)(2,1)S(1)} %collective-permute-done.10.rest_3_) | copy-start | bytes 1671172
  56.7 10.6 %collective-permute-start.13 = (bf16[4,272,256]{2,1,0:T(8,128)(2,1)S(1)}, bf16[4,272,256]{2,1,0:T(8,128)(2,1)S(1)}, u32[]{:S(2)}, u32[]{:S(2)}) collective-permute-start(bf16[4,272,256]{2,1,0:T(8,128)(2,1)S(1)} %broadcast_select_fusion.1), channel_id=1, source_target_pairs={{0,8},{4,36},{8,16},{12,44},{16,24},{20,52},{24,0},{28,60},{32,40}... | collective-permute-start | bytes 1671176 | tf_op jit(solution)/shard_map/ppermute | solution.py:65
  59.8 8.7 %collective-permute-start.14 = (bf16[4,272,256]{2,1,0:T(8,128)(2,1)S(1)}, bf16[4,272,256]{2,1,0:T(8,128)(2,1)S(1)}, u32[]{:S(2)}, u32[]{:S(2)}) collective-permute-start(bf16[4,272,256]{2,1,0:T(8,128)(2,1)S(1)} %collective-permute-done.11.rest_4_), channel_id=1, source_target_pairs={{0,24},{4,228},{8,0},{12,236},{16,8},{20,244},{24,16},{28,252},{32... | collective-permute-start | bytes 1671176 | tf_op jit(solution)/shard_map/ppermute | solution.py:65
  60.2 14.8 %copy-start.3 = (bf16[128,128,128]{2,1,0:T(8,128)(2,1)S(1)}, bf16[128,128,128]{2,1,0:T(8,128)(2,1)}, u32[]{:S(2)}) copy-start(bf16[128,128,128]{2,1,0:T(8,128)(2,1)} %own.9) | copy-start | bytes 12582916
  67.3 8.9 %copy-start.8 = (bf16[4,272,256]{2,1,0:T(8,128)(2,1)}, bf16[4,272,256]{2,1,0:T(8,128)(2,1)S(1)}, u32[]{:S(2)}) copy-start(bf16[4,272,256]{2,1,0:T(8,128)(2,1)S(1)} %collective-permute-done.13.rest_0_) | copy-start | bytes 1671172
  68.5 7.8 %copy-start.9 = (bf16[4,272,256]{2,1,0:T(8,128)(2,1)}, bf16[4,272,256]{2,1,0:T(8,128)(2,1)S(1)}, u32[]{:S(2)}) copy-start(bf16[4,272,256]{2,1,0:T(8,128)(2,1)S(1)} %collective-permute-done.14.rest_1_) | copy-start | bytes 1671172
  68.6 12.5 %collective-permute-start.15 = (bf16[2,272,256]{2,1,0:T(8,128)(2,1)S(1)}, bf16[2,272,256]{2,1,0:T(8,128)(2,1)S(1)}, u32[]{:S(2)}, u32[]{:S(2)}) collective-permute-start(bf16[2,272,256]{2,1,0:T(8,128)(2,1)S(1)} %slice.44), channel_id=1, source_target_pairs={{4,36},{12,44},{20,52},{28,60},{36,68},{44,76},{52,84},{60,92},{68... | collective-permute-start | bytes 835592 | tf_op jit(solution)/shard_map/ppermute | solution.py:65
  72.0 9.1 %collective-permute-start.16 = (bf16[2,272,256]{2,1,0:T(8,128)(2,1)S(1)}, bf16[2,272,256]{2,1,0:T(8,128)(2,1)S(1)}, u32[]{:S(2)}, u32[]{:S(2)}) collective-permute-start(bf16[2,272,256]{2,1,0:T(8,128)(2,1)S(1)} %slice.45), channel_id=1, source_target_pairs={{4,228},{12,236},{20,244},{28,252},{36,4},{44,12},{52,20},{60,28},... | collective-permute-start | bytes 835592 | tf_op jit(solution)/shard_map/ppermute | solution.py:65
  86.1 1.8 collective-permute-start.18
  86.4 2.7 %collective-permute-start.17 = (f32[2,128,256]{2,1,0:T(8,128)}, f32[2,128,256]{2,1,0:T(8,128)S(1)}, u32[]{:S(2)}, u32[]{:S(2)}) collective-permute-start(f32[2,128,256]{2,1,0:T(8,128)} %get-tuple-element.79), channel_id=1, source_target_pairs={{0,4},{4,0},{8,12},{12,8},{16,20},{20,16},{24,28},{28,24},{32,36},... | collective-permute-start | bytes 786440 | tf_op jit(solution)/shard_map/ppermute | solution.py:73
  90.0 10.6 %copy-start.23 = (bf16[256,256]{1,0:T(8,128)(2,1)S(1)}, bf16[256,256]{1,0:T(8,128)(2,1)}, u32[]{:S(2)}) copy-start(bf16[256,256]{1,0:T(8,128)(2,1)} %param.15) | copy-start | bytes 393220
  90.0 10.5 %copy-start.27 = (f32[256]{0:T(256)S(1)}, f32[256]{0:T(256)}, u32[]{:S(2)}) copy-start(f32[256]{0:T(256)} %param.10) | copy-start | bytes 3076
  90.8 6.5 %collective-permute-start.20 = (bf16[256,256]{1,0:T(8,128)(2,1)S(1)}, bf16[256,256]{1,0:T(8,128)(2,1)S(1)}, u32[]{:S(2)}, u32[]{:S(2)}) collective-permute-start(bf16[256,256]{1,0:T(8,128)(2,1)S(1)} %convolution_convert_fusion.1), channel_id=1, source_target_pairs={{0,2},{1,3},{2,0},{3,1},{4,6},{5,7},{6,4},{7,5},{8,10},{9,11},{10,... | collective-permute-start | bytes 393224 | tf_op jit(solution)/shard_map/ppermute | solution.py:77
  93.8 6.7 %collective-permute-start.21 = (bf16[256,256]{1,0:T(8,128)(2,1)S(1)}, bf16[256,256]{1,0:T(8,128)(2,1)S(1)}, u32[]{:S(2)}, u32[]{:S(2)}) collective-permute-start(bf16[256,256]{1,0:T(8,128)(2,1)S(1)} %convolution_convert_fusion), channel_id=1, source_target_pairs={{0,3},{1,0},{2,1},{3,2},{4,7},{5,4},{6,5},{7,6},{8,11},{9,8},{10,9... | collective-permute-start | bytes 393224 | tf_op jit(solution)/shard_map/ppermute | solution.py:77
  94.6 5.9 %collective-permute-start.19 = (bf16[256,256]{1,0:T(8,128)(2,1)S(1)}, bf16[256,256]{1,0:T(8,128)(2,1)S(1)}, u32[]{:S(2)}, u32[]{:S(2)}) collective-permute-start(bf16[256,256]{1,0:T(8,128)(2,1)S(1)} %convolution_convert_fusion.2), channel_id=1, source_target_pairs={{0,1},{1,2},{2,3},{3,0},{4,5},{5,6},{6,7},{7,4},{8,9},{9,10},{10,1... | collective-permute-start | bytes 393224 | tf_op jit(solution)/shard_map/ppermute | solution.py:77
  101.6 5.4 %collective-permute-start.24 = (bf16[256,256]{1,0:T(8,128)(2,1)S(1)}, bf16[256,256]{1,0:T(8,128)(2,1)S(1)}, u32[]{:S(2)}, u32[]{:S(2)}) collective-permute-start(bf16[256,256]{1,0:T(8,128)(2,1)S(1)} %get-tuple-element.118), channel_id=1, source_target_pairs={{0,1},{1,2},{2,3},{3,0},{4,5},{5,6},{6,7},{7,4},{8,9},{9,10},{10,1... | collective-permute-start | bytes 393224 | tf_op jit(solution)/shard_map/ppermute | solution.py:77
  103.1 8.5 %collective-permute-start.23 = (bf16[256,256]{1,0:T(8,128)(2,1)S(1)}, bf16[256,256]{1,0:T(8,128)(2,1)S(1)}, u32[]{:S(2)}, u32[]{:S(2)}) collective-permute-start(bf16[256,256]{1,0:T(8,128)(2,1)S(1)} %get-tuple-element.118), channel_id=1, source_target_pairs={{0,2},{1,3},{2,0},{3,1},{4,6},{5,7},{6,4},{7,5},{8,10},{9,11},{10,... | collective-permute-start | bytes 393224 | tf_op jit(solution)/shard_map/ppermute | solution.py:77
  105.7 6.2 %collective-permute-start.22 = (bf16[256,256]{1,0:T(8,128)(2,1)S(1)}, bf16[256,256]{1,0:T(8,128)(2,1)S(1)}, u32[]{:S(2)}, u32[]{:S(2)}) collective-permute-start(bf16[256,256]{1,0:T(8,128)(2,1)S(1)} %get-tuple-element.118), channel_id=1, source_target_pairs={{0,3},{1,0},{2,1},{3,2},{4,7},{5,4},{6,5},{7,6},{8,11},{9,8},{10,9... | collective-permute-start | bytes 393224 | tf_op jit(solution)/shard_map/ppermute | solution.py:77
  112.3 4.1 %collective-permute-start.25 = (f32[520,256]{1,0:T(8,128)S(1)}, f32[520,256]{1,0:T(8,128)S(1)}, u32[]{:S(2)}, u32[]{:S(2)}) collective-permute-start(f32[520,256]{1,0:T(8,128)S(1)} %select_maximum_fusion), channel_id=1, source_target_pairs={{0,4},{4,0},{8,12},{12,8},{16,20},{20,16},{24,28},{28,24},{32,36},... | collective-permute-start | bytes 1597448 | tf_op jit(solution)/shard_map/ppermute | solution.py:73
  114.3 1.4 collective-permute-start.26
  122.1 12.3 %copy-start.16 = (bf16[1104,256]{1,0:T(8,128)(2,1)S(1)}, bf16[1104,256]{1,0:T(8,128)(2,1)}, u32[]{:S(2)}) copy-start(bf16[1104,256]{1,0:T(8,128)(2,1)} %get-tuple-element.85) | copy-start | bytes 1695748
  122.2 16.1 %collective-permute-start.27 = (bf16[1104,256]{1,0:T(8,128)(2,1)}, bf16[1104,256]{1,0:T(8,128)(2,1)S(1)}, u32[]{:S(2)}, u32[]{:S(2)}) collective-permute-start(bf16[1104,256]{1,0:T(8,128)(2,1)} %get-tuple-element.84), channel_id=1, source_target_pairs={{4,36},{12,44},{20,52},{28,60},{36,68},{44,76},{52,84},{60,92},{68... | collective-permute-start | bytes 1695752 | tf_op jit(solution)/shard_map/ppermute | solution.py:65
  134.4 3.9 %copy-start.14 = (bf16[1104,256]{1,0:T(8,128)(2,1)S(1)}, bf16[1104,256]{1,0:T(8,128)(2,1)}, u32[]{:S(2)}) copy-start(bf16[1104,256]{1,0:T(8,128)(2,1)} %get-tuple-element.82) | copy-start | bytes 1695748
  134.4 3.8 %copy-start.15 = (bf16[1104,256]{1,0:T(8,128)(2,1)S(1)}, bf16[1104,256]{1,0:T(8,128)(2,1)}, u32[]{:S(2)}) copy-start(bf16[1104,256]{1,0:T(8,128)(2,1)} %get-tuple-element.83) | copy-start | bytes 1695748
  135.7 12.1 %collective-permute-start.29 = (bf16[1104,256]{1,0:T(8,128)(2,1)S(1)}, bf16[1104,256]{1,0:T(8,128)(2,1)S(1)}, u32[]{:S(2)}, u32[]{:S(2)}) collective-permute-start(bf16[1104,256]{1,0:T(8,128)(2,1)S(1)} %broadcast_select_fusion), channel_id=1, source_target_pairs={{0,24},{4,228},{8,0},{12,236},{16,8},{20,244},{24,16},{28,252},{32... | collective-permute-start | bytes 1695752 | tf_op jit(solution)/shard_map/ppermute | solution.py:65
  138.3 10.0 %copy-start.13 = (bf16[1104,256]{1,0:T(8,128)(2,1)S(1)}, bf16[1104,256]{1,0:T(8,128)(2,1)}, u32[]{:S(2)}) copy-start(bf16[1104,256]{1,0:T(8,128)(2,1)} %get-tuple-element.90) | copy-start | bytes 1695748
  138.6 10.1 %copy-start.12 = (bf16[1104,256]{1,0:T(8,128)(2,1)S(1)}, bf16[1104,256]{1,0:T(8,128)(2,1)}, u32[]{:S(2)}) copy-start(bf16[1104,256]{1,0:T(8,128)(2,1)} %get-tuple-element.89) | copy-start | bytes 1695748
  138.6 9.8 %collective-permute-start.28 = (bf16[1104,256]{1,0:T(8,128)(2,1)S(1)}, bf16[1104,256]{1,0:T(8,128)(2,1)S(1)}, u32[]{:S(2)}, u32[]{:S(2)}) collective-permute-start(bf16[1104,256]{1,0:T(8,128)(2,1)S(1)} %fusion.3), channel_id=1, source_target_pairs={{0,8},{4,36},{8,16},{12,44},{16,24},{20,52},{24,0},{28,60},{32,40}... | collective-permute-start | bytes 1695752 | tf_op jit(solution)/shard_map/ppermute | solution.py:65
  148.5 10.0 %copy-start.11 = (bf16[1104,256]{1,0:T(8,128)(2,1)S(1)}, bf16[1104,256]{1,0:T(8,128)(2,1)}, u32[]{:S(2)}) copy-start(bf16[1104,256]{1,0:T(8,128)(2,1)} %get-tuple-element.94) | copy-start | bytes 1695748
  148.5 8.8 %collective-permute-start.31 = (bf16[1104,256]{1,0:T(8,128)(2,1)S(1)}, bf16[1104,256]{1,0:T(8,128)(2,1)S(1)}, u32[]{:S(2)}, u32[]{:S(2)}) collective-permute-start(bf16[1104,256]{1,0:T(8,128)(2,1)S(1)} %add_convert_fusion.2), channel_id=1, source_target_pairs={{0,24},{4,228},{8,0},{12,236},{16,8},{20,244},{24,16},{28,252},{32... | collective-permute-start | bytes 1695752 | tf_op jit(solution)/shard_map/ppermute | solution.py:65
  148.8 10.8 %copy-start.10 = (bf16[1104,256]{1,0:T(8,128)(2,1)S(1)}, bf16[1104,256]{1,0:T(8,128)(2,1)}, u32[]{:S(2)}) copy-start(bf16[1104,256]{1,0:T(8,128)(2,1)} %get-tuple-element.95) | copy-start | bytes 1695748
  148.8 9.8 %collective-permute-start.30 = (bf16[1104,256]{1,0:T(8,128)(2,1)S(1)}, bf16[1104,256]{1,0:T(8,128)(2,1)S(1)}, u32[]{:S(2)}, u32[]{:S(2)}) collective-permute-start(bf16[1104,256]{1,0:T(8,128)(2,1)S(1)} %add_convert_fusion.3), channel_id=1, source_target_pairs={{0,8},{4,36},{8,16},{12,44},{16,24},{20,52},{24,0},{28,60},{32,40}... | collective-permute-start | bytes 1695752 | tf_op jit(solution)/shard_map/ppermute | solution.py:65
  158.8 10.1 %collective-permute-start.32 = (bf16[1104,256]{1,0:T(8,128)(2,1)S(1)}, bf16[1104,256]{1,0:T(8,128)(2,1)S(1)}, u32[]{:S(2)}, u32[]{:S(2)}) collective-permute-start(bf16[1104,256]{1,0:T(8,128)(2,1)S(1)} %add_convert_fusion.1), channel_id=1, source_target_pairs={{0,8},{4,36},{8,16},{12,44},{16,24},{20,52},{24,0},{28,60},{32,40}... | collective-permute-start | bytes 1695752 | tf_op jit(solution)/shard_map/ppermute | solution.py:65
  159.8 9.1 %collective-permute-start.33 = (bf16[1104,256]{1,0:T(8,128)(2,1)S(1)}, bf16[1104,256]{1,0:T(8,128)(2,1)S(1)}, u32[]{:S(2)}, u32[]{:S(2)}) collective-permute-start(bf16[1104,256]{1,0:T(8,128)(2,1)S(1)} %add_convert_fusion), channel_id=1, source_target_pairs={{0,24},{4,228},{8,0},{12,236},{16,8},{20,244},{24,16},{28,252},{32... | collective-permute-start | bytes 1695752 | tf_op jit(solution)/shard_map/ppermute | solution.py:65
  161.8 7.1 %copy-start.1 = (bf16[1104,256]{1,0:T(8,128)(2,1)S(1)}, bf16[1104,256]{1,0:T(8,128)(2,1)}, u32[]{:S(2)}) copy-start(bf16[1104,256]{1,0:T(8,128)(2,1)} %get-tuple-element.93.h1) | copy-start | bytes 1695748
  169.1 5.6 %collective-permute-start.34 = (bf16[288,256]{1,0:T(8,128)(2,1)S(1)}, bf16[288,256]{1,0:T(8,128)(2,1)S(1)}, u32[]{:S(2)}, u32[]{:S(2)}) collective-permute-start(bf16[288,256]{1,0:T(8,128)(2,1)S(1)} %get-tuple-element.104), channel_id=1, source_target_pairs={{0,32},{4,12},{8,40},{12,20},{16,48},{20,28},{24,56},{28,4},{32,64... | collective-permute-start | bytes 442376 | tf_op jit(solution)/shard_map/ppermute | solution.py:65
  171.3 4.3 %collective-permute-start.35 = (bf16[288,256]{1,0:T(8,128)(2,1)S(1)}, bf16[288,256]{1,0:T(8,128)(2,1)S(1)}, u32[]{:S(2)}, u32[]{:S(2)}) collective-permute-start(bf16[288,256]{1,0:T(8,128)(2,1)S(1)} %get-tuple-element.105), channel_id=1, source_target_pairs={{0,224},{4,28},{8,232},{12,4},{16,240},{20,12},{24,248},{28,20},{3... | collective-permute-start | bytes 442376 | tf_op jit(solution)/shard_map/ppermute | solution.py:65
  171.9 5.5 %collective-permute-start.36 = (bf16[288,256]{1,0:T(8,128)(2,1)S(1)}, bf16[288,256]{1,0:T(8,128)(2,1)S(1)}, u32[]{:S(2)}, u32[]{:S(2)}) collective-permute-start(bf16[288,256]{1,0:T(8,128)(2,1)S(1)} %get-tuple-element.106), channel_id=1, source_target_pairs={{0,128},{4,20},{8,136},{12,28},{16,144},{20,4},{24,152},{28,12},{3... | collective-permute-start | bytes 442376 | tf_op jit(solution)/shard_map/ppermute | solution.py:65
  173.1 4.2 %collective-permute-start.37 = (bf16[288,256]{1,0:T(8,128)(2,1)S(1)}, bf16[288,256]{1,0:T(8,128)(2,1)S(1)}, u32[]{:S(2)}, u32[]{:S(2)}) collective-permute-start(bf16[288,256]{1,0:T(8,128)(2,1)S(1)} %get-tuple-element.107), channel_id=1, source_target_pairs={{0,96},{8,104},{16,112},{24,120},{32,128},{40,136},{48,144},{56,15... | collective-permute-start | bytes 442376 | tf_op jit(solution)/shard_map/ppermute | solution.py:65
  173.8 3.6 %collective-permute-start.38 = (bf16[288,256]{1,0:T(8,128)(2,1)S(1)}, bf16[288,256]{1,0:T(8,128)(2,1)S(1)}, u32[]{:S(2)}, u32[]{:S(2)}) collective-permute-start(bf16[288,256]{1,0:T(8,128)(2,1)S(1)} %get-tuple-element.108), channel_id=1, source_target_pairs={{0,160},{8,168},{16,176},{24,184},{32,192},{40,200},{48,208},{56,2... | collective-permute-start | bytes 442376 | tf_op jit(solution)/shard_map/ppermute | solution.py:65
  174.7 2.7 %collective-permute-start.39 = (bf16[288,256]{1,0:T(8,128)(2,1)S(1)}, bf16[288,256]{1,0:T(8,128)(2,1)S(1)}, u32[]{:S(2)}, u32[]{:S(2)}) collective-permute-start(bf16[288,256]{1,0:T(8,128)(2,1)S(1)} %get-tuple-element.109), channel_id=1, source_target_pairs={{0,64},{8,72},{16,80},{24,88},{32,96},{40,104},{48,112},{56,120},{... | collective-permute-start | bytes 442376 | tf_op jit(solution)/shard_map/ppermute | solution.py:65
  175.6 1.8 collective-permute-start.40
  179.0 22.8 %collective-permute-start.41 = (f32[1,256]{1,0:T(1,128)S(1)}, f32[1,256]{1,0:T(1,128)S(1)}, u32[]{:S(2)}, u32[]{:S(2)}) collective-permute-start(f32[1,256]{1,0:T(1,128)S(1)} %get-tuple-element.113), channel_id=1, source_target_pairs={{0,4},{8,12},{16,20},{24,28},{32,36},{40,44},{48,52},{56,60},{64,6... | collective-permute-start | bytes 3080 | tf_op jit(solution)/shard_map/ppermute | solution.py:620
  (7 other events, 11.4 us)

commit v6 on v4

--- a/solution.py
+++ b/solution.py
@@ -23,7 +23,7 @@
 MIB = 1 << 20
 VMEM = 54 * MIB
 
-LOW, HIGH, ACROSS = (0, 1, 7, 4), (2, 3, 6, 5), (0, 1, 3, 2)
+LOW, HIGH, ACROSS = (0, 1, 7, 2), (3, 4, 6, 5), (0, 1, 3, 2)
 GATHER_0 = tuple(
     tuple(k * NZ + j for j in group)
     for k, group in ((0, LOW), (1, LOW), (3, LOW), (2, LOW), (3, HIGH), (1, HIGH), (2, HIGH), (0, HIGH))
@@ -64,7 +64,7 @@
     return lax.ppermute(value, "dom", pairs)
 
 
-Z_UP, Z_DOWN, Z_UP_2, Z_DOWN_2, Z_FOUR = (1, 0), (-1, 0), (2, 0), (-2, 0), (4, 0)
+Z_UP, Z_DOWN, Z_UP_2, Z_DOWN_2 = (1, 0), (-1, 0), (2, 0), (-2, 0)
 X_UP, X_DOWN, X_TWO = (0, 1), (0, -1), (0, 2)
 
 
@@ -101,11 +101,11 @@
     j = (z - (chip >> 2)) & (NZ - 1)
     spot = (k * NZ + j) * 2 + (column & 1)
     mine = live & ((owner & 1) == core)
-    high = ((j >= 2) & (j <= 6)) & (j != 4)
+    high, back = (j >= 3) & (j <= 6), (j >= 2) & (j <= 5)
     on_0 = jnp.where(high & ((k == 1) | (k == 2)), 1, 0)
     on_1 = jnp.where(j == 4, 2, jnp.where((j == 3) | (j == 5), 1, 0))
     forward_call = jnp.where(core == 0, on_0, on_1)
-    backward_call = jnp.where(core == 0, jnp.where(high & ((k == 1) | (k == 2)), 0, 1), jnp.where(j == 4, 0, 1))
+    backward_call = jnp.where(core == 0, jnp.where(back & ((k == 1) | (k == 2)), 0, 1), jnp.where(j == 4, 0, 1))
     square = (2 * SLOTS, 2 * SLOTS)
     first = lax.broadcasted_iota(jnp.int32, square, 0)
     second = lax.broadcasted_iota(jnp.int32, square, 1)
@@ -231,8 +231,8 @@
     chosen = FORWARD_CHUNKS[call]
     chunks, rest = rest[: len(chosen)], rest[len(chosen) :]
     if call:
-        sums_before, weight_before, *rest = rest
-    sums, weight_out, blocks, held, sem, tile_sem = rest
+        own_before, sib_before, weight_before, *rest = rest
+    own_sums, sib_sums, weight_out, blocks, held, sem, tile_sem = rest
     core, x, z, y = place_of(lists)
     tiles = Tiles(lists, 0, call, call == 0, own, sib, held, tile_sem)
     tiles.start()
@@ -259,7 +259,11 @@
                 rights.append(blocks[spot >> 1, pl.ds(first, BLK), :])
             return total + jnp.dot(left, jnp.concatenate(rights, axis=0), preferred_element_type=F32)
 
-        sums[row] = lax.fori_loop(0, steps, step, sums_before[row] if call else jnp.zeros((BLK, WIDTH), F32))
+        sums, at = (own_sums, row) if row < 2 else (sib_sums, row - 2)
+        before = jnp.zeros((BLK, WIDTH), F32)
+        if call:
+            before = own_before[at] if row < 2 else sib_before[at]
+        sums[at] = lax.fori_loop(0, steps, step, before)
     if call:
         weight_out[...] = weight_before[...]
     for condition, spot in arrived:
@@ -281,11 +285,12 @@
     return pl.pallas_call(
         functools.partial(forward_kernel, call),
         out_shape=(
-            jax.ShapeDtypeStruct((4, BLK, WIDTH), F32),
+            jax.ShapeDtypeStruct((2, BLK, WIDTH), F32),
+            jax.ShapeDtypeStruct((2, BLK, WIDTH), F32),
             jax.ShapeDtypeStruct((NY, 2 * NX, W_ROWS, WIDTH), BF16),
         ),
         in_specs=[smem()] + [anywhere()] * (2 + len(chosen)) + [vmem()] * len(before),
-        out_specs=(vmem(),) * 2,
+        out_specs=(vmem(),) * 3,
         scratch_shapes=[
             pltpu.VMEM((NX * NZ, ROWS, WIDTH), BF16),
             pltpu.VMEM((2 * SLOTS + 1, BLK, BLK), BF16),
@@ -376,20 +381,21 @@
     )(lists, own, sib, scaled, weight_sums, bias_rows)
 
 
-def gather(block, core, early, call):
+def gather(block, core, lists, other_tiles, call):
     p1 = shift(block, Z_UP, X_UP)
     p2 = shift(block, Z_DOWN, X_DOWN)
-    p3 = shift(block, Z_FOUR, X_TWO)
-    pa = shift(jnp.stack([block, p1]), Z_UP_2)
-    pb = shift(jnp.stack([block, p2]), Z_DOWN_2)
-    low, pa, pb, *early = lax.optimization_barrier((jnp.stack([block, p1, p2, p3]), pa, pb, *early))
+    p3 = shift(block, Z_UP_2, X_TWO)
+    low, other_tiles = lax.optimization_barrier((jnp.stack([block, p1, p2, p3]), other_tiles))
     c1 = shift(low, X_UP, Z_UP)
     c2 = shift(low, X_DOWN, Z_DOWN)
+    pa = shift(jnp.stack([low[1], low[3]]), Z_UP_2)
+    pb = shift(jnp.stack([low[0], low[2]]), Z_DOWN_2)
+    c1, c2, pa, pb = lax.optimization_barrier((c1, c2, pa, pb))
     high = jnp.concatenate([pa, pb], axis=0)
-    c1, c2 = lax.optimization_barrier((c1, c2))
     c3 = shift(c1, X_UP, Z_UP)
     c4 = shift(jnp.where(core == 0, high, c2), X_DOWN, Z_DOWN)
-    c3, c4 = lax.optimization_barrier((c3, c4))
+    c3, c4, lists = lax.optimization_barrier((c3, c4, lists))
+    early = lists, other_tiles
     chunks = [low, c1, c2, c3, c4, None, None, high]
     sums = call(0, early, chunks, ())
     c5 = shift(jnp.where(core == 0, high, c3), X_UP, Z_UP)
@@ -465,23 +471,23 @@
 
 def message_kernel(line_bias, h1, jc1, jc2, ra, rb, m1, m2, m3, rest):
     own = rows_of(line_bias[...])
-    rest[...] = block_sum(0, h1, jc1, jc2) + block_sum(0, ra, rb)
+    rest[...] = block_sum(0, h1, jc1, jc2) + block_sum(0, rb)
     relayed = [chunk[2 * ROWS : 2 * ROWS + BIAS_ROWS, :].astype(F32)[0:3] for chunk in (ra, rb)]
-    m1[0:ROWS, :] = (block_sum(1, h1, jc1, jc2) + block_sum(1, ra)).astype(BF16)
+    m1[0:ROWS, :] = (block_sum(1, h1, jc1, jc2) + block_sum(0, ra)).astype(BF16)
     m1[ROWS:, :] = bias_block(own + [relayed[0]])
     m2[0:ROWS, :] = (block_sum(2, h1, jc1, jc2) + block_sum(1, rb)).astype(BF16)
     m2[ROWS:, :] = bias_block(own + [relayed[1]])
-    m3[0:ROWS, :] = block_sum(3, h1, jc1, jc2).astype(BF16)
-    m3[ROWS:, :] = bias_block(own)
-
-
-def last_kernel(lists, line_bias, rest, r1, r2, r3, ra, rb, scaled, feats_grad, weight_grad, bias, held):
+    m3[0:ROWS, :] = (block_sum(3, h1, jc1, jc2) + block_sum(1, ra)).astype(BF16)
+    m3[ROWS:, :] = bias_block(own + [relayed[0]])
+
+
+def last_kernel(lists, line_bias, rest, r1, r2, r3, rb, scaled, feats_grad, weight_grad, bias, held):
     total = rest[...] + block_sum(0, r1, r2, r3)
     feats_grad[...] = (scaled[...].astype(F32) + total[0:NODES]).astype(BF16)
     weight_grad[...] = total[NODES:ROWS]
     t1, t2, t3 = (chunk[ROWS:, :] for chunk in (r1, r2, r3))
-    ta, tb = (chunk[2 * ROWS :, :] for chunk in (ra, rb))
-    values = [line_bias[...], joined(t1), joined(ta), joined(t1, 3), joined(t3), joined(t2, 3), joined(tb), joined(t2)]
+    tb = rb[2 * ROWS :, :]
+    values = [line_bias[...], joined(t1), joined(t3), joined(t1, 3), joined(t3, 3), joined(t2, 3), joined(tb), joined(t2)]
     bias[...] = in_order(values, lists[6, 2], held)
 
 
@@ -514,9 +520,9 @@
     )
     jc1 = shift(add(q1, jnp.where(core == 0, zero, jb1)).astype(BF16), X_UP, Z_UP)
     jc2 = shift(add(q2, jb2).astype(BF16), X_DOWN, Z_DOWN)
-    jc1, jc2, pair_a, pair_b = lax.optimization_barrier((jc1, jc2, pair_a, pair_b))
     ra = shift(pair_a, Z_UP_2)
     rb = shift(pair_b, Z_DOWN_2)
+    jc1, jc2, ra, rb = lax.optimization_barrier((jc1, jc2, ra, rb))
     size = (ROWS + BIAS_ROWS, WIDTH)
     m1, m2, m3, rest = small_call(
         message_kernel,
@@ -527,12 +533,12 @@
     )
     r1 = shift(m1, Z_UP, X_UP)
     r2 = shift(m2, Z_DOWN, X_DOWN)
-    r3 = shift(m3, Z_FOUR, X_TWO)
+    r3 = shift(m3, Z_UP_2, X_TWO)
     return small_call(
         last_kernel,
         (((NODES, WIDTH), BF16), ((W_ROWS, WIDTH), F32), ((1, WIDTH), F32)),
         lists,
-        (line_bias, rest, r1, r2, r3, ra, rb, scaled),
+        (line_bias, rest, r1, r2, r3, rb, scaled),
         1,
     )
 
@@ -568,13 +574,14 @@
     ).reshape(NODES, 1)
 
     other_tiles = swap(tile_values, 1)
-    sums, weight_lane = gather(
+    sums, other_sums, weight_lane = gather(
         jnp.concatenate([feats, weight.T], axis=0),
         core,
-        (lists, other_tiles),
+        lists,
+        other_tiles,
         lambda call, early, chunks, before: forward(call, early[0], tile_values, early[1], chunks, before),
     )
-    neighbour_sum = (sums[:2] + swap(sums[2:], 1)).reshape(NODES, WIDTH)
+    neighbour_sum = (sums + swap(other_sums, 1)).reshape(NODES, WIDTH)
     weight_other = swap(weight_lane, 1)
     mixed = ((feats.astype(F32) + neighbour_sum) / degree).astype(BF16)
 

time: 200 us -> 190 us (0.950)
  waiting for transfers between devices: 79.4 us -> 68.2 us
  starting transfers between devices: 57.9 us -> 67.2 us
  Pallas kernels: 44.3 us -> 35.4 us
    ppermute x25, starting transfers between devices: 28.4 us -> 43.1 us  [shift(): return lax.ppermute(value, 'dom', pairs)]
    ppermute x1, waiting for transfers between devices: 17.9 us -> 9.68 us  [on_device(): lax.ppermute(bias_sum, 'dom', [(i, i + 1) for i in range(0, NZ * NX * 2,...]
    ppermute x6, starting transfers between devices: 18.3 us -> 13.1 us  [swap(): lax.ppermute(value, 'dom', [(i, i ^ bit) for i in range(NZ * NX * 2)])]
    pallas_call x2, Pallas kernels: 18.6 us -> 13.9 us  [backward(): pl.pallas_call(functools.partial(backward_kernel, call), out_shape=tuple(...]
    pallas_call x3, Pallas kernels: 21.2 us -> 17 us  [forward(): pl.pallas_call(functools.partial(forward_kernel, call), out_shape=(jax.Sh...]
    ppermute x25, waiting for transfers between devices: 49.8 us -> 46 us  [shift(): return lax.ppermute(value, 'dom', pairs)]
  transfers between devices with their start and end apart: 38 -> 38, of which waited for: 22 -> 19; matrix products, arithmetic and copies ran while one was open for 5% -> 5% of each run, Pallas kernels for 16% -> 13%
where the time goes in v6:
time: 190 us
  waiting for transfers between devices  68.2 us (36%)
  starting transfers between devices  67.2 us (35%)
  Pallas kernels  35.4 us (19%)
  other arithmetic  9.83 us (5%)
  local copies, waits for them, and re-layouts  4.33 us (2%)
  matrix products  2.47 us (1%)
  between operations  2.12 us (1%)
    ppermute x25, waiting for transfers between devices, shift(): return lax.ppermute(value, 'dom', pairs)  46 us
    ppermute x25, starting transfers between devices, shift(): return lax.ppermute(value, 'dom', pairs)  43.1 us
    pallas_call x3, Pallas kernels, forward(): pl.pallas_call(functools.partial(forward_kernel, call), out_shape=(jax.Sh...  17 us
    pallas_call x2, Pallas kernels, backward(): pl.pallas_call(functools.partial(backward_kernel, call), out_shape=tuple(...  13.9 us
    ppermute x6, starting transfers between devices, swap(): lax.ppermute(value, 'dom', [(i, i ^ bit) for i in range(NZ * NX * 2)])  13.1 us
    ppermute x1, waiting for transfers between devices, on_device(): lax.ppermute(bias_sum, 'dom', [(i, i + 1) for i in range(0, NZ * NX * 2,...  9.68 us
    ppermute x6, starting transfers between devices, y_shift(): return lax.ppermute(value, 'feat', [(y, (y + dy) % NY) for y in range(NY)])  9.61 us
    ppermute x6, waiting for transfers between devices, y_shift(): return lax.ppermute(value, 'feat', [(y, (y + dy) % NY) for y in range(NY)])  9.4 us
  transfers between devices with their start and end apart: 38, of which 19 were waited for; matrix products, arithmetic and copies ran while one was open for 5% of the time, Pallas kernels for 13%

profile of v6, /device:TPU:1, one launch (start us, length us, event | category | flops | bytes accessed | tf_op | source)
XLA Modules:
  0.0 189.5 jit_solution(11600128965876376407)
XLA Ops:
  0.6 3.3 %collective-permute-start.3 = (bf16[128,128,128]{2,1,0:T(8,128)(2,1)}, bf16[128,128,128]{2,1,0:T(8,128)(2,1)}, u32[]{:S(2)}, u32[]{:S(2)}) collective-permute-start(bf16[128,128,128]{2,1,0:T(8,128)(2,1)} %own.9), channel_id=1, source_target_pairs={{0,4},{4,0},{8,12},{12,8},{16,20},{20,16},{24,28},{28,24},{32,36},... | collective-permute-start | bytes 12582920 | tf_op jit(solution)/shard_map/ppermute | solution.py:72
  4.0 0.9 fusion.17
  4.9 0.8 collective-permute-start.1
  5.7 0.7 collective-permute-start
  6.4 1.0 collective-permute-start.2
  7.5 1.7 collective-permute-done.1
  9.2 3.2 %collective-permute-done = bf16[272,256]{1,0:T(8,128)(2,1)S(1)} collective-permute-done((bf16[272,256]{1,0:T(8,128)(2,1)S(1)}, bf16[272,256]{1,0:T(8,128)(2,1)S(1)}, u32[]{:S(2)}, u32[]{:S(2)}) %collective-permute-start) | collective-permute-done | bytes 139296 | tf_op jit(solution)/shard_map/ppermute | solution.py:64
  12.4 5.8 %collective-permute-start.5 = (bf16[4,272,256]{2,1,0:T(8,128)(2,1)S(1)}, bf16[4,272,256]{2,1,0:T(8,128)(2,1)S(1)}, u32[]{:S(2)}, u32[]{:S(2)}) collective-permute-start(bf16[4,272,256]{2,1,0:T(8,128)(2,1)S(1)} %pad_maximum_fusion.1.rest_0_), channel_id=1, source_target_pairs={{0,24},{4,228},{8,0},{12,236},{16,8},{20,244},{24,16},{28,252},{32... | collective-permute-start | bytes 1671176 | tf_op jit(solution)/shard_map/ppermute | solution.py:64
  18.3 0.7 collective-permute-start.6
  19.0 0.7 collective-permute-start.7
  19.8 4.9 %collective-permute-done.5.rest_2_ = bf16[4,272,256]{2,1,0:T(8,128)(2,1)S(1)} collective-permute-done((bf16[4,272,256]{2,1,0:T(8,128)(2,1)S(1)}, bf16[4,272,256]{2,1,0:T(8,128)(2,1)S(1)}, u32[]{:S(2)}, u32[]{:S(2)}) %collective-permute-start.5) | collective-permute-done | bytes 557088 | tf_op jit(solution)/shard_map/ppermute | solution.py:64
  24.7 6.8 %collective-permute-done.4.rest_1_ = bf16[4,272,256]{2,1,0:T(8,128)(2,1)S(1)} collective-permute-done((bf16[4,272,256]{2,1,0:T(8,128)(2,1)S(1)}, bf16[4,272,256]{2,1,0:T(8,128)(2,1)S(1)}, u32[]{:S(2)}, u32[]{:S(2)}) %collective-permute-start.4) | collective-permute-done | bytes 557088 | tf_op jit(solution)/shard_map/ppermute | solution.py:64
  32.3 0.9 collective-permute-start.8
  34.0 7.6 %collective-permute-start.10 = (s32[3,128]{1,0:T(4,128)S(1)}, s32[3,128]{1,0:T(4,128)S(1)}, u32[]{:S(2)}, u32[]{:S(2)}) collective-permute-start(s32[3,128]{1,0:T(4,128)S(1)} %add_add_fusion.1.own), channel_id=1, source_target_pairs={{0,4},{4,0},{8,12},{12,8},{16,20},{20,16},{24,28},{28,24},{32,36},... | collective-permute-start | bytes 4616 | tf_op jit(solution)/shard_map/ppermute | solution.py:72
  41.7 0.8 collective-permute-done.10.sib
  43.1 1.2 stack.83.place
  44.3 1.8 shard_map.114.lists
  46.2 2.7 %collective-permute-start.11 = (bf16[4,272,256]{2,1,0:T(8,128)(2,1)S(1)}, bf16[4,272,256]{2,1,0:T(8,128)(2,1)S(1)}, u32[]{:S(2)}, u32[]{:S(2)}) collective-permute-start(bf16[4,272,256]{2,1,0:T(8,128)(2,1)S(1)} %broadcast_select_fusion.1), channel_id=1, source_target_pairs={{0,8},{4,36},{8,16},{12,44},{16,24},{20,52},{24,0},{28,60},{32,40}... | collective-permute-start | bytes 1671176 | tf_op jit(solution)/shard_map/ppermute | solution.py:64
  48.9 3.1 %collective-permute-start.12 = (bf16[4,272,256]{2,1,0:T(8,128)(2,1)S(1)}, bf16[4,272,256]{2,1,0:T(8,128)(2,1)S(1)}, u32[]{:S(2)}, u32[]{:S(2)}) collective-permute-start(bf16[4,272,256]{2,1,0:T(8,128)(2,1)S(1)} %collective-permute-done.9.rest_4_), channel_id=1, source_target_pairs={{0,24},{4,228},{8,0},{12,236},{16,8},{20,244},{24,16},{28,252},{32... | collective-permute-start | bytes 1671176 | tf_op jit(solution)/shard_map/ppermute | solution.py:64
  52.0 7.9 %shard_map.115 = (f32[2,128,256]{2,1,0:T(8,128)}, f32[2,128,256]{2,1,0:T(8,128)}, bf16[4,8,16,256]{3,2,1,0:T(8,128)(2,1)}) custom-call(s32[8,256]{1,0:T(8,128)} %shard_map.114.lists, bf16[128,128,128]{2,1,0:T(8,128)(2,1)} %own.9, bf16[128,128,128]{2,1,0:T(8,128)(2,1)} %collective-permute-done.3.sib, bf16[4,272,256]{2,1,0:T(8,128)(2,1)} %copy-done.5, ...), custom_call_target="tpu_custom_call" | custom-call | flops 805306368 | bytes 6291456 | tf_op jit(solution)/shard_map/pallas_call | solution.py:285
  60.0 1.9 %collective-permute-start.13 = (bf16[2,272,256]{2,1,0:T(8,128)(2,1)S(1)}, bf16[2,272,256]{2,1,0:T(8,128)(2,1)S(1)}, u32[]{:S(2)}, u32[]{:S(2)}) collective-permute-start(bf16[2,272,256]{2,1,0:T(8,128)(2,1)S(1)} %slice.60), channel_id=1, source_target_pairs={{4,36},{12,44},{20,52},{28,60},{36,68},{44,76},{52,84},{60,92},{68... | collective-permute-start | bytes 835592 | tf_op jit(solution)/shard_map/ppermute | solution.py:64
  62.0 4.5 %collective-permute-start.14 = (bf16[2,272,256]{2,1,0:T(8,128)(2,1)S(1)}, bf16[2,272,256]{2,1,0:T(8,128)(2,1)S(1)}, u32[]{:S(2)}, u32[]{:S(2)}) collective-permute-start(bf16[2,272,256]{2,1,0:T(8,128)(2,1)S(1)} %slice.61), channel_id=1, source_target_pairs={{4,228},{12,236},{20,244},{28,252},{36,4},{44,12},{52,20},{60,28},... | collective-permute-start | bytes 835592 | tf_op jit(solution)/shard_map/ppermute | solution.py:64
  66.5 1.2 convert_reduce_fusion
  67.7 4.8 %shard_map.116 = (f32[2,128,256]{2,1,0:T(8,128)}, f32[2,128,256]{2,1,0:T(8,128)}, bf16[4,8,16,256]{3,2,1,0:T(8,128)(2,1)}) custom-call(s32[8,256]{1,0:T(8,128)} %shard_map.114.lists, bf16[128,128,128]{2,1,0:T(8,128)(2,1)} %own.9, bf16[128,128,128]{2,1,0:T(8,128)(2,1)} %collective-permute-done.3.sib, bf16[4,272,256]{2,1,0:T(8,128)(2,1)} %copy-done.8, ...), custom_call_target="tpu_custom_call" | custom-call | flops 268435456 | bytes 2097152 | tf_op jit(solution)/shard_map/pallas_call | solution.py:285
  73.3 4.3 %shard_map.117 = (f32[2,128,256]{2,1,0:T(8,128)}, f32[2,128,256]{2,1,0:T(8,128)}, bf16[4,8,16,256]{3,2,1,0:T(8,128)(2,1)}) custom-call(s32[8,256]{1,0:T(8,128)} %shard_map.114.lists, bf16[128,128,128]{2,1,0:T(8,128)(2,1)} %own.9, bf16[128,128,128]{2,1,0:T(8,128)(2,1)} %collective-permute-done.3.sib, bf16[2,272,256]{2,1,0:T(8,128)(2,1)} %copy-done.20, ...), custom_call_target="tpu_custom_call" | custom-call | flops 268435456 | bytes 2097152 | tf_op jit(solution)/shard_map/pallas_call | solution.py:285
  78.4 1.0 collective-permute-done.16
  79.4 1.0 select_bitcast_fusion.1
  80.6 0.8 copy-done.22
  82.3 3.0 %collective-permute-start.18 = (bf16[256,256]{1,0:T(8,128)(2,1)S(1)}, bf16[256,256]{1,0:T(8,128)(2,1)S(1)}, u32[]{:S(2)}, u32[]{:S(2)}) collective-permute-start(bf16[256,256]{1,0:T(8,128)(2,1)S(1)} %convolution_convert_fusion.1), channel_id=1, source_target_pairs={{0,2},{1,3},{2,0},{3,1},{4,6},{5,7},{6,4},{7,5},{8,10},{9,11},{10,... | collective-permute-start | bytes 393224 | tf_op jit(solution)/shard_map/ppermute | solution.py:76
  85.3 0.8 collective-permute-start.19
  86.0 0.7 collective-permute-start.17
  87.0 1.9 collective-permute-done.18
  88.8 3.2 %collective-permute-done.19 = bf16[256,256]{1,0:T(8,128)(2,1)S(1)} collective-permute-done((bf16[256,256]{1,0:T(8,128)(2,1)S(1)}, bf16[256,256]{1,0:T(8,128)(2,1)S(1)}, u32[]{:S(2)}, u32[]{:S(2)}) %collective-permute-start.19) | collective-permute-done | bytes 131104 | tf_op jit(solution)/shard_map/ppermute | solution.py:76
  92.0 0.8 fusion.18
  93.0 1.5 collective-permute-start.22
  94.5 2.6 %collective-permute-start.21 = (bf16[256,256]{1,0:T(8,128)(2,1)S(1)}, bf16[256,256]{1,0:T(8,128)(2,1)S(1)}, u32[]{:S(2)}, u32[]{:S(2)}) collective-permute-start(bf16[256,256]{1,0:T(8,128)(2,1)S(1)} %get-tuple-element.112), channel_id=1, source_target_pairs={{0,2},{1,3},{2,0},{3,1},{4,6},{5,7},{6,4},{7,5},{8,10},{9,11},{10,... | collective-permute-start | bytes 393224 | tf_op jit(solution)/shard_map/ppermute | solution.py:76
  97.1 1.1 collective-permute-start.20
  98.7 4.4 %collective-permute-done.21 = bf16[256,256]{1,0:T(8,128)(2,1)S(1)} collective-permute-done((bf16[256,256]{1,0:T(8,128)(2,1)S(1)}, bf16[256,256]{1,0:T(8,128)(2,1)S(1)}, u32[]{:S(2)}, u32[]{:S(2)}) %collective-permute-start.21) | collective-permute-done | bytes 131104 | tf_op jit(solution)/shard_map/ppermute | solution.py:76
  103.8 1.4 collective-permute-start.23
  105.9 1.3 collective-permute-done.24
  107.2 0.7 pad_maximum_fusion.4
  108.0 0.8 fusion.4.weight_sums
  109.4 4.2 %shard_map.119 = (bf16[1104,256]{1,0:T(8,128)(2,1)}, bf16[1104,256]{1,0:T(8,128)(2,1)}, bf16[1104,256]{1,0:T(8,128)(2,1)}) custom-call(s32[8,256]{1,0:T(8,128)} %shard_map.114.lists, bf16[128,128,128]{2,1,0:T(8,128)(2,1)} %own.9, bf16[128,128,128]{2,1,0:T(8,128)(2,1)} %collective-permute-done.3.sib, bf16[4,128,256]{2,1,0:T(8,128)(2,1)} %bitcast.79, ...), custom_call_target="tpu_custom_call" | custom-call | flops 402653184 | bytes 3145728 | tf_op jit(solution)/shard_map/pallas_call | solution.py:367
  113.7 2.1 %collective-permute-start.25 = (bf16[1104,256]{1,0:T(8,128)(2,1)}, bf16[1104,256]{1,0:T(8,128)(2,1)S(1)}, u32[]{:S(2)}, u32[]{:S(2)}) collective-permute-start(bf16[1104,256]{1,0:T(8,128)(2,1)} %get-tuple-element.82), channel_id=1, source_target_pairs={{4,36},{12,44},{20,52},{28,60},{36,68},{44,76},{52,84},{60,92},{68... | collective-permute-start | bytes 1695752 | tf_op jit(solution)/shard_map/ppermute | solution.py:64
  115.7 9.7 %shard_map.118 = (bf16[1104,256]{1,0:T(8,128)(2,1)}, bf16[1104,256]{1,0:T(8,128)(2,1)}, bf16[1104,256]{1,0:T(8,128)(2,1)}, bf16[1104,256]{1,0:T(8,128)(2,1)}, bf...) custom-call(s32[8,256]{1,0:T(8,128)} %shard_map.114.lists, ...), custom_call_target="tpu_custom_call" | custom-call | flops 1073741824 | bytes 8388608 | tf_op jit(solution)/shard_map/pallas_call | solution.py:367
  125.5 1.2 broadcast_select_fusion
  126.7 3.5 %collective-permute-start.27 = (bf16[1104,256]{1,0:T(8,128)(2,1)S(1)}, bf16[1104,256]{1,0:T(8,128)(2,1)S(1)}, u32[]{:S(2)}, u32[]{:S(2)}) collective-permute-start(bf16[1104,256]{1,0:T(8,128)(2,1)S(1)} %broadcast_select_fusion), channel_id=1, source_target_pairs={{0,24},{4,228},{8,0},{12,236},{16,8},{20,244},{24,16},{28,252},{32... | collective-permute-start | bytes 1695752 | tf_op jit(solution)/shard_map/ppermute | solution.py:64
  130.6 6.2 %collective-permute-done.27.ja2 = bf16[1104,256]{1,0:T(8,128)(2,1)S(1)} collective-permute-done((bf16[1104,256]{1,0:T(8,128)(2,1)S(1)}, bf16[1104,256]{1,0:T(8,128)(2,1)S(1)}, u32[]{:S(2)}, u32[]{:S(2)}) %collective-permute-start.27) | collective-permute-done | bytes 565280 | tf_op jit(solution)/shard_map/ppermute | solution.py:64
  136.8 4.0 %collective-permute-done.26.ja1 = bf16[1104,256]{1,0:T(8,128)(2,1)S(1)} collective-permute-done((bf16[1104,256]{1,0:T(8,128)(2,1)S(1)}, bf16[1104,256]{1,0:T(8,128)(2,1)S(1)}, u32[]{:S(2)}, u32[]{:S(2)}) %collective-permute-start.26) | collective-permute-done | bytes 565280 | tf_op jit(solution)/shard_map/ppermute | solution.py:64
  141.0 1.5 collective-permute-start.29
  142.9 7.0 %collective-permute-done.29 = bf16[1104,256]{1,0:T(8,128)(2,1)S(1)} collective-permute-done((bf16[1104,256]{1,0:T(8,128)(2,1)S(1)}, bf16[1104,256]{1,0:T(8,128)(2,1)S(1)}, u32[]{:S(2)}, u32[]{:S(2)}) %collective-permute-start.29) | collective-permute-done | bytes 565280 | tf_op jit(solution)/shard_map/ppermute | solution.py:64
  149.9 2.6 %collective-permute-done.28.jb1 = bf16[1104,256]{1,0:T(8,128)(2,1)S(1)} collective-permute-done((bf16[1104,256]{1,0:T(8,128)(2,1)S(1)}, bf16[1104,256]{1,0:T(8,128)(2,1)S(1)}, u32[]{:S(2)}, u32[]{:S(2)}) %collective-permute-start.28) | collective-permute-done | bytes 565280 | tf_op jit(solution)/shard_map/ppermute | solution.py:64
  153.0 2.7 %collective-permute-start.31 = (bf16[1104,256]{1,0:T(8,128)(2,1)S(1)}, bf16[1104,256]{1,0:T(8,128)(2,1)S(1)}, u32[]{:S(2)}, u32[]{:S(2)}) collective-permute-start(bf16[1104,256]{1,0:T(8,128)(2,1)S(1)} %add_convert_fusion), channel_id=1, source_target_pairs={{0,24},{4,228},{8,0},{12,236},{16,8},{20,244},{24,16},{28,252},{32... | collective-permute-start | bytes 1695752 | tf_op jit(solution)/shard_map/ppermute | solution.py:64
  155.8 1.0 shard_map.120
  156.7 0.7 collective-permute-start.32
  157.4 0.7 collective-permute-start.33
  158.1 5.8 %collective-permute-done.30.jc1 = bf16[1104,256]{1,0:T(8,128)(2,1)S(1)} collective-permute-done((bf16[1104,256]{1,0:T(8,128)(2,1)S(1)}, bf16[1104,256]{1,0:T(8,128)(2,1)S(1)}, u32[]{:S(2)}, u32[]{:S(2)}) %collective-permute-start.30) | collective-permute-done | bytes 565280 | tf_op jit(solution)/shard_map/ppermute | solution.py:64
  164.2 6.9 %collective-permute-start.34 = (bf16[288,256]{1,0:T(8,128)(2,1)S(1)}, bf16[288,256]{1,0:T(8,128)(2,1)S(1)}, u32[]{:S(2)}, u32[]{:S(2)}) collective-permute-start(bf16[288,256]{1,0:T(8,128)(2,1)S(1)} %get-tuple-element.102), channel_id=1, source_target_pairs={{0,32},{4,12},{8,40},{12,20},{16,48},{20,28},{24,56},{28,4},{32,64... | collective-permute-start | bytes 442376 | tf_op jit(solution)/shard_map/ppermute | solution.py:64
  171.1 1.9 collective-permute-start.36
  173.2 1.9 collective-permute-done.35.r2
  175.1 1.5 collective-permute-done.36.r3
  176.6 1.4 shard_map.122
  178.0 1.3 collective-permute-start.37
  179.3 9.7 %collective-permute-done.37 = f32[1,256]{1,0:T(1,128)S(1)} collective-permute-done((f32[1,256]{1,0:T(1,128)S(1)}, f32[1,256]{1,0:T(1,128)S(1)}, u32[]{:S(2)}, u32[]{:S(2)}) %collective-permute-start.37) | collective-permute-done | bytes 1056 | tf_op jit(solution)/shard_map/ppermute | solution.py:631
  (136 shorter events, 9.5 us)
Async XLA Ops:
  0.6 11.8 %collective-permute-start.3 = (bf16[128,128,128]{2,1,0:T(8,128)(2,1)}, bf16[128,128,128]{2,1,0:T(8,128)(2,1)}, u32[]{:S(2)}, u32[]{:S(2)}) collective-permute-start(bf16[128,128,128]{2,1,0:T(8,128)(2,1)} %own.9), channel_id=1, source_target_pairs={{0,4},{4,0},{8,12},{12,8},{16,20},{20,16},{24,28},{28,24},{32,36},... | collective-permute-start | bytes 12582920 | tf_op jit(solution)/shard_map/ppermute | solution.py:72
  4.9 4.3 %collective-permute-start.1 = (bf16[272,256]{1,0:T(8,128)(2,1)S(1)}, bf16[272,256]{1,0:T(8,128)(2,1)S(1)}, u32[]{:S(2)}, u32[]{:S(2)}) collective-permute-start(bf16[272,256]{1,0:T(8,128)(2,1)S(1)} %get-tuple-element.126), channel_id=1, source_target_pairs={{0,224},{4,28},{8,232},{12,4},{16,240},{20,12},{24,248},{28,20},{3... | collective-permute-start | bytes 417800 | tf_op jit(solution)/shard_map/ppermute | solution.py:64
  5.7 6.6 %collective-permute-start = (bf16[272,256]{1,0:T(8,128)(2,1)S(1)}, bf16[272,256]{1,0:T(8,128)(2,1)S(1)}, u32[]{:S(2)}, u32[]{:S(2)}) collective-permute-start(bf16[272,256]{1,0:T(8,128)(2,1)S(1)} %get-tuple-element.126), channel_id=1, source_target_pairs={{0,32},{4,12},{8,40},{12,20},{16,48},{20,28},{24,56},{28,4},{32,64... | collective-permute-start | bytes 417800 | tf_op jit(solution)/shard_map/ppermute | solution.py:64
  6.4 5.9 %collective-permute-start.2 = (bf16[272,256]{1,0:T(8,128)(2,1)S(1)}, bf16[272,256]{1,0:T(8,128)(2,1)S(1)}, u32[]{:S(2)}, u32[]{:S(2)}) collective-permute-start(bf16[272,256]{1,0:T(8,128)(2,1)S(1)} %get-tuple-element.126), channel_id=1, source_target_pairs={{0,64},{4,20},{8,72},{12,28},{16,80},{20,4},{24,88},{28,12},{32,96... | collective-permute-start | bytes 417800 | tf_op jit(solution)/shard_map/ppermute | solution.py:64
  12.4 7.3 %copy-start.5 = (bf16[4,272,256]{2,1,0:T(8,128)(2,1)}, bf16[4,272,256]{2,1,0:T(8,128)(2,1)S(1)}, u32[]{:S(2)}) copy-start(bf16[4,272,256]{2,1,0:T(8,128)(2,1)S(1)} %pad_maximum_fusion.1.rest_0_) | copy-start | bytes 1671172
  12.4 12.3 %collective-permute-start.5 = (bf16[4,272,256]{2,1,0:T(8,128)(2,1)S(1)}, bf16[4,272,256]{2,1,0:T(8,128)(2,1)S(1)}, u32[]{:S(2)}, u32[]{:S(2)}) collective-permute-start(bf16[4,272,256]{2,1,0:T(8,128)(2,1)S(1)} %pad_maximum_fusion.1.rest_0_), channel_id=1, source_target_pairs={{0,24},{4,228},{8,0},{12,236},{16,8},{20,244},{24,16},{28,252},{32... | collective-permute-start | bytes 1671176 | tf_op jit(solution)/shard_map/ppermute | solution.py:64
  18.2 13.3 %collective-permute-start.4 = (bf16[4,272,256]{2,1,0:T(8,128)(2,1)S(1)}, bf16[4,272,256]{2,1,0:T(8,128)(2,1)S(1)}, u32[]{:S(2)}, u32[]{:S(2)}) collective-permute-start(bf16[4,272,256]{2,1,0:T(8,128)(2,1)S(1)} %pad_maximum_fusion.1.rest_0_), channel_id=1, source_target_pairs={{0,8},{4,36},{8,16},{12,44},{16,24},{20,52},{24,0},{28,60},{32,40}... | collective-permute-start | bytes 1671176 | tf_op jit(solution)/shard_map/ppermute | solution.py:64
  18.3 1.4 collective-permute-start.6
  19.0 0.7 collective-permute-start.7
  24.7 7.0 %copy-start.6 = (bf16[4,272,256]{2,1,0:T(8,128)(2,1)}, bf16[4,272,256]{2,1,0:T(8,128)(2,1)S(1)}, u32[]{:S(2)}) copy-start(bf16[4,272,256]{2,1,0:T(8,128)(2,1)S(1)} %collective-permute-done.5.rest_2_) | copy-start | bytes 1671172
  31.6 2.4 %copy-start.26 = (s32[128]{0:T(128)S(1)}, s32[128]{0:T(128)}, u32[]{:S(2)}) copy-start(s32[128]{0:T(128)} %param.12) | copy-start | bytes 1540
  31.6 2.4 %copy-start.28 = (s32[128]{0:T(128)S(1)}, s32[128]{0:T(128)}, u32[]{:S(2)}) copy-start(s32[128]{0:T(128)} %param.13) | copy-start | bytes 1540
  31.6 14.6 %copy-start.4 = (bf16[4,272,256]{2,1,0:T(8,128)(2,1)}, bf16[4,272,256]{2,1,0:T(8,128)(2,1)S(1)}, u32[]{:S(2)}) copy-start(bf16[4,272,256]{2,1,0:T(8,128)(2,1)S(1)} %constant_dynamic-update-slice_fusion.rest_5_) | copy-start | bytes 1671172
  31.7 14.4 %collective-permute-start.9 = (bf16[4,272,256]{2,1,0:T(8,128)(2,1)S(1)}, bf16[4,272,256]{2,1,0:T(8,128)(2,1)S(1)}, u32[]{:S(2)}, u32[]{:S(2)}) collective-permute-start(bf16[4,272,256]{2,1,0:T(8,128)(2,1)S(1)} %broadcast_select_fusion.2), channel_id=1, source_target_pairs={{0,24},{4,228},{8,0},{12,236},{16,8},{20,244},{24,16},{28,252},{32... | collective-permute-start | bytes 1671176 | tf_op jit(solution)/shard_map/ppermute | solution.py:64
  32.3 13.8 %collective-permute-start.8 = (bf16[4,272,256]{2,1,0:T(8,128)(2,1)S(1)}, bf16[4,272,256]{2,1,0:T(8,128)(2,1)S(1)}, u32[]{:S(2)}, u32[]{:S(2)}) collective-permute-start(bf16[4,272,256]{2,1,0:T(8,128)(2,1)S(1)} %collective-permute-done.4.rest_1_), channel_id=1, source_target_pairs={{0,8},{4,36},{8,16},{12,44},{16,24},{20,52},{24,0},{28,60},{32,40}... | collective-permute-start | bytes 1671176 | tf_op jit(solution)/shard_map/ppermute | solution.py:64
  34.0 10.3 %copy-start.24 = (s32[3,128]{1,0:T(4,128)}, s32[3,128]{1,0:T(4,128)S(1)}, u32[]{:S(2)}) copy-start(s32[3,128]{1,0:T(4,128)S(1)} %add_add_fusion.1.own) | copy-start | bytes 4612
  34.0 8.4 %collective-permute-start.10 = (s32[3,128]{1,0:T(4,128)S(1)}, s32[3,128]{1,0:T(4,128)S(1)}, u32[]{:S(2)}, u32[]{:S(2)}) collective-permute-start(s32[3,128]{1,0:T(4,128)S(1)} %add_add_fusion.1.own), channel_id=1, source_target_pairs={{0,4},{4,0},{8,12},{12,8},{16,20},{20,16},{24,28},{28,24},{32,36},... | collective-permute-start | bytes 4616 | tf_op jit(solution)/shard_map/ppermute | solution.py:72
  42.5 1.8 copy-start.25
  46.1 5.8 %copy-start.18 = (bf16[4,272,256]{2,1,0:T(8,128)(2,1)}, bf16[4,272,256]{2,1,0:T(8,128)(2,1)S(1)}, u32[]{:S(2)}) copy-start(bf16[4,272,256]{2,1,0:T(8,128)(2,1)S(1)} %collective-permute-done.9.rest_4_) | copy-start | bytes 1671172
  46.1 5.8 %copy-start.7 = (bf16[4,272,256]{2,1,0:T(8,128)(2,1)}, bf16[4,272,256]{2,1,0:T(8,128)(2,1)S(1)}, u32[]{:S(2)}) copy-start(bf16[4,272,256]{2,1,0:T(8,128)(2,1)S(1)} %collective-permute-done.8.rest_3_) | copy-start | bytes 1671172
  46.2 13.7 %collective-permute-start.11 = (bf16[4,272,256]{2,1,0:T(8,128)(2,1)S(1)}, bf16[4,272,256]{2,1,0:T(8,128)(2,1)S(1)}, u32[]{:S(2)}, u32[]{:S(2)}) collective-permute-start(bf16[4,272,256]{2,1,0:T(8,128)(2,1)S(1)} %broadcast_select_fusion.1), channel_id=1, source_target_pairs={{0,8},{4,36},{8,16},{12,44},{16,24},{20,52},{24,0},{28,60},{32,40}... | collective-permute-start | bytes 1671176 | tf_op jit(solution)/shard_map/ppermute | solution.py:64
  48.9 11.0 %collective-permute-start.12 = (bf16[4,272,256]{2,1,0:T(8,128)(2,1)S(1)}, bf16[4,272,256]{2,1,0:T(8,128)(2,1)S(1)}, u32[]{:S(2)}, u32[]{:S(2)}) collective-permute-start(bf16[4,272,256]{2,1,0:T(8,128)(2,1)S(1)} %collective-permute-done.9.rest_4_), channel_id=1, source_target_pairs={{0,24},{4,228},{8,0},{12,236},{16,8},{20,244},{24,16},{28,252},{32... | collective-permute-start | bytes 1671176 | tf_op jit(solution)/shard_map/ppermute | solution.py:64
  52.0 14.6 %copy-start.3 = (bf16[128,128,128]{2,1,0:T(8,128)(2,1)S(1)}, bf16[128,128,128]{2,1,0:T(8,128)(2,1)}, u32[]{:S(2)}) copy-start(bf16[128,128,128]{2,1,0:T(8,128)(2,1)} %own.9) | copy-start | bytes 12582916
  59.9 7.8 %copy-start.8 = (bf16[4,272,256]{2,1,0:T(8,128)(2,1)}, bf16[4,272,256]{2,1,0:T(8,128)(2,1)S(1)}, u32[]{:S(2)}) copy-start(bf16[4,272,256]{2,1,0:T(8,128)(2,1)S(1)} %collective-permute-done.11.rest_0_) | copy-start | bytes 1671172
  59.9 7.8 %copy-start.9 = (bf16[4,272,256]{2,1,0:T(8,128)(2,1)}, bf16[4,272,256]{2,1,0:T(8,128)(2,1)S(1)}, u32[]{:S(2)}) copy-start(bf16[4,272,256]{2,1,0:T(8,128)(2,1)S(1)} %collective-permute-done.12.rest_1_) | copy-start | bytes 1671172
  60.0 12.5 %collective-permute-start.13 = (bf16[2,272,256]{2,1,0:T(8,128)(2,1)S(1)}, bf16[2,272,256]{2,1,0:T(8,128)(2,1)S(1)}, u32[]{:S(2)}, u32[]{:S(2)}) collective-permute-start(bf16[2,272,256]{2,1,0:T(8,128)(2,1)S(1)} %slice.60), channel_id=1, source_target_pairs={{4,36},{12,44},{20,52},{28,60},{36,68},{44,76},{52,84},{60,92},{68... | collective-permute-start | bytes 835592 | tf_op jit(solution)/shard_map/ppermute | solution.py:64
  62.0 10.6 %collective-permute-start.14 = (bf16[2,272,256]{2,1,0:T(8,128)(2,1)S(1)}, bf16[2,272,256]{2,1,0:T(8,128)(2,1)S(1)}, u32[]{:S(2)}, u32[]{:S(2)}) collective-permute-start(bf16[2,272,256]{2,1,0:T(8,128)(2,1)S(1)} %slice.61), channel_id=1, source_target_pairs={{4,228},{12,236},{20,244},{28,252},{36,4},{44,12},{52,20},{60,28},... | collective-permute-start | bytes 835592 | tf_op jit(solution)/shard_map/ppermute | solution.py:64
  77.6 1.8 collective-permute-start.16
  77.8 2.7 %collective-permute-start.15 = (f32[2,128,256]{2,1,0:T(8,128)}, f32[2,128,256]{2,1,0:T(8,128)S(1)}, u32[]{:S(2)}, u32[]{:S(2)}) collective-permute-start(f32[2,128,256]{2,1,0:T(8,128)} %get-tuple-element.77), channel_id=1, source_target_pairs={{0,4},{4,0},{8,12},{12,8},{16,20},{20,16},{24,28},{28,24},{32,36},... | collective-permute-start | bytes 786440 | tf_op jit(solution)/shard_map/ppermute | solution.py:72
  80.4 0.9 copy-start.22
  80.5 1.0 copy-start.19
  81.4 10.5 %copy-start.23 = (bf16[256,256]{1,0:T(8,128)(2,1)S(1)}, bf16[256,256]{1,0:T(8,128)(2,1)}, u32[]{:S(2)}) copy-start(bf16[256,256]{1,0:T(8,128)(2,1)} %param.15) | copy-start | bytes 393220
  81.5 10.5 %copy-start.27 = (f32[256]{0:T(256)S(1)}, f32[256]{0:T(256)}, u32[]{:S(2)}) copy-start(f32[256]{0:T(256)} %param.10) | copy-start | bytes 3076
  82.3 6.5 %collective-permute-start.18 = (bf16[256,256]{1,0:T(8,128)(2,1)S(1)}, bf16[256,256]{1,0:T(8,128)(2,1)S(1)}, u32[]{:S(2)}, u32[]{:S(2)}) collective-permute-start(bf16[256,256]{1,0:T(8,128)(2,1)S(1)} %convolution_convert_fusion.1), channel_id=1, source_target_pairs={{0,2},{1,3},{2,0},{3,1},{4,6},{5,7},{6,4},{7,5},{8,10},{9,11},{10,... | collective-permute-start | bytes 393224 | tf_op jit(solution)/shard_map/ppermute | solution.py:76
  85.3 6.7 %collective-permute-start.19 = (bf16[256,256]{1,0:T(8,128)(2,1)S(1)}, bf16[256,256]{1,0:T(8,128)(2,1)S(1)}, u32[]{:S(2)}, u32[]{:S(2)}) collective-permute-start(bf16[256,256]{1,0:T(8,128)(2,1)S(1)} %convolution_convert_fusion), channel_id=1, source_target_pairs={{0,3},{1,0},{2,1},{3,2},{4,7},{5,4},{6,5},{7,6},{8,11},{9,8},{10,9... | collective-permute-start | bytes 393224 | tf_op jit(solution)/shard_map/ppermute | solution.py:76
  86.0 5.9 %collective-permute-start.17 = (bf16[256,256]{1,0:T(8,128)(2,1)S(1)}, bf16[256,256]{1,0:T(8,128)(2,1)S(1)}, u32[]{:S(2)}, u32[]{:S(2)}) collective-permute-start(bf16[256,256]{1,0:T(8,128)(2,1)S(1)} %convolution_convert_fusion.2), channel_id=1, source_target_pairs={{0,1},{1,2},{2,3},{3,0},{4,5},{5,6},{6,7},{7,4},{8,9},{9,10},{10,1... | collective-permute-start | bytes 393224 | tf_op jit(solution)/shard_map/ppermute | solution.py:76
  93.0 5.4 %collective-permute-start.22 = (bf16[256,256]{1,0:T(8,128)(2,1)S(1)}, bf16[256,256]{1,0:T(8,128)(2,1)S(1)}, u32[]{:S(2)}, u32[]{:S(2)}) collective-permute-start(bf16[256,256]{1,0:T(8,128)(2,1)S(1)} %get-tuple-element.112), channel_id=1, source_target_pairs={{0,1},{1,2},{2,3},{3,0},{4,5},{5,6},{6,7},{7,4},{8,9},{9,10},{10,1... | collective-permute-start | bytes 393224 | tf_op jit(solution)/shard_map/ppermute | solution.py:76
  94.5 8.5 %collective-permute-start.21 = (bf16[256,256]{1,0:T(8,128)(2,1)S(1)}, bf16[256,256]{1,0:T(8,128)(2,1)S(1)}, u32[]{:S(2)}, u32[]{:S(2)}) collective-permute-start(bf16[256,256]{1,0:T(8,128)(2,1)S(1)} %get-tuple-element.112), channel_id=1, source_target_pairs={{0,2},{1,3},{2,0},{3,1},{4,6},{5,7},{6,4},{7,5},{8,10},{9,11},{10,... | collective-permute-start | bytes 393224 | tf_op jit(solution)/shard_map/ppermute | solution.py:76
  97.1 6.2 %collective-permute-start.20 = (bf16[256,256]{1,0:T(8,128)(2,1)S(1)}, bf16[256,256]{1,0:T(8,128)(2,1)S(1)}, u32[]{:S(2)}, u32[]{:S(2)}) collective-permute-start(bf16[256,256]{1,0:T(8,128)(2,1)S(1)} %get-tuple-element.112), channel_id=1, source_target_pairs={{0,3},{1,0},{2,1},{3,2},{4,7},{5,4},{6,5},{7,6},{8,11},{9,8},{10,9... | collective-permute-start | bytes 393224 | tf_op jit(solution)/shard_map/ppermute | solution.py:76
  103.8 4.2 %collective-permute-start.23 = (f32[520,256]{1,0:T(8,128)S(1)}, f32[520,256]{1,0:T(8,128)S(1)}, u32[]{:S(2)}, u32[]{:S(2)}) collective-permute-start(f32[520,256]{1,0:T(8,128)S(1)} %select_maximum_fusion), channel_id=1, source_target_pairs={{0,4},{4,0},{8,12},{12,8},{16,20},{20,16},{24,28},{28,24},{32,36},... | collective-permute-start | bytes 1597448 | tf_op jit(solution)/shard_map/ppermute | solution.py:72
  105.7 1.4 collective-permute-start.24
  113.7 11.8 %copy-start.16 = (bf16[1104,256]{1,0:T(8,128)(2,1)S(1)}, bf16[1104,256]{1,0:T(8,128)(2,1)}, u32[]{:S(2)}) copy-start(bf16[1104,256]{1,0:T(8,128)(2,1)} %get-tuple-element.83) | copy-start | bytes 1695748
  113.7 16.6 %collective-permute-start.25 = (bf16[1104,256]{1,0:T(8,128)(2,1)}, bf16[1104,256]{1,0:T(8,128)(2,1)S(1)}, u32[]{:S(2)}, u32[]{:S(2)}) collective-permute-start(bf16[1104,256]{1,0:T(8,128)(2,1)} %get-tuple-element.82), channel_id=1, source_target_pairs={{4,36},{12,44},{20,52},{28,60},{36,68},{44,76},{52,84},{60,92},{68... | collective-permute-start | bytes 1695752 | tf_op jit(solution)/shard_map/ppermute | solution.py:64
  125.5 4.8 %copy-start.14 = (bf16[1104,256]{1,0:T(8,128)(2,1)S(1)}, bf16[1104,256]{1,0:T(8,128)(2,1)}, u32[]{:S(2)}) copy-start(bf16[1104,256]{1,0:T(8,128)(2,1)} %get-tuple-element.80) | copy-start | bytes 1695748
  125.5 4.8 %copy-start.15 = (bf16[1104,256]{1,0:T(8,128)(2,1)S(1)}, bf16[1104,256]{1,0:T(8,128)(2,1)}, u32[]{:S(2)}) copy-start(bf16[1104,256]{1,0:T(8,128)(2,1)} %get-tuple-element.81) | copy-start | bytes 1695748
  126.7 10.1 %collective-permute-start.27 = (bf16[1104,256]{1,0:T(8,128)(2,1)S(1)}, bf16[1104,256]{1,0:T(8,128)(2,1)S(1)}, u32[]{:S(2)}, u32[]{:S(2)}) collective-permute-start(bf16[1104,256]{1,0:T(8,128)(2,1)S(1)} %broadcast_select_fusion), channel_id=1, source_target_pairs={{0,24},{4,228},{8,0},{12,236},{16,8},{20,244},{24,16},{28,252},{32... | collective-permute-start | bytes 1695752 | tf_op jit(solution)/shard_map/ppermute | solution.py:64
  130.3 10.6 %copy-start.13 = (bf16[1104,256]{1,0:T(8,128)(2,1)S(1)}, bf16[1104,256]{1,0:T(8,128)(2,1)}, u32[]{:S(2)}) copy-start(bf16[1104,256]{1,0:T(8,128)(2,1)} %get-tuple-element.88) | copy-start | bytes 1695748
  130.5 12.1 %copy-start.12 = (bf16[1104,256]{1,0:T(8,128)(2,1)S(1)}, bf16[1104,256]{1,0:T(8,128)(2,1)}, u32[]{:S(2)}) copy-start(bf16[1104,256]{1,0:T(8,128)(2,1)} %get-tuple-element.87) | copy-start | bytes 1695748
  130.5 10.3 %collective-permute-start.26 = (bf16[1104,256]{1,0:T(8,128)(2,1)S(1)}, bf16[1104,256]{1,0:T(8,128)(2,1)S(1)}, u32[]{:S(2)}, u32[]{:S(2)}) collective-permute-start(bf16[1104,256]{1,0:T(8,128)(2,1)S(1)} %fusion.3), channel_id=1, source_target_pairs={{0,8},{4,36},{8,16},{12,44},{16,24},{20,52},{24,0},{28,60},{32,40}... | collective-permute-start | bytes 1695752 | tf_op jit(solution)/shard_map/ppermute | solution.py:64
  141.0 11.5 %copy-start.11 = (bf16[1104,256]{1,0:T(8,128)(2,1)S(1)}, bf16[1104,256]{1,0:T(8,128)(2,1)}, u32[]{:S(2)}) copy-start(bf16[1104,256]{1,0:T(8,128)(2,1)} %get-tuple-element.92) | copy-start | bytes 1695748
  141.0 8.8 %collective-permute-start.29 = (bf16[1104,256]{1,0:T(8,128)(2,1)S(1)}, bf16[1104,256]{1,0:T(8,128)(2,1)S(1)}, u32[]{:S(2)}, u32[]{:S(2)}) collective-permute-start(bf16[1104,256]{1,0:T(8,128)(2,1)S(1)} %add_convert_fusion.2), channel_id=1, source_target_pairs={{0,24},{4,228},{8,0},{12,236},{16,8},{20,244},{24,16},{28,252},{32... | collective-permute-start | bytes 1695752 | tf_op jit(solution)/shard_map/ppermute | solution.py:64
  142.8 10.1 %copy-start.10 = (bf16[1104,256]{1,0:T(8,128)(2,1)S(1)}, bf16[1104,256]{1,0:T(8,128)(2,1)}, u32[]{:S(2)}) copy-start(bf16[1104,256]{1,0:T(8,128)(2,1)} %get-tuple-element.93) | copy-start | bytes 1695748
  142.8 9.8 %collective-permute-start.28 = (bf16[1104,256]{1,0:T(8,128)(2,1)S(1)}, bf16[1104,256]{1,0:T(8,128)(2,1)S(1)}, u32[]{:S(2)}, u32[]{:S(2)}) collective-permute-start(bf16[1104,256]{1,0:T(8,128)(2,1)S(1)} %add_convert_fusion.3), channel_id=1, source_target_pairs={{0,8},{4,36},{8,16},{12,44},{16,24},{20,52},{24,0},{28,60},{32,40}... | collective-permute-start | bytes 1695752 | tf_op jit(solution)/shard_map/ppermute | solution.py:64
  152.7 3.0 %copy-start.1 = (bf16[1104,256]{1,0:T(8,128)(2,1)S(1)}, bf16[1104,256]{1,0:T(8,128)(2,1)}, u32[]{:S(2)}) copy-start(bf16[1104,256]{1,0:T(8,128)(2,1)} %get-tuple-element.79.h0) | copy-start | bytes 1695748
  152.7 3.0 %copy-start.2 = (s32[8,256]{1,0:T(8,128)S(1)}, s32[8,256]{1,0:T(8,128)}, u32[]{:S(2)}) copy-start(s32[8,256]{1,0:T(8,128)} %shard_map.114.lists) | copy-start | bytes 24580
  152.7 11.2 %collective-permute-start.30 = (bf16[1104,256]{1,0:T(8,128)(2,1)S(1)}, bf16[1104,256]{1,0:T(8,128)(2,1)S(1)}, u32[]{:S(2)}, u32[]{:S(2)}) collective-permute-start(bf16[1104,256]{1,0:T(8,128)(2,1)S(1)} %add_convert_fusion.1), channel_id=1, source_target_pairs={{0,8},{4,36},{8,16},{12,44},{16,24},{20,52},{24,0},{28,60},{32,40}... | collective-permute-start | bytes 1695752 | tf_op jit(solution)/shard_map/ppermute | solution.py:64
  153.0 10.9 %collective-permute-start.31 = (bf16[1104,256]{1,0:T(8,128)(2,1)S(1)}, bf16[1104,256]{1,0:T(8,128)(2,1)S(1)}, u32[]{:S(2)}, u32[]{:S(2)}) collective-permute-start(bf16[1104,256]{1,0:T(8,128)(2,1)S(1)} %add_convert_fusion), channel_id=1, source_target_pairs={{0,24},{4,228},{8,0},{12,236},{16,8},{20,244},{24,16},{28,252},{32... | collective-permute-start | bytes 1695752 | tf_op jit(solution)/shard_map/ppermute | solution.py:64
  155.8 8.1 %copy-start = (bf16[1104,256]{1,0:T(8,128)(2,1)S(1)}, bf16[1104,256]{1,0:T(8,128)(2,1)}, u32[]{:S(2)}) copy-start(bf16[1104,256]{1,0:T(8,128)(2,1)} %get-tuple-element.91.h1) | copy-start | bytes 1695748
  156.7 1.4 collective-permute-start.32
  157.4 0.7 collective-permute-start.33
  164.2 9.0 %collective-permute-start.34 = (bf16[288,256]{1,0:T(8,128)(2,1)S(1)}, bf16[288,256]{1,0:T(8,128)(2,1)S(1)}, u32[]{:S(2)}, u32[]{:S(2)}) collective-permute-start(bf16[288,256]{1,0:T(8,128)(2,1)S(1)} %get-tuple-element.102), channel_id=1, source_target_pairs={{0,32},{4,12},{8,40},{12,20},{16,48},{20,28},{24,56},{28,4},{32,64... | collective-permute-start | bytes 442376 | tf_op jit(solution)/shard_map/ppermute | solution.py:64
  171.1 4.0 %collective-permute-start.35 = (bf16[288,256]{1,0:T(8,128)(2,1)S(1)}, bf16[288,256]{1,0:T(8,128)(2,1)S(1)}, u32[]{:S(2)}, u32[]{:S(2)}) collective-permute-start(bf16[288,256]{1,0:T(8,128)(2,1)S(1)} %get-tuple-element.103), channel_id=1, source_target_pairs={{0,224},{4,28},{8,232},{12,4},{16,240},{20,12},{24,248},{28,20},{3... | collective-permute-start | bytes 442376 | tf_op jit(solution)/shard_map/ppermute | solution.py:64
  171.1 5.5 %collective-permute-start.36 = (bf16[288,256]{1,0:T(8,128)(2,1)S(1)}, bf16[288,256]{1,0:T(8,128)(2,1)S(1)}, u32[]{:S(2)}, u32[]{:S(2)}) collective-permute-start(bf16[288,256]{1,0:T(8,128)(2,1)S(1)} %get-tuple-element.104), channel_id=1, source_target_pairs={{0,64},{4,20},{8,72},{12,28},{16,80},{20,4},{24,88},{28,12},{32,96... | collective-permute-start | bytes 442376 | tf_op jit(solution)/shard_map/ppermute | solution.py:64
  178.0 11.0 %collective-permute-start.37 = (f32[1,256]{1,0:T(1,128)S(1)}, f32[1,256]{1,0:T(1,128)S(1)}, u32[]{:S(2)}, u32[]{:S(2)}) collective-permute-start(f32[1,256]{1,0:T(1,128)S(1)} %get-tuple-element.107), channel_id=1, source_target_pairs={{0,4},{8,12},{16,20},{24,28},{32,36},{40,44},{48,52},{56,60},{64,6... | collective-permute-start | bytes 3080 | tf_op jit(solution)/shard_map/ppermute | solution.py:631
  (3 other events, 2.3 us)
